TPU v7x, 512 devices: a whole 4x4x16 slice. The times are simulated.
512 devices in a mesh: row: 16 (over z_lo, x), col: 32 (over z_hi, y, core).
Axes of the slice: x: 4, y: 4, z: 16 (z_hi: 4, z_lo: 4; z = z_hi * 4 + z_lo), core: 2. Of those that a mesh axis runs over, the one named last changes fastest.
Arguments:
- features: bfloat16 [65536, 256], P(('col', 'row')), may hold values from -6 to 6
- weight: bfloat16 [256, 256], replicated, may hold values from -0.375 to 0.375
- tile_values: bfloat16 [16, 32, 128, 128, 128], P('row', 'col'), as said below
- tile_rows: int32 [16, 32, 128], P('row', 'col'), may hold values from 0 to 31, as said below
- tile_cols: int32 [16, 32, 128], P('row', 'col'), may hold values from 0 to 15, as said below
- tile_count: int32 [16, 32], P('row', 'col'), may hold values from 16 to 128, as said below
- cotangent: bfloat16 [65536, 256], P(('row', 'col')), may hold values from -6 to 6
Outputs:
- activated: bfloat16 [65536, 256], P(('row', 'col'))
- grad_features: bfloat16 [65536, 256], P(('col', 'row'))
- grad_weight: float32 [256, 256], replicated
Inputs may be any that keep to these rules, and one draw needn't show every extreme that they name: `tile_count`: the number of live slots of each block: its slots below this number hold the block's nonzero tiles, the others are padding; at least one block has exactly 128. `tile_rows`: the 128 slots of one block name distinct (tile row, tile column) pairs. `tile_cols`: the 128 slots of one block name distinct (tile row, tile column) pairs. `tile_values`: edge weights are nonnegative; most entries of a tile are zero.
All inputs are finite; a program needn't handle non-finite values.
Results may differ from a plain program's by a relative error of at most 0.028.
Values may be sent and summed in bfloat16 or wider, within the bound.
No kernel may reach another device: no remote copies, remote signals or barrier semaphores. Data moves between devices by JAX's collectives and lax.ppermute only.
A program may use at most 64 MiB of HBM per device.

v0:
```python
import math

import jax
import jax.numpy as jnp
from jax import lax
from jax.sharding import PartitionSpec as P


def silu_slope(pre_act):
    sigmoid_part = jax.nn.sigmoid(pre_act)
    return sigmoid_part * (1.0 + pre_act * (1.0 - sigmoid_part))


def forward_products(source_tiles, slot_values, slot_rows, slot_cols, live_count, row_tiles):
    slot_total, tile_size = (slot_values.shape[0], slot_values.shape[1])
    feature_width = source_tiles.shape[-1]
    per_round = slot_total // 4

    def forward_one_round(round_index, running):
        start_slot = round_index * per_round
        round_values = lax.dynamic_slice_in_dim(slot_values, start_slot, per_round, 0)
        round_rows = lax.dynamic_slice_in_dim(slot_rows, start_slot, per_round, 0)
        round_cols = lax.dynamic_slice_in_dim(slot_cols, start_slot, per_round, 0)
        in_use = (start_slot + jnp.arange(per_round, dtype=jnp.int32) < live_count).astype(
            jnp.float32
        )
        gathered = source_tiles[round_cols]
        tile_products = jnp.einsum(
            "smk,skf->smf", round_values, gathered, preferred_element_type=jnp.float32
        )
        return running.at[round_rows].add(tile_products * in_use[:, None, None])

    round_count = (live_count + per_round - 1) // per_round
    zero_block = jnp.zeros((row_tiles, tile_size, feature_width), jnp.float32)
    return lax.fori_loop(0, round_count, forward_one_round, zero_block)


def backward_products(grad_tiles, slot_values, slot_rows, slot_cols, live_count, col_tiles):
    slot_total, tile_size = (slot_values.shape[0], slot_values.shape[1])
    feature_width = grad_tiles.shape[-1]
    per_round = slot_total // 4

    def backward_one_round(round_index, running):
        start_slot = round_index * per_round
        round_values = lax.dynamic_slice_in_dim(slot_values, start_slot, per_round, 0)
        round_rows = lax.dynamic_slice_in_dim(slot_rows, start_slot, per_round, 0)
        round_cols = lax.dynamic_slice_in_dim(slot_cols, start_slot, per_round, 0)
        in_use = (start_slot + jnp.arange(per_round, dtype=jnp.int32) < live_count).astype(
            jnp.float32
        )
        gathered = grad_tiles[round_rows]
        tile_products = jnp.einsum(
            "smk,smf->skf", round_values, gathered, preferred_element_type=jnp.float32
        )
        return running.at[round_cols].add(tile_products * in_use[:, None, None])

    round_count = (live_count + per_round - 1) // per_round
    zero_block = jnp.zeros((col_tiles, tile_size, feature_width), jnp.float32)
    return lax.fori_loop(0, round_count, backward_one_round, zero_block)


def shards(features, weight, tile_values, tile_rows, tile_cols, tile_count, cotangent):
    node_dev, feature_width = features.shape
    tile_size = tile_values.shape[-1]
    row_devices = lax.axis_size("row")
    col_devices = lax.axis_size("col")
    row_span = node_dev * col_devices
    col_span = node_dev * row_devices
    row_tiles = row_span // tile_size
    col_tiles = col_span // tile_size
    grad_scale = 1.0 / math.sqrt(node_dev * row_devices * col_devices)
    slot_values = tile_values[0, 0]
    slot_rows = tile_rows[0, 0]
    slot_cols = tile_cols[0, 0]
    live_count = tile_count[0, 0]
    column_block = lax.all_gather(features, "row", axis=0, tiled=True)
    source_tiles = column_block.reshape(col_tiles, tile_size, feature_width)
    partial_value = forward_products(
        source_tiles, slot_values, slot_rows, slot_cols, live_count, row_tiles
    )
    partial_value = partial_value.reshape(row_span, feature_width)
    aggregated = lax.psum_scatter(
        partial_value.astype(jnp.bfloat16), "col", scatter_dimension=0, tiled=True
    )
    pre_act = jnp.dot(aggregated, weight, preferred_element_type=jnp.float32)
    activated = jax.nn.silu(pre_act).astype(jnp.bfloat16)
    grad_pre = (cotangent.astype(jnp.float32) * silu_slope(pre_act)).astype(jnp.bfloat16)
    weight_part = jnp.einsum("nk,nf->kf", aggregated, grad_pre, preferred_element_type=jnp.float32)
    grad_weight = lax.psum(weight_part, ("row", "col")) * grad_scale
    grad_block = lax.all_gather(grad_pre, "col", axis=0, tiled=True)
    grad_tiles = grad_block.reshape(row_tiles, tile_size, feature_width)
    column_part = backward_products(
        grad_tiles, slot_values, slot_rows, slot_cols, live_count, col_tiles
    )
    column_part = column_part.reshape(col_span, feature_width)
    spread = lax.psum_scatter(
        column_part.astype(jnp.bfloat16), "row", scatter_dimension=0, tiled=True
    )
    grad_features = jnp.einsum(
        "nk,fk->nf", spread, weight, preferred_element_type=jnp.float32
    ).astype(jnp.bfloat16)
    return (activated, grad_features, grad_weight)


def solution(mesh):
    return jax.shard_map(
        shards,
        mesh=mesh,
        in_specs=(
            P(("col", "row"), None),
            P(),
            P("row", "col", None, None, None),
            P("row", "col", None),
            P("row", "col", None),
            P("row", "col"),
            P(("row", "col"), None),
        ),
        out_specs=(P(("row", "col"), None), P(("col", "row"), None), P()),
        check_vma=False,
    )
```

profile of v0, /device:TPU:1, one launch (start us, length us, event | category | flops | bytes accessed | tf_op | source)
XLA Modules:
  0.0 908.6 jit_solution(17715207225531856932)
XLA Ops:
  7.2 0.0 copy-start
  7.2 0.0 all-gather.3.cloned.1.call-start
  7.2 0.7 all-gather.3.cloned.1.call-update
  7.9 0.0 reduce-scatter.3.cloned.1.call-start
  8.6 83.1 %all-gather.3.cloned.1.call-done = bf16[2048,256]{1,0:T(8,128)(2,1)} async-done(((bf16[128,256]{1,0:T(8,128)(2,1)}), bf16[2048,256]{1,0:T(8,128)(2,1)}) %all-gather.3.cloned.1.call-update) | async-done | bytes 1048592 | tf_op jit(solution)/shard_map/all_gather | solution.py:76
  91.7 2.4 broadcast_in_dim.20
  94.2 30.7 %while.20 = (s32[]{:T(128)}, f32[32,128,256]{2,1,0:T(8,128)}, s32[]{:T(128)}, s32[128]{0:T(128)S(1)}, bf16[128,128,128]{2,1,0:T(8,128)(2,1)}, /*index=5*/s32[128...) while((s32[]{:T(128)}, f32[32,128,256]{2,1,0:T(8,128)}, ...), condition=%wide.region_2.3_spmd, body=%wide.region_0.2_spmd.sunk | while | flops 270533920 | bytes 24122684 | solution.py:35
  94.2 0.1 compare_select_fusion.6
  94.3 0.7 gather_fusion
  95.0 0.7 compare_convert_fusion.4
  95.7 3.9 convolution_multiply_fusion.4
  99.5 10.0 %scatter_fusion = f32[32,128,256]{2,1,0:T(8,128)} fusion(f32[32,128,256]{2,1,0:T(8,128)} %get-tuple-element.258, s32[32]{0:T(128)S(1)} %get-tuple-element.233, f32[32,128,256]{2,1,0:T(8,128)} %convolution_multiply_fusion.4), kind=kCustom, calls=%fused_computation.2.clone.1 | custom fusion | flops 1048576 | bytes 12583040 | tf_op jit(solution)/shard_map/while/body/scatter-add | solution.py:31
  109.5 0.1 compare_select_fusion.6
  109.6 0.7 gather_fusion
  110.3 0.7 compare_convert_fusion.4
  111.0 3.9 convolution_multiply_fusion.4
  114.9 10.0 %scatter_fusion = f32[32,128,256]{2,1,0:T(8,128)} fusion(f32[32,128,256]{2,1,0:T(8,128)} %get-tuple-element.258, s32[32]{0:T(128)S(1)} %get-tuple-element.233, f32[32,128,256]{2,1,0:T(8,128)} %convolution_multiply_fusion.4), kind=kCustom, calls=%fused_computation.2.clone.1 | custom fusion | flops 1048576 | bytes 12583040 | tf_op jit(solution)/shard_map/while/body/scatter-add | solution.py:31
  124.9 3.8 convert_element_type.38
  128.7 0.0 reduce-scatter.3.cloned.1.call-update
  128.8 0.0 all-gather.5.cloned.1.call-start
  128.8 158.7 %reduce-scatter.3.cloned.1.call-done = bf16[128,256]{1,0:T(8,128)(2,1)} async-done(((bf16[4096,256]{1,0:T(8,128)(2,1)}), bf16[128,256]{1,0:T(8,128)(2,1)}) %reduce-scatter.3.cloned.1.call-update) | async-done | bytes 65552 | tf_op jit(solution)/shard_map/reduce_scatter | solution.py:82
  287.5 1.7 multiply_convert_fusion
  289.2 0.0 all-gather.5.cloned.1.call-update
  289.2 0.0 all-reduce.2.cloned.1.call-start
  289.3 0.0 copy-start.2
  289.3 6.4 copy.10
  295.7 0.9 fusion.4
  296.6 0.0 all-reduce.2.cloned.1.call-update
  296.7 0.0 reduce-scatter.5.cloned.1.call-start
  296.7 68.5 %all-gather.5.cloned.1.call-done = bf16[4096,256]{1,0:T(8,128)(2,1)} async-done(((bf16[128,256]{1,0:T(8,128)(2,1)}), bf16[4096,256]{1,0:T(8,128)(2,1)}) %all-gather.5.cloned.1.call-update) | async-done | bytes 2097168 | tf_op jit(solution)/shard_map/all_gather | solution.py:90
  365.2 0.2 broadcast_in_dim.21
  365.4 30.9 %while.21 = (s32[]{:T(128)}, f32[16,128,256]{2,1,0:T(8,128)S(1)}, s32[]{:T(128)}, s32[128]{0:T(128)S(1)}, bf16[128,128,128]{1,2,0:T(8,128)(2,1)}, /*index=5*/s32...) while((s32[]{:T(128)}, f32[16,128,256]{2,1,0:T(8,128)S(1)}, ...), condition=%wide.region_6.7_spmd, body=%wide.region_4.6_spmd.sunk | while | flops 270533920 | bytes 24122684 | solution.py:59
  365.4 0.1 compare_select_fusion.7
  365.5 3.6 gather_fusion.1
  369.1 0.6 compare_convert_fusion.5
  369.7 4.6 convolution_multiply_fusion.5
  374.3 6.5 scatter_fusion.1
  380.8 0.1 compare_select_fusion.7
  380.9 3.6 gather_fusion.1
  384.5 0.6 compare_convert_fusion.5
  385.2 4.6 convolution_multiply_fusion.5
  389.8 6.5 scatter_fusion.1
  396.3 1.1 convert_element_type.43
  397.4 0.0 reduce-scatter.5.cloned.1.call-update
  397.4 423.9 %all-reduce.2.cloned.1.call-done = f32[256,256]{1,0:T(8,128)} async-done(((f32[256,256]{1,0:T(8,128)}), f32[256,256]{1,0:T(8,128)}) %all-reduce.2.cloned.1.call-update) | async-done | bytes 262160 | tf_op jit(solution)/shard_map/psum | solution.py:89
  821.4 1.7 broadcast_multiply_fusion
  823.0 77.3 %reduce-scatter.5.cloned.1.call-done = bf16[128,256]{1,0:T(8,128)(2,1)} async-done(((bf16[2048,256]{1,0:T(8,128)(2,1)}), bf16[128,256]{1,0:T(8,128)(2,1)}) %reduce-scatter.5.cloned.1.call-update) | async-done | bytes 65552 | tf_op jit(solution)/shard_map/reduce_scatter | solution.py:96
  900.4 1.7 convolution_convert_fusion
  (16 shorter events, 0.0 us)
Async XLA Ops:
  7.2 280.3 %copy-start = (bf16[256,256]{1,0:T(8,128)(2,1)S(1)}, bf16[256,256]{1,0:T(8,128)(2,1)}, u32[]{:S(2)}) copy-start(bf16[256,256]{1,0:T(8,128)(2,1)} %param.12) | copy-start | bytes 393220
  7.2 87.0 %copy-start.4 = (s32[1,1,128]{2,1,0:T(1,128)S(1)}, s32[1,1,128]{2,1,0:T(1,128)}, u32[]{:S(2)}) copy-start(s32[1,1,128]{2,1,0:T(1,128)} %param.14) | copy-start | bytes 1540
  7.2 87.0 %copy-start.5 = (s32[1,1,128]{2,1,0:T(1,128)S(1)}, s32[1,1,128]{2,1,0:T(1,128)}, u32[]{:S(2)}) copy-start(s32[1,1,128]{2,1,0:T(1,128)} %param.15) | copy-start | bytes 1540
  7.2 84.5 %all-gather.3.cloned.1.call-start = ((), (), s32[]{:S(2)}) async-start(), calls=%async_computation.2 | async-start | bytes 1114112 | tf_op jit(solution)/shard_map/all_gather | solution.py:76
  7.9 279.5 %reduce-scatter.3.cloned.1.call-start = ((), (), s32[]{:S(2)}) async-start(), calls=%async_computation.3 | async-start | bytes 2162688 | tf_op jit(solution)/shard_map/reduce_scatter | solution.py:82
  91.7 2.5 copy-start.1
  124.9 162.6 %copy-start.6 = (bf16[128,256]{1,0:T(8,128)(2,1)S(1)}, bf16[128,256]{1,0:T(8,128)(2,1)}, u32[]{:S(2)}) copy-start(bf16[128,256]{1,0:T(8,128)(2,1)} %param.17) | copy-start | bytes 196612
  128.8 236.4 %all-gather.5.cloned.1.call-start = ((), (), s32[]{:S(2)}) async-start(), calls=%async_computation.4 | async-start | bytes 2162688 | tf_op jit(solution)/shard_map/all_gather | solution.py:90
  289.2 532.2 %all-reduce.2.cloned.1.call-start = ((), (), s32[]{:S(2)}) async-start(), calls=%async_computation.6 | async-start | bytes 524288 | tf_op jit(solution)/shard_map/psum | solution.py:89
  289.3 6.4 copy-start.2
  289.3 6.4 copy-start.3
  296.7 603.7 %reduce-scatter.5.cloned.1.call-start = ((), (), s32[]{:S(2)}) async-start(), calls=%async_computation.5 | async-start | bytes 1114112 | tf_op jit(solution)/shard_map/reduce_scatter | solution.py:96
Sparse Core Ops, SparseCore 0:
  10.1 81.5 all-gather.2
  128.9 158.5 reduce-scatter.2
  291.2 73.9 all-gather.4
  371.1 450.2 all-reduce.1
  824.3 76.0 reduce-scatter.4
where the time goes:
time: 920 us; the launch traced here: 909 us
  waiting for transfers between devices  812 us (88%)
  other arithmetic  42.6 us (5%)
  matrix products  21.2 us (2%)
  local copies, waits for them, and re-layouts  17.7 us (2%)
  between operations  14.5 us (2%)
    psum x1, waiting for transfers between devices, shards(): grad_weight = lax.psum(weight_part, ('row', 'col')) * grad_scale  424 us
    reduce_scatter x1, waiting for transfers between devices, shards(): lax.psum_scatter(partial_value.astype(jnp.bfloat16), 'col', scatter_dimen...  159 us
    all_gather x1, waiting for transfers between devices, shards(): column_block = lax.all_gather(features, 'row', axis=0, tiled=True)  83.1 us
    reduce_scatter x1, waiting for transfers between devices, shards(): lax.psum_scatter(column_part.astype(jnp.bfloat16), 'row', scatter_dimensi...  77.3 us
    all_gather x1, waiting for transfers between devices, shards(): grad_block = lax.all_gather(grad_pre, 'col', axis=0, tiled=True)  68.5 us
    scatter-add x2, other arithmetic, forward_one_round(): return running.at[round_rows].add(tile_products * in_use[:, None, None])  20.1 us
  transfers between devices with their start and end apart: 5, of which 5 were waited for; matrix products, arithmetic and copies ran while one was open for 5% of the time, Pallas kernels for 0%

commit v1 on v0

v1 whole, which is shorter than its diff:
```python
import functools
import math

import jax
import jax.numpy as jnp
from jax import lax
from jax.experimental import pallas as pl
from jax.experimental.pallas import tpu as pltpu
from jax.sharding import PartitionSpec as P

TILE = 128
RING = 4
HALF = 16
UNROLL = 4
LIST = 192
VMEM_LIMIT = 24 * 1024 * 1024


def col_perm(move):
    pairs = []
    for c in range(32):
        zh, y, core = move(c // 8, (c // 2) % 4, c % 2)
        pairs.append((c, (zh % 4) * 8 + (y % 4) * 2 + core % 2))
    return pairs


def row_perm(move):
    pairs = []
    for r in range(16):
        zl, x = move(r // 4, r % 4)
        pairs.append((r, (zl % 4) * 4 + x % 4))
    return pairs


def send_zh(v, k):
    return lax.ppermute(v, "col", col_perm(lambda zh, y, c: (zh + k, y, c)))


def send_y(v, k):
    return lax.ppermute(v, "col", col_perm(lambda zh, y, c: (zh, y + k, c)))


def send_core(v):
    return lax.ppermute(v, "col", col_perm(lambda zh, y, c: (zh, y, c + 1)))


def send_zl(v, k):
    return lax.ppermute(v, "row", row_perm(lambda zl, x: (zl + k, x)))


def send_x(v, k):
    return lax.ppermute(v, "row", row_perm(lambda zl, x: (zl, x + k)))


def swap_zh(v, k):
    return lax.ppermute(v, "col", col_perm(lambda zh, y, c: (zh ^ k, y, c)))


def swap_y(v, k):
    return lax.ppermute(v, "col", col_perm(lambda zh, y, c: (zh, y ^ k, c)))


def swap_zl(v, k):
    return lax.ppermute(v, "row", row_perm(lambda zl, x: (zl ^ k, x)))


def swap_x(v, k):
    return lax.ppermute(v, "row", row_perm(lambda zl, x: (zl, x ^ k)))


def smem():
    return pl.BlockSpec(memory_space=pltpu.SMEM)


def vmem():
    return pl.BlockSpec(memory_space=pltpu.VMEM)


def plan_kernel(where, rows, cols, count, slots, sources, dests, groups, head, link):
    zl, x, zh, y, core = (where[i] for i in range(5))

    def clear(i, _):
        head[i] = -1
        return 0

    lax.fori_loop(0, 4 * HALF, clear, 0)

    def chain(s, _):
        r, c = rows[0, 0, s], cols[0, 0, s]
        mine = jnp.where((r & 1) == core, 1, 0)
        forward = mine * HALF + ((((r >> 1) & 3) - y) & 3) * 4 + (((r >> 3) - zh) & 3)
        backward = (3 - mine) * HALF + (((c & 3) - x) & 3) * 4 + (((c >> 2) - zl) & 3)
        link[0, s] = head[forward]
        head[forward] = s
        link[1, s] = head[backward]
        head[backward] = s
        return 0

    lax.fori_loop(0, count[0, 0], chain, 0)

    for q in range(4):
        way = q // 2

        def segment(d, pos, q=q, way=way):
            def more(state):
                return state[0] >= 0

            def emit(state):
                s, at = state
                r, c = rows[0, 0, s], cols[0, 0, s]
                if way == 0:
                    source = ((x - (c & 3)) & 3) * 4 + ((zl - (c >> 2)) & 3)
                else:
                    source = ((y - ((r >> 1) & 3)) & 3) * 4 + ((zh - (r >> 3)) & 3)
                slots[q, at] = s
                sources[q, at] = source
                dests[q, at >> 1] = d
                return link[way, s], at + 1

            _, at = lax.while_loop(more, emit, (head[q * HALF + d], pos))

            @pl.when((at & 1) == 1)
            def _():
                slots[q, at] = 0
                sources[q, at] = HALF

            return at + (at & 1)

        total = lax.fori_loop(0, HALF, segment, 0)

        for i in range(2 * UNROLL):
            slots[q, total + i] = 0
            sources[q, total + i] = HALF
            dests[q, (total >> 1) + (i >> 1)] = 0
        groups[q] = ((total >> 1) + UNROLL - 1) // UNROLL


def make_plan(where, rows, cols, count):
    i32 = jnp.int32
    return pl.pallas_call(
        plan_kernel,
        out_shape=(
            jax.ShapeDtypeStruct((4, LIST), i32),
            jax.ShapeDtypeStruct((4, LIST), i32),
            jax.ShapeDtypeStruct((4, LIST), i32),
            jax.ShapeDtypeStruct((4,), i32),
        ),
        in_specs=[smem()] * 4,
        out_specs=(smem(),) * 4,
        scratch_shapes=[pltpu.SMEM((4 * HALF,), i32), pltpu.SMEM((2, TILE), i32)],
        cost_estimate=pl.CostEstimate(flops=0, bytes_accessed=16 * 1024 * 1024, transcendentals=0),
        name="plan",
    )(where, rows, cols, count)


def turn_kernel(count, v, out):
    def step(i, _):
        for u in range(4):
            out[4 * i + u] = v[0, 0, 4 * i + u].T
        return 0

    lax.fori_loop(0, (count[0, 0] + 3) // 4, step, 0)


def turn_tiles(count, tile_values):
    return pl.pallas_call(
        turn_kernel,
        out_shape=jax.ShapeDtypeStruct(tile_values.shape[2:], tile_values.dtype),
        in_specs=[smem(), vmem()],
        out_specs=vmem(),
        compiler_params=pltpu.CompilerParams(vmem_limit_bytes=VMEM_LIMIT),
        cost_estimate=pl.CostEstimate(flops=0, bytes_accessed=24 * 1024 * 1024, transcendentals=0),
        name="turn",
    )(count, tile_values)


def spmm_kernel(q, has_start, slots, sources, dests, groups, v, s0, s1, s2, s3, *rest):
    if has_start:
        start, out, held, acc = rest
    else:
        out, held, acc = rest
    for k, part in enumerate((s0, s1, s2, s3)):
        held[RING * k : RING * (k + 1)] = part[...]
    held[HALF] = jnp.zeros_like(held[HALF])
    if has_start:
        acc[...] = start[...]
    else:
        acc[...] = jnp.zeros_like(acc)

    def step(g, _):
        products = []
        for u in range(UNROLL):
            at = (g * UNROLL + u) * 2
            left = jnp.concatenate([v[slots[q, at]], v[slots[q, at + 1]]], axis=1)
            right = jnp.concatenate([held[sources[q, at]], held[sources[q, at + 1]]], axis=0)
            products.append(jnp.dot(left, right, preferred_element_type=jnp.float32))
        for u in range(UNROLL):
            d = dests[q, g * UNROLL + u]
            acc[d] = acc[d] + products[u]
        return 0

    lax.fori_loop(0, groups[q], step, 0)
    out[...] = acc[...].astype(out.dtype)


def spmm(q, plan, v, parts, start=None, dtype=jnp.bfloat16):
    width = parts[0].shape[-1]
    extra = () if start is None else (start,)
    return pl.pallas_call(
        functools.partial(spmm_kernel, q, start is not None),
        out_shape=jax.ShapeDtypeStruct((HALF, TILE, width), dtype),
        in_specs=[smem()] * 4 + [vmem()] * (5 + len(extra)),
        out_specs=vmem(),
        scratch_shapes=[
            pltpu.VMEM((HALF + 1, TILE, width), jnp.bfloat16),
            pltpu.VMEM((HALF, TILE, width), jnp.float32),
        ],
        compiler_params=pltpu.CompilerParams(vmem_limit_bytes=VMEM_LIMIT),
        cost_estimate=pl.CostEstimate(
            flops=2 * 64 * TILE * TILE * width, bytes_accessed=12 * 1024 * 1024, transcendentals=0
        ),
        name="spmm",
    )(*plan, v, *parts, *extra)


def mid_kernel(a0, a1, a2, a3, w, cot, act_out, grad_out, part_out):
    f32 = jnp.float32
    total = a0[...].astype(f32) + a1[...].astype(f32) + a2[...].astype(f32) + a3[...].astype(f32)
    aggregated = total.astype(jnp.bfloat16)
    pre = jnp.dot(aggregated, w[...], preferred_element_type=f32)
    s = jax.nn.sigmoid(pre)
    act_out[...] = (pre * s).astype(jnp.bfloat16)
    grad = (cot[...].astype(f32) * (s * (1.0 + pre * (1.0 - s)))).astype(jnp.bfloat16)
    grad_out[...] = grad
    part_out[...] = lax.dot_general(
        aggregated, grad, (((0,), (0,)), ((), ())), preferred_element_type=f32
    )


def middle(parts, w, cot):
    n, width = cot.shape
    return pl.pallas_call(
        mid_kernel,
        out_shape=(
            jax.ShapeDtypeStruct((n, width), jnp.bfloat16),
            jax.ShapeDtypeStruct((n, width), jnp.bfloat16),
            jax.ShapeDtypeStruct((width, width), jnp.float32),
        ),
        compiler_params=pltpu.CompilerParams(vmem_limit_bytes=VMEM_LIMIT),
        name="middle",
    )(*parts, w, cot)


def last_kernel(a0, a1, a2, a3, w, out):
    f32 = jnp.float32
    total = a0[...].astype(f32) + a1[...].astype(f32) + a2[...].astype(f32) + a3[...].astype(f32)
    spread = total.astype(jnp.bfloat16)
    out[...] = lax.dot_general(
        spread, w[...], (((1,), (1,)), ((), ())), preferred_element_type=f32
    ).astype(jnp.bfloat16)


def last(parts, w):
    return pl.pallas_call(
        last_kernel,
        out_shape=jax.ShapeDtypeStruct(parts[0].shape, jnp.bfloat16),
        compiler_params=pltpu.CompilerParams(vmem_limit_bytes=VMEM_LIMIT),
        name="last",
    )(*parts, w)


def add4(a, b, c, d):
    f32 = jnp.float32
    return (a.astype(f32) + b.astype(f32) + c.astype(f32) + d.astype(f32)).astype(jnp.bfloat16)


def halve(part, bit, swap):
    low, high = jnp.split(part, 2, axis=0)
    keep = jnp.where(bit == 1, high, low)
    give = jnp.where(bit == 1, low, high)
    return keep + swap(give)


def join(part, bit, swap):
    other = swap(part)
    low = jnp.where(bit == 1, other, part)
    high = jnp.where(bit == 1, part, other)
    return jnp.concatenate([low, high], axis=0)


def total_over_all(part, x, y):
    xu, xv = (x ^ (x >> 1)) & 1, (x >> 1) & 1
    yu, yv = (y ^ (y >> 1)) & 1, (y >> 1) & 1
    part = halve(part, xu, lambda v: swap_x(v, 1))
    part = halve(part, xv, lambda v: swap_x(v, 3))
    part = halve(part, yu, lambda v: swap_y(v, 1))
    part = halve(part, yv, lambda v: swap_y(v, 3))
    part = part + swap_zl(part, 1)
    part = part + swap_zl(part, 2)
    part = part + send_core(part)
    part = part + swap_zh(part, 1)
    part = part + swap_zh(part, 3)
    part = join(part, yv, lambda v: swap_y(v, 3))
    part = join(part, yu, lambda v: swap_y(v, 1))
    part = join(part, xv, lambda v: swap_x(v, 3))
    return join(part, xu, lambda v: swap_x(v, 1))


def shards(features, weight, tile_values, tile_rows, tile_cols, tile_count, cotangent):
    node_dev, width = features.shape
    grad_scale = 1.0 / math.sqrt(node_dev * lax.axis_size("row") * lax.axis_size("col"))
    r, c = lax.axis_index("row"), lax.axis_index("col")
    zl, x, zh, y, core = r >> 2, r & 3, c >> 3, (c >> 1) & 3, c & 1
    where = jnp.stack([zl, x, zh, y, core]).astype(jnp.int32)
    tile = (1, node_dev, width)

    own = features.reshape(tile)
    line = jnp.concatenate([own] + [send_zl(own, k) for k in (1, 2, 3)], axis=0)
    source = [line] + [send_x(line, k) for k in (1, 2, 3)]
    plan = make_plan(where, tile_rows, tile_cols, tile_count)
    turned = turn_tiles(tile_count, tile_values)
    values = tile_values.reshape(tile_values.shape[2:])

    theirs = spmm(0, plan, values, source)
    got = send_core(theirs)
    mine = spmm(1, plan, values, source)
    paired = (mine.astype(jnp.float32) + got.astype(jnp.float32)).astype(jnp.bfloat16)
    blocks = [paired[4 * k : 4 * (k + 1)] for k in range(4)]
    blocks = add4(blocks[0], *[send_y(blocks[k], k) for k in (1, 2, 3)])
    pieces = [blocks[k] for k in range(4)]
    pieces = [pieces[0]] + [send_zh(pieces[k], k) for k in (1, 2, 3)]
    activated, grad_pre, weight_part = middle(pieces, weight, cotangent)

    own = grad_pre.reshape(tile)
    line = jnp.concatenate([own] + [send_zh(own, k) for k in (1, 2, 3)], axis=0)
    grads = [line] + [send_y(line, k) for k in (1, 2, 3)]
    other = send_core(jnp.concatenate(grads, axis=0))
    grad_weight = total_over_all(weight_part, x, y) * grad_scale

    first = spmm(2, plan, turned, grads, dtype=jnp.float32)
    others = [other[4 * k : 4 * (k + 1)] for k in range(4)]
    spread = spmm(3, plan, turned, others, start=first)
    blocks = [spread[4 * k : 4 * (k + 1)] for k in range(4)]
    blocks = add4(blocks[0], *[send_x(blocks[k], k) for k in (1, 2, 3)])
    pieces = [blocks[k] for k in range(4)]
    pieces = [pieces[0]] + [send_zl(pieces[k], k) for k in (1, 2, 3)]
    grad_features = last(pieces, weight)
    return (activated, grad_features, grad_weight)


def solution(mesh):
    return jax.shard_map(
        shards,
        mesh=mesh,
        in_specs=(
            P(("col", "row"), None),
            P(),
            P("row", "col", None, None, None),
            P("row", "col", None),
            P("row", "col", None),
            P("row", "col"),
            P(("row", "col"), None),
        ),
        out_specs=(P(("row", "col"), None), P(("col", "row"), None), P()),
        check_vma=False,
    )
```

time: 920 us -> 246 us (0.27)
  waiting for transfers between devices: 812 us -> 53.2 us
  starting transfers between devices: 0.2 us -> 162 us
  other arithmetic: 42.6 us -> 2.4 us
  matrix products: 21.2 us -> 0 us
  Pallas kernels: 0 us -> 14.6 us
  between operations: 14.5 us -> 2.1 us
  local copies, waits for them, and re-layouts: 17.7 us -> 8.06 us
    psum x1 -> x0, waiting for transfers between devices: 424 us -> none  [shards(): grad_weight = lax.psum(weight_part, ('row', 'col')) * grad_scale]
    reduce_scatter x2 -> x0, waiting for transfers between devices: 236 us -> none  [the longest x1 159 us: shards(): lax.psum_scatter(partial_value.astype(jnp.bfloat16), 'col', scatter_dimen...]
    ppermute x0 -> x39, starting transfers between devices: none -> 162 us  [the longest x6 40.6 us: send_zh(): return lax.ppermute(v, 'col', col_perm(lambda zh, y, c: (zh + k, y, c)))]
    all_gather x2 -> x0, waiting for transfers between devices: 152 us -> none  [the longest x1 83.1 us: shards(): column_block = lax.all_gather(features, 'row', axis=0, tiled=True)]
    ppermute x0 -> x39, waiting for transfers between devices: none -> 53.2 us  [the longest x6 12.4 us: send_x(): return lax.ppermute(v, 'row', row_perm(lambda zl, x: (zl, x + k)))]
    scatter-add x4 -> x0, other arithmetic: 33 us -> none  [the longest x2 20.1 us: forward_one_round(): return running.at[round_rows].add(tile_products * in_use[:, None, None])]
    dot_general x7 -> x0, matrix products: 21.2 us -> none  [the longest x2 9.18 us: backward_one_round(): jnp.einsum('smk,smf->skf', round_values, gathered, preferred_element_type...]
    pallas_call x0 -> x8, Pallas kernels: none -> 14.6 us  [the longest x4 7.67 us: spmm(): pl.pallas_call(functools.partial(spmm_kernel, q, start is not None), out_...]
  transfers between devices with their start and end apart: 5 -> 39, of which waited for: 5 -> 19; matrix products, arithmetic and copies ran while one was open for 5% -> 1% of each run, Pallas kernels for 0% -> 5%
where the time goes in v1:
time: 246 us; the launch traced here: 242 us
  starting transfers between devices  162 us (66%)
  waiting for transfers between devices  53.2 us (22%)
  Pallas kernels  14.6 us (6%)
  local copies, waits for them, and re-layouts  8.06 us (3%)
    ppermute x6, starting transfers between devices, send_zh(): return lax.ppermute(v, 'col', col_perm(lambda zh, y, c: (zh + k, y, c)))  40.6 us
    ppermute x6, starting transfers between devices, send_x(): return lax.ppermute(v, 'row', row_perm(lambda zl, x: (zl, x + k)))  22 us
    ppermute x6, starting transfers between devices, send_y(): return lax.ppermute(v, 'col', col_perm(lambda zh, y, c: (zh, y + k, c)))  18.8 us
    ppermute x6, starting transfers between devices, send_zl(): return lax.ppermute(v, 'row', row_perm(lambda zl, x: (zl + k, x)))  18.4 us
    ppermute x4, starting transfers between devices, swap_x(): return lax.ppermute(v, 'row', row_perm(lambda zl, x: (zl, x ^ k)))  17.4 us
    ppermute x3, starting transfers between devices, send_core(): return lax.ppermute(v, 'col', col_perm(lambda zh, y, c: (zh, y, c + 1)))  17.3 us
    ppermute x4, starting transfers between devices, swap_y(): return lax.ppermute(v, 'col', col_perm(lambda zh, y, c: (zh, y ^ k, c)))  13.3 us
    ppermute x6, waiting for transfers between devices, send_x(): return lax.ppermute(v, 'row', row_perm(lambda zl, x: (zl, x + k)))  12.4 us
  transfers between devices with their start and end apart: 39, of which 19 were waited for; matrix products, arithmetic and copies ran while one was open for 1% of the time, Pallas kernels for 5%

profile of v1, /device:TPU:1, one launch (start us, length us, event | category | flops | bytes accessed | tf_op | source)
XLA Modules:
  0.0 242.3 jit_solution(16520848612391745761)
XLA Ops:
  0.6 7.1 %collective-permute-start.2 = (bf16[1,128,256]{2,1,0:T(8,128)(2,1)}, bf16[1,128,256]{2,1,0:T(8,128)(2,1)S(1)}, u32[]{:S(2)}, u32[]{:S(2)}) collective-permute-start(bf16[1,128,256]{2,1,0:T(8,128)(2,1)} %bitcast.31), channel_id=1, source_target_pairs={{0,384},{32,416},{64,448},{96,480},{128,0},{160,32},{192,64},{224,... | collective-permute-start | bytes 196616 | tf_op jit(solution)/shard_map/ppermute | solution.py:48
  9.6 2.2 collective-permute-start
  13.9 2.8 %collective-permute-done = bf16[1,128,256]{2,1,0:T(8,128)(2,1)S(1)} collective-permute-done((bf16[1,128,256]{2,1,0:T(8,128)(2,1)}, bf16[1,128,256]{2,1,0:T(8,128)(2,1)S(1)}, u32[]{:S(2)}, u32[]{:S(2)}) %collective-permute-start) | collective-permute-done | bytes 65568 | tf_op jit(solution)/shard_map/ppermute | solution.py:48
  17.6 4.3 %collective-permute-start.5 = (bf16[4,128,256]{2,1,0:T(8,128)(2,1)S(1)}, bf16[4,128,256]{2,1,0:T(8,128)(2,1)S(1)}, u32[]{:S(2)}, u32[]{:S(2)}) collective-permute-start(bf16[4,128,256]{2,1,0:T(8,128)(2,1)S(1)} %pad_maximum_fusion.s0), channel_id=1, source_target_pairs={{0,96},{32,0},{64,32},{96,64},{128,224},{160,128},{192,160},{224,1... | collective-permute-start | bytes 786440 | tf_op jit(solution)/shard_map/ppermute | solution.py:52
  21.9 2.4 %collective-permute-start.4 = (bf16[4,128,256]{2,1,0:T(8,128)(2,1)S(1)}, bf16[4,128,256]{2,1,0:T(8,128)(2,1)S(1)}, u32[]{:S(2)}, u32[]{:S(2)}) collective-permute-start(bf16[4,128,256]{2,1,0:T(8,128)(2,1)S(1)} %pad_maximum_fusion.s0), channel_id=1, source_target_pairs={{0,64},{32,96},{64,0},{96,32},{128,192},{160,224},{192,128},{224,1... | collective-permute-start | bytes 786440 | tf_op jit(solution)/shard_map/ppermute | solution.py:52
  24.4 2.5 %collective-permute-start.3 = (bf16[4,128,256]{2,1,0:T(8,128)(2,1)S(1)}, bf16[4,128,256]{2,1,0:T(8,128)(2,1)S(1)}, u32[]{:S(2)}, u32[]{:S(2)}) collective-permute-start(bf16[4,128,256]{2,1,0:T(8,128)(2,1)S(1)} %pad_maximum_fusion.s0), channel_id=1, source_target_pairs={{0,32},{32,64},{64,96},{96,0},{128,160},{160,192},{192,224},{224,1... | collective-permute-start | bytes 786440 | tf_op jit(solution)/shard_map/ppermute | solution.py:52
  28.2 4.5 %plan.1 = (s32[4,192]{1,0:T(4,128)}, s32[4,192]{1,0:T(4,128)}, s32[4,192]{1,0:T(4,128)}, s32[4]{0:T(128)}) custom-call(s32[5]{0:T(128)} %stack.23.where, s32[1,1,128]{2,1,0:T(1,128)} %rows.1, s32[1,1,128]{2,1,0:T(1,128)} %cols.1, s32[1,1]{1,0:T(1,128)S(6)} %copy.16.count), custom_call_target="tpu_custom_call" | custom-call | bytes 16777216 | tf_op jit(solution)/shard_map/plan/pallas_call | solution.py:140
  32.8 5.1 %collective-permute-done.3.s1 = bf16[4,128,256]{2,1,0:T(8,128)(2,1)S(1)} collective-permute-done((bf16[4,128,256]{2,1,0:T(8,128)(2,1)S(1)}, bf16[4,128,256]{2,1,0:T(8,128)(2,1)S(1)}, u32[]{:S(2)}, u32[]{:S(2)}) %collective-permute-start.3) | collective-permute-done | bytes 262176 | tf_op jit(solution)/shard_map/ppermute | solution.py:52
  37.9 2.2 copy-done
  44.6 3.9 %collective-permute-start.6 = (bf16[16,128,256]{2,1,0:T(8,128)(2,1)S(1)}, bf16[16,128,256]{2,1,0:T(8,128)(2,1)S(1)}, u32[]{:S(2)}, u32[]{:S(2)}) collective-permute-start(bf16[16,128,256]{2,1,0:T(8,128)(2,1)S(1)} %spmm.5), channel_id=1, source_target_pairs={{0,1},{1,0},{2,3},{3,2},{4,5},{5,4},{6,7},{7,6},{8,9},{9,8},{10,11... | collective-permute-start | bytes 3145736 | tf_op jit(solution)/shard_map/ppermute | solution.py:44
  51.1 3.0 %collective-permute-start.7 = (bf16[4,128,256]{2,1,0:T(8,128)(2,1)S(1)}, bf16[4,128,256]{2,1,0:T(8,128)(2,1)S(1)}, u32[]{:S(2)}, u32[]{:S(2)}) collective-permute-start(bf16[4,128,256]{2,1,0:T(8,128)(2,1)S(1)} %get-tuple-element.24), channel_id=1, source_target_pairs={{0,2},{1,3},{2,4},{3,5},{4,6},{5,7},{6,0},{7,1},{8,10},{9,11},{10,... | collective-permute-start | bytes 786440 | tf_op jit(solution)/shard_map/ppermute | solution.py:40
  54.1 3.5 %collective-permute-start.9 = (bf16[4,128,256]{2,1,0:T(8,128)(2,1)S(1)}, bf16[4,128,256]{2,1,0:T(8,128)(2,1)S(1)}, u32[]{:S(2)}, u32[]{:S(2)}) collective-permute-start(bf16[4,128,256]{2,1,0:T(8,128)(2,1)S(1)} %get-tuple-element.25), channel_id=1, source_target_pairs={{0,6},{1,7},{2,0},{3,1},{4,2},{5,3},{6,4},{7,5},{8,14},{9,15},{10,... | collective-permute-start | bytes 786440 | tf_op jit(solution)/shard_map/ppermute | solution.py:40
  57.7 4.1 %collective-permute-start.8 = (bf16[4,128,256]{2,1,0:T(8,128)(2,1)S(1)}, bf16[4,128,256]{2,1,0:T(8,128)(2,1)S(1)}, u32[]{:S(2)}, u32[]{:S(2)}) collective-permute-start(bf16[4,128,256]{2,1,0:T(8,128)(2,1)S(1)} %get-tuple-element.26), channel_id=1, source_target_pairs={{0,4},{1,5},{2,6},{3,7},{4,0},{5,1},{6,2},{7,3},{8,12},{9,13},{10,... | collective-permute-start | bytes 786440 | tf_op jit(solution)/shard_map/ppermute | solution.py:40
  61.8 2.7 %collective-permute-done.9 = bf16[4,128,256]{2,1,0:T(8,128)(2,1)S(1)} collective-permute-done((bf16[4,128,256]{2,1,0:T(8,128)(2,1)S(1)}, bf16[4,128,256]{2,1,0:T(8,128)(2,1)S(1)}, u32[]{:S(2)}, u32[]{:S(2)}) %collective-permute-start.9) | collective-permute-done | bytes 262176 | tf_op jit(solution)/shard_map/ppermute | solution.py:40
  64.5 3.4 %collective-permute-done.8 = bf16[4,128,256]{2,1,0:T(8,128)(2,1)S(1)} collective-permute-done((bf16[4,128,256]{2,1,0:T(8,128)(2,1)S(1)}, bf16[4,128,256]{2,1,0:T(8,128)(2,1)S(1)}, u32[]{:S(2)}, u32[]{:S(2)}) %collective-permute-start.8) | collective-permute-done | bytes 262176 | tf_op jit(solution)/shard_map/ppermute | solution.py:40
  68.1 9.9 %collective-permute-start.12 = (bf16[128,256]{1,0:T(8,128)(2,1)S(1)}, bf16[128,256]{1,0:T(8,128)(2,1)S(1)}, u32[]{:S(2)}, u32[]{:S(2)}) collective-permute-start(bf16[128,256]{1,0:T(8,128)(2,1)S(1)} %get-tuple-element.33), channel_id=1, source_target_pairs={{0,24},{1,25},{2,26},{3,27},{4,28},{5,29},{6,30},{7,31},{8,0},{9,1... | collective-permute-start | bytes 196616 | tf_op jit(solution)/shard_map/ppermute | solution.py:36
  78.0 7.1 %collective-permute-start.11 = (bf16[128,256]{1,0:T(8,128)(2,1)S(1)}, bf16[128,256]{1,0:T(8,128)(2,1)S(1)}, u32[]{:S(2)}, u32[]{:S(2)}) collective-permute-start(bf16[128,256]{1,0:T(8,128)(2,1)S(1)} %get-tuple-element.34), channel_id=1, source_target_pairs={{0,16},{1,17},{2,18},{3,19},{4,20},{5,21},{6,22},{7,23},{8,24},{9,... | collective-permute-start | bytes 196616 | tf_op jit(solution)/shard_map/ppermute | solution.py:36
  85.1 7.3 %collective-permute-start.10 = (bf16[128,256]{1,0:T(8,128)(2,1)S(1)}, bf16[128,256]{1,0:T(8,128)(2,1)S(1)}, u32[]{:S(2)}, u32[]{:S(2)}) collective-permute-start(bf16[128,256]{1,0:T(8,128)(2,1)S(1)} %get-tuple-element.35), channel_id=1, source_target_pairs={{0,8},{1,9},{2,10},{3,11},{4,12},{5,13},{6,14},{7,15},{8,16},{9,17... | collective-permute-start | bytes 196616 | tf_op jit(solution)/shard_map/ppermute | solution.py:36
  92.4 4.2 %collective-permute-done.10.a1 = bf16[128,256]{1,0:T(8,128)(2,1)S(1)} collective-permute-done((bf16[128,256]{1,0:T(8,128)(2,1)S(1)}, bf16[128,256]{1,0:T(8,128)(2,1)S(1)}, u32[]{:S(2)}, u32[]{:S(2)}) %collective-permute-start.10) | collective-permute-done | bytes 65568 | tf_op jit(solution)/shard_map/ppermute | solution.py:36
  97.5 2.3 collective-permute-start.26
  99.8 3.8 %collective-permute-done.26 = f32[128,256]{1,0:T(8,128)S(1)} collective-permute-done((f32[128,256]{1,0:T(8,128)S(1)}, f32[128,256]{1,0:T(8,128)S(1)}, u32[]{:S(2)}, u32[]{:S(2)}) %collective-permute-start.26) | collective-permute-done | bytes 131104 | tf_op jit(solution)/shard_map/ppermute | solution.py:68
  103.7 8.9 %collective-permute-start.27 = (f32[64,256]{1,0:T(8,128)S(1)}, f32[64,256]{1,0:T(8,128)S(1)}, u32[]{:S(2)}, u32[]{:S(2)}) collective-permute-start(f32[64,256]{1,0:T(8,128)S(1)} %slice_select_fusion.1), channel_id=1, source_target_pairs={{0,96},{32,64},{64,32},{96,0},{128,224},{160,192},{192,160},{224,1... | collective-permute-start | bytes 196616 | tf_op jit(solution)/shard_map/ppermute | solution.py:68
  114.2 3.8 %collective-permute-start.28 = (f32[32,256]{1,0:T(8,128)S(1)}, f32[32,256]{1,0:T(8,128)S(1)}, u32[]{:S(2)}, u32[]{:S(2)}) collective-permute-start(f32[32,256]{1,0:T(8,128)S(1)} %slice_select_fusion.2), channel_id=1, source_target_pairs={{0,2},{1,3},{2,0},{3,1},{4,6},{5,7},{6,4},{7,5},{8,10},{9,11},{10,... | collective-permute-start | bytes 98312 | tf_op jit(solution)/shard_map/ppermute | solution.py:60
  118.0 4.3 %collective-permute-start.15 = (bf16[1,128,256]{2,1,0:T(8,128)(2,1)S(1)}, bf16[1,128,256]{2,1,0:T(8,128)(2,1)S(1)}, u32[]{:S(2)}, u32[]{:S(2)}) collective-permute-start(bf16[1,128,256]{2,1,0:T(8,128)(2,1)S(1)} %bitcast.27), channel_id=1, source_target_pairs={{0,24},{1,25},{2,26},{3,27},{4,28},{5,29},{6,30},{7,31},{8,0},{9,1... | collective-permute-start | bytes 196616 | tf_op jit(solution)/shard_map/ppermute | solution.py:36
  122.3 5.2 %collective-permute-start.14 = (bf16[1,128,256]{2,1,0:T(8,128)(2,1)S(1)}, bf16[1,128,256]{2,1,0:T(8,128)(2,1)S(1)}, u32[]{:S(2)}, u32[]{:S(2)}) collective-permute-start(bf16[1,128,256]{2,1,0:T(8,128)(2,1)S(1)} %bitcast.28), channel_id=1, source_target_pairs={{0,16},{1,17},{2,18},{3,19},{4,20},{5,21},{6,22},{7,23},{8,24},{9,... | collective-permute-start | bytes 196616 | tf_op jit(solution)/shard_map/ppermute | solution.py:36
  127.5 6.8 %collective-permute-start.13 = (bf16[1,128,256]{2,1,0:T(8,128)(2,1)S(1)}, bf16[1,128,256]{2,1,0:T(8,128)(2,1)S(1)}, u32[]{:S(2)}, u32[]{:S(2)}) collective-permute-start(bf16[1,128,256]{2,1,0:T(8,128)(2,1)S(1)} %bitcast.29), channel_id=1, source_target_pairs={{0,8},{1,9},{2,10},{3,11},{4,12},{5,13},{6,14},{7,15},{8,16},{9,17... | collective-permute-start | bytes 196616 | tf_op jit(solution)/shard_map/ppermute | solution.py:36
  134.4 3.1 %collective-permute-start.29 = (f32[16,256]{1,0:T(8,128)S(1)}, f32[16,256]{1,0:T(8,128)S(1)}, u32[]{:S(2)}, u32[]{:S(2)}) collective-permute-start(f32[16,256]{1,0:T(8,128)S(1)} %slice_select_fusion.3), channel_id=1, source_target_pairs={{0,6},{1,7},{2,4},{3,5},{4,2},{5,3},{6,0},{7,1},{8,14},{9,15},{10,... | collective-permute-start | bytes 49160 | tf_op jit(solution)/shard_map/ppermute | solution.py:60
  137.5 2.5 %collective-permute-done.29 = f32[16,256]{1,0:T(8,128)S(1)} collective-permute-done((f32[16,256]{1,0:T(8,128)S(1)}, f32[16,256]{1,0:T(8,128)S(1)}, u32[]{:S(2)}, u32[]{:S(2)}) %collective-permute-start.29) | collective-permute-done | bytes 16416 | tf_op jit(solution)/shard_map/ppermute | solution.py:60
  140.1 3.4 %collective-permute-start.30 = (f32[16,256]{1,0:T(8,128)S(1)}, f32[16,256]{1,0:T(8,128)S(1)}, u32[]{:S(2)}, u32[]{:S(2)}) collective-permute-start(f32[16,256]{1,0:T(8,128)S(1)} %select_add_fusion.3), channel_id=1, source_target_pairs={{0,128},{32,160},{64,192},{96,224},{128,0},{160,32},{192,64},{224,... | collective-permute-start | bytes 49160 | tf_op jit(solution)/shard_map/ppermute | solution.py:64
  143.6 3.8 %collective-permute-start.18 = (bf16[4,128,256]{2,1,0:T(8,128)(2,1)S(1)}, bf16[4,128,256]{2,1,0:T(8,128)(2,1)S(1)}, u32[]{:S(2)}, u32[]{:S(2)}) collective-permute-start(bf16[4,128,256]{2,1,0:T(8,128)(2,1)S(1)} %pad_maximum_fusion.1.s0), channel_id=1, source_target_pairs={{0,6},{1,7},{2,0},{3,1},{4,2},{5,3},{6,4},{7,5},{8,14},{9,15},{10,... | collective-permute-start | bytes 786440 | tf_op jit(solution)/shard_map/ppermute | solution.py:40
  149.3 2.5 %collective-permute-start.16 = (bf16[4,128,256]{2,1,0:T(8,128)(2,1)S(1)}, bf16[4,128,256]{2,1,0:T(8,128)(2,1)S(1)}, u32[]{:S(2)}, u32[]{:S(2)}) collective-permute-start(bf16[4,128,256]{2,1,0:T(8,128)(2,1)S(1)} %pad_maximum_fusion.1.s0), channel_id=1, source_target_pairs={{0,2},{1,3},{2,4},{3,5},{4,6},{5,7},{6,0},{7,1},{8,10},{9,11},{10,... | collective-permute-start | bytes 786440 | tf_op jit(solution)/shard_map/ppermute | solution.py:40
  151.9 3.8 %collective-permute-start.31 = (f32[16,256]{1,0:T(8,128)S(1)}, f32[16,256]{1,0:T(8,128)S(1)}, u32[]{:S(2)}, u32[]{:S(2)}) collective-permute-start(f32[16,256]{1,0:T(8,128)S(1)} %add.59), channel_id=1, source_target_pairs={{0,256},{32,288},{64,320},{96,352},{128,384},{160,416},{192,448},{... | collective-permute-start | bytes 49160 | tf_op jit(solution)/shard_map/ppermute | solution.py:64
  157.2 8.6 %collective-permute-start.32 = (f32[16,256]{1,0:T(8,128)S(1)}, f32[16,256]{1,0:T(8,128)S(1)}, u32[]{:S(2)}, u32[]{:S(2)}) collective-permute-start(f32[16,256]{1,0:T(8,128)S(1)} %add.60), channel_id=1, source_target_pairs={{0,1},{1,0},{2,3},{3,2},{4,5},{5,4},{6,7},{7,6},{8,9},{9,8},{10,11... | collective-permute-start | bytes 49160 | tf_op jit(solution)/shard_map/ppermute | solution.py:44
  166.7 3.6 %collective-permute-start.33 = (f32[16,256]{1,0:T(8,128)S(1)}, f32[16,256]{1,0:T(8,128)S(1)}, u32[]{:S(2)}, u32[]{:S(2)}) collective-permute-start(f32[16,256]{1,0:T(8,128)S(1)} %add.61), channel_id=1, source_target_pairs={{0,8},{1,9},{2,10},{3,11},{4,12},{5,13},{6,14},{7,15},{8,0},{9,1},... | collective-permute-start | bytes 49160 | tf_op jit(solution)/shard_map/ppermute | solution.py:56
  170.3 4.8 %collective-permute-done.33 = f32[16,256]{1,0:T(8,128)S(1)} collective-permute-done((f32[16,256]{1,0:T(8,128)S(1)}, f32[16,256]{1,0:T(8,128)S(1)}, u32[]{:S(2)}, u32[]{:S(2)}) %collective-permute-start.33) | collective-permute-done | bytes 16416 | tf_op jit(solution)/shard_map/ppermute | solution.py:56
  175.1 3.4 %collective-permute-start.34 = (f32[16,256]{1,0:T(8,128)S(1)}, f32[16,256]{1,0:T(8,128)S(1)}, u32[]{:S(2)}, u32[]{:S(2)}) collective-permute-start(f32[16,256]{1,0:T(8,128)S(1)} %add.62), channel_id=1, source_target_pairs={{0,24},{1,25},{2,26},{3,27},{4,28},{5,29},{6,30},{7,31},{8,16},{9,... | collective-permute-start | bytes 49160 | tf_op jit(solution)/shard_map/ppermute | solution.py:56
  178.6 4.9 %collective-permute-done.34 = f32[16,256]{1,0:T(8,128)S(1)} collective-permute-done((f32[16,256]{1,0:T(8,128)S(1)}, f32[16,256]{1,0:T(8,128)S(1)}, u32[]{:S(2)}, u32[]{:S(2)}) %collective-permute-start.34) | collective-permute-done | bytes 16416 | tf_op jit(solution)/shard_map/ppermute | solution.py:56
  183.5 3.4 %collective-permute-start.35 = (f32[16,256]{1,0:T(8,128)S(1)}, f32[16,256]{1,0:T(8,128)S(1)}, u32[]{:S(2)}, u32[]{:S(2)}) collective-permute-start(f32[16,256]{1,0:T(8,128)S(1)} %add.63), channel_id=1, source_target_pairs={{0,6},{1,7},{2,4},{3,5},{4,2},{5,3},{6,0},{7,1},{8,14},{9,15},{10,... | collective-permute-start | bytes 49160 | tf_op jit(solution)/shard_map/ppermute | solution.py:60
  186.9 4.8 %collective-permute-start.19 = (bf16[16,128,256]{2,1,0:T(8,128)(2,1)S(1)}, bf16[16,128,256]{2,1,0:T(8,128)(2,1)S(1)}, u32[]{:S(2)}, u32[]{:S(2)}) collective-permute-start(bf16[16,128,256]{2,1,0:T(8,128)(2,1)S(1)} %constant_dynamic-update-slice_fusion), channel_id=1, source_target_pairs={{0,1},{1,0},{2,3},{3,2},{4,5},{5,4},{6,7},{7,6},{8,9},{9,8},{10,11... | collective-permute-start | bytes 3145736 | tf_op jit(solution)/shard_map/ppermute | solution.py:44
  191.8 2.9 %collective-permute-start.36 = (f32[32,256]{1,0:T(8,128)S(1)}, f32[32,256]{1,0:T(8,128)S(1)}, u32[]{:S(2)}, u32[]{:S(2)}) collective-permute-start(f32[32,256]{1,0:T(8,128)S(1)} %pad_maximum_fusion.4), channel_id=1, source_target_pairs={{0,2},{1,3},{2,0},{3,1},{4,6},{5,7},{6,4},{7,5},{8,10},{9,11},{10,... | collective-permute-start | bytes 98312 | tf_op jit(solution)/shard_map/ppermute | solution.py:60
  196.5 4.3 %collective-permute-start.37 = (f32[64,256]{1,0:T(8,128)S(1)}, f32[64,256]{1,0:T(8,128)S(1)}, u32[]{:S(2)}, u32[]{:S(2)}) collective-permute-start(f32[64,256]{1,0:T(8,128)S(1)} %pad_maximum_fusion.3), channel_id=1, source_target_pairs={{0,96},{32,64},{64,32},{96,0},{128,224},{160,192},{192,160},{224,1... | collective-permute-start | bytes 196616 | tf_op jit(solution)/shard_map/ppermute | solution.py:68
  200.9 2.2 copy-done.1
  209.8 3.6 %collective-permute-start.20 = (bf16[4,128,256]{2,1,0:T(8,128)(2,1)S(1)}, bf16[4,128,256]{2,1,0:T(8,128)(2,1)S(1)}, u32[]{:S(2)}, u32[]{:S(2)}) collective-permute-start(bf16[4,128,256]{2,1,0:T(8,128)(2,1)S(1)} %get-tuple-element.17), channel_id=1, source_target_pairs={{0,32},{32,64},{64,96},{96,0},{128,160},{160,192},{192,224},{224,1... | collective-permute-start | bytes 786440 | tf_op jit(solution)/shard_map/ppermute | solution.py:52
  213.5 5.3 %collective-permute-start.22 = (bf16[4,128,256]{2,1,0:T(8,128)(2,1)S(1)}, bf16[4,128,256]{2,1,0:T(8,128)(2,1)S(1)}, u32[]{:S(2)}, u32[]{:S(2)}) collective-permute-start(bf16[4,128,256]{2,1,0:T(8,128)(2,1)S(1)} %get-tuple-element.18), channel_id=1, source_target_pairs={{0,96},{32,0},{64,32},{96,64},{128,224},{160,128},{192,160},{224,1... | collective-permute-start | bytes 786440 | tf_op jit(solution)/shard_map/ppermute | solution.py:52
  218.7 3.8 %collective-permute-start.21 = (bf16[4,128,256]{2,1,0:T(8,128)(2,1)S(1)}, bf16[4,128,256]{2,1,0:T(8,128)(2,1)S(1)}, u32[]{:S(2)}, u32[]{:S(2)}) collective-permute-start(bf16[4,128,256]{2,1,0:T(8,128)(2,1)S(1)} %get-tuple-element.19), channel_id=1, source_target_pairs={{0,64},{32,96},{64,0},{96,32},{128,192},{160,224},{192,128},{224,1... | collective-permute-start | bytes 786440 | tf_op jit(solution)/shard_map/ppermute | solution.py:52
  224.9 4.9 %collective-permute-done.21 = bf16[4,128,256]{2,1,0:T(8,128)(2,1)S(1)} collective-permute-done((bf16[4,128,256]{2,1,0:T(8,128)(2,1)S(1)}, bf16[4,128,256]{2,1,0:T(8,128)(2,1)S(1)}, u32[]{:S(2)}, u32[]{:S(2)}) %collective-permute-start.21) | collective-permute-done | bytes 262176 | tf_op jit(solution)/shard_map/ppermute | solution.py:52
  233.9 3.4 %collective-permute-start.23 = (bf16[128,256]{1,0:T(8,128)(2,1)S(1)}, bf16[128,256]{1,0:T(8,128)(2,1)S(1)}, u32[]{:S(2)}, u32[]{:S(2)}) collective-permute-start(bf16[128,256]{1,0:T(8,128)(2,1)S(1)} %get-tuple-element.31), channel_id=1, source_target_pairs={{0,128},{32,160},{64,192},{96,224},{128,256},{160,288},{192,320},{... | collective-permute-start | bytes 196616 | tf_op jit(solution)/shard_map/ppermute | solution.py:48
  238.0 3.5 %collective-permute-done.23.a1 = bf16[128,256]{1,0:T(8,128)(2,1)S(1)} collective-permute-done((bf16[128,256]{1,0:T(8,128)(2,1)S(1)}, bf16[128,256]{1,0:T(8,128)(2,1)S(1)}, u32[]{:S(2)}, u32[]{:S(2)}) %collective-permute-start.23) | collective-permute-done | bytes 65568 | tf_op jit(solution)/shard_map/ppermute | solution.py:48
  (101 shorter events, 36.1 us)
Async XLA Ops:
  0.6 11.2 %collective-permute-start.2 = (bf16[1,128,256]{2,1,0:T(8,128)(2,1)}, bf16[1,128,256]{2,1,0:T(8,128)(2,1)S(1)}, u32[]{:S(2)}, u32[]{:S(2)}) collective-permute-start(bf16[1,128,256]{2,1,0:T(8,128)(2,1)} %bitcast.31), channel_id=1, source_target_pairs={{0,384},{32,416},{64,448},{96,480},{128,0},{160,32},{192,64},{224,... | collective-permute-start | bytes 196616 | tf_op jit(solution)/shard_map/ppermute | solution.py:48
  7.7 6.2 %collective-permute-start.1 = (bf16[1,128,256]{2,1,0:T(8,128)(2,1)}, bf16[1,128,256]{2,1,0:T(8,128)(2,1)S(1)}, u32[]{:S(2)}, u32[]{:S(2)}) collective-permute-start(bf16[1,128,256]{2,1,0:T(8,128)(2,1)} %bitcast.32), channel_id=1, source_target_pairs={{0,256},{32,288},{64,320},{96,352},{128,384},{160,416},{192,448},{... | collective-permute-start | bytes 196616 | tf_op jit(solution)/shard_map/ppermute | solution.py:48
  9.6 7.1 %collective-permute-start = (bf16[1,128,256]{2,1,0:T(8,128)(2,1)}, bf16[1,128,256]{2,1,0:T(8,128)(2,1)S(1)}, u32[]{:S(2)}, u32[]{:S(2)}) collective-permute-start(bf16[1,128,256]{2,1,0:T(8,128)(2,1)} %bitcast.33), channel_id=1, source_target_pairs={{0,128},{32,160},{64,192},{96,224},{128,256},{160,288},{192,320},{... | collective-permute-start | bytes 196616 | tf_op jit(solution)/shard_map/ppermute | solution.py:48
  17.6 15.2 %collective-permute-start.5 = (bf16[4,128,256]{2,1,0:T(8,128)(2,1)S(1)}, bf16[4,128,256]{2,1,0:T(8,128)(2,1)S(1)}, u32[]{:S(2)}, u32[]{:S(2)}) collective-permute-start(bf16[4,128,256]{2,1,0:T(8,128)(2,1)S(1)} %pad_maximum_fusion.s0), channel_id=1, source_target_pairs={{0,96},{32,0},{64,32},{96,64},{128,224},{160,128},{192,160},{224,1... | collective-permute-start | bytes 786440 | tf_op jit(solution)/shard_map/ppermute | solution.py:52
  21.9 10.9 %collective-permute-start.4 = (bf16[4,128,256]{2,1,0:T(8,128)(2,1)S(1)}, bf16[4,128,256]{2,1,0:T(8,128)(2,1)S(1)}, u32[]{:S(2)}, u32[]{:S(2)}) collective-permute-start(bf16[4,128,256]{2,1,0:T(8,128)(2,1)S(1)} %pad_maximum_fusion.s0), channel_id=1, source_target_pairs={{0,64},{32,96},{64,0},{96,32},{128,192},{160,224},{192,128},{224,1... | collective-permute-start | bytes 786440 | tf_op jit(solution)/shard_map/ppermute | solution.py:52
  24.4 13.6 %collective-permute-start.3 = (bf16[4,128,256]{2,1,0:T(8,128)(2,1)S(1)}, bf16[4,128,256]{2,1,0:T(8,128)(2,1)S(1)}, u32[]{:S(2)}, u32[]{:S(2)}) collective-permute-start(bf16[4,128,256]{2,1,0:T(8,128)(2,1)S(1)} %pad_maximum_fusion.s0), channel_id=1, source_target_pairs={{0,32},{32,64},{64,96},{96,0},{128,160},{160,192},{192,224},{224,1... | collective-permute-start | bytes 786440 | tf_op jit(solution)/shard_map/ppermute | solution.py:52
  37.9 2.2 copy-start
  40.8 0.7 copy-start.6
  44.6 6.2 %collective-permute-start.6 = (bf16[16,128,256]{2,1,0:T(8,128)(2,1)S(1)}, bf16[16,128,256]{2,1,0:T(8,128)(2,1)S(1)}, u32[]{:S(2)}, u32[]{:S(2)}) collective-permute-start(bf16[16,128,256]{2,1,0:T(8,128)(2,1)S(1)} %spmm.5), channel_id=1, source_target_pairs={{0,1},{1,0},{2,3},{3,2},{4,5},{5,4},{6,7},{7,6},{8,9},{9,8},{10,11... | collective-permute-start | bytes 3145736 | tf_op jit(solution)/shard_map/ppermute | solution.py:44
  51.1 45.6 %copy-start.2 = (bf16[256,256]{1,0:T(8,128)(2,1)S(1)}, bf16[256,256]{1,0:T(8,128)(2,1)}, u32[]{:S(2)}) copy-start(bf16[256,256]{1,0:T(8,128)(2,1)} %w.3) | copy-start | bytes 393220
  51.1 45.6 %copy-start.3 = (bf16[128,256]{1,0:T(8,128)(2,1)S(1)}, bf16[128,256]{1,0:T(8,128)(2,1)}, u32[]{:S(2)}) copy-start(bf16[128,256]{1,0:T(8,128)(2,1)} %cot.1) | copy-start | bytes 196612
  51.1 10.6 %collective-permute-start.7 = (bf16[4,128,256]{2,1,0:T(8,128)(2,1)S(1)}, bf16[4,128,256]{2,1,0:T(8,128)(2,1)S(1)}, u32[]{:S(2)}, u32[]{:S(2)}) collective-permute-start(bf16[4,128,256]{2,1,0:T(8,128)(2,1)S(1)} %get-tuple-element.24), channel_id=1, source_target_pairs={{0,2},{1,3},{2,4},{3,5},{4,6},{5,7},{6,0},{7,1},{8,10},{9,11},{10,... | collective-permute-start | bytes 786440 | tf_op jit(solution)/shard_map/ppermute | solution.py:40
  54.1 10.4 %collective-permute-start.9 = (bf16[4,128,256]{2,1,0:T(8,128)(2,1)S(1)}, bf16[4,128,256]{2,1,0:T(8,128)(2,1)S(1)}, u32[]{:S(2)}, u32[]{:S(2)}) collective-permute-start(bf16[4,128,256]{2,1,0:T(8,128)(2,1)S(1)} %get-tuple-element.25), channel_id=1, source_target_pairs={{0,6},{1,7},{2,0},{3,1},{4,2},{5,3},{6,4},{7,5},{8,14},{9,15},{10,... | collective-permute-start | bytes 786440 | tf_op jit(solution)/shard_map/ppermute | solution.py:40
  57.7 10.3 %collective-permute-start.8 = (bf16[4,128,256]{2,1,0:T(8,128)(2,1)S(1)}, bf16[4,128,256]{2,1,0:T(8,128)(2,1)S(1)}, u32[]{:S(2)}, u32[]{:S(2)}) collective-permute-start(bf16[4,128,256]{2,1,0:T(8,128)(2,1)S(1)} %get-tuple-element.26), channel_id=1, source_target_pairs={{0,4},{1,5},{2,6},{3,7},{4,0},{5,1},{6,2},{7,3},{8,12},{9,13},{10,... | collective-permute-start | bytes 786440 | tf_op jit(solution)/shard_map/ppermute | solution.py:40
  68.1 24.3 %collective-permute-start.12 = (bf16[128,256]{1,0:T(8,128)(2,1)S(1)}, bf16[128,256]{1,0:T(8,128)(2,1)S(1)}, u32[]{:S(2)}, u32[]{:S(2)}) collective-permute-start(bf16[128,256]{1,0:T(8,128)(2,1)S(1)} %get-tuple-element.33), channel_id=1, source_target_pairs={{0,24},{1,25},{2,26},{3,27},{4,28},{5,29},{6,30},{7,31},{8,0},{9,1... | collective-permute-start | bytes 196616 | tf_op jit(solution)/shard_map/ppermute | solution.py:36
  78.0 14.4 %collective-permute-start.11 = (bf16[128,256]{1,0:T(8,128)(2,1)S(1)}, bf16[128,256]{1,0:T(8,128)(2,1)S(1)}, u32[]{:S(2)}, u32[]{:S(2)}) collective-permute-start(bf16[128,256]{1,0:T(8,128)(2,1)S(1)} %get-tuple-element.34), channel_id=1, source_target_pairs={{0,16},{1,17},{2,18},{3,19},{4,20},{5,21},{6,22},{7,23},{8,24},{9,... | collective-permute-start | bytes 196616 | tf_op jit(solution)/shard_map/ppermute | solution.py:36
  85.1 11.5 %collective-permute-start.10 = (bf16[128,256]{1,0:T(8,128)(2,1)S(1)}, bf16[128,256]{1,0:T(8,128)(2,1)S(1)}, u32[]{:S(2)}, u32[]{:S(2)}) collective-permute-start(bf16[128,256]{1,0:T(8,128)(2,1)S(1)} %get-tuple-element.35), channel_id=1, source_target_pairs={{0,8},{1,9},{2,10},{3,11},{4,12},{5,13},{6,14},{7,15},{8,16},{9,17... | collective-permute-start | bytes 196616 | tf_op jit(solution)/shard_map/ppermute | solution.py:36
  97.5 6.1 %collective-permute-start.26 = (f32[128,256]{1,0:T(8,128)S(1)}, f32[128,256]{1,0:T(8,128)S(1)}, u32[]{:S(2)}, u32[]{:S(2)}) collective-permute-start(f32[128,256]{1,0:T(8,128)S(1)} %slice_select_fusion), channel_id=1, source_target_pairs={{0,32},{32,0},{64,96},{96,64},{128,160},{160,128},{192,224},{224,1... | collective-permute-start | bytes 393224 | tf_op jit(solution)/shard_map/ppermute | solution.py:68
  103.7 10.5 %collective-permute-start.27 = (f32[64,256]{1,0:T(8,128)S(1)}, f32[64,256]{1,0:T(8,128)S(1)}, u32[]{:S(2)}, u32[]{:S(2)}) collective-permute-start(f32[64,256]{1,0:T(8,128)S(1)} %slice_select_fusion.1), channel_id=1, source_target_pairs={{0,96},{32,64},{64,32},{96,0},{128,224},{160,192},{192,160},{224,1... | collective-permute-start | bytes 196616 | tf_op jit(solution)/shard_map/ppermute | solution.py:68
  114.2 20.1 %collective-permute-start.28 = (f32[32,256]{1,0:T(8,128)S(1)}, f32[32,256]{1,0:T(8,128)S(1)}, u32[]{:S(2)}, u32[]{:S(2)}) collective-permute-start(f32[32,256]{1,0:T(8,128)S(1)} %slice_select_fusion.2), channel_id=1, source_target_pairs={{0,2},{1,3},{2,0},{3,1},{4,6},{5,7},{6,4},{7,5},{8,10},{9,11},{10,... | collective-permute-start | bytes 98312 | tf_op jit(solution)/shard_map/ppermute | solution.py:60
  118.0 25.5 %collective-permute-start.15 = (bf16[1,128,256]{2,1,0:T(8,128)(2,1)S(1)}, bf16[1,128,256]{2,1,0:T(8,128)(2,1)S(1)}, u32[]{:S(2)}, u32[]{:S(2)}) collective-permute-start(bf16[1,128,256]{2,1,0:T(8,128)(2,1)S(1)} %bitcast.27), channel_id=1, source_target_pairs={{0,24},{1,25},{2,26},{3,27},{4,28},{5,29},{6,30},{7,31},{8,0},{9,1... | collective-permute-start | bytes 196616 | tf_op jit(solution)/shard_map/ppermute | solution.py:36
  122.3 21.2 %collective-permute-start.14 = (bf16[1,128,256]{2,1,0:T(8,128)(2,1)S(1)}, bf16[1,128,256]{2,1,0:T(8,128)(2,1)S(1)}, u32[]{:S(2)}, u32[]{:S(2)}) collective-permute-start(bf16[1,128,256]{2,1,0:T(8,128)(2,1)S(1)} %bitcast.28), channel_id=1, source_target_pairs={{0,16},{1,17},{2,18},{3,19},{4,20},{5,21},{6,22},{7,23},{8,24},{9,... | collective-permute-start | bytes 196616 | tf_op jit(solution)/shard_map/ppermute | solution.py:36
  127.5 16.0 %collective-permute-start.13 = (bf16[1,128,256]{2,1,0:T(8,128)(2,1)S(1)}, bf16[1,128,256]{2,1,0:T(8,128)(2,1)S(1)}, u32[]{:S(2)}, u32[]{:S(2)}) collective-permute-start(bf16[1,128,256]{2,1,0:T(8,128)(2,1)S(1)} %bitcast.29), channel_id=1, source_target_pairs={{0,8},{1,9},{2,10},{3,11},{4,12},{5,13},{6,14},{7,15},{8,16},{9,17... | collective-permute-start | bytes 196616 | tf_op jit(solution)/shard_map/ppermute | solution.py:36
  134.4 5.7 %collective-permute-start.29 = (f32[16,256]{1,0:T(8,128)S(1)}, f32[16,256]{1,0:T(8,128)S(1)}, u32[]{:S(2)}, u32[]{:S(2)}) collective-permute-start(f32[16,256]{1,0:T(8,128)S(1)} %slice_select_fusion.3), channel_id=1, source_target_pairs={{0,6},{1,7},{2,4},{3,5},{4,2},{5,3},{6,0},{7,1},{8,14},{9,15},{10,... | collective-permute-start | bytes 49160 | tf_op jit(solution)/shard_map/ppermute | solution.py:60
  140.1 11.8 %collective-permute-start.30 = (f32[16,256]{1,0:T(8,128)S(1)}, f32[16,256]{1,0:T(8,128)S(1)}, u32[]{:S(2)}, u32[]{:S(2)}) collective-permute-start(f32[16,256]{1,0:T(8,128)S(1)} %select_add_fusion.3), channel_id=1, source_target_pairs={{0,128},{32,160},{64,192},{96,224},{128,0},{160,32},{192,64},{224,... | collective-permute-start | bytes 49160 | tf_op jit(solution)/shard_map/ppermute | solution.py:64
  143.6 43.3 %collective-permute-start.18 = (bf16[4,128,256]{2,1,0:T(8,128)(2,1)S(1)}, bf16[4,128,256]{2,1,0:T(8,128)(2,1)S(1)}, u32[]{:S(2)}, u32[]{:S(2)}) collective-permute-start(bf16[4,128,256]{2,1,0:T(8,128)(2,1)S(1)} %pad_maximum_fusion.1.s0), channel_id=1, source_target_pairs={{0,6},{1,7},{2,0},{3,1},{4,2},{5,3},{6,4},{7,5},{8,14},{9,15},{10,... | collective-permute-start | bytes 786440 | tf_op jit(solution)/shard_map/ppermute | solution.py:40
  147.4 31.1 %collective-permute-start.17 = (bf16[4,128,256]{2,1,0:T(8,128)(2,1)S(1)}, bf16[4,128,256]{2,1,0:T(8,128)(2,1)S(1)}, u32[]{:S(2)}, u32[]{:S(2)}) collective-permute-start(bf16[4,128,256]{2,1,0:T(8,128)(2,1)S(1)} %pad_maximum_fusion.1.s0), channel_id=1, source_target_pairs={{0,4},{1,5},{2,6},{3,7},{4,0},{5,1},{6,2},{7,3},{8,12},{9,13},{10,... | collective-permute-start | bytes 786440 | tf_op jit(solution)/shard_map/ppermute | solution.py:40
  149.3 29.2 %collective-permute-start.16 = (bf16[4,128,256]{2,1,0:T(8,128)(2,1)S(1)}, bf16[4,128,256]{2,1,0:T(8,128)(2,1)S(1)}, u32[]{:S(2)}, u32[]{:S(2)}) collective-permute-start(bf16[4,128,256]{2,1,0:T(8,128)(2,1)S(1)} %pad_maximum_fusion.1.s0), channel_id=1, source_target_pairs={{0,2},{1,3},{2,4},{3,5},{4,6},{5,7},{6,0},{7,1},{8,10},{9,11},{10,... | collective-permute-start | bytes 786440 | tf_op jit(solution)/shard_map/ppermute | solution.py:40
  151.9 5.4 %collective-permute-start.31 = (f32[16,256]{1,0:T(8,128)S(1)}, f32[16,256]{1,0:T(8,128)S(1)}, u32[]{:S(2)}, u32[]{:S(2)}) collective-permute-start(f32[16,256]{1,0:T(8,128)S(1)} %add.59), channel_id=1, source_target_pairs={{0,256},{32,288},{64,320},{96,352},{128,384},{160,416},{192,448},{... | collective-permute-start | bytes 49160 | tf_op jit(solution)/shard_map/ppermute | solution.py:64
  157.2 9.4 %collective-permute-start.32 = (f32[16,256]{1,0:T(8,128)S(1)}, f32[16,256]{1,0:T(8,128)S(1)}, u32[]{:S(2)}, u32[]{:S(2)}) collective-permute-start(f32[16,256]{1,0:T(8,128)S(1)} %add.60), channel_id=1, source_target_pairs={{0,1},{1,0},{2,3},{3,2},{4,5},{5,4},{6,7},{7,6},{8,9},{9,8},{10,11... | collective-permute-start | bytes 49160 | tf_op jit(solution)/shard_map/ppermute | solution.py:44
  166.7 8.4 %collective-permute-start.33 = (f32[16,256]{1,0:T(8,128)S(1)}, f32[16,256]{1,0:T(8,128)S(1)}, u32[]{:S(2)}, u32[]{:S(2)}) collective-permute-start(f32[16,256]{1,0:T(8,128)S(1)} %add.61), channel_id=1, source_target_pairs={{0,8},{1,9},{2,10},{3,11},{4,12},{5,13},{6,14},{7,15},{8,0},{9,1},... | collective-permute-start | bytes 49160 | tf_op jit(solution)/shard_map/ppermute | solution.py:56
  175.1 8.4 %collective-permute-start.34 = (f32[16,256]{1,0:T(8,128)S(1)}, f32[16,256]{1,0:T(8,128)S(1)}, u32[]{:S(2)}, u32[]{:S(2)}) collective-permute-start(f32[16,256]{1,0:T(8,128)S(1)} %add.62), channel_id=1, source_target_pairs={{0,24},{1,25},{2,26},{3,27},{4,28},{5,29},{6,30},{7,31},{8,16},{9,... | collective-permute-start | bytes 49160 | tf_op jit(solution)/shard_map/ppermute | solution.py:56
  183.5 8.3 %collective-permute-start.35 = (f32[16,256]{1,0:T(8,128)S(1)}, f32[16,256]{1,0:T(8,128)S(1)}, u32[]{:S(2)}, u32[]{:S(2)}) collective-permute-start(f32[16,256]{1,0:T(8,128)S(1)} %add.63), channel_id=1, source_target_pairs={{0,6},{1,7},{2,4},{3,5},{4,2},{5,3},{6,0},{7,1},{8,14},{9,15},{10,... | collective-permute-start | bytes 49160 | tf_op jit(solution)/shard_map/ppermute | solution.py:60
  186.9 20.9 %collective-permute-start.19 = (bf16[16,128,256]{2,1,0:T(8,128)(2,1)S(1)}, bf16[16,128,256]{2,1,0:T(8,128)(2,1)S(1)}, u32[]{:S(2)}, u32[]{:S(2)}) collective-permute-start(bf16[16,128,256]{2,1,0:T(8,128)(2,1)S(1)} %constant_dynamic-update-slice_fusion), channel_id=1, source_target_pairs={{0,1},{1,0},{2,3},{3,2},{4,5},{5,4},{6,7},{7,6},{8,9},{9,8},{10,11... | collective-permute-start | bytes 3145736 | tf_op jit(solution)/shard_map/ppermute | solution.py:44
  191.8 4.7 %collective-permute-start.36 = (f32[32,256]{1,0:T(8,128)S(1)}, f32[32,256]{1,0:T(8,128)S(1)}, u32[]{:S(2)}, u32[]{:S(2)}) collective-permute-start(f32[32,256]{1,0:T(8,128)S(1)} %pad_maximum_fusion.4), channel_id=1, source_target_pairs={{0,2},{1,3},{2,0},{3,1},{4,6},{5,7},{6,4},{7,5},{8,10},{9,11},{10,... | collective-permute-start | bytes 98312 | tf_op jit(solution)/shard_map/ppermute | solution.py:60
  196.5 9.4 %collective-permute-start.37 = (f32[64,256]{1,0:T(8,128)S(1)}, f32[64,256]{1,0:T(8,128)S(1)}, u32[]{:S(2)}, u32[]{:S(2)}) collective-permute-start(f32[64,256]{1,0:T(8,128)S(1)} %pad_maximum_fusion.3), channel_id=1, source_target_pairs={{0,96},{32,64},{64,32},{96,0},{128,224},{160,192},{192,160},{224,1... | collective-permute-start | bytes 196616 | tf_op jit(solution)/shard_map/ppermute | solution.py:68
  200.9 2.2 copy-start.1
  203.1 0.7 copy-start.5
  203.1 0.7 copy-start.7
  203.1 0.8 copy-start.9
  203.1 0.8 copy-start.11
  205.9 16.6 %collective-permute-start.38 = (f32[128,256]{1,0:T(8,128)S(1)}, f32[128,256]{1,0:T(8,128)S(1)}, u32[]{:S(2)}, u32[]{:S(2)}) collective-permute-start(f32[128,256]{1,0:T(8,128)S(1)} %pad_maximum_fusion.2), channel_id=1, source_target_pairs={{0,32},{32,0},{64,96},{96,64},{128,160},{160,128},{192,224},{224,1... | collective-permute-start | bytes 393224 | tf_op jit(solution)/shard_map/ppermute | solution.py:68
  209.8 13.7 %collective-permute-start.20 = (bf16[4,128,256]{2,1,0:T(8,128)(2,1)S(1)}, bf16[4,128,256]{2,1,0:T(8,128)(2,1)S(1)}, u32[]{:S(2)}, u32[]{:S(2)}) collective-permute-start(bf16[4,128,256]{2,1,0:T(8,128)(2,1)S(1)} %get-tuple-element.17), channel_id=1, source_target_pairs={{0,32},{32,64},{64,96},{96,0},{128,160},{160,192},{192,224},{224,1... | collective-permute-start | bytes 786440 | tf_op jit(solution)/shard_map/ppermute | solution.py:52
  213.5 11.5 %collective-permute-start.22 = (bf16[4,128,256]{2,1,0:T(8,128)(2,1)S(1)}, bf16[4,128,256]{2,1,0:T(8,128)(2,1)S(1)}, u32[]{:S(2)}, u32[]{:S(2)}) collective-permute-start(bf16[4,128,256]{2,1,0:T(8,128)(2,1)S(1)} %get-tuple-element.18), channel_id=1, source_target_pairs={{0,96},{32,0},{64,32},{96,64},{128,224},{160,128},{192,160},{224,1... | collective-permute-start | bytes 786440 | tf_op jit(solution)/shard_map/ppermute | solution.py:52
  218.7 11.1 %collective-permute-start.21 = (bf16[4,128,256]{2,1,0:T(8,128)(2,1)S(1)}, bf16[4,128,256]{2,1,0:T(8,128)(2,1)S(1)}, u32[]{:S(2)}, u32[]{:S(2)}) collective-permute-start(bf16[4,128,256]{2,1,0:T(8,128)(2,1)S(1)} %get-tuple-element.19), channel_id=1, source_target_pairs={{0,64},{32,96},{64,0},{96,32},{128,192},{160,224},{192,128},{224,1... | collective-permute-start | bytes 786440 | tf_op jit(solution)/shard_map/ppermute | solution.py:52
  230.0 8.0 %collective-permute-start.25 = (bf16[128,256]{1,0:T(8,128)(2,1)S(1)}, bf16[128,256]{1,0:T(8,128)(2,1)S(1)}, u32[]{:S(2)}, u32[]{:S(2)}) collective-permute-start(bf16[128,256]{1,0:T(8,128)(2,1)S(1)} %get-tuple-element.29), channel_id=1, source_target_pairs={{0,384},{32,416},{64,448},{96,480},{128,0},{160,32},{192,64},{224,... | collective-permute-start | bytes 196616 | tf_op jit(solution)/shard_map/ppermute | solution.py:48
  231.9 6.0 %collective-permute-start.24 = (bf16[128,256]{1,0:T(8,128)(2,1)S(1)}, bf16[128,256]{1,0:T(8,128)(2,1)S(1)}, u32[]{:S(2)}, u32[]{:S(2)}) collective-permute-start(bf16[128,256]{1,0:T(8,128)(2,1)S(1)} %get-tuple-element.30), channel_id=1, source_target_pairs={{0,256},{32,288},{64,320},{96,352},{128,384},{160,416},{192,448},{... | collective-permute-start | bytes 196616 | tf_op jit(solution)/shard_map/ppermute | solution.py:48
  233.9 7.6 %collective-permute-start.23 = (bf16[128,256]{1,0:T(8,128)(2,1)S(1)}, bf16[128,256]{1,0:T(8,128)(2,1)S(1)}, u32[]{:S(2)}, u32[]{:S(2)}) collective-permute-start(bf16[128,256]{1,0:T(8,128)(2,1)S(1)} %get-tuple-element.31), channel_id=1, source_target_pairs={{0,128},{32,160},{64,192},{96,224},{128,256},{160,288},{192,320},{... | collective-permute-start | bytes 196616 | tf_op jit(solution)/shard_map/ppermute | solution.py:48
  (3 other events, 2.0 us)

commit v2 on v0

v2 whole, which is shorter than its diff:
```python
import functools
import math

import jax
import jax.numpy as jnp
from jax import lax
from jax.experimental import pallas as pl
from jax.experimental.pallas import tpu as pltpu
from jax.sharding import PartitionSpec as P

TILE = 128
ROWS = 16
COLS = 32
HALF = 16
GROUP = 8
UNROLL = 4
LIST = 192
VMEM_LIMIT = 24 * 1024 * 1024
BF16 = jnp.bfloat16
F32 = jnp.float32


def send_y(v, k):
    pairs = [(c, (c // 8) * 8 + ((c // 2 + k) % 4) * 2 + c % 2) for c in range(COLS)]
    return lax.ppermute(v, "col", pairs)


def send_core(v):
    return lax.ppermute(v, "col", [(c, c ^ 1) for c in range(COLS)])


def trade_row(v):
    return lax.all_to_all(v, "row", 0, 0)


def trade_zh(v):
    groups = [[zh * 8 + rest for zh in range(4)] for rest in range(8)]
    return lax.all_to_all(v, "col", 0, 0, axis_index_groups=groups)


def smem():
    return pl.BlockSpec(memory_space=pltpu.SMEM)


def vmem():
    return pl.BlockSpec(memory_space=pltpu.VMEM)


def params():
    return pltpu.CompilerParams(vmem_limit_bytes=VMEM_LIMIT)


def cost(flops, mib):
    return pl.CostEstimate(flops=flops, bytes_accessed=mib * 1024 * 1024, transcendentals=0)


def forward_kernel(where, rows, cols, count, v, xs, give, keep, acc):
    y, core = where[1], where[2]
    acc[...] = jnp.zeros_like(acc)
    live = count[0, 0]

    def step(g, _):
        products, dests = [], []
        for u in range(GROUP):
            s = g * GROUP + u
            r = rows[0, 0, s]
            mine = jnp.where((r & 1) == core, HALF, 0)
            d = mine + ((((r >> 1) & 3) - y) & 3) * 4 + (r >> 3)
            dests.append(jnp.where(s < live, d, 2 * HALF))
            products.append(
                jnp.dot(v[0, 0, s], xs[cols[0, 0, s]], preferred_element_type=F32)
            )
        for u in range(GROUP):
            acc[dests[u]] = acc[dests[u]] + products[u]
        return 0

    lax.fori_loop(0, (live + GROUP - 1) // GROUP, step, 0)
    give[...] = acc[:HALF].astype(BF16)
    keep[...] = acc[HALF : 2 * HALF].astype(BF16)


def forward(where, rows, cols, count, values, xs):
    width = xs.shape[-1]
    half = jax.ShapeDtypeStruct((HALF, TILE, width), BF16)
    return pl.pallas_call(
        forward_kernel,
        out_shape=(half, half),
        in_specs=[smem()] * 4 + [vmem()] * 2,
        out_specs=(vmem(), vmem()),
        scratch_shapes=[pltpu.VMEM((2 * HALF + 1, TILE, width), F32)],
        compiler_params=params(),
        cost_estimate=cost(2 * 128 * TILE * TILE * width, 7),
        name="forward",
    )(where, rows, cols, count, values, xs)


def plan_kernel(where, rows, cols, count, slots, sources, dests, groups, head, link):
    zh, y, core = where[0], where[1], where[2]

    def clear(i, _):
        head[i] = -1
        return 0

    lax.fori_loop(0, 2 * HALF, clear, 0)

    def chain(s, _):
        r, c = rows[0, 0, s], cols[0, 0, s]
        at = jnp.where((r & 1) == core, 0, HALF) + c
        link[s] = head[at]
        head[at] = s
        return 0

    lax.fori_loop(0, count[0, 0], chain, 0)

    for q in range(2):

        def segment(d, pos, q=q):
            def more(state):
                return state[0] >= 0

            def emit(state):
                s, at = state
                r = rows[0, 0, s]
                slots[q, at] = s
                sources[q, at] = ((y - ((r >> 1) & 3)) & 3) * 4 + (r >> 3)
                dests[q, at >> 1] = d
                return link[s], at + 1

            _, at = lax.while_loop(more, emit, (head[q * HALF + d], pos))

            @pl.when((at & 1) == 1)
            def _():
                slots[q, at] = 0
                sources[q, at] = HALF

            return at + (at & 1)

        total = lax.fori_loop(0, HALF, segment, 0)

        for i in range(2 * UNROLL):
            slots[q, total + i] = 0
            sources[q, total + i] = HALF
            dests[q, (total >> 1) + (i >> 1)] = 0
        groups[q] = ((total >> 1) + UNROLL - 1) // UNROLL


def make_plan(where, rows, cols, count):
    i32 = jnp.int32
    lists = jax.ShapeDtypeStruct((2, LIST), i32)
    return pl.pallas_call(
        plan_kernel,
        out_shape=(lists, lists, lists, jax.ShapeDtypeStruct((2,), i32)),
        in_specs=[smem()] * 4,
        out_specs=(smem(),) * 4,
        scratch_shapes=[pltpu.SMEM((2 * HALF,), i32), pltpu.SMEM((TILE,), i32)],
        cost_estimate=cost(0, 8),
        name="plan",
    )(where, rows, cols, count)


def turn_kernel(count, v, out):
    def step(i, _):
        for u in range(4):
            out[4 * i + u] = v[0, 0, 4 * i + u].T
        return 0

    lax.fori_loop(0, (count[0, 0] + 3) // 4, step, 0)


def turn_tiles(count, tile_values):
    return pl.pallas_call(
        turn_kernel,
        out_shape=jax.ShapeDtypeStruct(tile_values.shape[2:], tile_values.dtype),
        in_specs=[smem(), vmem()],
        out_specs=vmem(),
        compiler_params=params(),
        cost_estimate=cost(0, 10),
        name="turn",
    )(count, tile_values)


def middle_kernel(got, w, cot, act_out, grad_out, part_out):
    total = got[0].astype(F32)
    for i in range(1, 4):
        total = total + got[i].astype(F32)
    aggregated = total.astype(BF16)
    pre = jnp.dot(aggregated, w[...], preferred_element_type=F32)
    s = jax.nn.sigmoid(pre)
    act_out[...] = (pre * s).astype(BF16)
    grad = (cot[...].astype(F32) * (s * (1.0 + pre * (1.0 - s)))).astype(BF16)
    grad_out[...] = grad
    part = lax.dot_general(aggregated, grad, (((0,), (0,)), ((), ())), preferred_element_type=F32)
    part_out[...] = part.reshape(part_out.shape).astype(BF16)


def middle(got, w, cot):
    n, width = cot.shape
    rows = jax.ShapeDtypeStruct((n, width), BF16)
    return pl.pallas_call(
        middle_kernel,
        out_shape=(rows, rows, jax.ShapeDtypeStruct((ROWS, width // ROWS, width), BF16)),
        compiler_params=params(),
        cost_estimate=cost(4 * n * width * width, 1),
        name="middle",
    )(got, w, cot)


def pack_kernel(grad, parts, out):
    total = parts[0].astype(F32)
    for i in range(1, ROWS):
        total = total + parts[i].astype(F32)
    part = total.astype(BF16)
    for i in range(4):
        out[i, :TILE] = grad[...]
        out[i, TILE:] = part


def pack(grad, parts):
    n, width = grad.shape
    return pl.pallas_call(
        pack_kernel,
        out_shape=jax.ShapeDtypeStruct((4, n + parts.shape[1], width), BF16),
        compiler_params=params(),
        cost_estimate=cost(0, 1),
        name="pack",
    )(grad, parts)


def fold_kernel(got, out):
    total = got[0, TILE:].astype(F32)
    for i in range(1, 4):
        total = total + got[i, TILE:].astype(F32)
    for i in range(4):
        out[TILE * i : TILE * (i + 1)] = got[i, :TILE]
    out[4 * TILE :] = total.astype(BF16)


def fold(got):
    extra, width = got.shape[1] - TILE, got.shape[2]
    return pl.pallas_call(
        fold_kernel,
        out_shape=jax.ShapeDtypeStruct((4 * TILE + extra, width), BF16),
        compiler_params=params(),
        cost_estimate=cost(0, 1),
        name="fold",
    )(got)


def collect_kernel(where, l0, l1, l2, l3, out, slices):
    y = where[1]
    rows = 4 * TILE
    for k, line in enumerate((l0, l1, l2, l3)):
        out[rows * k : rows * (k + 1)] = line[:rows]
        slices[(y - k) & 3] = line[rows:].astype(F32)
    out[4 * rows :] = ((slices[0] + slices[1]) + (slices[2] + slices[3])).astype(BF16)


def collect(where, lines):
    rows, width = lines[0].shape
    extra = rows - 4 * TILE
    return pl.pallas_call(
        collect_kernel,
        out_shape=jax.ShapeDtypeStruct((HALF * TILE + extra, width), BF16),
        in_specs=[smem()] + [vmem()] * 4,
        out_specs=vmem(),
        scratch_shapes=[pltpu.VMEM((4, extra, width), F32)],
        compiler_params=params(),
        cost_estimate=cost(0, 3),
        name="collect",
    )(where, *lines)


def gather_products(q, slots, sources, dests, groups, v, grads, held, acc):
    rows = HALF * TILE
    held[:rows] = grads[:rows]
    held[rows:] = jnp.zeros((TILE, held.shape[1]), BF16)

    def tile(at):
        return held[pl.ds(pl.multiple_of(sources[q, at] * TILE, TILE), TILE)]

    def step(g, _):
        products = []
        for u in range(UNROLL):
            at = (g * UNROLL + u) * 2
            left = jnp.concatenate([v[slots[q, at]], v[slots[q, at + 1]]], axis=1)
            right = jnp.concatenate([tile(at), tile(at + 1)], axis=0)
            products.append(jnp.dot(left, right, preferred_element_type=F32))
        for u in range(UNROLL):
            d = dests[q, g * UNROLL + u]
            acc[d] = acc[d] + products[u]
        return 0

    lax.fori_loop(0, groups[q], step, 0)


def first_kernel(slots, sources, dests, groups, v, grads, acc, held):
    acc[...] = jnp.zeros_like(acc)
    gather_products(0, slots, sources, dests, groups, v, grads, held, acc)


def second_kernel(slots, sources, dests, groups, v, grads, mine, start, out, held, acc):
    acc[...] = start[...]
    gather_products(1, slots, sources, dests, groups, v, grads, held, acc)
    rows = HALF * TILE
    part = (mine[rows:].astype(F32) + grads[rows:].astype(F32)).astype(BF16)
    for d in range(HALF):
        out[d, :TILE] = acc[d].astype(BF16)
        out[d, TILE:] = part


def backward(plan, v, mine, theirs):
    rows, width = mine.shape
    extra = rows - HALF * TILE
    held = pltpu.VMEM(((HALF + 1) * TILE, width), BF16)
    sums = (HALF, TILE, width)
    work = cost(2 * 64 * TILE * TILE * width, 8)
    first = pl.pallas_call(
        first_kernel,
        out_shape=jax.ShapeDtypeStruct(sums, F32),
        in_specs=[smem()] * 4 + [vmem()] * 2,
        out_specs=vmem(),
        scratch_shapes=[held],
        compiler_params=params(),
        cost_estimate=work,
        name="first",
    )(*plan, v, mine)
    return pl.pallas_call(
        second_kernel,
        out_shape=jax.ShapeDtypeStruct((HALF, TILE + extra, width), BF16),
        in_specs=[smem()] * 4 + [vmem()] * 4,
        out_specs=vmem(),
        scratch_shapes=[held, pltpu.VMEM(sums, F32)],
        compiler_params=params(),
        cost_estimate=work,
        name="second",
    )(*plan, v, theirs, mine, first)


def last_kernel(scale, got, w, grad_out, weight_out):
    total = got[0, :TILE].astype(F32)
    for i in range(1, ROWS):
        total = total + got[i, :TILE].astype(F32)
    grad_out[...] = lax.dot_general(
        total.astype(BF16), w[...], (((1,), (1,)), ((), ())), preferred_element_type=F32
    ).astype(BF16)
    extra = got.shape[1] - TILE
    for i in range(ROWS):
        weight_out[extra * i : extra * (i + 1)] = got[i, TILE:].astype(F32) * scale


def last(got, w, scale):
    width = w.shape[0]
    return pl.pallas_call(
        functools.partial(last_kernel, scale),
        out_shape=(
            jax.ShapeDtypeStruct((TILE, width), BF16),
            jax.ShapeDtypeStruct((width, width), F32),
        ),
        compiler_params=params(),
        cost_estimate=cost(2 * TILE * width * width, 1),
        name="last",
    )(got, w)


def shards(features, weight, tile_values, tile_rows, tile_cols, tile_count, cotangent):
    node_dev = features.shape[0]
    grad_scale = 1.0 / math.sqrt(node_dev * lax.axis_size("row") * lax.axis_size("col"))
    c = lax.axis_index("col")
    where = jnp.stack([c >> 3, (c >> 1) & 3, c & 1]).astype(jnp.int32)

    xs = trade_row(jnp.broadcast_to(features[None], (ROWS,) + features.shape))
    give, keep = forward(where, tile_rows, tile_cols, tile_count, tile_values, xs)
    got = send_core(give)
    paired = (keep.astype(F32) + got.astype(F32)).astype(BF16).reshape(4, 4, TILE, -1)
    others = [send_y(paired[k], k).astype(F32) for k in (1, 2, 3)]
    block = (paired[0].astype(F32) + others[0] + others[1] + others[2]).astype(BF16)
    plan = make_plan(where, tile_rows, tile_cols, tile_count)
    turned = turn_tiles(tile_count, tile_values)
    activated, grad_pre, part = middle(trade_zh(block), weight, cotangent)

    line = fold(trade_zh(pack(grad_pre, trade_row(part))))
    mine = collect(where, [line] + [send_y(line, k) for k in (1, 2, 3)])
    spread = backward(plan, turned, mine, send_core(mine))
    grad_features, grad_weight = last(trade_row(spread), weight, grad_scale)
    return (activated, grad_features, grad_weight)


def solution(mesh):
    return jax.shard_map(
        shards,
        mesh=mesh,
        in_specs=(
            P(("col", "row"), None),
            P(),
            P("row", "col", None, None, None),
            P("row", "col", None),
            P("row", "col", None),
            P("row", "col"),
            P(("row", "col"), None),
        ),
        out_specs=(P(("row", "col"), None), P(("col", "row"), None), P()),
        check_vma=False,
    )
```

time: 920 us -> 211 us (0.23); the launches traced: 909 us -> 210 us
  waiting for transfers between devices: 812 us -> 38.3 us
  blocking collectives: 0 us -> 106 us
  starting transfers between devices: 0.2 us -> 43 us
  other arithmetic: 42.6 us -> 0.54 us
  matrix products: 21.2 us -> 0 us
  Pallas kernels: 0 us -> 15 us
  between operations: 14.5 us -> 1.51 us
  local copies, waits for them, and re-layouts: 17.7 us -> 6.42 us
    psum x1 -> x0, waiting for transfers between devices: 424 us -> none  [shards(): grad_weight = lax.psum(weight_part, ('row', 'col')) * grad_scale]
    reduce_scatter x2 -> x0, waiting for transfers between devices: 236 us -> none  [the longest x1 159 us: shards(): lax.psum_scatter(partial_value.astype(jnp.bfloat16), 'col', scatter_dimen...]
    all_gather x2 -> x0, waiting for transfers between devices: 152 us -> none  [the longest x1 83.1 us: shards(): column_block = lax.all_gather(features, 'row', axis=0, tiled=True)]
    all_to_all x0 -> x4, blocking collectives: none -> 106 us  [the longest x2 60.2 us: trade_row(): return lax.all_to_all(v, 'row', 0, 0)]
    ppermute x0 -> x8, starting transfers between devices: none -> 33.9 us  [the longest x6 22 us: send_y(): return lax.ppermute(v, 'col', pairs)]
    scatter-add x4 -> x0, other arithmetic: 33 us -> none  [the longest x2 20.1 us: forward_one_round(): return running.at[round_rows].add(tile_products * in_use[:, None, None])]
    all_to_all x0 -> x1, waiting for transfers between devices: none -> 21.4 us  [trade_row(): return lax.all_to_all(v, 'row', 0, 0)]
    dot_general x7 -> x0, matrix products: 21.2 us -> none  [the longest x2 9.18 us: backward_one_round(): jnp.einsum('smk,smf->skf', round_values, gathered, preferred_element_type...]
  transfers between devices with their start and end apart: 5 -> 9, of which waited for: 5 -> 8; matrix products, arithmetic and copies ran while one was open for 5% -> 0% of each run, Pallas kernels for 0% -> 3%
where the time goes in v2:
time: 211 us; the launch traced here: 210 us
  blocking collectives  106 us (50%)
  starting transfers between devices  43 us (20%)
  waiting for transfers between devices  38.3 us (18%)
  Pallas kernels  15 us (7%)
  local copies, waits for them, and re-layouts  6.42 us (3%)
    all_to_all x2, blocking collectives, trade_row(): return lax.all_to_all(v, 'row', 0, 0)  60.2 us
    all_to_all x2, blocking collectives, trade_zh(): return lax.all_to_all(v, 'col', 0, 0, axis_index_groups=groups)  45.4 us
    ppermute x6, starting transfers between devices, send_y(): return lax.ppermute(v, 'col', pairs)  22 us
    all_to_all x1, waiting for transfers between devices, trade_row(): return lax.all_to_all(v, 'row', 0, 0)  21.4 us
    ppermute x6, waiting for transfers between devices, send_y(): return lax.ppermute(v, 'col', pairs)  14.6 us
    ppermute x2, starting transfers between devices, send_core(): return lax.ppermute(v, 'col', [(c, c ^ 1) for c in range(COLS)])  11.9 us
    all_to_all x1, starting transfers between devices, trade_row(): return lax.all_to_all(v, 'row', 0, 0)  9.01 us
    unnamed x22, local copies, waits for them, and re-layouts  4.42 us
  transfers between devices with their start and end apart: 9, of which 8 were waited for; matrix products, arithmetic and copies ran while one was open for 0% of the time, Pallas kernels for 3%

profile of v2, /device:TPU:1, one launch (start us, length us, event | category | flops | bytes accessed | tf_op | source)
XLA Modules:
  0.0 210.3 jit_solution(17651102765262656594)
XLA Ops:
  0.6 0.0 copy-start.10
  0.6 0.0 copy-start.9
  0.7 2.0 broadcast_in_dim.2
  2.6 9.0 %all-to-all-start = ((bf16[16,128,256]{2,1,0:T(8,128)(2,1)}), bf16[16,128,256]{2,1,0:T(8,128)(2,1)S(1)}, u32[]{:S(2)}, u32[]{:S(2)}) async-start(bf16[16,128,256]{2,1,0:T(8,128)(2,1)} %broadcast_in_dim.2), calls=%async_computation | async-start | bytes 2097152 | tf_op jit(solution)/shard_map/all_to_all | solution.py:33
  12.3 0.1 pad_add_fusion.where
  12.4 21.4 %all-to-all-done.xs = bf16[16,128,256]{2,1,0:T(8,128)(2,1)S(1)} async-done(((bf16[16,128,256]{2,1,0:T(8,128)(2,1)}), bf16[16,128,256]{2,1,0:T(8,128)(2,1)S(1)}, u32[]{:S(2)}, u32[]{:S(2)}) %all-to-all-start) | async-done | bytes 1048608 | tf_op jit(solution)/shard_map/all_to_all | solution.py:33
  33.7 0.0 copy-done.10
  33.7 0.0 copy-done.9
  33.7 2.2 %copy-done = bf16[1,1,128,128,128]{4,3,2,1,0:T(8,128)(2,1)S(1)} copy-done((bf16[1,1,128,128,128]{4,3,2,1,0:T(8,128)(2,1)S(1)}, bf16[1,1,128,128,128]{4,3,2,1,0:T(8,128)(2,1)}, u32[]{:S(2)}) %copy-start) | copy-done | bytes 4194328
  35.9 3.5 %forward.1 = (bf16[16,128,256]{2,1,0:T(8,128)(2,1)S(1)}, bf16[16,128,256]{2,1,0:T(8,128)(2,1)S(1)}) custom-call(s32[3]{0:T(128)S(1)} %pad_add_fusion.where, s32[1,1,128]{2,1,0:T(1,128)S(1)} %copy-done.9, s32[1,1,128]{2,1,0:T(1,128)S(1)} %copy-done.10, s32[1,1]{1,0:T(1,128)S(6)} %copy.10.count, bf16[1,1,128,128,128]{4,3,2,1,0:T(8,128)(2,1)S(1)} %copy-done, ...), custom_call_target="tpu_custom_call" | custom-call | flops 1073741824 | bytes 7340032 | tf_op jit(solution)/shard_map/forward/pallas_call | solution.py:85
  39.4 4.2 %collective-permute-start = (bf16[16,128,256]{2,1,0:T(8,128)(2,1)S(1)}, bf16[16,128,256]{2,1,0:T(8,128)(2,1)S(1)}, u32[]{:S(2)}, u32[]{:S(2)}) collective-permute-start(bf16[16,128,256]{2,1,0:T(8,128)(2,1)S(1)} %get-tuple-element.15), channel_id=1, source_target_pairs={{0,1},{1,0},{2,3},{3,2},{4,5},{5,4},{6,7},{7,6},{8,9},{9,8},{10,11... | collective-permute-start | bytes 3145736 | tf_op jit(solution)/shard_map/ppermute | solution.py:29
  43.6 2.3 %collective-permute-done = bf16[16,128,256]{2,1,0:T(8,128)(2,1)S(1)} collective-permute-done((bf16[16,128,256]{2,1,0:T(8,128)(2,1)S(1)}, bf16[16,128,256]{2,1,0:T(8,128)(2,1)S(1)}, u32[]{:S(2)}, u32[]{:S(2)}) %collective-permute-start) | collective-permute-done | bytes 1048608 | tf_op jit(solution)/shard_map/ppermute | solution.py:29
  45.9 0.3 add_convert_fusion
  46.2 0.0 copy-start.2
  46.2 0.0 copy-start.3
  46.2 0.1 fusion
  46.3 4.1 %collective-permute-start.1 = (bf16[4,128,256]{2,1,0:T(8,128)(2,1)S(1)}, bf16[4,128,256]{2,1,0:T(8,128)(2,1)S(1)}, u32[]{:S(2)}, u32[]{:S(2)}) collective-permute-start(bf16[4,128,256]{2,1,0:T(8,128)(2,1)S(1)} %get-tuple-element.25), channel_id=1, source_target_pairs={{0,2},{1,3},{2,4},{3,5},{4,6},{5,7},{6,0},{7,1},{8,10},{9,11},{10,... | collective-permute-start | bytes 786440 | tf_op jit(solution)/shard_map/ppermute | solution.py:25
  50.4 3.4 %collective-permute-start.3 = (bf16[4,128,256]{2,1,0:T(8,128)(2,1)S(1)}, bf16[4,128,256]{2,1,0:T(8,128)(2,1)S(1)}, u32[]{:S(2)}, u32[]{:S(2)}) collective-permute-start(bf16[4,128,256]{2,1,0:T(8,128)(2,1)S(1)} %get-tuple-element.26), channel_id=1, source_target_pairs={{0,6},{1,7},{2,0},{3,1},{4,2},{5,3},{6,4},{7,5},{8,14},{9,15},{10,... | collective-permute-start | bytes 786440 | tf_op jit(solution)/shard_map/ppermute | solution.py:25
  53.7 3.8 %collective-permute-start.2 = (bf16[4,128,256]{2,1,0:T(8,128)(2,1)S(1)}, bf16[4,128,256]{2,1,0:T(8,128)(2,1)S(1)}, u32[]{:S(2)}, u32[]{:S(2)}) collective-permute-start(bf16[4,128,256]{2,1,0:T(8,128)(2,1)S(1)} %get-tuple-element.27), channel_id=1, source_target_pairs={{0,4},{1,5},{2,6},{3,7},{4,0},{5,1},{6,2},{7,3},{8,12},{9,13},{10,... | collective-permute-start | bytes 786440 | tf_op jit(solution)/shard_map/ppermute | solution.py:25
  57.6 0.6 collective-permute-done.1
  58.2 1.6 collective-permute-done.3
  59.8 4.6 %collective-permute-done.2 = bf16[4,128,256]{2,1,0:T(8,128)(2,1)S(1)} collective-permute-done((bf16[4,128,256]{2,1,0:T(8,128)(2,1)S(1)}, bf16[4,128,256]{2,1,0:T(8,128)(2,1)S(1)}, u32[]{:S(2)}, u32[]{:S(2)}) %collective-permute-start.2) | collective-permute-done | bytes 262176 | tf_op jit(solution)/shard_map/ppermute | solution.py:25
  64.3 0.1 add_convert_fusion.1
  64.5 24.6 %all_to_all.25.got = bf16[4,128,256]{2,1,0:T(8,128)(2,1)S(1)} all-to-all(bf16[4,128,256]{2,1,0:T(8,128)(2,1)S(1)} %add_convert_fusion.1), channel_id=1, replica_groups={{0,8,16,24},{1,9,17,25},{2,10,18,26},{3,11,19,27},{4,12,20,28},{5,13,21..., dimensions={0} | all-to-all | bytes 524288 | tf_op jit(solution)/shard_map/all_to_all | solution.py:38
  89.1 0.0 copy-done.2
  89.1 0.0 copy-done.3
  89.1 0.8 middle.1
  90.0 20.1 %all_to_all.26.parts = bf16[16,16,256]{2,1,0:T(8,128)(2,1)S(1)} all-to-all(bf16[16,16,256]{2,1,0:T(8,128)(2,1)S(1)} %get-tuple-element.22), channel_id=1, replica_groups=mesh['row'=16,'col'=32] {'row'}, dimensions={0} | all-to-all | bytes 262144 | tf_op jit(solution)/shard_map/all_to_all | solution.py:33
  110.1 20.8 %all_to_all.27.got = bf16[4,144,256]{2,1,0:T(8,128)(2,1)S(1)} all-to-all(bf16[4,144,256]{2,1,0:T(8,128)(2,1)S(1)} %pack.1), channel_id=1, replica_groups={{0,8,16,24},{1,9,17,25},{2,10,18,26},{3,11,19,27},{4,12,20,28},{5,13,21..., dimensions={0} | all-to-all | bytes 589824 | tf_op jit(solution)/shard_map/all_to_all | solution.py:38
  130.9 6.4 %collective-permute-start.6 = (bf16[528,256]{1,0:T(8,128)(2,1)S(1)}, bf16[528,256]{1,0:T(8,128)(2,1)S(1)}, u32[]{:S(2)}, u32[]{:S(2)}) collective-permute-start(bf16[528,256]{1,0:T(8,128)(2,1)S(1)} %fold.1.l0), channel_id=1, source_target_pairs={{0,6},{1,7},{2,0},{3,1},{4,2},{5,3},{6,4},{7,5},{8,14},{9,15},{10,... | collective-permute-start | bytes 811016 | tf_op jit(solution)/shard_map/ppermute | solution.py:25
  137.3 2.2 %collective-permute-start.5 = (bf16[528,256]{1,0:T(8,128)(2,1)S(1)}, bf16[528,256]{1,0:T(8,128)(2,1)S(1)}, u32[]{:S(2)}, u32[]{:S(2)}) collective-permute-start(bf16[528,256]{1,0:T(8,128)(2,1)S(1)} %fold.1.l0), channel_id=1, source_target_pairs={{0,4},{1,5},{2,6},{3,7},{4,0},{5,1},{6,2},{7,3},{8,12},{9,13},{10,... | collective-permute-start | bytes 811016 | tf_op jit(solution)/shard_map/ppermute | solution.py:25
  139.4 2.2 %collective-permute-start.4 = (bf16[528,256]{1,0:T(8,128)(2,1)S(1)}, bf16[528,256]{1,0:T(8,128)(2,1)S(1)}, u32[]{:S(2)}, u32[]{:S(2)}) collective-permute-start(bf16[528,256]{1,0:T(8,128)(2,1)S(1)} %fold.1.l0), channel_id=1, source_target_pairs={{0,2},{1,3},{2,4},{3,5},{4,6},{5,7},{6,0},{7,1},{8,10},{9,11},{10,... | collective-permute-start | bytes 811016 | tf_op jit(solution)/shard_map/ppermute | solution.py:25
  141.7 0.3 collective-permute-done.6.l3
  142.0 4.1 %collective-permute-done.5.l2 = bf16[528,256]{1,0:T(8,128)(2,1)S(1)} collective-permute-done((bf16[528,256]{1,0:T(8,128)(2,1)S(1)}, bf16[528,256]{1,0:T(8,128)(2,1)S(1)}, u32[]{:S(2)}, u32[]{:S(2)}) %collective-permute-start.5) | collective-permute-done | bytes 270368 | tf_op jit(solution)/shard_map/ppermute | solution.py:25
  146.1 3.5 %collective-permute-done.4.l1 = bf16[528,256]{1,0:T(8,128)(2,1)S(1)} collective-permute-done((bf16[528,256]{1,0:T(8,128)(2,1)S(1)}, bf16[528,256]{1,0:T(8,128)(2,1)S(1)}, u32[]{:S(2)}, u32[]{:S(2)}) %collective-permute-start.4) | collective-permute-done | bytes 270368 | tf_op jit(solution)/shard_map/ppermute | solution.py:25
  149.6 0.0 copy-done.7
  149.6 0.6 collect.1.grads.mine
  150.2 7.7 %collective-permute-start.7 = (bf16[2064,256]{1,0:T(8,128)(2,1)S(1)}, bf16[2064,256]{1,0:T(8,128)(2,1)S(1)}, u32[]{:S(2)}, u32[]{:S(2)}) collective-permute-start(bf16[2064,256]{1,0:T(8,128)(2,1)S(1)} %collect.1.grads.mine), channel_id=1, source_target_pairs={{0,1},{1,0},{2,3},{3,2},{4,5},{5,4},{6,7},{7,6},{8,9},{9,8},{10,11... | collective-permute-start | bytes 3170312 | tf_op jit(solution)/shard_map/ppermute | solution.py:29
  157.9 3.5 %plan.1 = (s32[2,192]{1,0:T(2,128)}, s32[2,192]{1,0:T(2,128)}, s32[2,192]{1,0:T(2,128)}, s32[2]{0:T(128)}) custom-call(s32[3]{0:T(128)} %copy-done.7, s32[1,1,128]{2,1,0:T(1,128)} %rows.3, s32[1,1,128]{2,1,0:T(1,128)} %cols.3, s32[1,1]{1,0:T(1,128)S(6)} %copy.10.count), custom_call_target="tpu_custom_call" | custom-call | bytes 8388608 | tf_op jit(solution)/shard_map/plan/pallas_call | solution.py:150
  161.4 0.0 copy-start.1
  161.4 2.2 %copy-done.1 = bf16[1,1,128,128,128]{4,3,2,1,0:T(8,128)(2,1)S(1)} copy-done((bf16[1,1,128,128,128]{4,3,2,1,0:T(8,128)(2,1)S(1)}, bf16[1,1,128,128,128]{4,3,2,1,0:T(8,128)(2,1)}, u32[]{:S(2)}) %copy-start.1) | copy-done | bytes 4194328
  163.6 1.3 turn.1.v
  164.9 0.0 copy-done.4
  165.0 2.1 first.1.start
  167.0 0.0 collective-permute-done.7.grads
  167.0 2.2 %second.1 = bf16[16,144,256]{2,1,0:T(8,128)(2,1)S(1)} custom-call(s32[2,192]{1,0:T(2,128)S(1)} %copy-done.4, s32[2,192]{1,0:T(2,128)S(1)} %copy-done.5, s32[2,192]{1,0:T(2,128)S(1)} %copy-done.6, s32[2]{0:T(128)S(1)} %copy-done.8, bf16[128,128,128]{2,1,0:T(8,128)(2,1)S(1)} %turn.1.v, bf16[2064,256]{1,0:T(8,128)(2,1)S(1)} %collective-permute-done.7.grads, ...), custom_call_target="tpu_custom_call" | custom-call | flops 536870912 | bytes 8388608 | tf_op jit(solution)/shard_map/second/pallas_call | solution.py:327
  169.2 40.1 %all_to_all.28.got = bf16[16,144,256]{2,1,0:T(8,128)(2,1)S(1)} all-to-all(bf16[16,144,256]{2,1,0:T(8,128)(2,1)S(1)} %second.1), channel_id=1, replica_groups=mesh['row'=16,'col'=32] {'row'}, dimensions={0} | all-to-all | bytes 2359296 | tf_op jit(solution)/shard_map/all_to_all | solution.py:33
  209.3 0.9 last.1
  (11 shorter events, 0.1 us)
Async XLA Ops:
  0.6 33.1 %copy-start.10 = (s32[1,1,128]{2,1,0:T(1,128)S(1)}, s32[1,1,128]{2,1,0:T(1,128)}, u32[]{:S(2)}) copy-start(s32[1,1,128]{2,1,0:T(1,128)} %cols.3) | copy-start | bytes 1540
  0.6 33.1 %copy-start.9 = (s32[1,1,128]{2,1,0:T(1,128)S(1)}, s32[1,1,128]{2,1,0:T(1,128)}, u32[]{:S(2)}) copy-start(s32[1,1,128]{2,1,0:T(1,128)} %rows.3) | copy-start | bytes 1540
  2.6 31.1 %all-to-all-start = ((bf16[16,128,256]{2,1,0:T(8,128)(2,1)}), bf16[16,128,256]{2,1,0:T(8,128)(2,1)S(1)}, u32[]{:S(2)}, u32[]{:S(2)}) async-start(bf16[16,128,256]{2,1,0:T(8,128)(2,1)} %broadcast_in_dim.2), calls=%async_computation | async-start | bytes 2097152 | tf_op jit(solution)/shard_map/all_to_all | solution.py:33
  12.4 137.2 %copy-start.7 = (s32[3]{0:T(128)}, s32[3]{0:T(128)S(1)}, u32[]{:S(2)}) copy-start(s32[3]{0:T(128)S(1)} %pad_add_fusion.where) | copy-start | bytes 40
  33.7 2.2 %copy-start = (bf16[1,1,128,128,128]{4,3,2,1,0:T(8,128)(2,1)S(1)}, bf16[1,1,128,128,128]{4,3,2,1,0:T(8,128)(2,1)}, u32[]{:S(2)}) copy-start(bf16[1,1,128,128,128]{4,3,2,1,0:T(8,128)(2,1)} %v.3) | copy-start | bytes 12582916
  39.4 6.5 %collective-permute-start = (bf16[16,128,256]{2,1,0:T(8,128)(2,1)S(1)}, bf16[16,128,256]{2,1,0:T(8,128)(2,1)S(1)}, u32[]{:S(2)}, u32[]{:S(2)}) collective-permute-start(bf16[16,128,256]{2,1,0:T(8,128)(2,1)S(1)} %get-tuple-element.15), channel_id=1, source_target_pairs={{0,1},{1,0},{2,3},{3,2},{4,5},{5,4},{6,7},{7,6},{8,9},{9,8},{10,11... | collective-permute-start | bytes 3145736 | tf_op jit(solution)/shard_map/ppermute | solution.py:29
  46.2 42.9 %copy-start.2 = (bf16[256,256]{1,0:T(8,128)(2,1)S(1)}, bf16[256,256]{1,0:T(8,128)(2,1)}, u32[]{:S(2)}) copy-start(bf16[256,256]{1,0:T(8,128)(2,1)} %w.3) | copy-start | bytes 393220
  46.2 42.9 %copy-start.3 = (bf16[128,256]{1,0:T(8,128)(2,1)S(1)}, bf16[128,256]{1,0:T(8,128)(2,1)}, u32[]{:S(2)}) copy-start(bf16[128,256]{1,0:T(8,128)(2,1)} %cot.1) | copy-start | bytes 196612
  46.3 11.9 %collective-permute-start.1 = (bf16[4,128,256]{2,1,0:T(8,128)(2,1)S(1)}, bf16[4,128,256]{2,1,0:T(8,128)(2,1)S(1)}, u32[]{:S(2)}, u32[]{:S(2)}) collective-permute-start(bf16[4,128,256]{2,1,0:T(8,128)(2,1)S(1)} %get-tuple-element.25), channel_id=1, source_target_pairs={{0,2},{1,3},{2,4},{3,5},{4,6},{5,7},{6,0},{7,1},{8,10},{9,11},{10,... | collective-permute-start | bytes 786440 | tf_op jit(solution)/shard_map/ppermute | solution.py:25
  50.4 9.4 %collective-permute-start.3 = (bf16[4,128,256]{2,1,0:T(8,128)(2,1)S(1)}, bf16[4,128,256]{2,1,0:T(8,128)(2,1)S(1)}, u32[]{:S(2)}, u32[]{:S(2)}) collective-permute-start(bf16[4,128,256]{2,1,0:T(8,128)(2,1)S(1)} %get-tuple-element.26), channel_id=1, source_target_pairs={{0,6},{1,7},{2,0},{3,1},{4,2},{5,3},{6,4},{7,5},{8,14},{9,15},{10,... | collective-permute-start | bytes 786440 | tf_op jit(solution)/shard_map/ppermute | solution.py:25
  53.7 10.6 %collective-permute-start.2 = (bf16[4,128,256]{2,1,0:T(8,128)(2,1)S(1)}, bf16[4,128,256]{2,1,0:T(8,128)(2,1)S(1)}, u32[]{:S(2)}, u32[]{:S(2)}) collective-permute-start(bf16[4,128,256]{2,1,0:T(8,128)(2,1)S(1)} %get-tuple-element.27), channel_id=1, source_target_pairs={{0,4},{1,5},{2,6},{3,7},{4,0},{5,1},{6,2},{7,3},{8,12},{9,13},{10,... | collective-permute-start | bytes 786440 | tf_op jit(solution)/shard_map/ppermute | solution.py:25
  130.9 11.1 %collective-permute-start.6 = (bf16[528,256]{1,0:T(8,128)(2,1)S(1)}, bf16[528,256]{1,0:T(8,128)(2,1)S(1)}, u32[]{:S(2)}, u32[]{:S(2)}) collective-permute-start(bf16[528,256]{1,0:T(8,128)(2,1)S(1)} %fold.1.l0), channel_id=1, source_target_pairs={{0,6},{1,7},{2,0},{3,1},{4,2},{5,3},{6,4},{7,5},{8,14},{9,15},{10,... | collective-permute-start | bytes 811016 | tf_op jit(solution)/shard_map/ppermute | solution.py:25
  137.3 8.8 %collective-permute-start.5 = (bf16[528,256]{1,0:T(8,128)(2,1)S(1)}, bf16[528,256]{1,0:T(8,128)(2,1)S(1)}, u32[]{:S(2)}, u32[]{:S(2)}) collective-permute-start(bf16[528,256]{1,0:T(8,128)(2,1)S(1)} %fold.1.l0), channel_id=1, source_target_pairs={{0,4},{1,5},{2,6},{3,7},{4,0},{5,1},{6,2},{7,3},{8,12},{9,13},{10,... | collective-permute-start | bytes 811016 | tf_op jit(solution)/shard_map/ppermute | solution.py:25
  139.4 10.1 %collective-permute-start.4 = (bf16[528,256]{1,0:T(8,128)(2,1)S(1)}, bf16[528,256]{1,0:T(8,128)(2,1)S(1)}, u32[]{:S(2)}, u32[]{:S(2)}) collective-permute-start(bf16[528,256]{1,0:T(8,128)(2,1)S(1)} %fold.1.l0), channel_id=1, source_target_pairs={{0,2},{1,3},{2,4},{3,5},{4,6},{5,7},{6,0},{7,1},{8,10},{9,11},{10,... | collective-permute-start | bytes 811016 | tf_op jit(solution)/shard_map/ppermute | solution.py:25
  150.2 16.8 %collective-permute-start.7 = (bf16[2064,256]{1,0:T(8,128)(2,1)S(1)}, bf16[2064,256]{1,0:T(8,128)(2,1)S(1)}, u32[]{:S(2)}, u32[]{:S(2)}) collective-permute-start(bf16[2064,256]{1,0:T(8,128)(2,1)S(1)} %collect.1.grads.mine), channel_id=1, source_target_pairs={{0,1},{1,0},{2,3},{3,2},{4,5},{5,4},{6,7},{7,6},{8,9},{9,8},{10,11... | collective-permute-start | bytes 3170312 | tf_op jit(solution)/shard_map/ppermute | solution.py:29
  161.4 2.2 %copy-start.1 = (bf16[1,1,128,128,128]{4,3,2,1,0:T(8,128)(2,1)S(1)}, bf16[1,1,128,128,128]{4,3,2,1,0:T(8,128)(2,1)}, u32[]{:S(2)}) copy-start(bf16[1,1,128,128,128]{4,3,2,1,0:T(8,128)(2,1)} %v.3) | copy-start | bytes 12582916
  163.6 1.4 copy-start.4
  163.6 1.4 copy-start.5
  163.6 1.4 copy-start.6
  163.6 1.4 copy-start.8

commit v3 on v2

--- a/solution.py
+++ b/solution.py
@@ -9,12 +9,16 @@
 from jax.sharding import PartitionSpec as P
 
 TILE = 128
+SLOTS = 128
 ROWS = 16
 COLS = 32
 HALF = 16
-GROUP = 8
 UNROLL = 4
-LIST = 192
+SOURCE = 192
+TARGET = 384
+LENGTH = 480
+PLAN = 512
+CHUNK = 16
 VMEM_LIMIT = 24 * 1024 * 1024
 BF16 = jnp.bfloat16
 F32 = jnp.float32
@@ -54,111 +58,79 @@
     return pl.CostEstimate(flops=flops, bytes_accessed=mib * 1024 * 1024, transcendentals=0)
 
 
-def forward_kernel(where, rows, cols, count, v, xs, give, keep, acc):
+def plan_kernel(where, rows, cols, count, plan, head, link):
     y, core = where[1], where[2]
-    acc[...] = jnp.zeros_like(acc)
-    live = count[0, 0]
-
-    def step(g, _):
-        products, dests = [], []
-        for u in range(GROUP):
-            s = g * GROUP + u
-            r = rows[0, 0, s]
-            mine = jnp.where((r & 1) == core, HALF, 0)
-            d = mine + ((((r >> 1) & 3) - y) & 3) * 4 + (r >> 3)
-            dests.append(jnp.where(s < live, d, 2 * HALF))
-            products.append(
-                jnp.dot(v[0, 0, s], xs[cols[0, 0, s]], preferred_element_type=F32)
-            )
-        for u in range(GROUP):
-            acc[dests[u]] = acc[dests[u]] + products[u]
-        return 0
-
-    lax.fori_loop(0, (live + GROUP - 1) // GROUP, step, 0)
-    give[...] = acc[:HALF].astype(BF16)
-    keep[...] = acc[HALF : 2 * HALF].astype(BF16)
-
-
-def forward(where, rows, cols, count, values, xs):
-    width = xs.shape[-1]
-    half = jax.ShapeDtypeStruct((HALF, TILE, width), BF16)
-    return pl.pallas_call(
-        forward_kernel,
-        out_shape=(half, half),
-        in_specs=[smem()] * 4 + [vmem()] * 2,
-        out_specs=(vmem(), vmem()),
-        scratch_shapes=[pltpu.VMEM((2 * HALF + 1, TILE, width), F32)],
-        compiler_params=params(),
-        cost_estimate=cost(2 * 128 * TILE * TILE * width, 7),
-        name="forward",
-    )(where, rows, cols, count, values, xs)
-
-
-def plan_kernel(where, rows, cols, count, slots, sources, dests, groups, head, link):
-    zh, y, core = where[0], where[1], where[2]
 
     def clear(i, _):
         head[i] = -1
         return 0
 
-    lax.fori_loop(0, 2 * HALF, clear, 0)
+    lax.fori_loop(0, 4 * HALF, clear, 0)
 
     def chain(s, _):
         r, c = rows[0, 0, s], cols[0, 0, s]
-        at = jnp.where((r & 1) == core, 0, HALF) + c
-        link[s] = head[at]
-        head[at] = s
+        mine = jnp.where((r & 1) == core, HALF, 0)
+        forth = mine + ((((r >> 1) & 3) - y) & 3) * 4 + (r >> 3)
+        back = 3 * HALF - mine + c
+        link[0, s] = head[forth]
+        head[forth] = s
+        link[1, s] = head[back]
+        head[back] = s
         return 0
 
     lax.fori_loop(0, count[0, 0], chain, 0)
 
-    for q in range(2):
-
-        def segment(d, pos, q=q):
+    for q in range(4):
+        way = q // 2
+        blank = (0, HALF) if way == 0 else (SLOTS, 0)
+
+        def segment(d, pos, q=q, way=way, blank=blank):
             def more(state):
                 return state[0] >= 0
 
             def emit(state):
                 s, at = state
                 r = rows[0, 0, s]
-                slots[q, at] = s
-                sources[q, at] = ((y - ((r >> 1) & 3)) & 3) * 4 + (r >> 3)
-                dests[q, at >> 1] = d
-                return link[s], at + 1
+                plan[q, at] = s
+                if way == 0:
+                    plan[q, SOURCE + at] = cols[0, 0, s]
+                else:
+                    plan[q, SOURCE + at] = ((y - ((r >> 1) & 3)) & 3) * 4 + (r >> 3)
+                plan[q, TARGET + (at >> 1)] = d
+                return link[way, s], at + 1
 
             _, at = lax.while_loop(more, emit, (head[q * HALF + d], pos))
 
             @pl.when((at & 1) == 1)
             def _():
-                slots[q, at] = 0
-                sources[q, at] = HALF
+                plan[q, at], plan[q, SOURCE + at] = blank
 
             return at + (at & 1)
 
         total = lax.fori_loop(0, HALF, segment, 0)
 
         for i in range(2 * UNROLL):
-            slots[q, total + i] = 0
-            sources[q, total + i] = HALF
-            dests[q, (total >> 1) + (i >> 1)] = 0
-        groups[q] = ((total >> 1) + UNROLL - 1) // UNROLL
+            plan[q, total + i], plan[q, SOURCE + total + i] = blank
+            plan[q, TARGET + (total >> 1) + (i >> 1)] = 0
+        plan[q, LENGTH] = ((total >> 1) + UNROLL - 1) // UNROLL
 
 
 def make_plan(where, rows, cols, count):
     i32 = jnp.int32
-    lists = jax.ShapeDtypeStruct((2, LIST), i32)
     return pl.pallas_call(
         plan_kernel,
-        out_shape=(lists, lists, lists, jax.ShapeDtypeStruct((2,), i32)),
+        out_shape=jax.ShapeDtypeStruct((4, PLAN), i32),
         in_specs=[smem()] * 4,
-        out_specs=(smem(),) * 4,
-        scratch_shapes=[pltpu.SMEM((2 * HALF,), i32), pltpu.SMEM((TILE,), i32)],
-        cost_estimate=cost(0, 8),
+        out_specs=smem(),
+        scratch_shapes=[pltpu.SMEM((4 * HALF,), i32), pltpu.SMEM((2, SLOTS), i32)],
+        cost_estimate=cost(0, 16),
         name="plan",
     )(where, rows, cols, count)
 
 
 def turn_kernel(count, v, out):
+    out[SLOTS] = jnp.zeros((TILE, TILE), BF16)
+
     def step(i, _):
         for u in range(4):
             out[4 * i + u] = v[0, 0, 4 * i + u].T
@@ -170,7 +142,7 @@
 def turn_tiles(count, tile_values):
     return pl.pallas_call(
         turn_kernel,
-        out_shape=jax.ShapeDtypeStruct(tile_values.shape[2:], tile_values.dtype),
+        out_shape=jax.ShapeDtypeStruct((SLOTS + 1, TILE, TILE), BF16),
         in_specs=[smem(), vmem()],
         out_specs=vmem(),
         compiler_params=params(),
@@ -270,37 +242,77 @@
     )(where, *lines)
 
 
-def gather_products(q, slots, sources, dests, groups, v, grads, held, acc):
-    rows = HALF * TILE
-    held[:rows] = grads[:rows]
-    held[rows:] = jnp.zeros((TILE, held.shape[1]), BF16)
-
+def fetch_tiles(live, v, tiles, sems):
+    def chunk(i):
+        part = pl.ds(i * CHUNK, CHUNK)
+        return pltpu.make_async_copy(v.at[part], tiles.at[part], sems.at[i])
+
+    for i in range(SLOTS // CHUNK):
+        pl.when(i * CHUNK < live)(chunk(i).start)
+
+    def arrive():
+        for i in range(SLOTS // CHUNK):
+            pl.when(i * CHUNK < live)(chunk(i).wait)
+
+    return arrive
+
+
+def add_products(q, plan, tiles, held, acc):
     def tile(at):
-        return held[pl.ds(pl.multiple_of(sources[q, at] * TILE, TILE), TILE)]
+        return held[pl.ds(pl.multiple_of(plan[q, SOURCE + at] * TILE, TILE), TILE)]
 
     def step(g, _):
         products = []
         for u in range(UNROLL):
             at = (g * UNROLL + u) * 2
-            left = jnp.concatenate([v[slots[q, at]], v[slots[q, at + 1]]], axis=1)
+            left = jnp.concatenate([tiles[plan[q, at]], tiles[plan[q, at + 1]]], axis=1)
             right = jnp.concatenate([tile(at), tile(at + 1)], axis=0)
             products.append(jnp.dot(left, right, preferred_element_type=F32))
         for u in range(UNROLL):
-            d = dests[q, g * UNROLL + u]
+            d = plan[q, TARGET + g * UNROLL + u]
             acc[d] = acc[d] + products[u]
         return 0
 
-    lax.fori_loop(0, groups[q], step, 0)
-
-
-def first_kernel(slots, sources, dests, groups, v, grads, acc, held):
+    lax.fori_loop(0, plan[q, LENGTH], step, 0)
+
+
+def forward_kernel(q, count, plan, v, xs, out, tiles, held, acc, sems):
+    arrive = fetch_tiles(count[0, 0], v, tiles, sems)
+    held[: HALF * TILE] = xs[...].reshape(HALF * TILE, xs.shape[2])
+    held[HALF * TILE :] = jnp.zeros((TILE, xs.shape[2]), BF16)
     acc[...] = jnp.zeros_like(acc)
-    gather_products(0, slots, sources, dests, groups, v, grads, held, acc)
-
-
-def second_kernel(slots, sources, dests, groups, v, grads, mine, start, out, held, acc):
+    arrive()
+    add_products(q, plan, tiles, held, acc)
+    out[...] = acc[...].astype(BF16)
+
+
+def forward(q, count, plan, v, xs):
+    width = xs.shape[2]
+    return pl.pallas_call(
+        functools.partial(forward_kernel, q),
+        out_shape=jax.ShapeDtypeStruct((HALF, TILE, width), BF16),
+        in_specs=[smem()] * 2 + [pl.BlockSpec(memory_space=pltpu.HBM), vmem()],
+        out_specs=vmem(),
+        scratch_shapes=[
+            pltpu.VMEM((SLOTS, TILE, TILE), BF16),
+            pltpu.VMEM(((HALF + 1) * TILE, width), BF16),
+            pltpu.VMEM((HALF, TILE, width), F32),
+            pltpu.SemaphoreType.DMA((SLOTS // CHUNK,)),
+        ],
+        compiler_params=pltpu.CompilerParams(vmem_limit_bytes=50 * 1024 * 1024),
+        cost_estimate=cost(2 * 64 * TILE * TILE * width, 8),
+        name="forward",
+    )(count, plan, v, xs)
+
+
+def first_kernel(plan, v, grads, acc):
+    acc[...] = jnp.zeros_like(acc)
+    add_products(2, plan, v, grads, acc)
+
+
+def second_kernel(plan, v, grads, mine, start, out, acc):
     acc[...] = start[...]
-    gather_products(1, slots, sources, dests, groups, v, grads, held, acc)
+    add_products(3, plan, v, grads, acc)
     rows = HALF * TILE
     part = (mine[rows:].astype(F32) + grads[rows:].astype(F32)).astype(BF16)
     for d in range(HALF):
@@ -310,30 +322,27 @@
 
 def backward(plan, v, mine, theirs):
     rows, width = mine.shape
-    extra = rows - HALF * TILE
-    held = pltpu.VMEM(((HALF + 1) * TILE, width), BF16)
     sums = (HALF, TILE, width)
     work = cost(2 * 64 * TILE * TILE * width, 8)
     first = pl.pallas_call(
         first_kernel,
         out_shape=jax.ShapeDtypeStruct(sums, F32),
-        in_specs=[smem()] * 4 + [vmem()] * 2,
+        in_specs=[smem()] + [vmem()] * 2,
         out_specs=vmem(),
-        scratch_shapes=[held],
         compiler_params=params(),
         cost_estimate=work,
         name="first",
-    )(*plan, v, mine)
+    )(plan, v, mine)
     return pl.pallas_call(
         second_kernel,
-        out_shape=jax.ShapeDtypeStruct((HALF, TILE + extra, width), BF16),
-        in_specs=[smem()] * 4 + [vmem()] * 4,
+        out_shape=jax.ShapeDtypeStruct((HALF, TILE + rows - HALF * TILE, width), BF16),
+        in_specs=[smem()] + [vmem()] * 4,
         out_specs=vmem(),
-        scratch_shapes=[held, pltpu.VMEM(sums, F32)],
+        scratch_shapes=[pltpu.VMEM(sums, F32)],
         compiler_params=params(),
         cost_estimate=work,
         name="second",
-    )(*plan, v, theirs, mine, first)
+    )(plan, v, theirs, mine, first)
 
 
 def last_kernel(scale, got, w, grad_out, weight_out):
@@ -369,19 +378,22 @@
     where = jnp.stack([c >> 3, (c >> 1) & 3, c & 1]).astype(jnp.int32)
 
     xs = trade_row(jnp.broadcast_to(features[None], (ROWS,) + features.shape))
-    give, keep = forward(where, tile_rows, tile_cols, tile_count, tile_values, xs)
-    got = send_core(give)
+    plan = make_plan(where, tile_rows, tile_cols, tile_count)
+    turned = turn_tiles(tile_count, tile_values)
+    values = tile_values.reshape(tile_values.shape[2:])
+    plan, turned, xs = lax.optimization_barrier((plan, turned, xs))
+
+    got = send_core(forward(0, tile_count, plan, values, xs))
+    keep = forward(1, tile_count, plan, values, xs)
     paired = (keep.astype(F32) + got.astype(F32)).astype(BF16).reshape(4, 4, TILE, -1)
     others = [send_y(paired[k], k).astype(F32) for k in (1, 2, 3)]
     block = (paired[0].astype(F32) + others[0] + others[1] + others[2]).astype(BF16)
-    plan = make_plan(where, tile_rows, tile_cols, tile_count)
-    turned = turn_tiles(tile_count, tile_values)
     activated, grad_pre, part = middle(trade_zh(block), weight, cotangent)
 
     line = fold(trade_zh(pack(grad_pre, trade_row(part))))
     mine = collect(where, [line] + [send_y(line, k) for k in (1, 2, 3)])
-    spread = backward(plan, turned, mine, send_core(mine))
-    grad_features, grad_weight = last(trade_row(spread), weight, grad_scale)
+    spread = trade_row(backward(plan, turned, mine, send_core(mine)))
+    grad_features, grad_weight = last(spread, weight, grad_scale)
     return (activated, grad_features, grad_weight)
 
 

time: 211 us -> 200 us (0.948)
  waiting for transfers between devices: 38.3 us -> 27.2 us
    all_to_all x1, waiting for transfers between devices: 21.4 us -> 12.3 us  [trade_row(): return lax.all_to_all(v, 'row', 0, 0)]
    ppermute x6, starting transfers between devices: 22 us -> 18.1 us  [send_y(): return lax.ppermute(v, 'col', pairs)]
    ppermute x2, starting transfers between devices: 11.9 us -> 15.8 us  [send_core(): return lax.ppermute(v, 'col', [(c, c ^ 1) for c in range(COLS)])]
    all_to_all x2, blocking collectives: 60.2 us -> 56.7 us  [trade_row(): return lax.all_to_all(v, 'row', 0, 0)]
    all_to_all x2, blocking collectives: 45.4 us -> 47.7 us  [trade_zh(): return lax.all_to_all(v, 'col', 0, 0, axis_index_groups=groups)]
    pallas_call x3 -> x4, Pallas kernels: 8.25 us -> 9.65 us  [the longest x2 5.31 us: forward(): pl.pallas_call(functools.partial(forward_kernel, q), out_shape=jax.ShapeD...]
    unnamed x22 -> x18, local copies, waits for them, and re-layouts: 4.42 us -> 4.85 us
  transfers between devices with their start and end apart: 9 -> 9, of which waited for: 8 -> 7; matrix products, arithmetic and copies ran while one was open for 0% -> 0% of each run, Pallas kernels for 3% -> 4%
where the time goes in v3:
time: 200 us; the launch traced here: 199 us
  blocking collectives  104 us (52%)
  starting transfers between devices  42.9 us (21%)
  waiting for transfers between devices  27.2 us (14%)
  Pallas kernels  15.1 us (8%)
  local copies, waits for them, and re-layouts  6.86 us (3%)
    all_to_all x2, blocking collectives, trade_row(): return lax.all_to_all(v, 'row', 0, 0)  56.7 us
    all_to_all x2, blocking collectives, trade_zh(): return lax.all_to_all(v, 'col', 0, 0, axis_index_groups=groups)  47.7 us
    ppermute x6, starting transfers between devices, send_y(): return lax.ppermute(v, 'col', pairs)  18.1 us
    ppermute x2, starting transfers between devices, send_core(): return lax.ppermute(v, 'col', [(c, c ^ 1) for c in range(COLS)])  15.8 us
    ppermute x6, waiting for transfers between devices, send_y(): return lax.ppermute(v, 'col', pairs)  14.3 us
    all_to_all x1, waiting for transfers between devices, trade_row(): return lax.all_to_all(v, 'row', 0, 0)  12.3 us
    all_to_all x1, starting transfers between devices, trade_row(): return lax.all_to_all(v, 'row', 0, 0)  9.01 us
    pallas_call x2, Pallas kernels, forward(): pl.pallas_call(functools.partial(forward_kernel, q), out_shape=jax.ShapeD...  5.31 us
  transfers between devices with their start and end apart: 9, of which 7 were waited for; matrix products, arithmetic and copies ran while one was open for 0% of the time, Pallas kernels for 4%

profile of v3, /device:TPU:1, one launch (start us, length us, event | category | flops | bytes accessed | tf_op | source)
XLA Modules:
  0.0 199.2 jit_solution(17864656988318732331)
XLA Ops:
  0.6 1.9 broadcast_in_dim.2
  2.6 9.0 %all-to-all-start = ((bf16[16,128,256]{2,1,0:T(8,128)(2,1)}), bf16[16,128,256]{2,1,0:T(8,128)(2,1)S(1)}, u32[]{:S(2)}, u32[]{:S(2)}) async-start(bf16[16,128,256]{2,1,0:T(8,128)(2,1)} %broadcast_in_dim.2), calls=%async_computation | async-start | bytes 2097152 | tf_op jit(solution)/shard_map/all_to_all | solution.py:37
  12.3 0.0 copy-start.1
  12.3 2.2 %copy-done.1 = bf16[1,1,128,128,128]{4,3,2,1,0:T(8,128)(2,1)S(1)} copy-done((bf16[1,1,128,128,128]{4,3,2,1,0:T(8,128)(2,1)S(1)}, bf16[1,1,128,128,128]{4,3,2,1,0:T(8,128)(2,1)}, u32[]{:S(2)}) %copy-start.1) | copy-done | bytes 4194328
  14.4 0.4 turn.1.v
  14.9 0.0 copy-start
  14.9 1.9 copy-done
  16.8 0.7 pad_add_fusion.where
  17.5 3.9 %plan.1 = s32[4,512]{1,0:T(4,128)} custom-call(s32[3]{0:T(128)} %pad_add_fusion.where, s32[1,1,128]{2,1,0:T(1,128)} %rows.1, s32[1,1,128]{2,1,0:T(1,128)} %cols.1, s32[1,1]{1,0:T(1,128)S(6)} %copy.10.count), custom_call_target="tpu_custom_call" | custom-call | bytes 16777216 | tf_op jit(solution)/shard_map/plan/pallas_call | solution.py:120
  21.4 12.3 %all-to-all-done.xs = bf16[16,128,256]{2,1,0:T(8,128)(2,1)S(1)} async-done(((bf16[16,128,256]{2,1,0:T(8,128)(2,1)}), bf16[16,128,256]{2,1,0:T(8,128)(2,1)S(1)}, u32[]{:S(2)}, u32[]{:S(2)}) %all-to-all-start) | async-done | bytes 1048608 | tf_op jit(solution)/shard_map/all_to_all | solution.py:37
  33.7 0.7 copy-done.3
  34.4 2.5 %forward.3 = bf16[16,128,256]{2,1,0:T(8,128)(2,1)S(1)} custom-call(s32[1,1]{1,0:T(1,128)S(6)} %copy.10.count, s32[4,512]{1,0:T(4,128)S(1)} %copy-done.3, bf16[128,128,128]{2,1,0:T(8,128)(2,1)} %bitcast.6, bf16[16,128,256]{2,1,0:T(8,128)(2,1)S(1)} %all-to-all-done.xs), custom_call_target="tpu_custom_call" | custom-call | flops 536870912 | bytes 8388608 | tf_op jit(solution)/shard_map/forward/pallas_call | solution.py:291
  36.9 8.3 %collective-permute-start = (bf16[16,128,256]{2,1,0:T(8,128)(2,1)S(1)}, bf16[16,128,256]{2,1,0:T(8,128)(2,1)S(1)}, u32[]{:S(2)}, u32[]{:S(2)}) collective-permute-start(bf16[16,128,256]{2,1,0:T(8,128)(2,1)S(1)} %forward.3), channel_id=1, source_target_pairs={{0,1},{1,0},{2,3},{3,2},{4,5},{5,4},{6,7},{7,6},{8,9},{9,8},{10,11... | collective-permute-start | bytes 3145736 | tf_op jit(solution)/shard_map/ppermute | solution.py:33
  45.3 0.0 slice-start
  45.3 2.8 %forward.2 = bf16[16,128,256]{2,1,0:T(8,128)(2,1)S(1)} custom-call(s32[1,1]{1,0:T(1,128)S(6)} %copy.10.count, s32[4,512]{1,0:T(4,128)S(1)} %copy-done.3, bf16[128,128,128]{2,1,0:T(8,128)(2,1)} %bitcast.7, bf16[16,128,256]{2,1,0:T(8,128)(2,1)S(1)} %all-to-all-done.xs), custom_call_target="tpu_custom_call" | custom-call | flops 536870912 | bytes 8388608 | tf_op jit(solution)/shard_map/forward/pallas_call | solution.py:291
  48.1 0.0 slice-start.1
  48.1 0.0 collective-permute-done
  48.1 0.3 add_convert_fusion
  48.5 0.0 copy-start.2
  48.5 0.0 copy-start.5
  48.5 0.1 fusion
  48.6 2.2 %collective-permute-start.1 = (bf16[4,128,256]{2,1,0:T(8,128)(2,1)S(1)}, bf16[4,128,256]{2,1,0:T(8,128)(2,1)S(1)}, u32[]{:S(2)}, u32[]{:S(2)}) collective-permute-start(bf16[4,128,256]{2,1,0:T(8,128)(2,1)S(1)} %get-tuple-element.19), channel_id=1, source_target_pairs={{0,2},{1,3},{2,4},{3,5},{4,6},{5,7},{6,0},{7,1},{8,10},{9,11},{10,... | collective-permute-start | bytes 786440 | tf_op jit(solution)/shard_map/ppermute | solution.py:29
  50.8 4.6 %collective-permute-start.3 = (bf16[4,128,256]{2,1,0:T(8,128)(2,1)S(1)}, bf16[4,128,256]{2,1,0:T(8,128)(2,1)S(1)}, u32[]{:S(2)}, u32[]{:S(2)}) collective-permute-start(bf16[4,128,256]{2,1,0:T(8,128)(2,1)S(1)} %get-tuple-element.20), channel_id=1, source_target_pairs={{0,6},{1,7},{2,0},{3,1},{4,2},{5,3},{6,4},{7,5},{8,14},{9,15},{10,... | collective-permute-start | bytes 786440 | tf_op jit(solution)/shard_map/ppermute | solution.py:29
  55.3 0.0 copy-start.6
  55.3 1.9 collective-permute-start.2
  57.3 0.0 collective-permute-done.1
  57.3 1.8 collective-permute-done.3
  59.1 4.9 %collective-permute-done.2 = bf16[4,128,256]{2,1,0:T(8,128)(2,1)S(1)} collective-permute-done((bf16[4,128,256]{2,1,0:T(8,128)(2,1)S(1)}, bf16[4,128,256]{2,1,0:T(8,128)(2,1)S(1)}, u32[]{:S(2)}, u32[]{:S(2)}) %collective-permute-start.2) | collective-permute-done | bytes 262176 | tf_op jit(solution)/shard_map/ppermute | solution.py:29
  64.0 0.1 add_convert_fusion.1
  64.1 26.1 %all_to_all.25.got = bf16[4,128,256]{2,1,0:T(8,128)(2,1)S(1)} all-to-all(bf16[4,128,256]{2,1,0:T(8,128)(2,1)S(1)} %add_convert_fusion.1), channel_id=1, replica_groups={{0,8,16,24},{1,9,17,25},{2,10,18,26},{3,11,19,27},{4,12,20,28},{5,13,21..., dimensions={0} | all-to-all | bytes 524288 | tf_op jit(solution)/shard_map/all_to_all | solution.py:42
  90.3 0.0 copy-done.2
  90.3 0.8 middle.1
  91.1 19.4 %all_to_all.26.parts = bf16[16,16,256]{2,1,0:T(8,128)(2,1)S(1)} all-to-all(bf16[16,16,256]{2,1,0:T(8,128)(2,1)S(1)} %get-tuple-element.16), channel_id=1, replica_groups=mesh['row'=16,'col'=32] {'row'}, dimensions={0} | all-to-all | bytes 262144 | tf_op jit(solution)/shard_map/all_to_all | solution.py:37
  110.5 21.6 %all_to_all.27.got = bf16[4,144,256]{2,1,0:T(8,128)(2,1)S(1)} all-to-all(bf16[4,144,256]{2,1,0:T(8,128)(2,1)S(1)} %pack.1), channel_id=1, replica_groups={{0,8,16,24},{1,9,17,25},{2,10,18,26},{3,11,19,27},{4,12,20,28},{5,13,21..., dimensions={0} | all-to-all | bytes 589824 | tf_op jit(solution)/shard_map/all_to_all | solution.py:42
  132.1 4.4 %collective-permute-start.6 = (bf16[528,256]{1,0:T(8,128)(2,1)S(1)}, bf16[528,256]{1,0:T(8,128)(2,1)S(1)}, u32[]{:S(2)}, u32[]{:S(2)}) collective-permute-start(bf16[528,256]{1,0:T(8,128)(2,1)S(1)} %fold.1.l0), channel_id=1, source_target_pairs={{0,6},{1,7},{2,0},{3,1},{4,2},{5,3},{6,4},{7,5},{8,14},{9,15},{10,... | collective-permute-start | bytes 811016 | tf_op jit(solution)/shard_map/ppermute | solution.py:29
  136.6 3.0 %collective-permute-start.5 = (bf16[528,256]{1,0:T(8,128)(2,1)S(1)}, bf16[528,256]{1,0:T(8,128)(2,1)S(1)}, u32[]{:S(2)}, u32[]{:S(2)}) collective-permute-start(bf16[528,256]{1,0:T(8,128)(2,1)S(1)} %fold.1.l0), channel_id=1, source_target_pairs={{0,4},{1,5},{2,6},{3,7},{4,0},{5,1},{6,2},{7,3},{8,12},{9,13},{10,... | collective-permute-start | bytes 811016 | tf_op jit(solution)/shard_map/ppermute | solution.py:29
  139.6 1.9 collective-permute-start.4
  141.5 0.6 collective-permute-done.6.l3
  142.1 3.2 %collective-permute-done.5.l2 = bf16[528,256]{1,0:T(8,128)(2,1)S(1)} collective-permute-done((bf16[528,256]{1,0:T(8,128)(2,1)S(1)}, bf16[528,256]{1,0:T(8,128)(2,1)S(1)}, u32[]{:S(2)}, u32[]{:S(2)}) %collective-permute-start.5) | collective-permute-done | bytes 270368 | tf_op jit(solution)/shard_map/ppermute | solution.py:29
  145.3 3.8 %collective-permute-done.4.l1 = bf16[528,256]{1,0:T(8,128)(2,1)S(1)} collective-permute-done((bf16[528,256]{1,0:T(8,128)(2,1)S(1)}, bf16[528,256]{1,0:T(8,128)(2,1)S(1)}, u32[]{:S(2)}, u32[]{:S(2)}) %collective-permute-start.4) | collective-permute-done | bytes 270368 | tf_op jit(solution)/shard_map/ppermute | solution.py:29
  149.1 0.0 copy-done.6
  149.1 0.6 collect.1.grads.mine
  149.8 7.4 %collective-permute-start.7 = (bf16[2064,256]{1,0:T(8,128)(2,1)S(1)}, bf16[2064,256]{1,0:T(8,128)(2,1)S(1)}, u32[]{:S(2)}, u32[]{:S(2)}) collective-permute-start(bf16[2064,256]{1,0:T(8,128)(2,1)S(1)} %collect.1.grads.mine), channel_id=1, source_target_pairs={{0,1},{1,0},{2,3},{3,2},{4,5},{5,4},{6,7},{7,6},{8,9},{9,8},{10,11... | collective-permute-start | bytes 3170312 | tf_op jit(solution)/shard_map/ppermute | solution.py:33
  157.2 1.6 first.1.start
  158.8 0.7 collective-permute-done.7.grads
  159.5 1.4 second.1
  160.9 37.4 %all_to_all.28.got = bf16[16,144,256]{2,1,0:T(8,128)(2,1)S(1)} all-to-all(bf16[16,144,256]{2,1,0:T(8,128)(2,1)S(1)} %second.1), channel_id=1, replica_groups=mesh['row'=16,'col'=32] {'row'}, dimensions={0} | all-to-all | bytes 2359296 | tf_op jit(solution)/shard_map/all_to_all | solution.py:37
  198.3 0.9 last.1
  (9 shorter events, 0.1 us)
Async XLA Ops:
  2.6 31.1 %all-to-all-start = ((bf16[16,128,256]{2,1,0:T(8,128)(2,1)}), bf16[16,128,256]{2,1,0:T(8,128)(2,1)S(1)}, u32[]{:S(2)}, u32[]{:S(2)}) async-start(bf16[16,128,256]{2,1,0:T(8,128)(2,1)} %broadcast_in_dim.2), calls=%async_computation | async-start | bytes 2097152 | tf_op jit(solution)/shard_map/all_to_all | solution.py:37
  12.3 2.2 %copy-start.1 = (bf16[1,1,128,128,128]{4,3,2,1,0:T(8,128)(2,1)S(1)}, bf16[1,1,128,128,128]{4,3,2,1,0:T(8,128)(2,1)}, u32[]{:S(2)}) copy-start(bf16[1,1,128,128,128]{4,3,2,1,0:T(8,128)(2,1)} %v.1) | copy-start | bytes 12582916
  14.9 2.0 copy-start
  33.7 0.7 copy-start.3
  36.9 11.2 %collective-permute-start = (bf16[16,128,256]{2,1,0:T(8,128)(2,1)S(1)}, bf16[16,128,256]{2,1,0:T(8,128)(2,1)S(1)}, u32[]{:S(2)}, u32[]{:S(2)}) collective-permute-start(bf16[16,128,256]{2,1,0:T(8,128)(2,1)S(1)} %forward.3), channel_id=1, source_target_pairs={{0,1},{1,0},{2,3},{3,2},{4,5},{5,4},{6,7},{7,6},{8,9},{9,8},{10,11... | collective-permute-start | bytes 3145736 | tf_op jit(solution)/shard_map/ppermute | solution.py:33
  45.3 111.9 %slice-start = ((s8[4227072]{0:T(1024)(128)(4,1)}), s8[32768]{0:T(1024)(128)(4,1)S(1)}, s32[]{:S(2)}) async-start(s8[4227072]{0:T(1024)(128)(4,1)} %bitcast.4), calls=%async_computation.5 | async-start | bytes 65536
  48.1 109.1 %slice-start.1 = ((s8[4227072]{0:T(1024)(128)(4,1)}), s8[4194304]{0:T(1024)(128)(4,1)S(1)}, s32[]{:S(2)}) async-start(s8[4227072]{0:T(1024)(128)(4,1)} %bitcast.4), calls=%async_computation.6 | async-start | bytes 8388608
  48.5 41.8 %copy-start.2 = (bf16[256,256]{1,0:T(8,128)(2,1)S(1)}, bf16[256,256]{1,0:T(8,128)(2,1)}, u32[]{:S(2)}) copy-start(bf16[256,256]{1,0:T(8,128)(2,1)} %w.3) | copy-start | bytes 393220
  48.5 41.8 %copy-start.5 = (bf16[128,256]{1,0:T(8,128)(2,1)S(1)}, bf16[128,256]{1,0:T(8,128)(2,1)}, u32[]{:S(2)}) copy-start(bf16[128,256]{1,0:T(8,128)(2,1)} %cot.1) | copy-start | bytes 196612
  48.6 8.7 %collective-permute-start.1 = (bf16[4,128,256]{2,1,0:T(8,128)(2,1)S(1)}, bf16[4,128,256]{2,1,0:T(8,128)(2,1)S(1)}, u32[]{:S(2)}, u32[]{:S(2)}) collective-permute-start(bf16[4,128,256]{2,1,0:T(8,128)(2,1)S(1)} %get-tuple-element.19), channel_id=1, source_target_pairs={{0,2},{1,3},{2,4},{3,5},{4,6},{5,7},{6,0},{7,1},{8,10},{9,11},{10,... | collective-permute-start | bytes 786440 | tf_op jit(solution)/shard_map/ppermute | solution.py:29
  50.8 8.3 %collective-permute-start.3 = (bf16[4,128,256]{2,1,0:T(8,128)(2,1)S(1)}, bf16[4,128,256]{2,1,0:T(8,128)(2,1)S(1)}, u32[]{:S(2)}, u32[]{:S(2)}) collective-permute-start(bf16[4,128,256]{2,1,0:T(8,128)(2,1)S(1)} %get-tuple-element.20), channel_id=1, source_target_pairs={{0,6},{1,7},{2,0},{3,1},{4,2},{5,3},{6,4},{7,5},{8,14},{9,15},{10,... | collective-permute-start | bytes 786440 | tf_op jit(solution)/shard_map/ppermute | solution.py:29
  55.3 93.8 %copy-start.6 = (s32[3]{0:T(128)S(1)}, s32[3]{0:T(128)}, u32[]{:S(2)}) copy-start(s32[3]{0:T(128)} %pad_add_fusion.where) | copy-start | bytes 40
  55.3 8.6 %collective-permute-start.2 = (bf16[4,128,256]{2,1,0:T(8,128)(2,1)S(1)}, bf16[4,128,256]{2,1,0:T(8,128)(2,1)S(1)}, u32[]{:S(2)}, u32[]{:S(2)}) collective-permute-start(bf16[4,128,256]{2,1,0:T(8,128)(2,1)S(1)} %get-tuple-element.21), channel_id=1, source_target_pairs={{0,4},{1,5},{2,6},{3,7},{4,0},{5,1},{6,2},{7,3},{8,12},{9,13},{10,... | collective-permute-start | bytes 786440 | tf_op jit(solution)/shard_map/ppermute | solution.py:29
  91.1 66.1 %copy-start.4 = (s32[4,512]{1,0:T(4,128)S(1)}, s32[4,512]{1,0:T(4,128)}, u32[]{:S(2)}) copy-start(s32[4,512]{1,0:T(4,128)} %plan.1) | copy-start | bytes 24580
  132.1 10.0 %collective-permute-start.6 = (bf16[528,256]{1,0:T(8,128)(2,1)S(1)}, bf16[528,256]{1,0:T(8,128)(2,1)S(1)}, u32[]{:S(2)}, u32[]{:S(2)}) collective-permute-start(bf16[528,256]{1,0:T(8,128)(2,1)S(1)} %fold.1.l0), channel_id=1, source_target_pairs={{0,6},{1,7},{2,0},{3,1},{4,2},{5,3},{6,4},{7,5},{8,14},{9,15},{10,... | collective-permute-start | bytes 811016 | tf_op jit(solution)/shard_map/ppermute | solution.py:29
  136.6 8.7 %collective-permute-start.5 = (bf16[528,256]{1,0:T(8,128)(2,1)S(1)}, bf16[528,256]{1,0:T(8,128)(2,1)S(1)}, u32[]{:S(2)}, u32[]{:S(2)}) collective-permute-start(bf16[528,256]{1,0:T(8,128)(2,1)S(1)} %fold.1.l0), channel_id=1, source_target_pairs={{0,4},{1,5},{2,6},{3,7},{4,0},{5,1},{6,2},{7,3},{8,12},{9,13},{10,... | collective-permute-start | bytes 811016 | tf_op jit(solution)/shard_map/ppermute | solution.py:29
  139.6 9.5 %collective-permute-start.4 = (bf16[528,256]{1,0:T(8,128)(2,1)S(1)}, bf16[528,256]{1,0:T(8,128)(2,1)S(1)}, u32[]{:S(2)}, u32[]{:S(2)}) collective-permute-start(bf16[528,256]{1,0:T(8,128)(2,1)S(1)} %fold.1.l0), channel_id=1, source_target_pairs={{0,2},{1,3},{2,4},{3,5},{4,6},{5,7},{6,0},{7,1},{8,10},{9,11},{10,... | collective-permute-start | bytes 811016 | tf_op jit(solution)/shard_map/ppermute | solution.py:29
  149.8 9.7 %collective-permute-start.7 = (bf16[2064,256]{1,0:T(8,128)(2,1)S(1)}, bf16[2064,256]{1,0:T(8,128)(2,1)S(1)}, u32[]{:S(2)}, u32[]{:S(2)}) collective-permute-start(bf16[2064,256]{1,0:T(8,128)(2,1)S(1)} %collect.1.grads.mine), channel_id=1, source_target_pairs={{0,1},{1,0},{2,3},{3,2},{4,5},{5,4},{6,7},{7,6},{8,9},{9,8},{10,11... | collective-permute-start | bytes 3170312 | tf_op jit(solution)/shard_map/ppermute | solution.py:33

commit v4 on v3

--- a/solution.py
+++ b/solution.py
@@ -13,7 +13,7 @@
 ROWS = 16
 COLS = 32
 HALF = 16
-UNROLL = 4
+UNROLL = 8
 SOURCE = 192
 TARGET = 384
 LENGTH = 480
@@ -37,6 +37,16 @@
     return lax.all_to_all(v, "row", 0, 0)
 
 
+def swap_zh(v, k):
+    pairs = [(c, ((c // 8) ^ k) * 8 + c % 8) for c in range(COLS)]
+    return lax.ppermute(v, "col", pairs)
+
+
+def trade_near(v):
+    groups = [[zh * 8 + rest for rest in range(8)] for zh in range(4)]
+    return lax.all_to_all(v, "col", 0, 0, axis_index_groups=groups)
+
+
 def trade_zh(v):
     groups = [[zh * 8 + rest for zh in range(4)] for rest in range(8)]
     return lax.all_to_all(v, "col", 0, 0, axis_index_groups=groups)
@@ -59,7 +69,7 @@
 
 
 def plan_kernel(where, rows, cols, count, plan, head, link):
-    y, core = where[1], where[2]
+    zh, y, core = where[0], where[1], where[2]
 
     def clear(i, _):
         head[i] = -1
@@ -95,7 +105,9 @@
                 if way == 0:
                     plan[q, SOURCE + at] = cols[0, 0, s]
                 else:
-                    plan[q, SOURCE + at] = ((y - ((r >> 1) & 3)) & 3) * 4 + (r >> 3)
+                    far = (r >> 3) ^ zh
+                    near = (y - ((r >> 1) & 3)) & 3
+                    plan[q, SOURCE + at] = near * 4 + (far ^ (far >> 1))
                 plan[q, TARGET + (at >> 1)] = d
                 return link[way, s], at + 1
 
@@ -129,8 +141,6 @@
 
 
 def turn_kernel(count, v, out):
-    out[SLOTS] = jnp.zeros((TILE, TILE), BF16)
-
     def step(i, _):
         for u in range(4):
             out[4 * i + u] = v[0, 0, 4 * i + u].T
@@ -142,7 +152,7 @@
 def turn_tiles(count, tile_values):
     return pl.pallas_call(
         turn_kernel,
-        out_shape=jax.ShapeDtypeStruct((SLOTS + 1, TILE, TILE), BF16),
+        out_shape=jax.ShapeDtypeStruct((SLOTS, TILE, TILE), BF16),
         in_specs=[smem(), vmem()],
         out_specs=vmem(),
         compiler_params=params(),
@@ -177,69 +187,23 @@
     )(got, w, cot)
 
 
-def pack_kernel(grad, parts, out):
+def sum_parts_kernel(parts, out):
     total = parts[0].astype(F32)
-    for i in range(1, ROWS):
+    for i in range(1, parts.shape[0]):
         total = total + parts[i].astype(F32)
     part = total.astype(BF16)
-    for i in range(4):
-        out[i, :TILE] = grad[...]
-        out[i, TILE:] = part
-
-
-def pack(grad, parts):
-    n, width = grad.shape
-    return pl.pallas_call(
-        pack_kernel,
-        out_shape=jax.ShapeDtypeStruct((4, n + parts.shape[1], width), BF16),
+    for i in range(out.shape[0]):
+        out[i] = part
+
+
+def sum_parts(parts, copies):
+    return pl.pallas_call(
+        sum_parts_kernel,
+        out_shape=jax.ShapeDtypeStruct((copies,) + parts.shape[1:], BF16),
         compiler_params=params(),
         cost_estimate=cost(0, 1),
-        name="pack",
-    )(grad, parts)
-
-
-def fold_kernel(got, out):
-    total = got[0, TILE:].astype(F32)
-    for i in range(1, 4):
-        total = total + got[i, TILE:].astype(F32)
-    for i in range(4):
-        out[TILE * i : TILE * (i + 1)] = got[i, :TILE]
-    out[4 * TILE :] = total.astype(BF16)
-
-
-def fold(got):
-    extra, width = got.shape[1] - TILE, got.shape[2]
-    return pl.pallas_call(
-        fold_kernel,
-        out_shape=jax.ShapeDtypeStruct((4 * TILE + extra, width), BF16),
-        compiler_params=params(),
-        cost_estimate=cost(0, 1),
-        name="fold",
-    )(got)
-
-
-def collect_kernel(where, l0, l1, l2, l3, out, slices):
-    y = where[1]
-    rows = 4 * TILE
-    for k, line in enumerate((l0, l1, l2, l3)):
-        out[rows * k : rows * (k + 1)] = line[:rows]
-        slices[(y - k) & 3] = line[rows:].astype(F32)
-    out[4 * rows :] = ((slices[0] + slices[1]) + (slices[2] + slices[3])).astype(BF16)
-
-
-def collect(where, lines):
-    rows, width = lines[0].shape
-    extra = rows - 4 * TILE
-    return pl.pallas_call(
-        collect_kernel,
-        out_shape=jax.ShapeDtypeStruct((HALF * TILE + extra, width), BF16),
-        in_specs=[smem()] + [vmem()] * 4,
-        out_specs=vmem(),
-        scratch_shapes=[pltpu.VMEM((4, extra, width), F32)],
-        compiler_params=params(),
-        cost_estimate=cost(0, 3),
-        name="collect",
-    )(where, *lines)
+        name="sum_parts",
+    )(parts)
 
 
 def fetch_tiles(live, v, tiles, sems):
@@ -276,7 +240,7 @@
     lax.fori_loop(0, plan[q, LENGTH], step, 0)
 
 
-def forward_kernel(q, count, plan, v, xs, out, tiles, held, acc, sems):
+def forward_kernel(q, count, plan, v, xs, out, tiles, sems, held, acc):
     arrive = fetch_tiles(count[0, 0], v, tiles, sems)
     held[: HALF * TILE] = xs[...].reshape(HALF * TILE, xs.shape[2])
     held[HALF * TILE :] = jnp.zeros((TILE, xs.shape[2]), BF16)
@@ -286,63 +250,64 @@
     out[...] = acc[...].astype(BF16)
 
 
-def forward(q, count, plan, v, xs):
-    width = xs.shape[2]
-    return pl.pallas_call(
-        functools.partial(forward_kernel, q),
-        out_shape=jax.ShapeDtypeStruct((HALF, TILE, width), BF16),
-        in_specs=[smem()] * 2 + [pl.BlockSpec(memory_space=pltpu.HBM), vmem()],
-        out_specs=vmem(),
-        scratch_shapes=[
-            pltpu.VMEM((SLOTS, TILE, TILE), BF16),
-            pltpu.VMEM(((HALF + 1) * TILE, width), BF16),
-            pltpu.VMEM((HALF, TILE, width), F32),
-            pltpu.SemaphoreType.DMA((SLOTS // CHUNK,)),
-        ],
-        compiler_params=pltpu.CompilerParams(vmem_limit_bytes=50 * 1024 * 1024),
-        cost_estimate=cost(2 * 64 * TILE * TILE * width, 8),
-        name="forward",
-    )(count, plan, v, xs)
-
-
-def first_kernel(plan, v, grads, acc):
+def first_kernel(count, plan, v, grads, acc, tiles, sems):
+    arrive = fetch_tiles(count[0, 0], v, tiles, sems)
     acc[...] = jnp.zeros_like(acc)
-    add_products(2, plan, v, grads, acc)
-
-
-def second_kernel(plan, v, grads, mine, start, out, acc):
+    tiles[SLOTS] = jnp.zeros((TILE, TILE), BF16)
+    arrive()
+    add_products(2, plan, tiles, grads, acc)
+
+
+def second_kernel(count, plan, v, grads, parts, start, out, tiles, sems, acc):
+    arrive = fetch_tiles(count[0, 0], v, tiles, sems)
     acc[...] = start[...]
-    add_products(3, plan, v, grads, acc)
-    rows = HALF * TILE
-    part = (mine[rows:].astype(F32) + grads[rows:].astype(F32)).astype(BF16)
+    tiles[SLOTS] = jnp.zeros((TILE, TILE), BF16)
+    total = parts[0].astype(F32)
+    for i in range(1, parts.shape[0]):
+        total = total + parts[i].astype(F32)
+    part = total.astype(BF16)
+    arrive()
+    add_products(3, plan, tiles, grads, acc)
     for d in range(HALF):
         out[d, :TILE] = acc[d].astype(BF16)
         out[d, TILE:] = part
 
 
-def backward(plan, v, mine, theirs):
-    rows, width = mine.shape
+def block_product(kernel, name, out, scratch, count, plan, v, *operands):
+    return pl.pallas_call(
+        kernel,
+        out_shape=out,
+        in_specs=[smem()] * 2 + [pl.BlockSpec(memory_space=pltpu.HBM)] + [vmem()] * len(operands),
+        out_specs=vmem(),
+        scratch_shapes=[
+            pltpu.VMEM((SLOTS + 1, TILE, TILE), BF16),
+            pltpu.SemaphoreType.DMA((SLOTS // CHUNK,)),
+            *scratch,
+        ],
+        compiler_params=pltpu.CompilerParams(vmem_limit_bytes=50 * 1024 * 1024),
+        cost_estimate=cost(2 * 64 * TILE * TILE * out.shape[2], 8),
+        name=name,
+    )(count, plan, v, *operands)
+
+
+def forward(q, count, plan, v, xs):
+    width = xs.shape[2]
+    kernel = functools.partial(forward_kernel, q)
+    out = jax.ShapeDtypeStruct((HALF, TILE, width), BF16)
+    scratch = [pltpu.VMEM(((HALF + 1) * TILE, width), BF16), pltpu.VMEM((HALF, TILE, width), F32)]
+    return block_product(kernel, "forward", out, scratch, count, plan, v, xs)
+
+
+def backward(count, plan, v, mine, theirs, parts):
+    width = mine.shape[1]
     sums = (HALF, TILE, width)
-    work = cost(2 * 64 * TILE * TILE * width, 8)
-    first = pl.pallas_call(
-        first_kernel,
-        out_shape=jax.ShapeDtypeStruct(sums, F32),
-        in_specs=[smem()] + [vmem()] * 2,
-        out_specs=vmem(),
-        compiler_params=params(),
-        cost_estimate=work,
-        name="first",
-    )(plan, v, mine)
-    return pl.pallas_call(
-        second_kernel,
-        out_shape=jax.ShapeDtypeStruct((HALF, TILE + rows - HALF * TILE, width), BF16),
-        in_specs=[smem()] + [vmem()] * 4,
-        out_specs=vmem(),
-        scratch_shapes=[pltpu.VMEM(sums, F32)],
-        compiler_params=params(),
-        cost_estimate=work,
-        name="second",
-    )(plan, v, theirs, mine, first)
+    out = jax.ShapeDtypeStruct(sums, F32)
+    first = block_product(first_kernel, "first", out, [], count, plan, v, mine)
+    out = jax.ShapeDtypeStruct((HALF, TILE + parts.shape[1], width), BF16)
+    scratch = [pltpu.VMEM(sums, F32)]
+    return block_product(
+        second_kernel, "second", out, scratch, count, plan, v, theirs, parts, first
+    )
 
 
 def last_kernel(scale, got, w, grad_out, weight_out):
@@ -390,9 +355,14 @@
     block = (paired[0].astype(F32) + others[0] + others[1] + others[2]).astype(BF16)
     activated, grad_pre, part = middle(trade_zh(block), weight, cotangent)
 
-    line = fold(trade_zh(pack(grad_pre, trade_row(part))))
-    mine = collect(where, [line] + [send_y(line, k) for k in (1, 2, 3)])
-    spread = trade_row(backward(plan, turned, mine, send_core(mine)))
+    part = sum_parts(trade_row(part), 4)
+    pair = jnp.concatenate([grad_pre, swap_zh(grad_pre, 1)], axis=0)
+    line = jnp.concatenate([pair, swap_zh(pair, 3)], axis=0)
+    line, part = lax.optimization_barrier((line, part))
+    part = sum_parts(trade_zh(part), 8)
+    mine = jnp.concatenate([line] + [send_y(line, k) for k in (1, 2, 3)], axis=0)
+    mine, part = lax.optimization_barrier((mine, part))
+    spread = trade_row(backward(tile_count, plan, turned, mine, send_core(mine), trade_near(part)))
     grad_features, grad_weight = last(spread, weight, grad_scale)
     return (activated, grad_features, grad_weight)
 

time: 200 us -> 215 us (1.075)
  starting transfers between devices: 42.9 us -> 73 us
  blocking collectives: 104 us -> 76.5 us
  Pallas kernels: 15.1 us -> 22.6 us
  waiting for transfers between devices: 27.2 us -> 30.4 us
    all_to_all x2 -> x1, blocking collectives: 56.7 us -> 35.7 us  [trade_row(): return lax.all_to_all(v, 'row', 0, 0)]
    all_to_all x1 -> x2, starting transfers between devices: 9.01 us -> 21.2 us  [trade_row(): return lax.all_to_all(v, 'row', 0, 0)]
    ppermute x0 -> x2, waiting for transfers between devices: none -> 12.1 us  [swap_zh(): return lax.ppermute(v, 'col', pairs)]
    all_to_all x2, blocking collectives: 47.7 us -> 40.8 us  [trade_zh(): return lax.all_to_all(v, 'col', 0, 0, axis_index_groups=groups)]
    ppermute x0 -> x2, starting transfers between devices: none -> 6.75 us  [swap_zh(): return lax.ppermute(v, 'col', pairs)]
    ppermute x6, waiting for transfers between devices: 14.3 us -> 7.55 us  [send_y(): return lax.ppermute(v, 'col', pairs)]
    pallas_call x8 -> x7, Pallas kernels: 9.4 us -> 15.3 us  [the longest x4 13.5 us: block_product(): pl.pallas_call(kernel, out_shape=out, in_specs=[smem()] * 2 + [pl.BlockSp...]
    all_to_all x0 -> x1, starting transfers between devices: none -> 4.62 us  [trade_near(): return lax.all_to_all(v, 'col', 0, 0, axis_index_groups=groups)]
  transfers between devices with their start and end apart: 9 -> 13, of which waited for: 7 -> 7; matrix products, arithmetic and copies ran while one was open for 0% -> 0% of each run, Pallas kernels for 4% -> 6%
where the time goes in v4:
time: 215 us; the launch traced here: 213 us
  blocking collectives  76.5 us (36%)
  starting transfers between devices  73 us (34%)
  waiting for transfers between devices  30.4 us (14%)
  Pallas kernels  22.6 us (11%)
  local copies, waits for them, and re-layouts  8.17 us (4%)
    all_to_all x2, blocking collectives, trade_zh(): return lax.all_to_all(v, 'col', 0, 0, axis_index_groups=groups)  40.8 us
    all_to_all x1, blocking collectives, trade_row(): return lax.all_to_all(v, 'row', 0, 0)  35.7 us
    all_to_all x2, starting transfers between devices, trade_row(): return lax.all_to_all(v, 'row', 0, 0)  21.2 us
    ppermute x6, starting transfers between devices, send_y(): return lax.ppermute(v, 'col', pairs)  20.7 us
    ppermute x2, starting transfers between devices, send_core(): return lax.ppermute(v, 'col', [(c, c ^ 1) for c in range(COLS)])  19.8 us
    pallas_call x4, Pallas kernels, block_product(): pl.pallas_call(kernel, out_shape=out, in_specs=[smem()] * 2 + [pl.BlockSp...  13.5 us
    ppermute x2, waiting for transfers between devices, swap_zh(): return lax.ppermute(v, 'col', pairs)  12.1 us
    all_to_all x2, waiting for transfers between devices, trade_row(): return lax.all_to_all(v, 'row', 0, 0)  10.2 us
  transfers between devices with their start and end apart: 13, of which 7 were waited for; matrix products, arithmetic and copies ran while one was open for 0% of the time, Pallas kernels for 6%

profile of v4, /device:TPU:1, one launch (start us, length us, event | category | flops | bytes accessed | tf_op | source)
XLA Modules:
  0.0 213.5 jit_solution(10419589534367311808)
XLA Ops:
  0.6 1.9 broadcast_in_dim.2
  2.6 9.0 %all-to-all-start = ((bf16[16,128,256]{2,1,0:T(8,128)(2,1)}), bf16[16,128,256]{2,1,0:T(8,128)(2,1)S(1)}, u32[]{:S(2)}, u32[]{:S(2)}) async-start(bf16[16,128,256]{2,1,0:T(8,128)(2,1)} %broadcast_in_dim.2), calls=%async_computation | async-start | bytes 2097152 | tf_op jit(solution)/shard_map/all_to_all | solution.py:37
  12.3 0.0 copy-start.1
  12.3 2.2 %copy-done.1 = bf16[1,1,128,128,128]{4,3,2,1,0:T(8,128)(2,1)S(1)} copy-done((bf16[1,1,128,128,128]{4,3,2,1,0:T(8,128)(2,1)S(1)}, bf16[1,1,128,128,128]{4,3,2,1,0:T(8,128)(2,1)}, u32[]{:S(2)}) %copy-start.1) | copy-done | bytes 4194328
  14.4 1.1 turn.1.v
  15.6 1.9 copy-done
  17.5 0.6 pad_add_fusion.where
  18.1 5.3 %plan.1 = s32[4,512]{1,0:T(4,128)} custom-call(s32[3]{0:T(128)} %pad_add_fusion.where, s32[1,1,128]{2,1,0:T(1,128)} %rows.1, s32[1,1,128]{2,1,0:T(1,128)} %cols.1, s32[1,1]{1,0:T(1,128)S(6)} %copy.10.count), custom_call_target="tpu_custom_call" | custom-call | bytes 16777216 | tf_op jit(solution)/shard_map/plan/pallas_call | solution.py:132
  23.5 10.2 %all-to-all-done.xs = bf16[16,128,256]{2,1,0:T(8,128)(2,1)S(1)} async-done(((bf16[16,128,256]{2,1,0:T(8,128)(2,1)}), bf16[16,128,256]{2,1,0:T(8,128)(2,1)S(1)}, u32[]{:S(2)}, u32[]{:S(2)}) %all-to-all-start) | async-done | bytes 1048608 | tf_op jit(solution)/shard_map/all_to_all | solution.py:37
  33.7 0.7 copy-done.4
  34.4 3.3 %forward.3 = bf16[16,128,256]{2,1,0:T(8,128)(2,1)S(1)} custom-call(s32[1,1]{1,0:T(1,128)S(6)} %copy.10.count, s32[4,512]{1,0:T(4,128)S(1)} %copy-done.4, bf16[128,128,128]{2,1,0:T(8,128)(2,1)} %bitcast.4, bf16[16,128,256]{2,1,0:T(8,128)(2,1)S(1)} %all-to-all-done.xs), custom_call_target="tpu_custom_call" | custom-call | flops 536870912 | bytes 8388608 | tf_op jit(solution)/shard_map/forward/pallas_call | solution.py:277
  37.7 5.4 %collective-permute-start = (bf16[16,128,256]{2,1,0:T(8,128)(2,1)S(1)}, bf16[16,128,256]{2,1,0:T(8,128)(2,1)S(1)}, u32[]{:S(2)}, u32[]{:S(2)}) collective-permute-start(bf16[16,128,256]{2,1,0:T(8,128)(2,1)S(1)} %forward.3), channel_id=1, source_target_pairs={{0,1},{1,0},{2,3},{3,2},{4,5},{5,4},{6,7},{7,6},{8,9},{9,8},{10,11... | collective-permute-start | bytes 3145736 | tf_op jit(solution)/shard_map/ppermute | solution.py:33
  43.2 3.0 %forward.2 = bf16[16,128,256]{2,1,0:T(8,128)(2,1)S(1)} custom-call(s32[1,1]{1,0:T(1,128)S(6)} %copy.10.count, s32[4,512]{1,0:T(4,128)S(1)} %copy-done.4, bf16[128,128,128]{2,1,0:T(8,128)(2,1)} %bitcast.5, bf16[16,128,256]{2,1,0:T(8,128)(2,1)S(1)} %all-to-all-done.xs), custom_call_target="tpu_custom_call" | custom-call | flops 536870912 | bytes 8388608 | tf_op jit(solution)/shard_map/forward/pallas_call | solution.py:277
  46.2 0.0 collective-permute-done
  46.2 0.4 add_convert_fusion
  46.6 0.0 copy-start.3
  46.6 0.0 copy-start.6
  46.6 0.1 fusion
  46.7 2.3 %collective-permute-start.1 = (bf16[4,128,256]{2,1,0:T(8,128)(2,1)S(1)}, bf16[4,128,256]{2,1,0:T(8,128)(2,1)S(1)}, u32[]{:S(2)}, u32[]{:S(2)}) collective-permute-start(bf16[4,128,256]{2,1,0:T(8,128)(2,1)S(1)} %get-tuple-element.27), channel_id=1, source_target_pairs={{0,2},{1,3},{2,4},{3,5},{4,6},{5,7},{6,0},{7,1},{8,10},{9,11},{10,... | collective-permute-start | bytes 786440 | tf_op jit(solution)/shard_map/ppermute | solution.py:29
  49.0 4.2 %collective-permute-start.3 = (bf16[4,128,256]{2,1,0:T(8,128)(2,1)S(1)}, bf16[4,128,256]{2,1,0:T(8,128)(2,1)S(1)}, u32[]{:S(2)}, u32[]{:S(2)}) collective-permute-start(bf16[4,128,256]{2,1,0:T(8,128)(2,1)S(1)} %get-tuple-element.28), channel_id=1, source_target_pairs={{0,6},{1,7},{2,0},{3,1},{4,2},{5,3},{6,4},{7,5},{8,14},{9,15},{10,... | collective-permute-start | bytes 786440 | tf_op jit(solution)/shard_map/ppermute | solution.py:29
  53.2 2.8 %collective-permute-start.2 = (bf16[4,128,256]{2,1,0:T(8,128)(2,1)S(1)}, bf16[4,128,256]{2,1,0:T(8,128)(2,1)S(1)}, u32[]{:S(2)}, u32[]{:S(2)}) collective-permute-start(bf16[4,128,256]{2,1,0:T(8,128)(2,1)S(1)} %get-tuple-element.29), channel_id=1, source_target_pairs={{0,4},{1,5},{2,6},{3,7},{4,0},{5,1},{6,2},{7,3},{8,12},{9,13},{10,... | collective-permute-start | bytes 786440 | tf_op jit(solution)/shard_map/ppermute | solution.py:29
  55.9 1.4 collective-permute-done.1
  57.3 1.1 collective-permute-done.3
  58.4 5.0 %collective-permute-done.2 = bf16[4,128,256]{2,1,0:T(8,128)(2,1)S(1)} collective-permute-done((bf16[4,128,256]{2,1,0:T(8,128)(2,1)S(1)}, bf16[4,128,256]{2,1,0:T(8,128)(2,1)S(1)}, u32[]{:S(2)}, u32[]{:S(2)}) %collective-permute-start.2) | collective-permute-done | bytes 262176 | tf_op jit(solution)/shard_map/ppermute | solution.py:29
  63.5 0.1 add_convert_fusion.1
  63.6 25.6 %all_to_all.30.got = bf16[4,128,256]{2,1,0:T(8,128)(2,1)S(1)} all-to-all(bf16[4,128,256]{2,1,0:T(8,128)(2,1)S(1)} %add_convert_fusion.1), channel_id=1, replica_groups={{0,8,16,24},{1,9,17,25},{2,10,18,26},{3,11,19,27},{4,12,20,28},{5,13,21..., dimensions={0} | all-to-all | bytes 524288 | tf_op jit(solution)/shard_map/all_to_all | solution.py:52
  89.2 1.0 middle.1
  90.2 12.2 %all-to-all-start.2 = ((bf16[16,16,256]{2,1,0:T(8,128)(2,1)}), bf16[16,16,256]{2,1,0:T(8,128)(2,1)S(1)}, u32[]{:S(2)}, u32[]{:S(2)}) async-start(bf16[16,16,256]{2,1,0:T(8,128)(2,1)} %get-tuple-element.20), calls=%async_computation.2 | async-start | bytes 262144 | tf_op jit(solution)/shard_map/all_to_all | solution.py:37
  102.4 3.8 %collective-permute-start.4 = (bf16[128,256]{1,0:T(8,128)(2,1)S(1)}, bf16[128,256]{1,0:T(8,128)(2,1)S(1)}, u32[]{:S(2)}, u32[]{:S(2)}) collective-permute-start(bf16[128,256]{1,0:T(8,128)(2,1)S(1)} %get-tuple-element.19), channel_id=1, source_target_pairs={{0,8},{1,9},{2,10},{3,11},{4,12},{5,13},{6,14},{7,15},{8,0},{9,1},... | collective-permute-start | bytes 196616 | tf_op jit(solution)/shard_map/ppermute | solution.py:42
  106.2 5.1 %collective-permute-done.4 = bf16[128,256]{1,0:T(8,128)(2,1)S(1)} collective-permute-done((bf16[128,256]{1,0:T(8,128)(2,1)S(1)}, bf16[128,256]{1,0:T(8,128)(2,1)S(1)}, u32[]{:S(2)}, u32[]{:S(2)}) %collective-permute-start.4) | collective-permute-done | bytes 65568 | tf_op jit(solution)/shard_map/ppermute | solution.py:42
  111.4 2.9 %collective-permute-start.5 = (bf16[256,256]{1,0:T(8,128)(2,1)S(1)}, bf16[256,256]{1,0:T(8,128)(2,1)S(1)}, u32[]{:S(2)}, u32[]{:S(2)}) collective-permute-start(bf16[256,256]{1,0:T(8,128)(2,1)S(1)} %pad_maximum_fusion.2), channel_id=1, source_target_pairs={{0,24},{1,25},{2,26},{3,27},{4,28},{5,29},{6,30},{7,31},{8,16},{9,... | collective-permute-start | bytes 393224 | tf_op jit(solution)/shard_map/ppermute | solution.py:42
  114.3 7.0 %collective-permute-done.5 = bf16[256,256]{1,0:T(8,128)(2,1)S(1)} collective-permute-done((bf16[256,256]{1,0:T(8,128)(2,1)S(1)}, bf16[256,256]{1,0:T(8,128)(2,1)S(1)}, u32[]{:S(2)}, u32[]{:S(2)}) %collective-permute-start.5) | collective-permute-done | bytes 131104 | tf_op jit(solution)/shard_map/ppermute | solution.py:42
  121.3 0.0 all-to-all-done.2.parts
  121.3 6.2 %collective-permute-start.8 = (bf16[512,256]{1,0:T(8,128)(2,1)S(1)}, bf16[512,256]{1,0:T(8,128)(2,1)S(1)}, u32[]{:S(2)}, u32[]{:S(2)}) collective-permute-start(bf16[512,256]{1,0:T(8,128)(2,1)S(1)} %pad_maximum_fusion.1), channel_id=1, source_target_pairs={{0,6},{1,7},{2,0},{3,1},{4,2},{5,3},{6,4},{7,5},{8,14},{9,15},{10,... | collective-permute-start | bytes 786440 | tf_op jit(solution)/shard_map/ppermute | solution.py:29
  127.5 3.3 %collective-permute-start.7 = (bf16[512,256]{1,0:T(8,128)(2,1)S(1)}, bf16[512,256]{1,0:T(8,128)(2,1)S(1)}, u32[]{:S(2)}, u32[]{:S(2)}) collective-permute-start(bf16[512,256]{1,0:T(8,128)(2,1)S(1)} %pad_maximum_fusion.1), channel_id=1, source_target_pairs={{0,4},{1,5},{2,6},{3,7},{4,0},{5,1},{6,2},{7,3},{8,12},{9,13},{10,... | collective-permute-start | bytes 786440 | tf_op jit(solution)/shard_map/ppermute | solution.py:29
  130.9 1.9 collective-permute-start.6
  132.8 15.3 %all_to_all.31.parts = bf16[4,16,256]{2,1,0:T(8,128)(2,1)S(1)} all-to-all(bf16[4,16,256]{2,1,0:T(8,128)(2,1)S(1)} %sum_parts.2), channel_id=1, replica_groups={{0,8,16,24},{1,9,17,25},{2,10,18,26},{3,11,19,27},{4,12,20,28},{5,13,21..., dimensions={0} | all-to-all | bytes 65536 | tf_op jit(solution)/shard_map/all_to_all | solution.py:52
  148.0 0.6 sum_parts.3
  148.7 0.1 pad_maximum_fusion.grads
  148.8 14.3 %collective-permute-start.9 = (bf16[2048,256]{1,0:T(8,128)(2,1)S(1)}, bf16[2048,256]{1,0:T(8,128)(2,1)S(1)}, u32[]{:S(2)}, u32[]{:S(2)}) collective-permute-start(bf16[2048,256]{1,0:T(8,128)(2,1)S(1)} %pad_maximum_fusion.grads), channel_id=1, source_target_pairs={{0,1},{1,0},{2,3},{3,2},{4,5},{5,4},{6,7},{7,6},{8,9},{9,8},{10,11... | collective-permute-start | bytes 3145736 | tf_op jit(solution)/shard_map/ppermute | solution.py:33
  163.1 4.6 %all-to-all-start.4 = ((bf16[8,16,256]{2,1,0:T(8,128)(2,1)}), bf16[8,16,256]{2,1,0:T(8,128)(2,1)S(1)}, u32[]{:S(2)}, u32[]{:S(2)}) async-start(bf16[8,16,256]{2,1,0:T(8,128)(2,1)} %sum_parts.3), calls=%async_computation.4 | async-start | bytes 131072 | tf_op jit(solution)/shard_map/all_to_all | solution.py:47
  167.7 2.9 %first.1.start = f32[16,128,256]{2,1,0:T(8,128)S(1)} custom-call(s32[1,1]{1,0:T(1,128)S(6)} %copy.10.count, s32[4,512]{1,0:T(4,128)S(1)} %copy-done.5, bf16[128,128,128]{2,1,0:T(8,128)(2,1)} %copy-done, bf16[2048,256]{1,0:T(8,128)(2,1)S(1)} %pad_maximum_fusion.grads), custom_call_target="tpu_custom_call" | custom-call | flops 536870912 | bytes 8388608 | tf_op jit(solution)/shard_map/first/pallas_call | solution.py:277
  170.7 1.3 copy-done.2
  172.0 0.6 all-to-all-done.4.parts
  172.6 0.0 collective-permute-done.9.grads
  172.6 4.3 %second.1 = bf16[16,144,256]{2,1,0:T(8,128)(2,1)S(1)} custom-call(s32[1,1]{1,0:T(1,128)S(6)} %copy.10.count, s32[4,512]{1,0:T(4,128)S(1)} %copy-done.5, bf16[128,128,128]{2,1,0:T(8,128)(2,1)} %copy-done, bf16[2048,256]{1,0:T(8,128)(2,1)S(1)} %collective-permute-done.9.grads, bf16[8,16,256]{2,1,0:T(8,128)(2,1)S(1)} %all-to-all-done.4.parts, ...), custom_call_target="tpu_custom_call" | custom-call | flops 536870912 | bytes 8388608 | tf_op jit(solution)/shard_map/second/pallas_call | solution.py:277
  176.9 35.7 %all_to_all.32.got = bf16[16,144,256]{2,1,0:T(8,128)(2,1)S(1)} all-to-all(bf16[16,144,256]{2,1,0:T(8,128)(2,1)S(1)} %second.1), channel_id=1, replica_groups=mesh['row'=16,'col'=32] {'row'}, dimensions={0} | all-to-all | bytes 2359296 | tf_op jit(solution)/shard_map/all_to_all | solution.py:37
  212.5 0.9 last.1
  (13 shorter events, 0.1 us)
Async XLA Ops:
  2.6 31.1 %all-to-all-start = ((bf16[16,128,256]{2,1,0:T(8,128)(2,1)}), bf16[16,128,256]{2,1,0:T(8,128)(2,1)S(1)}, u32[]{:S(2)}, u32[]{:S(2)}) async-start(bf16[16,128,256]{2,1,0:T(8,128)(2,1)} %broadcast_in_dim.2), calls=%async_computation | async-start | bytes 2097152 | tf_op jit(solution)/shard_map/all_to_all | solution.py:37
  12.3 2.2 %copy-start.1 = (bf16[1,1,128,128,128]{4,3,2,1,0:T(8,128)(2,1)S(1)}, bf16[1,1,128,128,128]{4,3,2,1,0:T(8,128)(2,1)}, u32[]{:S(2)}) copy-start(bf16[1,1,128,128,128]{4,3,2,1,0:T(8,128)(2,1)} %v.1) | copy-start | bytes 12582916
  15.6 1.9 copy-start
  33.7 0.7 copy-start.4
  37.7 8.5 %collective-permute-start = (bf16[16,128,256]{2,1,0:T(8,128)(2,1)S(1)}, bf16[16,128,256]{2,1,0:T(8,128)(2,1)S(1)}, u32[]{:S(2)}, u32[]{:S(2)}) collective-permute-start(bf16[16,128,256]{2,1,0:T(8,128)(2,1)S(1)} %forward.3), channel_id=1, source_target_pairs={{0,1},{1,0},{2,3},{3,2},{4,5},{5,4},{6,7},{7,6},{8,9},{9,8},{10,11... | collective-permute-start | bytes 3145736 | tf_op jit(solution)/shard_map/ppermute | solution.py:33
  46.6 42.6 %copy-start.3 = (bf16[256,256]{1,0:T(8,128)(2,1)S(1)}, bf16[256,256]{1,0:T(8,128)(2,1)}, u32[]{:S(2)}) copy-start(bf16[256,256]{1,0:T(8,128)(2,1)} %w.3) | copy-start | bytes 393220
  46.6 42.6 %copy-start.6 = (bf16[128,256]{1,0:T(8,128)(2,1)S(1)}, bf16[128,256]{1,0:T(8,128)(2,1)}, u32[]{:S(2)}) copy-start(bf16[128,256]{1,0:T(8,128)(2,1)} %cot.1) | copy-start | bytes 196612
  46.7 10.6 %collective-permute-start.1 = (bf16[4,128,256]{2,1,0:T(8,128)(2,1)S(1)}, bf16[4,128,256]{2,1,0:T(8,128)(2,1)S(1)}, u32[]{:S(2)}, u32[]{:S(2)}) collective-permute-start(bf16[4,128,256]{2,1,0:T(8,128)(2,1)S(1)} %get-tuple-element.27), channel_id=1, source_target_pairs={{0,2},{1,3},{2,4},{3,5},{4,6},{5,7},{6,0},{7,1},{8,10},{9,11},{10,... | collective-permute-start | bytes 786440 | tf_op jit(solution)/shard_map/ppermute | solution.py:29
  49.0 9.4 %collective-permute-start.3 = (bf16[4,128,256]{2,1,0:T(8,128)(2,1)S(1)}, bf16[4,128,256]{2,1,0:T(8,128)(2,1)S(1)}, u32[]{:S(2)}, u32[]{:S(2)}) collective-permute-start(bf16[4,128,256]{2,1,0:T(8,128)(2,1)S(1)} %get-tuple-element.28), channel_id=1, source_target_pairs={{0,6},{1,7},{2,0},{3,1},{4,2},{5,3},{6,4},{7,5},{8,14},{9,15},{10,... | collective-permute-start | bytes 786440 | tf_op jit(solution)/shard_map/ppermute | solution.py:29
  53.2 10.3 %collective-permute-start.2 = (bf16[4,128,256]{2,1,0:T(8,128)(2,1)S(1)}, bf16[4,128,256]{2,1,0:T(8,128)(2,1)S(1)}, u32[]{:S(2)}, u32[]{:S(2)}) collective-permute-start(bf16[4,128,256]{2,1,0:T(8,128)(2,1)S(1)} %get-tuple-element.29), channel_id=1, source_target_pairs={{0,4},{1,5},{2,6},{3,7},{4,0},{5,1},{6,2},{7,3},{8,12},{9,13},{10,... | collective-permute-start | bytes 786440 | tf_op jit(solution)/shard_map/ppermute | solution.py:29
  89.2 78.6 %copy-start.5 = (s32[4,512]{1,0:T(4,128)S(1)}, s32[4,512]{1,0:T(4,128)}, u32[]{:S(2)}) copy-start(s32[4,512]{1,0:T(4,128)} %plan.1) | copy-start | bytes 24580
  90.2 31.1 %all-to-all-start.2 = ((bf16[16,16,256]{2,1,0:T(8,128)(2,1)}), bf16[16,16,256]{2,1,0:T(8,128)(2,1)S(1)}, u32[]{:S(2)}, u32[]{:S(2)}) async-start(bf16[16,16,256]{2,1,0:T(8,128)(2,1)} %get-tuple-element.20), calls=%async_computation.2 | async-start | bytes 262144 | tf_op jit(solution)/shard_map/all_to_all | solution.py:37
  102.4 8.9 %collective-permute-start.4 = (bf16[128,256]{1,0:T(8,128)(2,1)S(1)}, bf16[128,256]{1,0:T(8,128)(2,1)S(1)}, u32[]{:S(2)}, u32[]{:S(2)}) collective-permute-start(bf16[128,256]{1,0:T(8,128)(2,1)S(1)} %get-tuple-element.19), channel_id=1, source_target_pairs={{0,8},{1,9},{2,10},{3,11},{4,12},{5,13},{6,14},{7,15},{8,0},{9,1},... | collective-permute-start | bytes 196616 | tf_op jit(solution)/shard_map/ppermute | solution.py:42
  111.4 9.9 %collective-permute-start.5 = (bf16[256,256]{1,0:T(8,128)(2,1)S(1)}, bf16[256,256]{1,0:T(8,128)(2,1)S(1)}, u32[]{:S(2)}, u32[]{:S(2)}) collective-permute-start(bf16[256,256]{1,0:T(8,128)(2,1)S(1)} %pad_maximum_fusion.2), channel_id=1, source_target_pairs={{0,24},{1,25},{2,26},{3,27},{4,28},{5,29},{6,30},{7,31},{8,16},{9,... | collective-permute-start | bytes 393224 | tf_op jit(solution)/shard_map/ppermute | solution.py:42
  121.3 27.4 %collective-permute-start.8 = (bf16[512,256]{1,0:T(8,128)(2,1)S(1)}, bf16[512,256]{1,0:T(8,128)(2,1)S(1)}, u32[]{:S(2)}, u32[]{:S(2)}) collective-permute-start(bf16[512,256]{1,0:T(8,128)(2,1)S(1)} %pad_maximum_fusion.1), channel_id=1, source_target_pairs={{0,6},{1,7},{2,0},{3,1},{4,2},{5,3},{6,4},{7,5},{8,14},{9,15},{10,... | collective-permute-start | bytes 786440 | tf_op jit(solution)/shard_map/ppermute | solution.py:29
  127.5 21.2 %collective-permute-start.7 = (bf16[512,256]{1,0:T(8,128)(2,1)S(1)}, bf16[512,256]{1,0:T(8,128)(2,1)S(1)}, u32[]{:S(2)}, u32[]{:S(2)}) collective-permute-start(bf16[512,256]{1,0:T(8,128)(2,1)S(1)} %pad_maximum_fusion.1), channel_id=1, source_target_pairs={{0,4},{1,5},{2,6},{3,7},{4,0},{5,1},{6,2},{7,3},{8,12},{9,13},{10,... | collective-permute-start | bytes 786440 | tf_op jit(solution)/shard_map/ppermute | solution.py:29
  130.9 17.8 %collective-permute-start.6 = (bf16[512,256]{1,0:T(8,128)(2,1)S(1)}, bf16[512,256]{1,0:T(8,128)(2,1)S(1)}, u32[]{:S(2)}, u32[]{:S(2)}) collective-permute-start(bf16[512,256]{1,0:T(8,128)(2,1)S(1)} %pad_maximum_fusion.1), channel_id=1, source_target_pairs={{0,2},{1,3},{2,4},{3,5},{4,6},{5,7},{6,0},{7,1},{8,10},{9,11},{10,... | collective-permute-start | bytes 786440 | tf_op jit(solution)/shard_map/ppermute | solution.py:29
  148.8 23.8 %collective-permute-start.9 = (bf16[2048,256]{1,0:T(8,128)(2,1)S(1)}, bf16[2048,256]{1,0:T(8,128)(2,1)S(1)}, u32[]{:S(2)}, u32[]{:S(2)}) collective-permute-start(bf16[2048,256]{1,0:T(8,128)(2,1)S(1)} %pad_maximum_fusion.grads), channel_id=1, source_target_pairs={{0,1},{1,0},{2,3},{3,2},{4,5},{5,4},{6,7},{7,6},{8,9},{9,8},{10,11... | collective-permute-start | bytes 3145736 | tf_op jit(solution)/shard_map/ppermute | solution.py:33
  163.1 9.5 %all-to-all-start.4 = ((bf16[8,16,256]{2,1,0:T(8,128)(2,1)}), bf16[8,16,256]{2,1,0:T(8,128)(2,1)S(1)}, u32[]{:S(2)}, u32[]{:S(2)}) async-start(bf16[8,16,256]{2,1,0:T(8,128)(2,1)} %sum_parts.3), calls=%async_computation.4 | async-start | bytes 131072 | tf_op jit(solution)/shard_map/all_to_all | solution.py:47
  170.6 1.3 copy-start.2

commit v5 on v2

v5 whole, which is shorter than its diff:
```python
import functools
import math

import jax
import jax.numpy as jnp
from jax import lax
from jax.experimental import pallas as pl
from jax.experimental.pallas import tpu as pltpu
from jax.sharding import PartitionSpec as P

TILE = 128
ROWS = 16
COLS = 32
HALF = 16
GROUP = 8
CHUNK = 16
SLOTS = 128
VMEM_LIMIT = 24 * 1024 * 1024
BF16 = jnp.bfloat16
F32 = jnp.float32


def send_y(v, k):
    pairs = [(c, (c // 8) * 8 + ((c // 2 + k) % 4) * 2 + c % 2) for c in range(COLS)]
    return lax.ppermute(v, "col", pairs)


def send_core(v):
    return lax.ppermute(v, "col", [(c, c ^ 1) for c in range(COLS)])


def trade_row(v):
    return lax.all_to_all(v, "row", 0, 0)


def trade_zh(v):
    groups = [[zh * 8 + rest for zh in range(4)] for rest in range(8)]
    return lax.all_to_all(v, "col", 0, 0, axis_index_groups=groups)


def smem():
    return pl.BlockSpec(memory_space=pltpu.SMEM)


def vmem():
    return pl.BlockSpec(memory_space=pltpu.VMEM)


def params():
    return pltpu.CompilerParams(vmem_limit_bytes=VMEM_LIMIT)


def cost(flops, mib):
    return pl.CostEstimate(flops=flops, bytes_accessed=mib * 1024 * 1024, transcendentals=0)


def choose_slots(parity, where, rows, slots):
    live = where[3]

    def pick(g, found):
        for u in range(GROUP):
            s = g * GROUP + u
            slots[found] = s
            chosen = ((rows[0, 0, s] & 1) == parity) & (s < live)
            found = found + jnp.where(chosen, 1, 0)
        return found

    return lax.fori_loop(0, (live + GROUP - 1) // GROUP, pick, 0)


def add_products(found, slots, tile, source, target, acc):
    def step(g, _):
        products, targets = [], []
        for u in range(GROUP):
            at = g * GROUP + u
            s = jnp.where(at < found, slots[at], 0)
            targets.append(jnp.where(at < found, target(s), HALF))
            products.append(jnp.dot(tile(s), source(s), preferred_element_type=F32))
        for u in range(GROUP):
            acc[targets[u]] = acc[targets[u]] + products[u]
        return 0

    lax.fori_loop(0, (found + GROUP - 1) // GROUP, step, 0)


def fetch_tiles(live, v, tiles, sems):
    def chunk(i):
        part = pl.ds(i * CHUNK, CHUNK)
        return pltpu.make_async_copy(v.at[0, 0, part], tiles.at[part], sems.at[i])

    for i in range(SLOTS // CHUNK):
        pl.when(i * CHUNK < live)(chunk(i).start)

    def arrive():
        for i in range(SLOTS // CHUNK):
            pl.when(i * CHUNK < live)(chunk(i).wait)

    return arrive


def forward_kernel(other, where, rows, cols, v, xs, out, slots, acc, tiles, sems):
    y, core = where[1], where[2]
    arrive = fetch_tiles(where[3], v, tiles, sems)
    acc[...] = jnp.zeros_like(acc)
    found = choose_slots(core ^ other, where, rows, slots)

    def target(s):
        r = rows[0, 0, s]
        return ((((r >> 1) & 3) - y) & 3) * 4 + (r >> 3)

    arrive()
    add_products(found, slots, lambda s: tiles[s], lambda s: xs[cols[0, 0, s]], target, acc)
    out[...] = acc[:HALF].astype(BF16)


def forward(other, where, rows, cols, values, xs):
    width = xs.shape[-1]
    return pl.pallas_call(
        functools.partial(forward_kernel, other),
        out_shape=jax.ShapeDtypeStruct((HALF, TILE, width), BF16),
        in_specs=[smem()] * 3 + [pl.BlockSpec(memory_space=pltpu.HBM), vmem()],
        out_specs=vmem(),
        scratch_shapes=[
            pltpu.SMEM((SLOTS + GROUP,), jnp.int32),
            pltpu.VMEM((HALF + 1, TILE, width), F32),
            pltpu.VMEM((SLOTS, TILE, TILE), BF16),
            pltpu.SemaphoreType.DMA((SLOTS // CHUNK,)),
        ],
        compiler_params=pltpu.CompilerParams(vmem_limit_bytes=50 * 1024 * 1024),
        cost_estimate=cost(2 * 64 * TILE * TILE * width, 7),
        name="forward",
    )(where, rows, cols, values, xs)


def turn_kernel(where, v, out):
    def step(i, _):
        for u in range(4):
            out[4 * i + u] = v[0, 0, 4 * i + u].T
        return 0

    lax.fori_loop(0, (where[3] + 3) // 4, step, 0)


def turn_tiles(where, tile_values):
    return pl.pallas_call(
        turn_kernel,
        out_shape=jax.ShapeDtypeStruct(tile_values.shape[2:], tile_values.dtype),
        in_specs=[smem(), vmem()],
        out_specs=vmem(),
        compiler_params=params(),
        cost_estimate=cost(0, 10),
        name="turn",
    )(where, tile_values)


def middle_kernel(got, w, cot, act_out, grad_out, part_out):
    total = got[0].astype(F32)
    for i in range(1, 4):
        total = total + got[i].astype(F32)
    aggregated = total.astype(BF16)
    pre = jnp.dot(aggregated, w[...], preferred_element_type=F32)
    s = jax.nn.sigmoid(pre)
    act_out[...] = (pre * s).astype(BF16)
    grad = (cot[...].astype(F32) * (s * (1.0 + pre * (1.0 - s)))).astype(BF16)
    grad_out[...] = grad
    part = lax.dot_general(aggregated, grad, (((0,), (0,)), ((), ())), preferred_element_type=F32)
    part_out[...] = part.reshape(part_out.shape).astype(BF16)


def middle(got, w, cot):
    n, width = cot.shape
    rows = jax.ShapeDtypeStruct((n, width), BF16)
    return pl.pallas_call(
        middle_kernel,
        out_shape=(rows, rows, jax.ShapeDtypeStruct((ROWS, width // ROWS, width), BF16)),
        compiler_params=params(),
        cost_estimate=cost(4 * n * width * width, 1),
        name="middle",
    )(got, w, cot)


def pack_kernel(grad, parts, out):
    total = parts[0].astype(F32)
    for i in range(1, ROWS):
        total = total + parts[i].astype(F32)
    part = total.astype(BF16)
    for i in range(4):
        out[i, :TILE] = grad[...]
        out[i, TILE:] = part


def pack(grad, parts):
    n, width = grad.shape
    return pl.pallas_call(
        pack_kernel,
        out_shape=jax.ShapeDtypeStruct((4, n + parts.shape[1], width), BF16),
        compiler_params=params(),
        cost_estimate=cost(0, 1),
        name="pack",
    )(grad, parts)


def fold_kernel(got, out):
    total = got[0, TILE:].astype(F32)
    for i in range(1, 4):
        total = total + got[i, TILE:].astype(F32)
    for i in range(4):
        out[TILE * i : TILE * (i + 1)] = got[i, :TILE]
    out[4 * TILE :] = total.astype(BF16)


def fold(got):
    extra, width = got.shape[1] - TILE, got.shape[2]
    return pl.pallas_call(
        fold_kernel,
        out_shape=jax.ShapeDtypeStruct((4 * TILE + extra, width), BF16),
        compiler_params=params(),
        cost_estimate=cost(0, 1),
        name="fold",
    )(got)


def collect_kernel(where, l0, l1, l2, l3, out, slices):
    y = where[1]
    rows = 4 * TILE
    for k, line in enumerate((l0, l1, l2, l3)):
        out[rows * k : rows * (k + 1)] = line[:rows]
        slices[(y - k) & 3] = line[rows:].astype(F32)
    out[4 * rows :] = ((slices[0] + slices[1]) + (slices[2] + slices[3])).astype(BF16)


def collect(where, lines):
    rows, width = lines[0].shape
    extra = rows - 4 * TILE
    return pl.pallas_call(
        collect_kernel,
        out_shape=jax.ShapeDtypeStruct((HALF * TILE + extra, width), BF16),
        in_specs=[smem()] + [vmem()] * 4,
        out_specs=vmem(),
        scratch_shapes=[pltpu.VMEM((4, extra, width), F32)],
        compiler_params=params(),
        cost_estimate=cost(0, 3),
        name="collect",
    )(where, *lines)


def backward_half(other, where, rows, cols, v, grads, slots, acc):
    y, core = where[1], where[2]
    found = choose_slots(core ^ other, where, rows, slots)

    def source(s):
        r = rows[0, 0, s]
        at = ((y - ((r >> 1) & 3)) & 3) * 4 + (r >> 3)
        return grads[pl.ds(pl.multiple_of(at * TILE, TILE), TILE)]

    add_products(found, slots, lambda s: v[s], source, lambda s: cols[0, 0, s], acc)


def first_kernel(where, rows, cols, v, grads, out, slots, acc):
    acc[...] = jnp.zeros_like(acc)
    backward_half(0, where, rows, cols, v, grads, slots, acc)
    out[...] = acc[:HALF]


def second_kernel(where, rows, cols, v, grads, mine, start, out, slots, acc):
    acc[:HALF] = start[...]
    acc[HALF] = jnp.zeros_like(acc[HALF])
    backward_half(1, where, rows, cols, v, grads, slots, acc)
    rest = HALF * TILE
    part = (mine[rest:].astype(F32) + grads[rest:].astype(F32)).astype(BF16)
    for d in range(HALF):
        out[d, :TILE] = acc[d].astype(BF16)
        out[d, TILE:] = part


def backward(where, rows, cols, v, mine, theirs):
    extra, width = mine.shape[0] - HALF * TILE, mine.shape[1]
    scratch = [
        pltpu.SMEM((SLOTS + GROUP,), jnp.int32),
        pltpu.VMEM((HALF + 1, TILE, width), F32),
    ]
    work = cost(2 * 64 * TILE * TILE * width, 8)
    first = pl.pallas_call(
        first_kernel,
        out_shape=jax.ShapeDtypeStruct((HALF, TILE, width), F32),
        in_specs=[smem()] * 3 + [vmem()] * 2,
        out_specs=vmem(),
        scratch_shapes=scratch,
        compiler_params=params(),
        cost_estimate=work,
        name="first",
    )(where, rows, cols, v, mine)
    return pl.pallas_call(
        second_kernel,
        out_shape=jax.ShapeDtypeStruct((HALF, TILE + extra, width), BF16),
        in_specs=[smem()] * 3 + [vmem()] * 4,
        out_specs=vmem(),
        scratch_shapes=scratch,
        compiler_params=params(),
        cost_estimate=work,
        name="second",
    )(where, rows, cols, v, theirs, mine, first)


def last_kernel(scale, got, w, grad_out, weight_out):
    total = got[0, :TILE].astype(F32)
    for i in range(1, ROWS):
        total = total + got[i, :TILE].astype(F32)
    grad_out[...] = lax.dot_general(
        total.astype(BF16), w[...], (((1,), (1,)), ((), ())), preferred_element_type=F32
    ).astype(BF16)
    extra = got.shape[1] - TILE
    for i in range(ROWS):
        weight_out[extra * i : extra * (i + 1)] = got[i, TILE:].astype(F32) * scale


def last(got, w, scale):
    width = w.shape[0]
    return pl.pallas_call(
        functools.partial(last_kernel, scale),
        out_shape=(
            jax.ShapeDtypeStruct((TILE, width), BF16),
            jax.ShapeDtypeStruct((width, width), F32),
        ),
        compiler_params=params(),
        cost_estimate=cost(2 * TILE * width * width, 1),
        name="last",
    )(got, w)


def shards(features, weight, tile_values, tile_rows, tile_cols, tile_count, cotangent):
    node_dev = features.shape[0]
    grad_scale = 1.0 / math.sqrt(node_dev * lax.axis_size("row") * lax.axis_size("col"))
    c = lax.axis_index("col")
    where = jnp.stack([c >> 3, (c >> 1) & 3, c & 1, tile_count[0, 0]]).astype(jnp.int32)

    features, where = lax.optimization_barrier((features, where))
    xs = trade_row(jnp.broadcast_to(features[None], (ROWS,) + features.shape))
    xs, where = lax.optimization_barrier((xs, where))
    block = (where, tile_rows, tile_cols)
    got = send_core(forward(1, *block, tile_values, xs))
    keep = forward(0, *block, tile_values, xs)
    paired = (keep.astype(F32) + got.astype(F32)).astype(BF16).reshape(4, 4, TILE, -1)
    others = [send_y(paired[k], k).astype(F32) for k in (1, 2, 3)]
    rows = (paired[0].astype(F32) + others[0] + others[1] + others[2]).astype(BF16)
    turned = turn_tiles(where, tile_values)
    rows, turned = lax.optimization_barrier((rows, turned))
    activated, grad_pre, part = middle(trade_zh(rows), weight, cotangent)

    line = fold(trade_zh(pack(grad_pre, trade_row(part))))
    mine = collect(where, [line] + [send_y(line, k) for k in (1, 2, 3)])
    spread = backward(*block, turned, mine, send_core(mine))
    grad_features, grad_weight = last(trade_row(spread), weight, grad_scale)
    return (activated, grad_features, grad_weight)


def solution(mesh):
    return jax.shard_map(
        shards,
        mesh=mesh,
        in_specs=(
            P(("col", "row"), None),
            P(),
            P("row", "col", None, None, None),
            P("row", "col", None),
            P("row", "col", None),
            P("row", "col"),
            P(("row", "col"), None),
        ),
        out_specs=(P(("row", "col"), None), P(("col", "row"), None), P()),
        check_vma=False,
    )
```

time: 211 us -> 201 us (0.953)
  blocking collectives: 106 us -> 137 us
  waiting for transfers between devices: 38.3 us -> 14.7 us
  starting transfers between devices: 43 us -> 32.4 us
  local copies, waits for them, and re-layouts: 6.42 us -> 1.01 us
    all_to_all x2 -> x3, blocking collectives: 60.2 us -> 88 us  [trade_row(): return lax.all_to_all(v, 'row', 0, 0)]
    all_to_all x1 -> x0, waiting for transfers between devices: 21.4 us -> none  [trade_row(): return lax.all_to_all(v, 'row', 0, 0)]
    all_to_all x1 -> x0, starting transfers between devices: 9.01 us -> none  [trade_row(): return lax.all_to_all(v, 'row', 0, 0)]
    unnamed x22 -> x10, local copies, waits for them, and re-layouts: 4.42 us -> 0.03 us
    all_to_all x2, blocking collectives: 45.4 us -> 48.9 us  [trade_zh(): return lax.all_to_all(v, 'col', 0, 0, axis_index_groups=groups)]
    ppermute x6, starting transfers between devices: 22 us -> 19.5 us  [send_y(): return lax.ppermute(v, 'col', pairs)]
  transfers between devices with their start and end apart: 9 -> 8, of which waited for: 8 -> 6; matrix products, arithmetic and copies ran while one was open for 0% -> 0% of each run, Pallas kernels for 3% -> 3%
where the time goes in v5:
time: 201 us; the launch traced here: 200 us
  blocking collectives  137 us (68%)
  starting transfers between devices  32.4 us (16%)
  waiting for transfers between devices  14.7 us (7%)
  Pallas kernels  12.9 us (6%)
    all_to_all x3, blocking collectives, trade_row(): return lax.all_to_all(v, 'row', 0, 0)  88 us
    all_to_all x2, blocking collectives, trade_zh(): return lax.all_to_all(v, 'col', 0, 0, axis_index_groups=groups)  48.9 us
    ppermute x6, starting transfers between devices, send_y(): return lax.ppermute(v, 'col', pairs)  19.5 us
    ppermute x6, waiting for transfers between devices, send_y(): return lax.ppermute(v, 'col', pairs)  14 us
    ppermute x2, starting transfers between devices, send_core(): return lax.ppermute(v, 'col', [(c, c ^ 1) for c in range(COLS)])  12.9 us
    pallas_call x2, Pallas kernels, forward(): pl.pallas_call(functools.partial(forward_kernel, other), out_shape=jax.Sh...  5.7 us
  transfers between devices with their start and end apart: 8, of which 6 were waited for; matrix products, arithmetic and copies ran while one was open for 0% of the time, Pallas kernels for 3%

profile of v5, /device:TPU:1, one launch (start us, length us, event | category | flops | bytes accessed | tf_op | source)
XLA Modules:
  0.0 199.9 jit_solution(735848815549713939)
XLA Ops:
  0.6 0.0 copy-start.4
  0.6 0.0 copy-start.3
  1.3 0.1 pad_add_fusion.where
  1.4 0.9 broadcast_in_dim.2
  2.3 33.7 %all_to_all.25.xs = bf16[16,128,256]{2,1,0:T(8,128)(2,1)S(1)} all-to-all(bf16[16,128,256]{2,1,0:T(8,128)(2,1)S(1)} %broadcast_in_dim.2), channel_id=1, replica_groups=mesh['row'=16,'col'=32] {'row'}, dimensions={0} | all-to-all | bytes 2097152 | tf_op jit(solution)/shard_map/all_to_all | solution.py:33
  36.0 0.0 copy-done.4
  36.0 0.0 copy-done.3
  36.0 3.0 %forward.3 = bf16[16,128,256]{2,1,0:T(8,128)(2,1)S(1)} custom-call(s32[4]{0:T(128)S(1)} %pad_add_fusion.where, s32[1,1,128]{2,1,0:T(1,128)S(1)} %copy-done.3, s32[1,1,128]{2,1,0:T(1,128)S(1)} %copy-done.4, bf16[1,1,128,128,128]{4,3,2,1,0:T(8,128)(2,1)} %v.5, bf16[16,128,256]{2,1,0:T(8,128)(2,1)S(1)} %all_to_all.25.xs), custom_call_target="tpu_custom_call" | custom-call | flops 536870912 | bytes 7340032 | tf_op jit(solution)/shard_map/forward/pallas_call | solution.py:118
  39.0 5.2 %collective-permute-start = (bf16[16,128,256]{2,1,0:T(8,128)(2,1)S(1)}, bf16[16,128,256]{2,1,0:T(8,128)(2,1)S(1)}, u32[]{:S(2)}, u32[]{:S(2)}) collective-permute-start(bf16[16,128,256]{2,1,0:T(8,128)(2,1)S(1)} %forward.3), channel_id=1, source_target_pairs={{0,1},{1,0},{2,3},{3,2},{4,5},{5,4},{6,7},{7,6},{8,9},{9,8},{10,11... | collective-permute-start | bytes 3145736 | tf_op jit(solution)/shard_map/ppermute | solution.py:29
  44.2 2.7 %forward.2 = bf16[16,128,256]{2,1,0:T(8,128)(2,1)S(1)} custom-call(s32[4]{0:T(128)S(1)} %pad_add_fusion.where, s32[1,1,128]{2,1,0:T(1,128)S(1)} %copy-done.3, s32[1,1,128]{2,1,0:T(1,128)S(1)} %copy-done.4, bf16[1,1,128,128,128]{4,3,2,1,0:T(8,128)(2,1)} %v.5, bf16[16,128,256]{2,1,0:T(8,128)(2,1)S(1)} %all_to_all.25.xs), custom_call_target="tpu_custom_call" | custom-call | flops 536870912 | bytes 7340032 | tf_op jit(solution)/shard_map/forward/pallas_call | solution.py:118
  46.9 0.0 copy-start
  46.9 0.0 collective-permute-done
  46.9 0.3 add_convert_fusion
  47.2 0.1 fusion
  47.3 3.2 %collective-permute-start.1 = (bf16[4,128,256]{2,1,0:T(8,128)(2,1)S(1)}, bf16[4,128,256]{2,1,0:T(8,128)(2,1)S(1)}, u32[]{:S(2)}, u32[]{:S(2)}) collective-permute-start(bf16[4,128,256]{2,1,0:T(8,128)(2,1)S(1)} %get-tuple-element.25), channel_id=1, source_target_pairs={{0,2},{1,3},{2,4},{3,5},{4,6},{5,7},{6,0},{7,1},{8,10},{9,11},{10,... | collective-permute-start | bytes 786440 | tf_op jit(solution)/shard_map/ppermute | solution.py:25
  50.5 3.6 %collective-permute-start.3 = (bf16[4,128,256]{2,1,0:T(8,128)(2,1)S(1)}, bf16[4,128,256]{2,1,0:T(8,128)(2,1)S(1)}, u32[]{:S(2)}, u32[]{:S(2)}) collective-permute-start(bf16[4,128,256]{2,1,0:T(8,128)(2,1)S(1)} %get-tuple-element.26), channel_id=1, source_target_pairs={{0,6},{1,7},{2,0},{3,1},{4,2},{5,3},{6,4},{7,5},{8,14},{9,15},{10,... | collective-permute-start | bytes 786440 | tf_op jit(solution)/shard_map/ppermute | solution.py:25
  54.1 0.0 copy-start.1
  54.1 0.0 copy-start.2
  54.1 2.4 %collective-permute-start.2 = (bf16[4,128,256]{2,1,0:T(8,128)(2,1)S(1)}, bf16[4,128,256]{2,1,0:T(8,128)(2,1)S(1)}, u32[]{:S(2)}, u32[]{:S(2)}) collective-permute-start(bf16[4,128,256]{2,1,0:T(8,128)(2,1)S(1)} %get-tuple-element.27), channel_id=1, source_target_pairs={{0,4},{1,5},{2,6},{3,7},{4,0},{5,1},{6,2},{7,3},{8,12},{9,13},{10,... | collective-permute-start | bytes 786440 | tf_op jit(solution)/shard_map/ppermute | solution.py:25
  56.5 0.0 copy-done
  56.5 1.3 turn.1.v
  57.8 0.0 collective-permute-done.1
  57.8 2.6 %collective-permute-done.3 = bf16[4,128,256]{2,1,0:T(8,128)(2,1)S(1)} collective-permute-done((bf16[4,128,256]{2,1,0:T(8,128)(2,1)S(1)}, bf16[4,128,256]{2,1,0:T(8,128)(2,1)S(1)}, u32[]{:S(2)}, u32[]{:S(2)}) %collective-permute-start.3) | collective-permute-done | bytes 262176 | tf_op jit(solution)/shard_map/ppermute | solution.py:25
  60.4 3.7 %collective-permute-done.2 = bf16[4,128,256]{2,1,0:T(8,128)(2,1)S(1)} collective-permute-done((bf16[4,128,256]{2,1,0:T(8,128)(2,1)S(1)}, bf16[4,128,256]{2,1,0:T(8,128)(2,1)S(1)}, u32[]{:S(2)}, u32[]{:S(2)}) %collective-permute-start.2) | collective-permute-done | bytes 262176 | tf_op jit(solution)/shard_map/ppermute | solution.py:25
  64.1 0.1 add_convert_fusion.1
  64.2 29.2 %all_to_all.26.got = bf16[4,128,256]{2,1,0:T(8,128)(2,1)S(1)} all-to-all(bf16[4,128,256]{2,1,0:T(8,128)(2,1)S(1)} %add_convert_fusion.1), channel_id=1, replica_groups={{0,8,16,24},{1,9,17,25},{2,10,18,26},{3,11,19,27},{4,12,20,28},{5,13,21..., dimensions={0} | all-to-all | bytes 524288 | tf_op jit(solution)/shard_map/all_to_all | solution.py:38
  93.5 0.0 copy-done.1
  93.5 0.0 copy-done.2
  93.5 0.8 middle.1
  94.3 16.6 %all_to_all.27.parts = bf16[16,16,256]{2,1,0:T(8,128)(2,1)S(1)} all-to-all(bf16[16,16,256]{2,1,0:T(8,128)(2,1)S(1)} %get-tuple-element.22), channel_id=1, replica_groups=mesh['row'=16,'col'=32] {'row'}, dimensions={0} | all-to-all | bytes 262144 | tf_op jit(solution)/shard_map/all_to_all | solution.py:33
  110.9 19.7 %all_to_all.28.got = bf16[4,144,256]{2,1,0:T(8,128)(2,1)S(1)} all-to-all(bf16[4,144,256]{2,1,0:T(8,128)(2,1)S(1)} %pack.1), channel_id=1, replica_groups={{0,8,16,24},{1,9,17,25},{2,10,18,26},{3,11,19,27},{4,12,20,28},{5,13,21..., dimensions={0} | all-to-all | bytes 589824 | tf_op jit(solution)/shard_map/all_to_all | solution.py:38
  130.6 5.9 %collective-permute-start.6 = (bf16[528,256]{1,0:T(8,128)(2,1)S(1)}, bf16[528,256]{1,0:T(8,128)(2,1)S(1)}, u32[]{:S(2)}, u32[]{:S(2)}) collective-permute-start(bf16[528,256]{1,0:T(8,128)(2,1)S(1)} %fold.1.l0), channel_id=1, source_target_pairs={{0,6},{1,7},{2,0},{3,1},{4,2},{5,3},{6,4},{7,5},{8,14},{9,15},{10,... | collective-permute-start | bytes 811016 | tf_op jit(solution)/shard_map/ppermute | solution.py:25
  136.5 2.6 %collective-permute-start.5 = (bf16[528,256]{1,0:T(8,128)(2,1)S(1)}, bf16[528,256]{1,0:T(8,128)(2,1)S(1)}, u32[]{:S(2)}, u32[]{:S(2)}) collective-permute-start(bf16[528,256]{1,0:T(8,128)(2,1)S(1)} %fold.1.l0), channel_id=1, source_target_pairs={{0,4},{1,5},{2,6},{3,7},{4,0},{5,1},{6,2},{7,3},{8,12},{9,13},{10,... | collective-permute-start | bytes 811016 | tf_op jit(solution)/shard_map/ppermute | solution.py:25
  139.1 1.9 collective-permute-start.4
  141.1 0.4 collective-permute-done.6.l3
  141.5 3.8 %collective-permute-done.5.l2 = bf16[528,256]{1,0:T(8,128)(2,1)S(1)} collective-permute-done((bf16[528,256]{1,0:T(8,128)(2,1)S(1)}, bf16[528,256]{1,0:T(8,128)(2,1)S(1)}, u32[]{:S(2)}, u32[]{:S(2)}) %collective-permute-start.5) | collective-permute-done | bytes 270368 | tf_op jit(solution)/shard_map/ppermute | solution.py:25
  145.3 3.5 %collective-permute-done.4.l1 = bf16[528,256]{1,0:T(8,128)(2,1)S(1)} collective-permute-done((bf16[528,256]{1,0:T(8,128)(2,1)S(1)}, bf16[528,256]{1,0:T(8,128)(2,1)S(1)}, u32[]{:S(2)}, u32[]{:S(2)}) %collective-permute-start.4) | collective-permute-done | bytes 270368 | tf_op jit(solution)/shard_map/ppermute | solution.py:25
  148.8 0.6 collect.1.grads.mine
  149.4 7.7 %collective-permute-start.7 = (bf16[2064,256]{1,0:T(8,128)(2,1)S(1)}, bf16[2064,256]{1,0:T(8,128)(2,1)S(1)}, u32[]{:S(2)}, u32[]{:S(2)}) collective-permute-start(bf16[2064,256]{1,0:T(8,128)(2,1)S(1)} %collect.1.grads.mine), channel_id=1, source_target_pairs={{0,1},{1,0},{2,3},{3,2},{4,5},{5,4},{6,7},{7,6},{8,9},{9,8},{10,11... | collective-permute-start | bytes 3170312 | tf_op jit(solution)/shard_map/ppermute | solution.py:29
  157.1 1.6 first.1.start
  158.7 0.7 collective-permute-done.7.grads
  159.4 1.9 second.1
  161.3 37.7 %all_to_all.29.got = bf16[16,144,256]{2,1,0:T(8,128)(2,1)S(1)} all-to-all(bf16[16,144,256]{2,1,0:T(8,128)(2,1)S(1)} %second.1), channel_id=1, replica_groups=mesh['row'=16,'col'=32] {'row'}, dimensions={0} | all-to-all | bytes 2359296 | tf_op jit(solution)/shard_map/all_to_all | solution.py:33
  199.0 0.9 last.1
  (2 shorter events, 0.1 us)
Async XLA Ops:
  0.6 35.4 %copy-start.4 = (s32[1,1,128]{2,1,0:T(1,128)S(1)}, s32[1,1,128]{2,1,0:T(1,128)}, u32[]{:S(2)}) copy-start(s32[1,1,128]{2,1,0:T(1,128)} %cols.7) | copy-start | bytes 1540
  0.6 35.4 %copy-start.3 = (s32[1,1,128]{2,1,0:T(1,128)S(1)}, s32[1,1,128]{2,1,0:T(1,128)}, u32[]{:S(2)}) copy-start(s32[1,1,128]{2,1,0:T(1,128)} %rows.7) | copy-start | bytes 1540
  39.0 7.9 %collective-permute-start = (bf16[16,128,256]{2,1,0:T(8,128)(2,1)S(1)}, bf16[16,128,256]{2,1,0:T(8,128)(2,1)S(1)}, u32[]{:S(2)}, u32[]{:S(2)}) collective-permute-start(bf16[16,128,256]{2,1,0:T(8,128)(2,1)S(1)} %forward.3), channel_id=1, source_target_pairs={{0,1},{1,0},{2,3},{3,2},{4,5},{5,4},{6,7},{7,6},{8,9},{9,8},{10,11... | collective-permute-start | bytes 3145736 | tf_op jit(solution)/shard_map/ppermute | solution.py:29
  46.9 9.6 %copy-start = (bf16[1,1,128,128,128]{4,3,2,1,0:T(8,128)(2,1)S(1)}, bf16[1,1,128,128,128]{4,3,2,1,0:T(8,128)(2,1)}, u32[]{:S(2)}) copy-start(bf16[1,1,128,128,128]{4,3,2,1,0:T(8,128)(2,1)} %v.5) | copy-start | bytes 12582916
  47.3 10.5 %collective-permute-start.1 = (bf16[4,128,256]{2,1,0:T(8,128)(2,1)S(1)}, bf16[4,128,256]{2,1,0:T(8,128)(2,1)S(1)}, u32[]{:S(2)}, u32[]{:S(2)}) collective-permute-start(bf16[4,128,256]{2,1,0:T(8,128)(2,1)S(1)} %get-tuple-element.25), channel_id=1, source_target_pairs={{0,2},{1,3},{2,4},{3,5},{4,6},{5,7},{6,0},{7,1},{8,10},{9,11},{10,... | collective-permute-start | bytes 786440 | tf_op jit(solution)/shard_map/ppermute | solution.py:25
  50.5 10.0 %collective-permute-start.3 = (bf16[4,128,256]{2,1,0:T(8,128)(2,1)S(1)}, bf16[4,128,256]{2,1,0:T(8,128)(2,1)S(1)}, u32[]{:S(2)}, u32[]{:S(2)}) collective-permute-start(bf16[4,128,256]{2,1,0:T(8,128)(2,1)S(1)} %get-tuple-element.26), channel_id=1, source_target_pairs={{0,6},{1,7},{2,0},{3,1},{4,2},{5,3},{6,4},{7,5},{8,14},{9,15},{10,... | collective-permute-start | bytes 786440 | tf_op jit(solution)/shard_map/ppermute | solution.py:25
  54.1 39.4 %copy-start.1 = (bf16[256,256]{1,0:T(8,128)(2,1)S(1)}, bf16[256,256]{1,0:T(8,128)(2,1)}, u32[]{:S(2)}) copy-start(bf16[256,256]{1,0:T(8,128)(2,1)} %w.3) | copy-start | bytes 393220
  54.1 39.4 %copy-start.2 = (bf16[128,256]{1,0:T(8,128)(2,1)S(1)}, bf16[128,256]{1,0:T(8,128)(2,1)}, u32[]{:S(2)}) copy-start(bf16[128,256]{1,0:T(8,128)(2,1)} %cot.1) | copy-start | bytes 196612
  54.1 10.0 %collective-permute-start.2 = (bf16[4,128,256]{2,1,0:T(8,128)(2,1)S(1)}, bf16[4,128,256]{2,1,0:T(8,128)(2,1)S(1)}, u32[]{:S(2)}, u32[]{:S(2)}) collective-permute-start(bf16[4,128,256]{2,1,0:T(8,128)(2,1)S(1)} %get-tuple-element.27), channel_id=1, source_target_pairs={{0,4},{1,5},{2,6},{3,7},{4,0},{5,1},{6,2},{7,3},{8,12},{9,13},{10,... | collective-permute-start | bytes 786440 | tf_op jit(solution)/shard_map/ppermute | solution.py:25
  130.6 10.9 %collective-permute-start.6 = (bf16[528,256]{1,0:T(8,128)(2,1)S(1)}, bf16[528,256]{1,0:T(8,128)(2,1)S(1)}, u32[]{:S(2)}, u32[]{:S(2)}) collective-permute-start(bf16[528,256]{1,0:T(8,128)(2,1)S(1)} %fold.1.l0), channel_id=1, source_target_pairs={{0,6},{1,7},{2,0},{3,1},{4,2},{5,3},{6,4},{7,5},{8,14},{9,15},{10,... | collective-permute-start | bytes 811016 | tf_op jit(solution)/shard_map/ppermute | solution.py:25
  136.5 8.8 %collective-permute-start.5 = (bf16[528,256]{1,0:T(8,128)(2,1)S(1)}, bf16[528,256]{1,0:T(8,128)(2,1)S(1)}, u32[]{:S(2)}, u32[]{:S(2)}) collective-permute-start(bf16[528,256]{1,0:T(8,128)(2,1)S(1)} %fold.1.l0), channel_id=1, source_target_pairs={{0,4},{1,5},{2,6},{3,7},{4,0},{5,1},{6,2},{7,3},{8,12},{9,13},{10,... | collective-permute-start | bytes 811016 | tf_op jit(solution)/shard_map/ppermute | solution.py:25
  139.1 9.6 %collective-permute-start.4 = (bf16[528,256]{1,0:T(8,128)(2,1)S(1)}, bf16[528,256]{1,0:T(8,128)(2,1)S(1)}, u32[]{:S(2)}, u32[]{:S(2)}) collective-permute-start(bf16[528,256]{1,0:T(8,128)(2,1)S(1)} %fold.1.l0), channel_id=1, source_target_pairs={{0,2},{1,3},{2,4},{3,5},{4,6},{5,7},{6,0},{7,1},{8,10},{9,11},{10,... | collective-permute-start | bytes 811016 | tf_op jit(solution)/shard_map/ppermute | solution.py:25
  149.4 10.0 %collective-permute-start.7 = (bf16[2064,256]{1,0:T(8,128)(2,1)S(1)}, bf16[2064,256]{1,0:T(8,128)(2,1)S(1)}, u32[]{:S(2)}, u32[]{:S(2)}) collective-permute-start(bf16[2064,256]{1,0:T(8,128)(2,1)S(1)} %collect.1.grads.mine), channel_id=1, source_target_pairs={{0,1},{1,0},{2,3},{3,2},{4,5},{5,4},{6,7},{7,6},{8,9},{9,8},{10,11... | collective-permute-start | bytes 3170312 | tf_op jit(solution)/shard_map/ppermute | solution.py:29

commit v6 on v5

--- a/solution.py
+++ b/solution.py
@@ -25,12 +25,22 @@
     return lax.ppermute(v, "col", pairs)
 
 
+def send_x(v, k):
+    pairs = [(r, (r // 4) * 4 + (r + k) % 4) for r in range(ROWS)]
+    return lax.ppermute(v, "row", pairs)
+
+
 def send_core(v):
     return lax.ppermute(v, "col", [(c, c ^ 1) for c in range(COLS)])
 
 
 def trade_row(v):
     return lax.all_to_all(v, "row", 0, 0)
+
+
+def trade_zl(v):
+    groups = [[zl * 4 + x for zl in range(4)] for x in range(4)]
+    return lax.all_to_all(v, "row", 0, 0, axis_index_groups=groups)
 
 
 def trade_zh(v):
@@ -81,6 +91,24 @@
         return 0
 
     lax.fori_loop(0, (found + GROUP - 1) // GROUP, step, 0)
+
+
+def pair_kernel(a, b, o0, o2, o1, o3):
+    for k, out in enumerate((o0, o1, o2, o3)):
+        block = slice(4 * k, 4 * (k + 1))
+        out[...] = (a[block].astype(F32) + b[block].astype(F32)).astype(BF16)
+
+
+def pair(a, b):
+    block = jax.ShapeDtypeStruct((4,) + a.shape[1:], BF16)
+    none, two, one, three = pl.pallas_call(
+        pair_kernel,
+        out_shape=(block,) * 4,
+        compiler_params=params(),
+        cost_estimate=cost(0, 4),
+        name="pair",
+    )(a, b)
+    return none, one, two, three
 
 
 def fetch_tiles(live, v, tiles, sems):
@@ -245,7 +273,7 @@
 
 
 def backward_half(other, where, rows, cols, v, grads, slots, acc):
-    y, core = where[1], where[2]
+    y, core, x = where[1], where[2], where[4]
     found = choose_slots(core ^ other, where, rows, slots)
 
     def source(s):
@@ -253,7 +281,11 @@
         at = ((y - ((r >> 1) & 3)) & 3) * 4 + (r >> 3)
         return grads[pl.ds(pl.multiple_of(at * TILE, TILE), TILE)]
 
-    add_products(found, slots, lambda s: v[s], source, lambda s: cols[0, 0, s], acc)
+    def target(s):
+        c = cols[0, 0, s]
+        return (((c & 3) - x) & 3) * 4 + (c >> 2)
+
+    add_products(found, slots, lambda s: v[s], source, target, acc)
 
 
 def first_kernel(where, rows, cols, v, grads, out, slots, acc):
@@ -262,15 +294,16 @@
     out[...] = acc[:HALF]
 
 
-def second_kernel(where, rows, cols, v, grads, mine, start, out, slots, acc):
+def second_kernel(where, rows, cols, v, grads, mine, start, o0, o2, o1, o3, slots, acc):
     acc[:HALF] = start[...]
     acc[HALF] = jnp.zeros_like(acc[HALF])
     backward_half(1, where, rows, cols, v, grads, slots, acc)
     rest = HALF * TILE
     part = (mine[rest:].astype(F32) + grads[rest:].astype(F32)).astype(BF16)
-    for d in range(HALF):
-        out[d, :TILE] = acc[d].astype(BF16)
-        out[d, TILE:] = part
+    for k, out in enumerate((o0, o1, o2, o3)):
+        for i in range(4):
+            out[TILE * i : TILE * (i + 1)] = acc[4 * k + i].astype(BF16)
+        out[4 * TILE :] = part
 
 
 def backward(where, rows, cols, v, mine, theirs):
@@ -290,27 +323,56 @@
         cost_estimate=work,
         name="first",
     )(where, rows, cols, v, mine)
-    return pl.pallas_call(
+    none, two, one, three = pl.pallas_call(
         second_kernel,
-        out_shape=jax.ShapeDtypeStruct((HALF, TILE + extra, width), BF16),
+        out_shape=(jax.ShapeDtypeStruct((4 * TILE + extra, width), BF16),) * 4,
         in_specs=[smem()] * 3 + [vmem()] * 4,
-        out_specs=vmem(),
+        out_specs=(vmem(),) * 4,
         scratch_shapes=scratch,
         compiler_params=params(),
         cost_estimate=work,
         name="second",
     )(where, rows, cols, v, theirs, mine, first)
+    return none, one, two, three
+
+
+def merge_kernel(where, p0, p2, p1, p3, out):
+    x = where[4]
+    parts = (p0, p1, p2, p3)
+    extra = p0.shape[0] - 4 * TILE
+    for i in range(4):
+        block = slice(TILE * i, TILE * (i + 1))
+        total = p0[block].astype(F32)
+        for part in parts[1:]:
+            total = total + part[block].astype(F32)
+        out[i, :TILE] = total.astype(BF16)
+        for k, part in enumerate(parts):
+            at = pl.multiple_of(TILE + ((x - k) & 3) * extra, extra)
+            out[i, pl.ds(at, extra)] = part[4 * TILE :]
+
+
+def merge(where, parts):
+    rows, width = parts[0].shape
+    return pl.pallas_call(
+        merge_kernel,
+        out_shape=jax.ShapeDtypeStruct((4, TILE + 4 * (rows - 4 * TILE), width), BF16),
+        in_specs=[smem()] + [vmem()] * 4,
+        out_specs=vmem(),
+        compiler_params=params(),
+        cost_estimate=cost(0, 2),
+        name="merge",
+    )(where, parts[0], parts[2], parts[1], parts[3])
 
 
 def last_kernel(scale, got, w, grad_out, weight_out):
     total = got[0, :TILE].astype(F32)
-    for i in range(1, ROWS):
+    for i in range(1, 4):
         total = total + got[i, :TILE].astype(F32)
     grad_out[...] = lax.dot_general(
         total.astype(BF16), w[...], (((1,), (1,)), ((), ())), preferred_element_type=F32
     ).astype(BF16)
     extra = got.shape[1] - TILE
-    for i in range(ROWS):
+    for i in range(4):
         weight_out[extra * i : extra * (i + 1)] = got[i, TILE:].astype(F32) * scale
 
 
@@ -331,8 +393,8 @@
 def shards(features, weight, tile_values, tile_rows, tile_cols, tile_count, cotangent):
     node_dev = features.shape[0]
     grad_scale = 1.0 / math.sqrt(node_dev * lax.axis_size("row") * lax.axis_size("col"))
-    c = lax.axis_index("col")
-    where = jnp.stack([c >> 3, (c >> 1) & 3, c & 1, tile_count[0, 0]]).astype(jnp.int32)
+    r, c = lax.axis_index("row"), lax.axis_index("col")
+    where = jnp.stack([c >> 3, (c >> 1) & 3, c & 1, tile_count[0, 0], r & 3]).astype(jnp.int32)
 
     features, where = lax.optimization_barrier((features, where))
     xs = trade_row(jnp.broadcast_to(features[None], (ROWS,) + features.shape))
@@ -340,9 +402,10 @@
     block = (where, tile_rows, tile_cols)
     got = send_core(forward(1, *block, tile_values, xs))
     keep = forward(0, *block, tile_values, xs)
-    paired = (keep.astype(F32) + got.astype(F32)).astype(BF16).reshape(4, 4, TILE, -1)
-    others = [send_y(paired[k], k).astype(F32) for k in (1, 2, 3)]
-    rows = (paired[0].astype(F32) + others[0] + others[1] + others[2]).astype(BF16)
+    paired = pair(keep, got)
+    got = [paired[0]] + [send_y(paired[k], k) for k in (2, 1, 3)]
+    got = [v.astype(F32) for v in got]
+    rows = (got[0] + got[1] + got[2] + got[3]).astype(BF16)
     turned = turn_tiles(where, tile_values)
     rows, turned = lax.optimization_barrier((rows, turned))
     activated, grad_pre, part = middle(trade_zh(rows), weight, cotangent)
@@ -350,7 +413,8 @@
     line = fold(trade_zh(pack(grad_pre, trade_row(part))))
     mine = collect(where, [line] + [send_y(line, k) for k in (1, 2, 3)])
     spread = backward(*block, turned, mine, send_core(mine))
-    grad_features, grad_weight = last(trade_row(spread), weight, grad_scale)
+    spread = [spread[0]] + [send_x(spread[k], k) for k in (1, 2, 3)]
+    grad_features, grad_weight = last(trade_zl(merge(where, spread)), weight, grad_scale)
     return (activated, grad_features, grad_weight)
 
 

time: 201 us -> 196 us (0.975)
  blocking collectives: 137 us -> 111 us
  starting transfers between devices: 32.4 us -> 43.2 us
  Pallas kernels: 12.9 us -> 17.6 us
  waiting for transfers between devices: 14.7 us -> 18.4 us
    all_to_all x3 -> x2, blocking collectives: 88 us -> 51.4 us  [trade_row(): return lax.all_to_all(v, 'row', 0, 0)]
    all_to_all x0 -> x1, blocking collectives: none -> 13.7 us  [trade_zl(): return lax.all_to_all(v, 'row', 0, 0, axis_index_groups=groups)]
    ppermute x0 -> x3, starting transfers between devices: none -> 11.2 us  [send_x(): return lax.ppermute(v, 'row', pairs)]
    ppermute x0 -> x3, waiting for transfers between devices: none -> 6.33 us  [send_x(): return lax.ppermute(v, 'row', pairs)]
    all_to_all x2, blocking collectives: 48.9 us -> 46.2 us  [trade_zh(): return lax.all_to_all(v, 'col', 0, 0, axis_index_groups=groups)]
  transfers between devices with their start and end apart: 8 -> 11, of which waited for: 6 -> 7; matrix products, arithmetic and copies ran while one was open for 0% -> 0% of each run, Pallas kernels for 3% -> 4%
where the time goes in v6:
time: 196 us; the launch traced here: 193 us
  blocking collectives  111 us (57%)
  starting transfers between devices  43.2 us (22%)
  waiting for transfers between devices  18.4 us (9%)
  Pallas kernels  17.6 us (9%)
    all_to_all x2, blocking collectives, trade_row(): return lax.all_to_all(v, 'row', 0, 0)  51.4 us
    all_to_all x2, blocking collectives, trade_zh(): return lax.all_to_all(v, 'col', 0, 0, axis_index_groups=groups)  46.2 us
    ppermute x6, starting transfers between devices, send_y(): return lax.ppermute(v, 'col', pairs)  21 us
    all_to_all x1, blocking collectives, trade_zl(): return lax.all_to_all(v, 'row', 0, 0, axis_index_groups=groups)  13.7 us
    ppermute x6, waiting for transfers between devices, send_y(): return lax.ppermute(v, 'col', pairs)  12.1 us
    ppermute x3, starting transfers between devices, send_x(): return lax.ppermute(v, 'row', pairs)  11.2 us
    ppermute x2, starting transfers between devices, send_core(): return lax.ppermute(v, 'col', [(c, c ^ 1) for c in range(COLS)])  11 us
    pallas_call x2, Pallas kernels, forward(): pl.pallas_call(functools.partial(forward_kernel, other), out_shape=jax.Sh...  7.5 us
  transfers between devices with their start and end apart: 11, of which 7 were waited for; matrix products, arithmetic and copies ran while one was open for 0% of the time, Pallas kernels for 4%

profile of v6, /device:TPU:1, one launch (start us, length us, event | category | flops | bytes accessed | tf_op | source)
XLA Modules:
  0.0 193.2 jit_solution(12395370590948369676)
XLA Ops:
  0.6 0.0 copy-start.4
  0.6 0.0 copy-start.3
  1.3 0.1 stack.19.where
  1.4 0.9 broadcast_in_dim.2
  2.3 33.7 %all_to_all.25.xs = bf16[16,128,256]{2,1,0:T(8,128)(2,1)S(1)} all-to-all(bf16[16,128,256]{2,1,0:T(8,128)(2,1)S(1)} %broadcast_in_dim.2), channel_id=1, replica_groups=mesh['row'=16,'col'=32] {'row'}, dimensions={0} | all-to-all | bytes 2097152 | tf_op jit(solution)/shard_map/all_to_all | solution.py:38
  36.0 0.0 copy-done.4
  36.0 0.0 copy-done.3
  36.0 3.8 %forward.3 = bf16[16,128,256]{2,1,0:T(8,128)(2,1)S(1)} custom-call(s32[5]{0:T(128)S(1)} %stack.19.where, s32[1,1,128]{2,1,0:T(1,128)S(1)} %copy-done.3, s32[1,1,128]{2,1,0:T(1,128)S(1)} %copy-done.4, bf16[1,1,128,128,128]{4,3,2,1,0:T(8,128)(2,1)} %v.5, bf16[16,128,256]{2,1,0:T(8,128)(2,1)S(1)} %all_to_all.25.xs), custom_call_target="tpu_custom_call" | custom-call | flops 536870912 | bytes 7340032 | tf_op jit(solution)/shard_map/forward/pallas_call | solution.py:146
  39.8 3.5 %collective-permute-start = (bf16[16,128,256]{2,1,0:T(8,128)(2,1)S(1)}, bf16[16,128,256]{2,1,0:T(8,128)(2,1)S(1)}, u32[]{:S(2)}, u32[]{:S(2)}) collective-permute-start(bf16[16,128,256]{2,1,0:T(8,128)(2,1)S(1)} %forward.3), channel_id=1, source_target_pairs={{0,1},{1,0},{2,3},{3,2},{4,5},{5,4},{6,7},{7,6},{8,9},{9,8},{10,11... | collective-permute-start | bytes 3145736 | tf_op jit(solution)/shard_map/ppermute | solution.py:34
  43.3 0.0 copy-start
  43.3 3.7 %forward.2.a = bf16[16,128,256]{2,1,0:T(8,128)(2,1)S(1)} custom-call(s32[5]{0:T(128)S(1)} %stack.19.where, s32[1,1,128]{2,1,0:T(1,128)S(1)} %copy-done.3, s32[1,1,128]{2,1,0:T(1,128)S(1)} %copy-done.4, bf16[1,1,128,128,128]{4,3,2,1,0:T(8,128)(2,1)} %v.5, bf16[16,128,256]{2,1,0:T(8,128)(2,1)S(1)} %all_to_all.25.xs), custom_call_target="tpu_custom_call" | custom-call | flops 536870912 | bytes 7340032 | tf_op jit(solution)/shard_map/forward/pallas_call | solution.py:146
  47.0 0.0 collective-permute-done.b
  47.0 0.2 pair.1
  47.3 4.8 %collective-permute-start.1 = (bf16[4,128,256]{2,1,0:T(8,128)(2,1)S(1)}, bf16[4,128,256]{2,1,0:T(8,128)(2,1)S(1)}, u32[]{:S(2)}, u32[]{:S(2)}) collective-permute-start(bf16[4,128,256]{2,1,0:T(8,128)(2,1)S(1)} %get-tuple-element.27), channel_id=1, source_target_pairs={{0,4},{1,5},{2,6},{3,7},{4,0},{5,1},{6,2},{7,3},{8,12},{9,13},{10,... | collective-permute-start | bytes 786440 | tf_op jit(solution)/shard_map/ppermute | solution.py:25
  52.1 1.9 collective-permute-start.2
  54.0 0.0 copy-start.1
  54.0 0.0 copy-start.2
  54.1 4.7 %collective-permute-start.3 = (bf16[4,128,256]{2,1,0:T(8,128)(2,1)S(1)}, bf16[4,128,256]{2,1,0:T(8,128)(2,1)S(1)}, u32[]{:S(2)}, u32[]{:S(2)}) collective-permute-start(bf16[4,128,256]{2,1,0:T(8,128)(2,1)S(1)} %get-tuple-element.29), channel_id=1, source_target_pairs={{0,6},{1,7},{2,0},{3,1},{4,2},{5,3},{6,4},{7,5},{8,14},{9,15},{10,... | collective-permute-start | bytes 786440 | tf_op jit(solution)/shard_map/ppermute | solution.py:25
  58.8 0.0 copy-done
  58.8 2.0 %turn.1.v = bf16[128,128,128]{2,1,0:T(8,128)(2,1)S(1)} custom-call(s32[5]{0:T(128)S(1)} %stack.19.where, bf16[1,1,128,128,128]{4,3,2,1,0:T(8,128)(2,1)S(1)} %copy-done), custom_call_target="tpu_custom_call" | custom-call | bytes 10485760 | tf_op jit(solution)/shard_map/turn/pallas_call | solution.py:173
  60.7 0.0 collective-permute-done.1
  60.8 3.4 %collective-permute-done.2 = bf16[4,128,256]{2,1,0:T(8,128)(2,1)S(1)} collective-permute-done((bf16[4,128,256]{2,1,0:T(8,128)(2,1)S(1)}, bf16[4,128,256]{2,1,0:T(8,128)(2,1)S(1)}, u32[]{:S(2)}, u32[]{:S(2)}) %collective-permute-start.2) | collective-permute-done | bytes 262176 | tf_op jit(solution)/shard_map/ppermute | solution.py:25
  64.1 0.6 collective-permute-done.3
  64.8 0.1 add_convert_fusion
  64.9 26.0 %all_to_all.26.got = bf16[4,128,256]{2,1,0:T(8,128)(2,1)S(1)} all-to-all(bf16[4,128,256]{2,1,0:T(8,128)(2,1)S(1)} %add_convert_fusion), channel_id=1, replica_groups={{0,8,16,24},{1,9,17,25},{2,10,18,26},{3,11,19,27},{4,12,20,28},{5,13,21..., dimensions={0} | all-to-all | bytes 524288 | tf_op jit(solution)/shard_map/all_to_all | solution.py:48
  90.9 0.8 middle.1
  91.7 17.7 %all_to_all.27.parts = bf16[16,16,256]{2,1,0:T(8,128)(2,1)S(1)} all-to-all(bf16[16,16,256]{2,1,0:T(8,128)(2,1)S(1)} %get-tuple-element.34), channel_id=1, replica_groups=mesh['row'=16,'col'=32] {'row'}, dimensions={0} | all-to-all | bytes 262144 | tf_op jit(solution)/shard_map/all_to_all | solution.py:38
  109.5 20.2 %all_to_all.28.got = bf16[4,144,256]{2,1,0:T(8,128)(2,1)S(1)} all-to-all(bf16[4,144,256]{2,1,0:T(8,128)(2,1)S(1)} %pack.1), channel_id=1, replica_groups={{0,8,16,24},{1,9,17,25},{2,10,18,26},{3,11,19,27},{4,12,20,28},{5,13,21..., dimensions={0} | all-to-all | bytes 589824 | tf_op jit(solution)/shard_map/all_to_all | solution.py:48
  129.8 5.2 %collective-permute-start.6 = (bf16[528,256]{1,0:T(8,128)(2,1)S(1)}, bf16[528,256]{1,0:T(8,128)(2,1)S(1)}, u32[]{:S(2)}, u32[]{:S(2)}) collective-permute-start(bf16[528,256]{1,0:T(8,128)(2,1)S(1)} %fold.1.l0), channel_id=1, source_target_pairs={{0,6},{1,7},{2,0},{3,1},{4,2},{5,3},{6,4},{7,5},{8,14},{9,15},{10,... | collective-permute-start | bytes 811016 | tf_op jit(solution)/shard_map/ppermute | solution.py:25
  135.0 1.9 collective-permute-start.5
  136.9 2.5 %collective-permute-start.4 = (bf16[528,256]{1,0:T(8,128)(2,1)S(1)}, bf16[528,256]{1,0:T(8,128)(2,1)S(1)}, u32[]{:S(2)}, u32[]{:S(2)}) collective-permute-start(bf16[528,256]{1,0:T(8,128)(2,1)S(1)} %fold.1.l0), channel_id=1, source_target_pairs={{0,2},{1,3},{2,4},{3,5},{4,6},{5,7},{6,0},{7,1},{8,10},{9,11},{10,... | collective-permute-start | bytes 811016 | tf_op jit(solution)/shard_map/ppermute | solution.py:25
  139.4 0.0 collective-permute-done.6.l3
  139.4 4.4 %collective-permute-done.5.l2 = bf16[528,256]{1,0:T(8,128)(2,1)S(1)} collective-permute-done((bf16[528,256]{1,0:T(8,128)(2,1)S(1)}, bf16[528,256]{1,0:T(8,128)(2,1)S(1)}, u32[]{:S(2)}, u32[]{:S(2)}) %collective-permute-start.5) | collective-permute-done | bytes 270368 | tf_op jit(solution)/shard_map/ppermute | solution.py:25
  143.8 3.7 %collective-permute-done.4.l1 = bf16[528,256]{1,0:T(8,128)(2,1)S(1)} collective-permute-done((bf16[528,256]{1,0:T(8,128)(2,1)S(1)}, bf16[528,256]{1,0:T(8,128)(2,1)S(1)}, u32[]{:S(2)}, u32[]{:S(2)}) %collective-permute-start.4) | collective-permute-done | bytes 270368 | tf_op jit(solution)/shard_map/ppermute | solution.py:25
  147.5 0.6 collect.1.grads.mine
  148.1 7.5 %collective-permute-start.7 = (bf16[2064,256]{1,0:T(8,128)(2,1)S(1)}, bf16[2064,256]{1,0:T(8,128)(2,1)S(1)}, u32[]{:S(2)}, u32[]{:S(2)}) collective-permute-start(bf16[2064,256]{1,0:T(8,128)(2,1)S(1)} %collect.1.grads.mine), channel_id=1, source_target_pairs={{0,1},{1,0},{2,3},{3,2},{4,5},{5,4},{6,7},{7,6},{8,9},{9,8},{10,11... | collective-permute-start | bytes 3170312 | tf_op jit(solution)/shard_map/ppermute | solution.py:34
  155.6 2.3 %first.1.start = f32[16,128,256]{2,1,0:T(8,128)S(1)} custom-call(s32[5]{0:T(128)S(1)} %stack.19.where, s32[1,1,128]{2,1,0:T(1,128)S(1)} %copy-done.3, s32[1,1,128]{2,1,0:T(1,128)S(1)} %copy-done.4, bf16[128,128,128]{2,1,0:T(8,128)(2,1)S(1)} %turn.1.v, bf16[2064,256]{1,0:T(8,128)(2,1)S(1)} %collect.1.grads.mine), custom_call_target="tpu_custom_call" | custom-call | flops 536870912 | bytes 8388608 | tf_op jit(solution)/shard_map/first/pallas_call | solution.py:316
  157.9 0.0 collective-permute-done.7.grads
  157.9 2.6 %second.1 = (bf16[528,256]{1,0:T(8,128)(2,1)S(1)}, bf16[528,256]{1,0:T(8,128)(2,1)S(1)}, bf16[528,256]{1,0:T(8,128)(2,1)S(1)}, bf16[528,256]{1,0:T(8,128)(2,1)S(1)}) custom-call(s32[5]{0:T(128)S(1)} %stack.19.where, s32[1,1,128]{2,1,0:T(1,128)S(1)} %copy-done.3, s32[1,1,128]{2,1,0:T(1,128)S(1)} %copy-done.4, bf16[128,128,128]{2,1,0:T(8,128)(2,1)S(1)} %turn.1.v, ...), custom_call_target="tpu_custom_call" | custom-call | flops 536870912 | bytes 8388608 | tf_op jit(solution)/shard_map/second/pallas_call | solution.py:326
  160.5 1.9 collective-permute-start.8
  162.4 4.9 %collective-permute-start.9 = (bf16[528,256]{1,0:T(8,128)(2,1)S(1)}, bf16[528,256]{1,0:T(8,128)(2,1)S(1)}, u32[]{:S(2)}, u32[]{:S(2)}) collective-permute-start(bf16[528,256]{1,0:T(8,128)(2,1)S(1)} %get-tuple-element.37), channel_id=1, source_target_pairs={{0,32},{32,64},{64,96},{96,0},{128,160},{160,192},{192,224},{224,1... | collective-permute-start | bytes 811016 | tf_op jit(solution)/shard_map/ppermute | solution.py:30
  167.3 4.3 %collective-permute-start.10 = (bf16[528,256]{1,0:T(8,128)(2,1)S(1)}, bf16[528,256]{1,0:T(8,128)(2,1)S(1)}, u32[]{:S(2)}, u32[]{:S(2)}) collective-permute-start(bf16[528,256]{1,0:T(8,128)(2,1)S(1)} %get-tuple-element.38), channel_id=1, source_target_pairs={{0,96},{32,0},{64,32},{96,64},{128,224},{160,128},{192,160},{224,1... | collective-permute-start | bytes 811016 | tf_op jit(solution)/shard_map/ppermute | solution.py:30
  171.7 0.3 collective-permute-done.8.p2
  171.9 6.0 %collective-permute-done.9.p1 = bf16[528,256]{1,0:T(8,128)(2,1)S(1)} collective-permute-done((bf16[528,256]{1,0:T(8,128)(2,1)S(1)}, bf16[528,256]{1,0:T(8,128)(2,1)S(1)}, u32[]{:S(2)}, u32[]{:S(2)}) %collective-permute-start.9) | collective-permute-done | bytes 270368 | tf_op jit(solution)/shard_map/ppermute | solution.py:30
  177.9 0.1 collective-permute-done.10.p3
  178.0 0.7 merge.1
  178.7 13.7 %all_to_all.29.got = bf16[4,192,256]{2,1,0:T(8,128)(2,1)S(1)} all-to-all(bf16[4,192,256]{2,1,0:T(8,128)(2,1)S(1)} %merge.1), channel_id=1, replica_groups={{0,128,256,384},{32,160,288,416},{64,192,320,448},{96,224,352,480},{1,1..., dimensions={0} | all-to-all | bytes 786432 | tf_op jit(solution)/shard_map/all_to_all | solution.py:43
  192.4 0.8 last.1
  (4 shorter events, 0.1 us)
Async XLA Ops:
  0.6 35.4 %copy-start.4 = (s32[1,1,128]{2,1,0:T(1,128)S(1)}, s32[1,1,128]{2,1,0:T(1,128)}, u32[]{:S(2)}) copy-start(s32[1,1,128]{2,1,0:T(1,128)} %cols.7) | copy-start | bytes 1540
  0.6 35.4 %copy-start.3 = (s32[1,1,128]{2,1,0:T(1,128)S(1)}, s32[1,1,128]{2,1,0:T(1,128)}, u32[]{:S(2)}) copy-start(s32[1,1,128]{2,1,0:T(1,128)} %rows.7) | copy-start | bytes 1540
  39.8 7.3 %collective-permute-start = (bf16[16,128,256]{2,1,0:T(8,128)(2,1)S(1)}, bf16[16,128,256]{2,1,0:T(8,128)(2,1)S(1)}, u32[]{:S(2)}, u32[]{:S(2)}) collective-permute-start(bf16[16,128,256]{2,1,0:T(8,128)(2,1)S(1)} %forward.3), channel_id=1, source_target_pairs={{0,1},{1,0},{2,3},{3,2},{4,5},{5,4},{6,7},{7,6},{8,9},{9,8},{10,11... | collective-permute-start | bytes 3145736 | tf_op jit(solution)/shard_map/ppermute | solution.py:34
  43.3 15.5 %copy-start = (bf16[1,1,128,128,128]{4,3,2,1,0:T(8,128)(2,1)S(1)}, bf16[1,1,128,128,128]{4,3,2,1,0:T(8,128)(2,1)}, u32[]{:S(2)}) copy-start(bf16[1,1,128,128,128]{4,3,2,1,0:T(8,128)(2,1)} %v.5) | copy-start | bytes 12582916
  47.3 13.5 %collective-permute-start.1 = (bf16[4,128,256]{2,1,0:T(8,128)(2,1)S(1)}, bf16[4,128,256]{2,1,0:T(8,128)(2,1)S(1)}, u32[]{:S(2)}, u32[]{:S(2)}) collective-permute-start(bf16[4,128,256]{2,1,0:T(8,128)(2,1)S(1)} %get-tuple-element.27), channel_id=1, source_target_pairs={{0,4},{1,5},{2,6},{3,7},{4,0},{5,1},{6,2},{7,3},{8,12},{9,13},{10,... | collective-permute-start | bytes 786440 | tf_op jit(solution)/shard_map/ppermute | solution.py:25
  52.1 12.0 %collective-permute-start.2 = (bf16[4,128,256]{2,1,0:T(8,128)(2,1)S(1)}, bf16[4,128,256]{2,1,0:T(8,128)(2,1)S(1)}, u32[]{:S(2)}, u32[]{:S(2)}) collective-permute-start(bf16[4,128,256]{2,1,0:T(8,128)(2,1)S(1)} %get-tuple-element.28), channel_id=1, source_target_pairs={{0,2},{1,3},{2,4},{3,5},{4,6},{5,7},{6,0},{7,1},{8,10},{9,11},{10,... | collective-permute-start | bytes 786440 | tf_op jit(solution)/shard_map/ppermute | solution.py:25
  54.0 36.9 %copy-start.1 = (bf16[256,256]{1,0:T(8,128)(2,1)S(1)}, bf16[256,256]{1,0:T(8,128)(2,1)}, u32[]{:S(2)}) copy-start(bf16[256,256]{1,0:T(8,128)(2,1)} %w.3) | copy-start | bytes 393220
  54.0 36.8 %copy-start.2 = (bf16[128,256]{1,0:T(8,128)(2,1)S(1)}, bf16[128,256]{1,0:T(8,128)(2,1)}, u32[]{:S(2)}) copy-start(bf16[128,256]{1,0:T(8,128)(2,1)} %cot.1) | copy-start | bytes 196612
  54.1 10.7 %collective-permute-start.3 = (bf16[4,128,256]{2,1,0:T(8,128)(2,1)S(1)}, bf16[4,128,256]{2,1,0:T(8,128)(2,1)S(1)}, u32[]{:S(2)}, u32[]{:S(2)}) collective-permute-start(bf16[4,128,256]{2,1,0:T(8,128)(2,1)S(1)} %get-tuple-element.29), channel_id=1, source_target_pairs={{0,6},{1,7},{2,0},{3,1},{4,2},{5,3},{6,4},{7,5},{8,14},{9,15},{10,... | collective-permute-start | bytes 786440 | tf_op jit(solution)/shard_map/ppermute | solution.py:25
  129.8 9.6 %collective-permute-start.6 = (bf16[528,256]{1,0:T(8,128)(2,1)S(1)}, bf16[528,256]{1,0:T(8,128)(2,1)S(1)}, u32[]{:S(2)}, u32[]{:S(2)}) collective-permute-start(bf16[528,256]{1,0:T(8,128)(2,1)S(1)} %fold.1.l0), channel_id=1, source_target_pairs={{0,6},{1,7},{2,0},{3,1},{4,2},{5,3},{6,4},{7,5},{8,14},{9,15},{10,... | collective-permute-start | bytes 811016 | tf_op jit(solution)/shard_map/ppermute | solution.py:25
  135.0 8.8 %collective-permute-start.5 = (bf16[528,256]{1,0:T(8,128)(2,1)S(1)}, bf16[528,256]{1,0:T(8,128)(2,1)S(1)}, u32[]{:S(2)}, u32[]{:S(2)}) collective-permute-start(bf16[528,256]{1,0:T(8,128)(2,1)S(1)} %fold.1.l0), channel_id=1, source_target_pairs={{0,4},{1,5},{2,6},{3,7},{4,0},{5,1},{6,2},{7,3},{8,12},{9,13},{10,... | collective-permute-start | bytes 811016 | tf_op jit(solution)/shard_map/ppermute | solution.py:25
  136.9 10.6 %collective-permute-start.4 = (bf16[528,256]{1,0:T(8,128)(2,1)S(1)}, bf16[528,256]{1,0:T(8,128)(2,1)S(1)}, u32[]{:S(2)}, u32[]{:S(2)}) collective-permute-start(bf16[528,256]{1,0:T(8,128)(2,1)S(1)} %fold.1.l0), channel_id=1, source_target_pairs={{0,2},{1,3},{2,4},{3,5},{4,6},{5,7},{6,0},{7,1},{8,10},{9,11},{10,... | collective-permute-start | bytes 811016 | tf_op jit(solution)/shard_map/ppermute | solution.py:25
  148.1 9.8 %collective-permute-start.7 = (bf16[2064,256]{1,0:T(8,128)(2,1)S(1)}, bf16[2064,256]{1,0:T(8,128)(2,1)S(1)}, u32[]{:S(2)}, u32[]{:S(2)}) collective-permute-start(bf16[2064,256]{1,0:T(8,128)(2,1)S(1)} %collect.1.grads.mine), channel_id=1, source_target_pairs={{0,1},{1,0},{2,3},{3,2},{4,5},{5,4},{6,7},{7,6},{8,9},{9,8},{10,11... | collective-permute-start | bytes 3170312 | tf_op jit(solution)/shard_map/ppermute | solution.py:34
  160.5 11.4 %collective-permute-start.8 = (bf16[528,256]{1,0:T(8,128)(2,1)S(1)}, bf16[528,256]{1,0:T(8,128)(2,1)S(1)}, u32[]{:S(2)}, u32[]{:S(2)}) collective-permute-start(bf16[528,256]{1,0:T(8,128)(2,1)S(1)} %get-tuple-element.36), channel_id=1, source_target_pairs={{0,64},{32,96},{64,0},{96,32},{128,192},{160,224},{192,128},{224,1... | collective-permute-start | bytes 811016 | tf_op jit(solution)/shard_map/ppermute | solution.py:30
  162.4 15.5 %collective-permute-start.9 = (bf16[528,256]{1,0:T(8,128)(2,1)S(1)}, bf16[528,256]{1,0:T(8,128)(2,1)S(1)}, u32[]{:S(2)}, u32[]{:S(2)}) collective-permute-start(bf16[528,256]{1,0:T(8,128)(2,1)S(1)} %get-tuple-element.37), channel_id=1, source_target_pairs={{0,32},{32,64},{64,96},{96,0},{128,160},{160,192},{192,224},{224,1... | collective-permute-start | bytes 811016 | tf_op jit(solution)/shard_map/ppermute | solution.py:30
  167.3 10.6 %collective-permute-start.10 = (bf16[528,256]{1,0:T(8,128)(2,1)S(1)}, bf16[528,256]{1,0:T(8,128)(2,1)S(1)}, u32[]{:S(2)}, u32[]{:S(2)}) collective-permute-start(bf16[528,256]{1,0:T(8,128)(2,1)S(1)} %get-tuple-element.38), channel_id=1, source_target_pairs={{0,96},{32,0},{64,32},{96,64},{128,224},{160,128},{192,160},{224,1... | collective-permute-start | bytes 811016 | tf_op jit(solution)/shard_map/ppermute | solution.py:30

commit v7 on v6

--- a/solution.py
+++ b/solution.py
@@ -32,6 +32,29 @@
 
 def send_core(v):
     return lax.ppermute(v, "col", [(c, c ^ 1) for c in range(COLS)])
+
+
+def swap_zl(v, k):
+    return lax.ppermute(v, "row", [(r, r ^ (4 * k)) for r in range(ROWS)])
+
+
+def swap_x(v, k):
+    return lax.ppermute(v, "row", [(r, r ^ k) for r in range(ROWS)])
+
+
+def swap_zh(v, k):
+    return lax.ppermute(v, "col", [(c, c ^ (8 * k)) for c in range(COLS)])
+
+
+def halve(part, bit, swap):
+    low, high = jnp.split(part, 2, axis=0)
+    give = jnp.where(bit == 1, low, high).astype(BF16)
+    return jnp.where(bit == 1, high, low) + swap(give).astype(F32)
+
+
+def exchange(part, swap):
+    part = part.astype(BF16)
+    return part.astype(F32) + swap(part).astype(F32)
 
 
 def trade_row(v):
@@ -114,7 +137,7 @@
 def fetch_tiles(live, v, tiles, sems):
     def chunk(i):
         part = pl.ds(i * CHUNK, CHUNK)
-        return pltpu.make_async_copy(v.at[0, 0, part], tiles.at[part], sems.at[i])
+        return pltpu.make_async_copy(v.at[part], tiles.at[part], sems.at[i])
 
     for i in range(SLOTS // CHUNK):
         pl.when(i * CHUNK < live)(chunk(i).start)
@@ -142,22 +165,9 @@
 
 
 def forward(other, where, rows, cols, values, xs):
-    width = xs.shape[-1]
-    return pl.pallas_call(
-        functools.partial(forward_kernel, other),
-        out_shape=jax.ShapeDtypeStruct((HALF, TILE, width), BF16),
-        in_specs=[smem()] * 3 + [pl.BlockSpec(memory_space=pltpu.HBM), vmem()],
-        out_specs=vmem(),
-        scratch_shapes=[
-            pltpu.SMEM((SLOTS + GROUP,), jnp.int32),
-            pltpu.VMEM((HALF + 1, TILE, width), F32),
-            pltpu.VMEM((SLOTS, TILE, TILE), BF16),
-            pltpu.SemaphoreType.DMA((SLOTS // CHUNK,)),
-        ],
-        compiler_params=pltpu.CompilerParams(vmem_limit_bytes=50 * 1024 * 1024),
-        cost_estimate=cost(2 * 64 * TILE * TILE * width, 7),
-        name="forward",
-    )(where, rows, cols, values, xs)
+    kernel = functools.partial(forward_kernel, other)
+    out = jax.ShapeDtypeStruct((HALF, TILE, xs.shape[-1]), BF16)
+    return block_product(kernel, "forward", out, where, rows, cols, values, xs)
 
 
 def turn_kernel(where, v, out):
@@ -191,8 +201,9 @@
     act_out[...] = (pre * s).astype(BF16)
     grad = (cot[...].astype(F32) * (s * (1.0 + pre * (1.0 - s)))).astype(BF16)
     grad_out[...] = grad
-    part = lax.dot_general(aggregated, grad, (((0,), (0,)), ((), ())), preferred_element_type=F32)
-    part_out[...] = part.reshape(part_out.shape).astype(BF16)
+    part_out[...] = lax.dot_general(
+        aggregated, grad, (((0,), (0,)), ((), ())), preferred_element_type=F32
+    )
 
 
 def middle(got, w, cot):
@@ -200,52 +211,11 @@
     rows = jax.ShapeDtypeStruct((n, width), BF16)
     return pl.pallas_call(
         middle_kernel,
-        out_shape=(rows, rows, jax.ShapeDtypeStruct((ROWS, width // ROWS, width), BF16)),
+        out_shape=(rows, rows, jax.ShapeDtypeStruct((width, width), F32)),
         compiler_params=params(),
         cost_estimate=cost(4 * n * width * width, 1),
         name="middle",
     )(got, w, cot)
-
-
-def pack_kernel(grad, parts, out):
-    total = parts[0].astype(F32)
-    for i in range(1, ROWS):
-        total = total + parts[i].astype(F32)
-    part = total.astype(BF16)
-    for i in range(4):
-        out[i, :TILE] = grad[...]
-        out[i, TILE:] = part
-
-
-def pack(grad, parts):
-    n, width = grad.shape
-    return pl.pallas_call(
-        pack_kernel,
-        out_shape=jax.ShapeDtypeStruct((4, n + parts.shape[1], width), BF16),
-        compiler_params=params(),
-        cost_estimate=cost(0, 1),
-        name="pack",
-    )(grad, parts)
-
-
-def fold_kernel(got, out):
-    total = got[0, TILE:].astype(F32)
-    for i in range(1, 4):
-        total = total + got[i, TILE:].astype(F32)
-    for i in range(4):
-        out[TILE * i : TILE * (i + 1)] = got[i, :TILE]
-    out[4 * TILE :] = total.astype(BF16)
-
-
-def fold(got):
-    extra, width = got.shape[1] - TILE, got.shape[2]
-    return pl.pallas_call(
-        fold_kernel,
-        out_shape=jax.ShapeDtypeStruct((4 * TILE + extra, width), BF16),
-        compiler_params=params(),
-        cost_estimate=cost(0, 1),
-        name="fold",
-    )(got)
 
 
 def collect_kernel(where, l0, l1, l2, l3, out, slices):
@@ -272,7 +242,7 @@
     )(where, *lines)
 
 
-def backward_half(other, where, rows, cols, v, grads, slots, acc):
+def backward_half(other, where, rows, cols, grads, slots, acc, tiles, arrive):
     y, core, x = where[1], where[2], where[4]
     found = choose_slots(core ^ other, where, rows, slots)
 
@@ -285,83 +255,81 @@
         c = cols[0, 0, s]
         return (((c & 3) - x) & 3) * 4 + (c >> 2)
 
-    add_products(found, slots, lambda s: v[s], source, target, acc)
-
-
-def first_kernel(where, rows, cols, v, grads, out, slots, acc):
+    arrive()
+    add_products(found, slots, lambda s: tiles[s], source, target, acc)
+
+
+def first_kernel(where, rows, cols, v, grads, out, slots, acc, tiles, sems):
+    arrive = fetch_tiles(where[3], v, tiles, sems)
     acc[...] = jnp.zeros_like(acc)
-    backward_half(0, where, rows, cols, v, grads, slots, acc)
+    backward_half(0, where, rows, cols, grads, slots, acc, tiles, arrive)
     out[...] = acc[:HALF]
 
 
-def second_kernel(where, rows, cols, v, grads, mine, start, o0, o2, o1, o3, slots, acc):
+def second_kernel(
+    where, rows, cols, v, grads, mine, start, o0, o2, o1, o3, part, slots, acc, tiles, sems
+):
+    arrive = fetch_tiles(where[3], v, tiles, sems)
     acc[:HALF] = start[...]
     acc[HALF] = jnp.zeros_like(acc[HALF])
-    backward_half(1, where, rows, cols, v, grads, slots, acc)
-    rest = HALF * TILE
-    part = (mine[rest:].astype(F32) + grads[rest:].astype(F32)).astype(BF16)
+    backward_half(1, where, rows, cols, grads, slots, acc, tiles, arrive)
     for k, out in enumerate((o0, o1, o2, o3)):
         for i in range(4):
             out[TILE * i : TILE * (i + 1)] = acc[4 * k + i].astype(BF16)
-        out[4 * TILE :] = part
+    rest = HALF * TILE
+    part[...] = (mine[rest:].astype(F32) + grads[rest:].astype(F32)).astype(BF16)
+
+
+def block_product(kernel, name, out, where, rows, cols, v, *operands):
+    width = operands[0].shape[-1]
+    return pl.pallas_call(
+        kernel,
+        out_shape=out,
+        in_specs=[smem()] * 3 + [pl.BlockSpec(memory_space=pltpu.HBM)] + [vmem()] * len(operands),
+        out_specs=jax.tree.map(lambda _: vmem(), out),
+        scratch_shapes=[
+            pltpu.SMEM((SLOTS + GROUP,), jnp.int32),
+            pltpu.VMEM((HALF + 1, TILE, width), F32),
+            pltpu.VMEM((SLOTS, TILE, TILE), BF16),
+            pltpu.SemaphoreType.DMA((SLOTS // CHUNK,)),
+        ],
+        compiler_params=pltpu.CompilerParams(vmem_limit_bytes=50 * 1024 * 1024),
+        cost_estimate=cost(2 * 64 * TILE * TILE * width, 8),
+        name=name,
+    )(where, rows, cols, v, *operands)
 
 
 def backward(where, rows, cols, v, mine, theirs):
     extra, width = mine.shape[0] - HALF * TILE, mine.shape[1]
-    scratch = [
-        pltpu.SMEM((SLOTS + GROUP,), jnp.int32),
-        pltpu.VMEM((HALF + 1, TILE, width), F32),
-    ]
-    work = cost(2 * 64 * TILE * TILE * width, 8)
-    first = pl.pallas_call(
-        first_kernel,
-        out_shape=jax.ShapeDtypeStruct((HALF, TILE, width), F32),
-        in_specs=[smem()] * 3 + [vmem()] * 2,
-        out_specs=vmem(),
-        scratch_shapes=scratch,
-        compiler_params=params(),
-        cost_estimate=work,
-        name="first",
-    )(where, rows, cols, v, mine)
-    none, two, one, three = pl.pallas_call(
-        second_kernel,
-        out_shape=(jax.ShapeDtypeStruct((4 * TILE + extra, width), BF16),) * 4,
-        in_specs=[smem()] * 3 + [vmem()] * 4,
-        out_specs=(vmem(),) * 4,
-        scratch_shapes=scratch,
-        compiler_params=params(),
-        cost_estimate=work,
-        name="second",
-    )(where, rows, cols, v, theirs, mine, first)
-    return none, one, two, three
-
-
-def merge_kernel(where, p0, p2, p1, p3, out):
-    x = where[4]
-    parts = (p0, p1, p2, p3)
-    extra = p0.shape[0] - 4 * TILE
+    out = jax.ShapeDtypeStruct((HALF, TILE, width), F32)
+    first = block_product(first_kernel, "first", out, where, rows, cols, v, mine)
+    block = jax.ShapeDtypeStruct((4 * TILE, width), BF16)
+    out = (block,) * 4 + (jax.ShapeDtypeStruct((extra, width), BF16),)
+    none, two, one, three, part = block_product(
+        second_kernel, "second", out, where, rows, cols, v, theirs, mine, first
+    )
+    return (none, one, two, three), part
+
+
+def merge_kernel(p0, p2, p1, p3, part, out):
     for i in range(4):
         block = slice(TILE * i, TILE * (i + 1))
         total = p0[block].astype(F32)
-        for part in parts[1:]:
-            total = total + part[block].astype(F32)
+        for other in (p1, p2, p3):
+            total = total + other[block].astype(F32)
         out[i, :TILE] = total.astype(BF16)
-        for k, part in enumerate(parts):
-            at = pl.multiple_of(TILE + ((x - k) & 3) * extra, extra)
-            out[i, pl.ds(at, extra)] = part[4 * TILE :]
-
-
-def merge(where, parts):
-    rows, width = parts[0].shape
+        out[i, TILE:] = part[...].astype(BF16)
+
+
+def merge(parts, part):
+    width = part.shape[1]
     return pl.pallas_call(
         merge_kernel,
-        out_shape=jax.ShapeDtypeStruct((4, TILE + 4 * (rows - 4 * TILE), width), BF16),
-        in_specs=[smem()] + [vmem()] * 4,
-        out_specs=vmem(),
+        out_shape=jax.ShapeDtypeStruct((4, TILE + part.shape[0], width), BF16),
         compiler_params=params(),
         cost_estimate=cost(0, 2),
         name="merge",
-    )(where, parts[0], parts[2], parts[1], parts[3])
+    )(parts[0], parts[2], parts[1], parts[3], part)
 
 
 def last_kernel(scale, got, w, grad_out, weight_out):
@@ -400,8 +368,9 @@
     xs = trade_row(jnp.broadcast_to(features[None], (ROWS,) + features.shape))
     xs, where = lax.optimization_barrier((xs, where))
     block = (where, tile_rows, tile_cols)
-    got = send_core(forward(1, *block, tile_values, xs))
-    keep = forward(0, *block, tile_values, xs)
+    values = tile_values.reshape(tile_values.shape[2:])
+    got = send_core(forward(1, *block, values, xs))
+    keep = forward(0, *block, values, xs)
     paired = pair(keep, got)
     got = [paired[0]] + [send_y(paired[k], k) for k in (2, 1, 3)]
     got = [v.astype(F32) for v in got]
@@ -410,11 +379,19 @@
     rows, turned = lax.optimization_barrier((rows, turned))
     activated, grad_pre, part = middle(trade_zh(rows), weight, cotangent)
 
-    line = fold(trade_zh(pack(grad_pre, trade_row(part))))
+    line = trade_zh(jnp.broadcast_to(grad_pre[None], (4,) + grad_pre.shape))
+    line = line.reshape(4 * TILE, -1)
+    part = halve(part, r >> 3, lambda v: swap_zl(v, 2))
+    part = halve(part, (r >> 2) & 1, lambda v: swap_zl(v, 1))
+    part = exchange(part, lambda v: swap_x(v, 1))
+    part = exchange(part, lambda v: swap_x(v, 3))
+    line = jnp.concatenate([line, part.astype(BF16)], axis=0)
     mine = collect(where, [line] + [send_y(line, k) for k in (1, 2, 3)])
-    spread = backward(*block, turned, mine, send_core(mine))
+    spread, part = backward(*block, turned, mine, send_core(mine))
     spread = [spread[0]] + [send_x(spread[k], k) for k in (1, 2, 3)]
-    grad_features, grad_weight = last(trade_zl(merge(where, spread)), weight, grad_scale)
+    part = exchange(part, lambda v: swap_zh(v, 1))
+    part = exchange(part, lambda v: swap_zh(v, 3))
+    grad_features, grad_weight = last(trade_zl(merge(spread, part)), weight, grad_scale)
     return (activated, grad_features, grad_weight)
 
 

time: 196 us -> 207 us (1.056); the launches traced: 193 us -> 206 us
  blocking collectives: 111 us -> 51.6 us
  starting transfers between devices: 43.2 us -> 93.4 us
  waiting for transfers between devices: 18.4 us -> 33.8 us
  local copies, waits for them, and re-layouts: 1.04 us -> 5.09 us
  Pallas kernels: 17.6 us -> 19.7 us
    all_to_all x2 -> x0, blocking collectives: 46.2 us -> none  [trade_zh(): return lax.all_to_all(v, 'col', 0, 0, axis_index_groups=groups)]
    ppermute x0 -> x6, starting transfers between devices: none -> 33.8 us  [the longest x2 14.7 us: swap_zh(): return lax.ppermute(v, 'col', [(c, c ^ 8 * k) for c in range(COLS)])]
    all_to_all x2 -> x1, blocking collectives: 51.4 us -> 33.7 us  [trade_row(): return lax.all_to_all(v, 'row', 0, 0)]
    all_to_all x0 -> x2, starting transfers between devices: none -> 14.5 us  [trade_zh(): return lax.all_to_all(v, 'col', 0, 0, axis_index_groups=groups)]
    all_to_all x0 -> x2, waiting for transfers between devices: none -> 13.2 us  [trade_zh(): return lax.all_to_all(v, 'col', 0, 0, axis_index_groups=groups)]
    ppermute x0 -> x6, waiting for transfers between devices: none -> 11.7 us  [the longest x2 5.46 us: swap_x(): return lax.ppermute(v, 'row', [(r, r ^ k) for r in range(ROWS)])]
    ppermute x3, waiting for transfers between devices: 6.33 us -> 0.01 us  [send_x(): return lax.ppermute(v, 'row', pairs)]
    all_to_all x1, blocking collectives: 13.7 us -> 17.9 us  [trade_zl(): return lax.all_to_all(v, 'row', 0, 0, axis_index_groups=groups)]
  transfers between devices with their start and end apart: 11 -> 19, of which waited for: 7 -> 9; matrix products, arithmetic and copies ran while one was open for 0% -> 0% of each run, Pallas kernels for 4% -> 5%
where the time goes in v7:
time: 207 us; the launch traced here: 206 us
  starting transfers between devices  93.4 us (45%)
  blocking collectives  51.6 us (25%)
  waiting for transfers between devices  33.8 us (16%)
  Pallas kernels  19.7 us (10%)
  local copies, waits for them, and re-layouts  5.09 us (2%)
    all_to_all x1, blocking collectives, trade_row(): return lax.all_to_all(v, 'row', 0, 0)  33.7 us
    ppermute x6, starting transfers between devices, send_y(): return lax.ppermute(v, 'col', pairs)  20.8 us
    all_to_all x1, blocking collectives, trade_zl(): return lax.all_to_all(v, 'row', 0, 0, axis_index_groups=groups)  17.9 us
    pallas_call x4, Pallas kernels, block_product(): pl.pallas_call(kernel, out_shape=out, in_specs=[smem()] * 3 + [pl.BlockSp...  15.2 us
    ppermute x2, starting transfers between devices, send_core(): return lax.ppermute(v, 'col', [(c, c ^ 1) for c in range(COLS)])  14.9 us
    ppermute x2, starting transfers between devices, swap_zh(): return lax.ppermute(v, 'col', [(c, c ^ 8 * k) for c in range(COLS)])  14.7 us
    all_to_all x2, starting transfers between devices, trade_zh(): return lax.all_to_all(v, 'col', 0, 0, axis_index_groups=groups)  14.5 us
    ppermute x2, starting transfers between devices, swap_zl(): return lax.ppermute(v, 'row', [(r, r ^ 4 * k) for r in range(ROWS)])  13.5 us
  transfers between devices with their start and end apart: 19, of which 9 were waited for; matrix products, arithmetic and copies ran while one was open for 0% of the time, Pallas kernels for 5%

profile of v7, /device:TPU:1, one launch (start us, length us, event | category | flops | bytes accessed | tf_op | source)
XLA Modules:
  0.0 206.3 jit_solution(12679200464805479839)
XLA Ops:
  1.3 0.1 stack.19.where
  1.4 0.9 broadcast_in_dim.4
  2.3 33.7 %all_to_all.20.xs = bf16[16,128,256]{2,1,0:T(8,128)(2,1)S(1)} all-to-all(bf16[16,128,256]{2,1,0:T(8,128)(2,1)S(1)} %broadcast_in_dim.4), channel_id=1, replica_groups=mesh['row'=16,'col'=32] {'row'}, dimensions={0} | all-to-all | bytes 2097152 | tf_op jit(solution)/shard_map/all_to_all | solution.py:61
  36.0 3.2 %forward.3 = bf16[16,128,256]{2,1,0:T(8,128)(2,1)S(1)} custom-call(s32[5]{0:T(128)S(1)} %stack.19.where, s32[1,1,128]{2,1,0:T(1,128)S(1)} %copy-done.5, s32[1,1,128]{2,1,0:T(1,128)S(1)} %copy-done.6, bf16[128,128,128]{2,1,0:T(8,128)(2,1)} %bitcast.8, bf16[16,128,256]{2,1,0:T(8,128)(2,1)S(1)} %all_to_all.20.xs), custom_call_target="tpu_custom_call" | custom-call | flops 536870912 | bytes 8388608 | tf_op jit(solution)/shard_map/forward/pallas_call | solution.py:285
  39.2 4.6 %collective-permute-start = (bf16[16,128,256]{2,1,0:T(8,128)(2,1)S(1)}, bf16[16,128,256]{2,1,0:T(8,128)(2,1)S(1)}, u32[]{:S(2)}, u32[]{:S(2)}) collective-permute-start(bf16[16,128,256]{2,1,0:T(8,128)(2,1)S(1)} %forward.3), channel_id=1, source_target_pairs={{0,1},{1,0},{2,3},{3,2},{4,5},{5,4},{6,7},{7,6},{8,9},{9,8},{10,11... | collective-permute-start | bytes 3145736 | tf_op jit(solution)/shard_map/ppermute | solution.py:34
  43.7 0.0 copy-start
  43.7 4.0 %forward.2.a = bf16[16,128,256]{2,1,0:T(8,128)(2,1)S(1)} custom-call(s32[5]{0:T(128)S(1)} %stack.19.where, s32[1,1,128]{2,1,0:T(1,128)S(1)} %copy-done.5, s32[1,1,128]{2,1,0:T(1,128)S(1)} %copy-done.6, bf16[128,128,128]{2,1,0:T(8,128)(2,1)} %bitcast.9, bf16[16,128,256]{2,1,0:T(8,128)(2,1)S(1)} %all_to_all.20.xs), custom_call_target="tpu_custom_call" | custom-call | flops 536870912 | bytes 8388608 | tf_op jit(solution)/shard_map/forward/pallas_call | solution.py:285
  47.8 0.2 pair.1
  48.0 6.4 %collective-permute-start.1 = (bf16[4,128,256]{2,1,0:T(8,128)(2,1)S(1)}, bf16[4,128,256]{2,1,0:T(8,128)(2,1)S(1)}, u32[]{:S(2)}, u32[]{:S(2)}) collective-permute-start(bf16[4,128,256]{2,1,0:T(8,128)(2,1)S(1)} %get-tuple-element.28), channel_id=1, source_target_pairs={{0,4},{1,5},{2,6},{3,7},{4,0},{5,1},{6,2},{7,3},{8,12},{9,13},{10,... | collective-permute-start | bytes 786440 | tf_op jit(solution)/shard_map/ppermute | solution.py:25
  54.4 1.9 collective-permute-start.2
  56.3 0.0 copy-start.3
  56.4 4.7 %collective-permute-start.3 = (bf16[4,128,256]{2,1,0:T(8,128)(2,1)S(1)}, bf16[4,128,256]{2,1,0:T(8,128)(2,1)S(1)}, u32[]{:S(2)}, u32[]{:S(2)}) collective-permute-start(bf16[4,128,256]{2,1,0:T(8,128)(2,1)S(1)} %get-tuple-element.30), channel_id=1, source_target_pairs={{0,6},{1,7},{2,0},{3,1},{4,2},{5,3},{6,4},{7,5},{8,14},{9,15},{10,... | collective-permute-start | bytes 786440 | tf_op jit(solution)/shard_map/ppermute | solution.py:25
  61.1 1.8 turn.1.v
  62.9 2.0 copy-done.1
  64.8 1.2 collective-permute-done.2
  66.0 0.8 add_convert_fusion
  66.9 11.1 %all-to-all-start.1 = ((bf16[4,128,256]{2,1,0:T(8,128)(2,1)}), bf16[4,128,256]{2,1,0:T(8,128)(2,1)S(1)}, u32[]{:S(2)}, u32[]{:S(2)}) async-start(bf16[4,128,256]{2,1,0:T(8,128)(2,1)} %add_convert_fusion), calls=%async_computation.1 | async-start | bytes 524288 | tf_op jit(solution)/shard_map/all_to_all | solution.py:71
  78.0 13.2 %all-to-all-done.1.got = bf16[4,128,256]{2,1,0:T(8,128)(2,1)S(1)} async-done(((bf16[4,128,256]{2,1,0:T(8,128)(2,1)}), bf16[4,128,256]{2,1,0:T(8,128)(2,1)S(1)}, u32[]{:S(2)}, u32[]{:S(2)}) %all-to-all-start.1) | async-done | bytes 262176 | tf_op jit(solution)/shard_map/all_to_all | solution.py:71
  91.2 0.8 middle.1
  92.0 10.6 %collective-permute-start.4 = (bf16[128,256]{1,0:T(8,128)(2,1)S(1)}, bf16[128,256]{1,0:T(8,128)(2,1)S(1)}, u32[]{:S(2)}, u32[]{:S(2)}) collective-permute-start(bf16[128,256]{1,0:T(8,128)(2,1)S(1)} %select_convert_fusion), channel_id=1, source_target_pairs={{0,256},{32,288},{64,320},{96,352},{128,384},{160,416},{192,448},{... | collective-permute-start | bytes 196616 | tf_op jit(solution)/shard_map/ppermute | solution.py:38
  102.6 0.7 broadcast_in_dim.5
  103.3 3.4 %all-to-all-start.2 = ((bf16[4,128,256]{2,1,0:T(8,128)(2,1)}), bf16[4,128,256]{2,1,0:T(8,128)(2,1)S(1)}, u32[]{:S(2)}, u32[]{:S(2)}) async-start(bf16[4,128,256]{2,1,0:T(8,128)(2,1)} %broadcast_in_dim.5), calls=%async_computation.2 | async-start | bytes 524288 | tf_op jit(solution)/shard_map/all_to_all | solution.py:71
  106.8 2.9 %collective-permute-start.5 = (bf16[64,256]{1,0:T(8,128)(2,1)S(1)}, bf16[64,256]{1,0:T(8,128)(2,1)S(1)}, u32[]{:S(2)}, u32[]{:S(2)}) collective-permute-start(bf16[64,256]{1,0:T(8,128)(2,1)S(1)} %select_convert_fusion.1), channel_id=1, source_target_pairs={{0,128},{32,160},{64,192},{96,224},{128,0},{160,32},{192,64},{224,... | collective-permute-start | bytes 98312 | tf_op jit(solution)/shard_map/ppermute | solution.py:38
  109.7 5.0 %collective-permute-done.5 = bf16[64,256]{1,0:T(8,128)(2,1)S(1)} collective-permute-done((bf16[64,256]{1,0:T(8,128)(2,1)S(1)}, bf16[64,256]{1,0:T(8,128)(2,1)S(1)}, u32[]{:S(2)}, u32[]{:S(2)}) %collective-permute-start.5) | collective-permute-done | bytes 32800 | tf_op jit(solution)/shard_map/ppermute | solution.py:38
  114.7 1.9 collective-permute-start.6
  116.6 3.0 %collective-permute-done.6 = bf16[64,256]{1,0:T(8,128)(2,1)S(1)} collective-permute-done((bf16[64,256]{1,0:T(8,128)(2,1)S(1)}, bf16[64,256]{1,0:T(8,128)(2,1)S(1)}, u32[]{:S(2)}, u32[]{:S(2)}) %collective-permute-start.6) | collective-permute-done | bytes 32800 | tf_op jit(solution)/shard_map/ppermute | solution.py:42
  119.6 3.7 %collective-permute-start.7 = (bf16[64,256]{1,0:T(8,128)(2,1)S(1)}, bf16[64,256]{1,0:T(8,128)(2,1)S(1)}, u32[]{:S(2)}, u32[]{:S(2)}) collective-permute-start(bf16[64,256]{1,0:T(8,128)(2,1)S(1)} %add_convert_fusion.3), channel_id=1, source_target_pairs={{0,96},{32,64},{64,32},{96,0},{128,224},{160,192},{192,160},{224,1... | collective-permute-start | bytes 98312 | tf_op jit(solution)/shard_map/ppermute | solution.py:42
  123.4 2.4 %collective-permute-done.7 = bf16[64,256]{1,0:T(8,128)(2,1)S(1)} collective-permute-done((bf16[64,256]{1,0:T(8,128)(2,1)S(1)}, bf16[64,256]{1,0:T(8,128)(2,1)S(1)}, u32[]{:S(2)}, u32[]{:S(2)}) %collective-permute-start.7) | collective-permute-done | bytes 32800 | tf_op jit(solution)/shard_map/ppermute | solution.py:42
  125.9 3.4 %collective-permute-start.10 = (bf16[576,256]{1,0:T(8,128)(2,1)S(1)}, bf16[576,256]{1,0:T(8,128)(2,1)S(1)}, u32[]{:S(2)}, u32[]{:S(2)}) collective-permute-start(bf16[576,256]{1,0:T(8,128)(2,1)S(1)} %pad_maximum_fusion.l0), channel_id=1, source_target_pairs={{0,6},{1,7},{2,0},{3,1},{4,2},{5,3},{6,4},{7,5},{8,14},{9,15},{10,... | collective-permute-start | bytes 884744 | tf_op jit(solution)/shard_map/ppermute | solution.py:25
  129.3 2.4 %collective-permute-start.9 = (bf16[576,256]{1,0:T(8,128)(2,1)S(1)}, bf16[576,256]{1,0:T(8,128)(2,1)S(1)}, u32[]{:S(2)}, u32[]{:S(2)}) collective-permute-start(bf16[576,256]{1,0:T(8,128)(2,1)S(1)} %pad_maximum_fusion.l0), channel_id=1, source_target_pairs={{0,4},{1,5},{2,6},{3,7},{4,0},{5,1},{6,2},{7,3},{8,12},{9,13},{10,... | collective-permute-start | bytes 884744 | tf_op jit(solution)/shard_map/ppermute | solution.py:25
  131.7 2.0 collective-permute-start.8
  133.7 1.7 collective-permute-done.10.l3
  135.4 3.0 %collective-permute-done.9.l2 = bf16[576,256]{1,0:T(8,128)(2,1)S(1)} collective-permute-done((bf16[576,256]{1,0:T(8,128)(2,1)S(1)}, bf16[576,256]{1,0:T(8,128)(2,1)S(1)}, u32[]{:S(2)}, u32[]{:S(2)}) %collective-permute-start.9) | collective-permute-done | bytes 294944 | tf_op jit(solution)/shard_map/ppermute | solution.py:25
  138.4 3.1 %collective-permute-done.8.l1 = bf16[576,256]{1,0:T(8,128)(2,1)S(1)} collective-permute-done((bf16[576,256]{1,0:T(8,128)(2,1)S(1)}, bf16[576,256]{1,0:T(8,128)(2,1)S(1)}, u32[]{:S(2)}, u32[]{:S(2)}) %collective-permute-start.8) | collective-permute-done | bytes 294944 | tf_op jit(solution)/shard_map/ppermute | solution.py:25
  141.4 0.6 collect.1.grads.mine
  142.1 10.4 %collective-permute-start.11 = (bf16[2112,256]{1,0:T(8,128)(2,1)S(1)}, bf16[2112,256]{1,0:T(8,128)(2,1)S(1)}, u32[]{:S(2)}, u32[]{:S(2)}) collective-permute-start(bf16[2112,256]{1,0:T(8,128)(2,1)S(1)} %collect.1.grads.mine), channel_id=1, source_target_pairs={{0,1},{1,0},{2,3},{3,2},{4,5},{5,4},{6,7},{7,6},{8,9},{9,8},{10,11... | collective-permute-start | bytes 3244040 | tf_op jit(solution)/shard_map/ppermute | solution.py:34
  152.4 3.8 %first.1.start = f32[16,128,256]{2,1,0:T(8,128)S(1)} custom-call(s32[5]{0:T(128)S(1)} %stack.19.where, s32[1,1,128]{2,1,0:T(1,128)S(1)} %copy-done.5, s32[1,1,128]{2,1,0:T(1,128)S(1)} %copy-done.6, bf16[128,128,128]{2,1,0:T(8,128)(2,1)} %copy-done.1, bf16[2112,256]{1,0:T(8,128)(2,1)S(1)} %collect.1.grads.mine), custom_call_target="tpu_custom_call" | custom-call | flops 536870912 | bytes 8388608 | tf_op jit(solution)/shard_map/first/pallas_call | solution.py:285
  156.3 1.4 copy-done.2
  157.6 4.2 %second.1 = (bf16[512,256]{1,0:T(8,128)(2,1)S(1)}, bf16[512,256]{1,0:T(8,128)(2,1)S(1)}, bf16[512,256]{1,0:T(8,128)(2,1)S(1)}, bf16[512,256]{1,0:T(8,128)(2,1)S(1)}, bf16[64,256]{1,0:T(8,128)(2,1)S(1)}) custom-call(s32[5]{0:T(128)S(1)} %stack.19.where, s32[1,1,128]{2,1,0:T(1,128)S(1)} %copy-done.5, s32[1,1,128]{2,1,0:T(1,128)S(1)} %copy-done.6, ...), custom_call_target="tpu_custom_call" | custom-call | flops 536870912 | bytes 8388608 | tf_op jit(solution)/shard_map/second/pallas_call | solution.py:285
  161.9 5.0 %collective-permute-start.15 = (bf16[64,256]{1,0:T(8,128)(2,1)S(1)}, bf16[64,256]{1,0:T(8,128)(2,1)S(1)}, u32[]{:S(2)}, u32[]{:S(2)}) collective-permute-start(bf16[64,256]{1,0:T(8,128)(2,1)S(1)} %get-tuple-element.40), channel_id=1, source_target_pairs={{0,8},{1,9},{2,10},{3,11},{4,12},{5,13},{6,14},{7,15},{8,0},{9,1},... | collective-permute-start | bytes 98312 | tf_op jit(solution)/shard_map/ppermute | solution.py:46
  166.9 2.9 %collective-permute-start.12 = (bf16[512,256]{1,0:T(8,128)(2,1)S(1)}, bf16[512,256]{1,0:T(8,128)(2,1)S(1)}, u32[]{:S(2)}, u32[]{:S(2)}) collective-permute-start(bf16[512,256]{1,0:T(8,128)(2,1)S(1)} %get-tuple-element.37), channel_id=1, source_target_pairs={{0,64},{32,96},{64,0},{96,32},{128,192},{160,224},{192,128},{224,1... | collective-permute-start | bytes 786440 | tf_op jit(solution)/shard_map/ppermute | solution.py:30
  169.8 4.3 %collective-permute-start.13 = (bf16[512,256]{1,0:T(8,128)(2,1)S(1)}, bf16[512,256]{1,0:T(8,128)(2,1)S(1)}, u32[]{:S(2)}, u32[]{:S(2)}) collective-permute-start(bf16[512,256]{1,0:T(8,128)(2,1)S(1)} %get-tuple-element.38), channel_id=1, source_target_pairs={{0,32},{32,64},{64,96},{96,0},{128,160},{160,192},{192,224},{224,1... | collective-permute-start | bytes 786440 | tf_op jit(solution)/shard_map/ppermute | solution.py:30
  174.1 2.2 %collective-permute-start.14 = (bf16[512,256]{1,0:T(8,128)(2,1)S(1)}, bf16[512,256]{1,0:T(8,128)(2,1)S(1)}, u32[]{:S(2)}, u32[]{:S(2)}) collective-permute-start(bf16[512,256]{1,0:T(8,128)(2,1)S(1)} %get-tuple-element.39), channel_id=1, source_target_pairs={{0,96},{32,0},{64,32},{96,64},{128,224},{160,128},{192,160},{224,1... | collective-permute-start | bytes 786440 | tf_op jit(solution)/shard_map/ppermute | solution.py:30
  176.3 9.7 %collective-permute-start.16 = (bf16[64,256]{1,0:T(8,128)(2,1)S(1)}, bf16[64,256]{1,0:T(8,128)(2,1)S(1)}, u32[]{:S(2)}, u32[]{:S(2)}) collective-permute-start(bf16[64,256]{1,0:T(8,128)(2,1)S(1)} %add_convert_fusion.1), channel_id=1, source_target_pairs={{0,24},{1,25},{2,26},{3,27},{4,28},{5,29},{6,30},{7,31},{8,16},{9,... | collective-permute-start | bytes 98312 | tf_op jit(solution)/shard_map/ppermute | solution.py:46
  186.1 1.3 collective-permute-done.16
  187.4 0.1 merge.1
  187.5 17.9 %all_to_all.21.got = bf16[4,192,256]{2,1,0:T(8,128)(2,1)S(1)} all-to-all(bf16[4,192,256]{2,1,0:T(8,128)(2,1)S(1)} %merge.1), channel_id=1, replica_groups={{0,128,256,384},{32,160,288,416},{64,192,320,448},{96,224,352,480},{1,1..., dimensions={0} | all-to-all | bytes 786432 | tf_op jit(solution)/shard_map/all_to_all | solution.py:66
  205.5 0.8 last.1
  (29 shorter events, 0.2 us)
Async XLA Ops:
  0.6 35.4 %copy-start.6 = (s32[1,1,128]{2,1,0:T(1,128)S(1)}, s32[1,1,128]{2,1,0:T(1,128)}, u32[]{:S(2)}) copy-start(s32[1,1,128]{2,1,0:T(1,128)} %cols.7) | copy-start | bytes 1540
  0.6 35.4 %copy-start.5 = (s32[1,1,128]{2,1,0:T(1,128)S(1)}, s32[1,1,128]{2,1,0:T(1,128)}, u32[]{:S(2)}) copy-start(s32[1,1,128]{2,1,0:T(1,128)} %rows.7) | copy-start | bytes 1540
  39.2 8.6 %collective-permute-start = (bf16[16,128,256]{2,1,0:T(8,128)(2,1)S(1)}, bf16[16,128,256]{2,1,0:T(8,128)(2,1)S(1)}, u32[]{:S(2)}, u32[]{:S(2)}) collective-permute-start(bf16[16,128,256]{2,1,0:T(8,128)(2,1)S(1)} %forward.3), channel_id=1, source_target_pairs={{0,1},{1,0},{2,3},{3,2},{4,5},{5,4},{6,7},{7,6},{8,9},{9,8},{10,11... | collective-permute-start | bytes 3145736 | tf_op jit(solution)/shard_map/ppermute | solution.py:34
  43.7 17.4 %copy-start = (bf16[1,1,128,128,128]{4,3,2,1,0:T(8,128)(2,1)S(1)}, bf16[1,1,128,128,128]{4,3,2,1,0:T(8,128)(2,1)}, u32[]{:S(2)}) copy-start(bf16[1,1,128,128,128]{4,3,2,1,0:T(8,128)(2,1)} %v.1) | copy-start | bytes 12582916
  48.0 16.8 %collective-permute-start.1 = (bf16[4,128,256]{2,1,0:T(8,128)(2,1)S(1)}, bf16[4,128,256]{2,1,0:T(8,128)(2,1)S(1)}, u32[]{:S(2)}, u32[]{:S(2)}) collective-permute-start(bf16[4,128,256]{2,1,0:T(8,128)(2,1)S(1)} %get-tuple-element.28), channel_id=1, source_target_pairs={{0,4},{1,5},{2,6},{3,7},{4,0},{5,1},{6,2},{7,3},{8,12},{9,13},{10,... | collective-permute-start | bytes 786440 | tf_op jit(solution)/shard_map/ppermute | solution.py:25
  54.4 11.6 %collective-permute-start.2 = (bf16[4,128,256]{2,1,0:T(8,128)(2,1)S(1)}, bf16[4,128,256]{2,1,0:T(8,128)(2,1)S(1)}, u32[]{:S(2)}, u32[]{:S(2)}) collective-permute-start(bf16[4,128,256]{2,1,0:T(8,128)(2,1)S(1)} %get-tuple-element.29), channel_id=1, source_target_pairs={{0,2},{1,3},{2,4},{3,5},{4,6},{5,7},{6,0},{7,1},{8,10},{9,11},{10,... | collective-permute-start | bytes 786440 | tf_op jit(solution)/shard_map/ppermute | solution.py:25
  56.3 34.8 %copy-start.3 = (bf16[256,256]{1,0:T(8,128)(2,1)S(1)}, bf16[256,256]{1,0:T(8,128)(2,1)}, u32[]{:S(2)}) copy-start(bf16[256,256]{1,0:T(8,128)(2,1)} %w.3) | copy-start | bytes 393220
  56.3 34.8 %copy-start.4 = (bf16[128,256]{1,0:T(8,128)(2,1)S(1)}, bf16[128,256]{1,0:T(8,128)(2,1)}, u32[]{:S(2)}) copy-start(bf16[128,256]{1,0:T(8,128)(2,1)} %cot.1) | copy-start | bytes 196612
  56.4 9.7 %collective-permute-start.3 = (bf16[4,128,256]{2,1,0:T(8,128)(2,1)S(1)}, bf16[4,128,256]{2,1,0:T(8,128)(2,1)S(1)}, u32[]{:S(2)}, u32[]{:S(2)}) collective-permute-start(bf16[4,128,256]{2,1,0:T(8,128)(2,1)S(1)} %get-tuple-element.30), channel_id=1, source_target_pairs={{0,6},{1,7},{2,0},{3,1},{4,2},{5,3},{6,4},{7,5},{8,14},{9,15},{10,... | collective-permute-start | bytes 786440 | tf_op jit(solution)/shard_map/ppermute | solution.py:25
  62.9 2.0 copy-start.1
  66.9 24.3 %all-to-all-start.1 = ((bf16[4,128,256]{2,1,0:T(8,128)(2,1)}), bf16[4,128,256]{2,1,0:T(8,128)(2,1)S(1)}, u32[]{:S(2)}, u32[]{:S(2)}) async-start(bf16[4,128,256]{2,1,0:T(8,128)(2,1)} %add_convert_fusion), calls=%async_computation.1 | async-start | bytes 524288 | tf_op jit(solution)/shard_map/all_to_all | solution.py:71
  92.0 14.7 %collective-permute-start.4 = (bf16[128,256]{1,0:T(8,128)(2,1)S(1)}, bf16[128,256]{1,0:T(8,128)(2,1)S(1)}, u32[]{:S(2)}, u32[]{:S(2)}) collective-permute-start(bf16[128,256]{1,0:T(8,128)(2,1)S(1)} %select_convert_fusion), channel_id=1, source_target_pairs={{0,256},{32,288},{64,320},{96,352},{128,384},{160,416},{192,448},{... | collective-permute-start | bytes 196616 | tf_op jit(solution)/shard_map/ppermute | solution.py:38
  103.3 22.5 %all-to-all-start.2 = ((bf16[4,128,256]{2,1,0:T(8,128)(2,1)}), bf16[4,128,256]{2,1,0:T(8,128)(2,1)S(1)}, u32[]{:S(2)}, u32[]{:S(2)}) async-start(bf16[4,128,256]{2,1,0:T(8,128)(2,1)} %broadcast_in_dim.5), calls=%async_computation.2 | async-start | bytes 524288 | tf_op jit(solution)/shard_map/all_to_all | solution.py:71
  106.8 7.9 %collective-permute-start.5 = (bf16[64,256]{1,0:T(8,128)(2,1)S(1)}, bf16[64,256]{1,0:T(8,128)(2,1)S(1)}, u32[]{:S(2)}, u32[]{:S(2)}) collective-permute-start(bf16[64,256]{1,0:T(8,128)(2,1)S(1)} %select_convert_fusion.1), channel_id=1, source_target_pairs={{0,128},{32,160},{64,192},{96,224},{128,0},{160,32},{192,64},{224,... | collective-permute-start | bytes 98312 | tf_op jit(solution)/shard_map/ppermute | solution.py:38
  114.7 5.0 %collective-permute-start.6 = (bf16[64,256]{1,0:T(8,128)(2,1)S(1)}, bf16[64,256]{1,0:T(8,128)(2,1)S(1)}, u32[]{:S(2)}, u32[]{:S(2)}) collective-permute-start(bf16[64,256]{1,0:T(8,128)(2,1)S(1)} %add_convert_fusion.4), channel_id=1, source_target_pairs={{0,32},{32,0},{64,96},{96,64},{128,160},{160,128},{192,224},{224,1... | collective-permute-start | bytes 98312 | tf_op jit(solution)/shard_map/ppermute | solution.py:42
  119.6 6.2 %collective-permute-start.7 = (bf16[64,256]{1,0:T(8,128)(2,1)S(1)}, bf16[64,256]{1,0:T(8,128)(2,1)S(1)}, u32[]{:S(2)}, u32[]{:S(2)}) collective-permute-start(bf16[64,256]{1,0:T(8,128)(2,1)S(1)} %add_convert_fusion.3), channel_id=1, source_target_pairs={{0,96},{32,64},{64,32},{96,0},{128,224},{160,192},{192,160},{224,1... | collective-permute-start | bytes 98312 | tf_op jit(solution)/shard_map/ppermute | solution.py:42
  125.9 9.5 %collective-permute-start.10 = (bf16[576,256]{1,0:T(8,128)(2,1)S(1)}, bf16[576,256]{1,0:T(8,128)(2,1)S(1)}, u32[]{:S(2)}, u32[]{:S(2)}) collective-permute-start(bf16[576,256]{1,0:T(8,128)(2,1)S(1)} %pad_maximum_fusion.l0), channel_id=1, source_target_pairs={{0,6},{1,7},{2,0},{3,1},{4,2},{5,3},{6,4},{7,5},{8,14},{9,15},{10,... | collective-permute-start | bytes 884744 | tf_op jit(solution)/shard_map/ppermute | solution.py:25
  129.3 9.1 %collective-permute-start.9 = (bf16[576,256]{1,0:T(8,128)(2,1)S(1)}, bf16[576,256]{1,0:T(8,128)(2,1)S(1)}, u32[]{:S(2)}, u32[]{:S(2)}) collective-permute-start(bf16[576,256]{1,0:T(8,128)(2,1)S(1)} %pad_maximum_fusion.l0), channel_id=1, source_target_pairs={{0,4},{1,5},{2,6},{3,7},{4,0},{5,1},{6,2},{7,3},{8,12},{9,13},{10,... | collective-permute-start | bytes 884744 | tf_op jit(solution)/shard_map/ppermute | solution.py:25
  131.7 9.7 %collective-permute-start.8 = (bf16[576,256]{1,0:T(8,128)(2,1)S(1)}, bf16[576,256]{1,0:T(8,128)(2,1)S(1)}, u32[]{:S(2)}, u32[]{:S(2)}) collective-permute-start(bf16[576,256]{1,0:T(8,128)(2,1)S(1)} %pad_maximum_fusion.l0), channel_id=1, source_target_pairs={{0,2},{1,3},{2,4},{3,5},{4,6},{5,7},{6,0},{7,1},{8,10},{9,11},{10,... | collective-permute-start | bytes 884744 | tf_op jit(solution)/shard_map/ppermute | solution.py:25
  142.1 15.6 %collective-permute-start.11 = (bf16[2112,256]{1,0:T(8,128)(2,1)S(1)}, bf16[2112,256]{1,0:T(8,128)(2,1)S(1)}, u32[]{:S(2)}, u32[]{:S(2)}) collective-permute-start(bf16[2112,256]{1,0:T(8,128)(2,1)S(1)} %collect.1.grads.mine), channel_id=1, source_target_pairs={{0,1},{1,0},{2,3},{3,2},{4,5},{5,4},{6,7},{7,6},{8,9},{9,8},{10,11... | collective-permute-start | bytes 3244040 | tf_op jit(solution)/shard_map/ppermute | solution.py:34
  156.3 1.4 copy-start.2
  161.9 14.4 %collective-permute-start.15 = (bf16[64,256]{1,0:T(8,128)(2,1)S(1)}, bf16[64,256]{1,0:T(8,128)(2,1)S(1)}, u32[]{:S(2)}, u32[]{:S(2)}) collective-permute-start(bf16[64,256]{1,0:T(8,128)(2,1)S(1)} %get-tuple-element.40), channel_id=1, source_target_pairs={{0,8},{1,9},{2,10},{3,11},{4,12},{5,13},{6,14},{7,15},{8,0},{9,1},... | collective-permute-start | bytes 98312 | tf_op jit(solution)/shard_map/ppermute | solution.py:46
  166.9 20.5 %collective-permute-start.12 = (bf16[512,256]{1,0:T(8,128)(2,1)S(1)}, bf16[512,256]{1,0:T(8,128)(2,1)S(1)}, u32[]{:S(2)}, u32[]{:S(2)}) collective-permute-start(bf16[512,256]{1,0:T(8,128)(2,1)S(1)} %get-tuple-element.37), channel_id=1, source_target_pairs={{0,64},{32,96},{64,0},{96,32},{128,192},{160,224},{192,128},{224,1... | collective-permute-start | bytes 786440 | tf_op jit(solution)/shard_map/ppermute | solution.py:30
  169.8 17.6 %collective-permute-start.13 = (bf16[512,256]{1,0:T(8,128)(2,1)S(1)}, bf16[512,256]{1,0:T(8,128)(2,1)S(1)}, u32[]{:S(2)}, u32[]{:S(2)}) collective-permute-start(bf16[512,256]{1,0:T(8,128)(2,1)S(1)} %get-tuple-element.38), channel_id=1, source_target_pairs={{0,32},{32,64},{64,96},{96,0},{128,160},{160,192},{192,224},{224,1... | collective-permute-start | bytes 786440 | tf_op jit(solution)/shard_map/ppermute | solution.py:30
  174.1 13.3 %collective-permute-start.14 = (bf16[512,256]{1,0:T(8,128)(2,1)S(1)}, bf16[512,256]{1,0:T(8,128)(2,1)S(1)}, u32[]{:S(2)}, u32[]{:S(2)}) collective-permute-start(bf16[512,256]{1,0:T(8,128)(2,1)S(1)} %get-tuple-element.39), channel_id=1, source_target_pairs={{0,96},{32,0},{64,32},{96,64},{128,224},{160,128},{192,160},{224,1... | collective-permute-start | bytes 786440 | tf_op jit(solution)/shard_map/ppermute | solution.py:30
  176.3 11.0 %collective-permute-start.16 = (bf16[64,256]{1,0:T(8,128)(2,1)S(1)}, bf16[64,256]{1,0:T(8,128)(2,1)S(1)}, u32[]{:S(2)}, u32[]{:S(2)}) collective-permute-start(bf16[64,256]{1,0:T(8,128)(2,1)S(1)} %add_convert_fusion.1), channel_id=1, source_target_pairs={{0,24},{1,25},{2,26},{3,27},{4,28},{5,29},{6,30},{7,31},{8,16},{9,... | collective-permute-start | bytes 98312 | tf_op jit(solution)/shard_map/ppermute | solution.py:46

commit v8 on v6

--- a/solution.py
+++ b/solution.py
@@ -12,7 +12,7 @@
 ROWS = 16
 COLS = 32
 HALF = 16
-GROUP = 8
+GROUP = 16
 CHUNK = 16
 SLOTS = 128
 VMEM_LIMIT = 24 * 1024 * 1024
@@ -64,33 +64,37 @@
     return pl.CostEstimate(flops=flops, bytes_accessed=mib * 1024 * 1024, transcendentals=0)
 
 
-def choose_slots(parity, where, rows, slots):
-    live = where[3]
-
-    def pick(g, found):
-        for u in range(GROUP):
-            s = g * GROUP + u
-            slots[found] = s
-            chosen = ((rows[0, 0, s] & 1) == parity) & (s < live)
-            found = found + jnp.where(chosen, 1, 0)
-        return found
-
-    return lax.fori_loop(0, (live + GROUP - 1) // GROUP, pick, 0)
-
-
-def add_products(found, slots, tile, source, target, acc):
-    def step(g, _):
+def choose_slots(parity, where, rows, slots, first, found):
+    for u in range(CHUNK):
+        s = first + u
+        slots[found] = s
+        chosen = ((rows[0, 0, s] & 1) == parity) & (s < where[3])
+        found = found + jnp.where(chosen, 1, 0)
+    return found
+
+
+def add_products(parity, where, rows, slots, arrive, tile, source, target, acc):
+    def group(found, first):
         products, targets = [], []
         for u in range(GROUP):
-            at = g * GROUP + u
+            at = first + u
             s = jnp.where(at < found, slots[at], 0)
             targets.append(jnp.where(at < found, target(s), HALF))
             products.append(jnp.dot(tile(s), source(s), preferred_element_type=F32))
         for u in range(GROUP):
             acc[targets[u]] = acc[targets[u]] + products[u]
-        return 0
-
-    lax.fori_loop(0, (found + GROUP - 1) // GROUP, step, 0)
+
+    def chunk(i, state):
+        found, done = state
+        arrive(i)
+        found = choose_slots(parity, where, rows, slots, i * CHUNK, found)
+        full = (found - done) >= GROUP
+        pl.when(full)(lambda: group(found, done))
+        return found, jnp.where(full, done + GROUP, done)
+
+    chunks = (where[3] + CHUNK - 1) // CHUNK
+    found, done = lax.fori_loop(0, chunks, chunk, (jnp.int32(0), jnp.int32(0)))
+    pl.when(done < found)(lambda: group(found, done))
 
 
 def pair_kernel(a, b, o0, o2, o1, o3):
@@ -111,34 +115,44 @@
     return none, one, two, three
 
 
-def fetch_tiles(live, v, tiles, sems):
+def fetch_chunks(live, v, tiles, sems):
     def chunk(i):
         part = pl.ds(i * CHUNK, CHUNK)
         return pltpu.make_async_copy(v.at[0, 0, part], tiles.at[part], sems.at[i])
 
     for i in range(SLOTS // CHUNK):
         pl.when(i * CHUNK < live)(chunk(i).start)
-
-    def arrive():
-        for i in range(SLOTS // CHUNK):
-            pl.when(i * CHUNK < live)(chunk(i).wait)
-
-    return arrive
+    return chunk
 
 
 def forward_kernel(other, where, rows, cols, v, xs, out, slots, acc, tiles, sems):
     y, core = where[1], where[2]
-    arrive = fetch_tiles(where[3], v, tiles, sems)
+    chunks = fetch_chunks(where[3], v, tiles, sems)
     acc[...] = jnp.zeros_like(acc)
-    found = choose_slots(core ^ other, where, rows, slots)
 
     def target(s):
         r = rows[0, 0, s]
         return ((((r >> 1) & 3) - y) & 3) * 4 + (r >> 3)
 
-    arrive()
-    add_products(found, slots, lambda s: tiles[s], lambda s: xs[cols[0, 0, s]], target, acc)
+    add_products(
+        core ^ other,
+        where,
+        rows,
+        slots,
+        lambda i: chunks(i).wait(),
+        lambda s: tiles[s],
+        lambda s: xs[cols[0, 0, s]],
+        target,
+        acc,
+    )
     out[...] = acc[:HALF].astype(BF16)
+
+
+def list_and_sums(width):
+    return [
+        pltpu.SMEM((SLOTS + GROUP,), jnp.int32),
+        pltpu.VMEM((HALF + 1, TILE, width), F32),
+    ]
 
 
 def forward(other, where, rows, cols, values, xs):
@@ -149,8 +163,7 @@
         in_specs=[smem()] * 3 + [pl.BlockSpec(memory_space=pltpu.HBM), vmem()],
         out_specs=vmem(),
         scratch_shapes=[
-            pltpu.SMEM((SLOTS + GROUP,), jnp.int32),
-            pltpu.VMEM((HALF + 1, TILE, width), F32),
+            *list_and_sums(width),
             pltpu.VMEM((SLOTS, TILE, TILE), BF16),
             pltpu.SemaphoreType.DMA((SLOTS // CHUNK,)),
         ],
@@ -160,25 +173,33 @@
     )(where, rows, cols, values, xs)
 
 
-def turn_kernel(where, v, out):
+def turn_kernel(where, v, out, tiles, sems):
+    chunks = fetch_chunks(where[3], v, tiles, sems)
+
     def step(i, _):
-        for u in range(4):
-            out[4 * i + u] = v[0, 0, 4 * i + u].T
+        chunks(i).wait()
+        for u in range(CHUNK):
+            out[i * CHUNK + u] = tiles[i * CHUNK + u].T
         return 0
 
-    lax.fori_loop(0, (where[3] + 3) // 4, step, 0)
-
-
-def turn_tiles(where, tile_values):
+    lax.fori_loop(0, (where[3] + CHUNK - 1) // CHUNK, step, 0)
+
+
+def turn_tiles(where, v):
+    shape = v.shape[2:]
     return pl.pallas_call(
         turn_kernel,
-        out_shape=jax.ShapeDtypeStruct(tile_values.shape[2:], tile_values.dtype),
-        in_specs=[smem(), vmem()],
+        out_shape=jax.ShapeDtypeStruct(shape, v.dtype),
+        in_specs=[smem(), pl.BlockSpec(memory_space=pltpu.HBM)],
         out_specs=vmem(),
-        compiler_params=params(),
+        scratch_shapes=[
+            pltpu.VMEM(shape, v.dtype),
+            pltpu.SemaphoreType.DMA((SLOTS // CHUNK,)),
+        ],
+        compiler_params=pltpu.CompilerParams(vmem_limit_bytes=46 * 1024 * 1024),
         cost_estimate=cost(0, 10),
         name="turn",
-    )(where, tile_values)
+    )(where, v)
 
 
 def middle_kernel(got, w, cot, act_out, grad_out, part_out):
@@ -274,7 +295,6 @@
 
 def backward_half(other, where, rows, cols, v, grads, slots, acc):
     y, core, x = where[1], where[2], where[4]
-    found = choose_slots(core ^ other, where, rows, slots)
 
     def source(s):
         r = rows[0, 0, s]
@@ -285,7 +305,9 @@
         c = cols[0, 0, s]
         return (((c & 3) - x) & 3) * 4 + (c >> 2)
 
-    add_products(found, slots, lambda s: v[s], source, target, acc)
+    add_products(
+        core ^ other, where, rows, slots, lambda i: None, lambda s: v[s], source, target, acc
+    )
 
 
 def first_kernel(where, rows, cols, v, grads, out, slots, acc):
@@ -308,10 +330,7 @@
 
 def backward(where, rows, cols, v, mine, theirs):
     extra, width = mine.shape[0] - HALF * TILE, mine.shape[1]
-    scratch = [
-        pltpu.SMEM((SLOTS + GROUP,), jnp.int32),
-        pltpu.VMEM((HALF + 1, TILE, width), F32),
-    ]
+    scratch = list_and_sums(width)
     work = cost(2 * 64 * TILE * TILE * width, 8)
     first = pl.pallas_call(
         first_kernel,

time: 196 us -> 194 us (0.990)
  Pallas kernels: 17.6 us -> 12.9 us
  blocking collectives: 111 us -> 113 us
    ppermute x2, starting transfers between devices: 11 us -> 14.9 us  [send_core(): return lax.ppermute(v, 'col', [(c, c ^ 1) for c in range(COLS)])]
    all_to_all x2, blocking collectives: 51.4 us -> 47.5 us  [trade_row(): return lax.all_to_all(v, 'row', 0, 0)]
    all_to_all x2, blocking collectives: 46.2 us -> 49.2 us  [trade_zh(): return lax.all_to_all(v, 'col', 0, 0, axis_index_groups=groups)]
    pallas_call x2, Pallas kernels: 7.5 us -> 4.75 us  [forward(): pl.pallas_call(functools.partial(forward_kernel, other), out_shape=jax.Sh...]
    all_to_all x1, blocking collectives: 13.7 us -> 16.3 us  [trade_zl(): return lax.all_to_all(v, 'row', 0, 0, axis_index_groups=groups)]
    ppermute x6, starting transfers between devices: 21 us -> 19 us  [send_y(): return lax.ppermute(v, 'col', pairs)]
  transfers between devices with their start and end apart: 11 -> 11, of which waited for: 7 -> 6; matrix products, arithmetic and copies ran while one was open for 0% -> 0% of each run, Pallas kernels for 4% -> 3%
where the time goes in v8:
time: 194 us; the launch traced here: 192 us
  blocking collectives  113 us (58%)
  starting transfers between devices  43.8 us (23%)
  waiting for transfers between devices  20 us (10%)
  Pallas kernels  12.9 us (7%)
    all_to_all x2, blocking collectives, trade_zh(): return lax.all_to_all(v, 'col', 0, 0, axis_index_groups=groups)  49.2 us
    all_to_all x2, blocking collectives, trade_row(): return lax.all_to_all(v, 'row', 0, 0)  47.5 us
    ppermute x6, starting transfers between devices, send_y(): return lax.ppermute(v, 'col', pairs)  19 us
    all_to_all x1, blocking collectives, trade_zl(): return lax.all_to_all(v, 'row', 0, 0, axis_index_groups=groups)  16.3 us
    ppermute x2, starting transfers between devices, send_core(): return lax.ppermute(v, 'col', [(c, c ^ 1) for c in range(COLS)])  14.9 us
    ppermute x6, waiting for transfers between devices, send_y(): return lax.ppermute(v, 'col', pairs)  12.7 us
    ppermute x3, starting transfers between devices, send_x(): return lax.ppermute(v, 'row', pairs)  9.82 us
    ppermute x3, waiting for transfers between devices, send_x(): return lax.ppermute(v, 'row', pairs)  6.45 us
  transfers between devices with their start and end apart: 11, of which 6 were waited for; matrix products, arithmetic and copies ran while one was open for 0% of the time, Pallas kernels for 3%

profile of v8, /device:TPU:1, one launch (start us, length us, event | category | flops | bytes accessed | tf_op | source)
XLA Modules:
  0.0 192.3 jit_solution(428280097315785238)
XLA Ops:
  0.6 0.0 copy-start.3
  0.6 0.0 copy-start.2
  1.3 0.1 stack.19.where
  1.4 0.9 broadcast_in_dim.2
  2.3 33.7 %all_to_all.25.xs = bf16[16,128,256]{2,1,0:T(8,128)(2,1)S(1)} all-to-all(bf16[16,128,256]{2,1,0:T(8,128)(2,1)S(1)} %broadcast_in_dim.2), channel_id=1, replica_groups=mesh['row'=16,'col'=32] {'row'}, dimensions={0} | all-to-all | bytes 2097152 | tf_op jit(solution)/shard_map/all_to_all | solution.py:38
  36.0 0.0 copy-done.3
  36.0 0.0 copy-done.2
  36.0 2.4 %forward.3 = bf16[16,128,256]{2,1,0:T(8,128)(2,1)S(1)} custom-call(s32[5]{0:T(128)S(1)} %stack.19.where, s32[1,1,128]{2,1,0:T(1,128)S(1)} %copy-done.2, s32[1,1,128]{2,1,0:T(1,128)S(1)} %copy-done.3, bf16[1,1,128,128,128]{4,3,2,1,0:T(8,128)(2,1)} %v.5, bf16[16,128,256]{2,1,0:T(8,128)(2,1)S(1)} %all_to_all.25.xs), custom_call_target="tpu_custom_call" | custom-call | flops 536870912 | bytes 7340032 | tf_op jit(solution)/shard_map/forward/pallas_call | solution.py:160
  38.4 7.0 %collective-permute-start = (bf16[16,128,256]{2,1,0:T(8,128)(2,1)S(1)}, bf16[16,128,256]{2,1,0:T(8,128)(2,1)S(1)}, u32[]{:S(2)}, u32[]{:S(2)}) collective-permute-start(bf16[16,128,256]{2,1,0:T(8,128)(2,1)S(1)} %forward.3), channel_id=1, source_target_pairs={{0,1},{1,0},{2,3},{3,2},{4,5},{5,4},{6,7},{7,6},{8,9},{9,8},{10,11... | collective-permute-start | bytes 3145736 | tf_op jit(solution)/shard_map/ppermute | solution.py:34
  45.4 2.4 %forward.2.a = bf16[16,128,256]{2,1,0:T(8,128)(2,1)S(1)} custom-call(s32[5]{0:T(128)S(1)} %stack.19.where, s32[1,1,128]{2,1,0:T(1,128)S(1)} %copy-done.2, s32[1,1,128]{2,1,0:T(1,128)S(1)} %copy-done.3, bf16[1,1,128,128,128]{4,3,2,1,0:T(8,128)(2,1)} %v.5, bf16[16,128,256]{2,1,0:T(8,128)(2,1)S(1)} %all_to_all.25.xs), custom_call_target="tpu_custom_call" | custom-call | flops 536870912 | bytes 7340032 | tf_op jit(solution)/shard_map/forward/pallas_call | solution.py:160
  47.8 0.0 collective-permute-done.b
  47.8 0.2 pair.1
  48.0 3.1 %collective-permute-start.1 = (bf16[4,128,256]{2,1,0:T(8,128)(2,1)S(1)}, bf16[4,128,256]{2,1,0:T(8,128)(2,1)S(1)}, u32[]{:S(2)}, u32[]{:S(2)}) collective-permute-start(bf16[4,128,256]{2,1,0:T(8,128)(2,1)S(1)} %get-tuple-element.27), channel_id=1, source_target_pairs={{0,4},{1,5},{2,6},{3,7},{4,0},{5,1},{6,2},{7,3},{8,12},{9,13},{10,... | collective-permute-start | bytes 786440 | tf_op jit(solution)/shard_map/ppermute | solution.py:25
  51.2 2.2 %collective-permute-start.2 = (bf16[4,128,256]{2,1,0:T(8,128)(2,1)S(1)}, bf16[4,128,256]{2,1,0:T(8,128)(2,1)S(1)}, u32[]{:S(2)}, u32[]{:S(2)}) collective-permute-start(bf16[4,128,256]{2,1,0:T(8,128)(2,1)S(1)} %get-tuple-element.28), channel_id=1, source_target_pairs={{0,2},{1,3},{2,4},{3,5},{4,6},{5,7},{6,0},{7,1},{8,10},{9,11},{10,... | collective-permute-start | bytes 786440 | tf_op jit(solution)/shard_map/ppermute | solution.py:25
  53.4 0.0 copy-start
  53.4 0.0 copy-start.1
  53.4 4.4 %collective-permute-start.3 = (bf16[4,128,256]{2,1,0:T(8,128)(2,1)S(1)}, bf16[4,128,256]{2,1,0:T(8,128)(2,1)S(1)}, u32[]{:S(2)}, u32[]{:S(2)}) collective-permute-start(bf16[4,128,256]{2,1,0:T(8,128)(2,1)S(1)} %get-tuple-element.29), channel_id=1, source_target_pairs={{0,6},{1,7},{2,0},{3,1},{4,2},{5,3},{6,4},{7,5},{8,14},{9,15},{10,... | collective-permute-start | bytes 786440 | tf_op jit(solution)/shard_map/ppermute | solution.py:25
  57.9 2.0 %turn.1.v = bf16[128,128,128]{2,1,0:T(8,128)(2,1)S(1)} custom-call(s32[5]{0:T(128)S(1)} %stack.19.where, bf16[1,1,128,128,128]{4,3,2,1,0:T(8,128)(2,1)} %v.5), custom_call_target="tpu_custom_call" | custom-call | bytes 10485760 | tf_op jit(solution)/shard_map/turn/pallas_call | solution.py:190
  59.9 0.0 collective-permute-done.1
  59.9 5.2 %collective-permute-done.2 = bf16[4,128,256]{2,1,0:T(8,128)(2,1)S(1)} collective-permute-done((bf16[4,128,256]{2,1,0:T(8,128)(2,1)S(1)}, bf16[4,128,256]{2,1,0:T(8,128)(2,1)S(1)}, u32[]{:S(2)}, u32[]{:S(2)}) %collective-permute-start.2) | collective-permute-done | bytes 262176 | tf_op jit(solution)/shard_map/ppermute | solution.py:25
  65.1 0.0 collective-permute-done.3
  65.1 0.1 add_convert_fusion
  65.3 29.7 %all_to_all.26.got = bf16[4,128,256]{2,1,0:T(8,128)(2,1)S(1)} all-to-all(bf16[4,128,256]{2,1,0:T(8,128)(2,1)S(1)} %add_convert_fusion), channel_id=1, replica_groups={{0,8,16,24},{1,9,17,25},{2,10,18,26},{3,11,19,27},{4,12,20,28},{5,13,21..., dimensions={0} | all-to-all | bytes 524288 | tf_op jit(solution)/shard_map/all_to_all | solution.py:48
  94.9 0.0 copy-done
  94.9 0.0 copy-done.1
  94.9 0.8 middle.1
  95.8 13.8 %all_to_all.27.parts = bf16[16,16,256]{2,1,0:T(8,128)(2,1)S(1)} all-to-all(bf16[16,16,256]{2,1,0:T(8,128)(2,1)S(1)} %get-tuple-element.34), channel_id=1, replica_groups=mesh['row'=16,'col'=32] {'row'}, dimensions={0} | all-to-all | bytes 262144 | tf_op jit(solution)/shard_map/all_to_all | solution.py:38
  109.7 19.5 %all_to_all.28.got = bf16[4,144,256]{2,1,0:T(8,128)(2,1)S(1)} all-to-all(bf16[4,144,256]{2,1,0:T(8,128)(2,1)S(1)} %pack.1), channel_id=1, replica_groups={{0,8,16,24},{1,9,17,25},{2,10,18,26},{3,11,19,27},{4,12,20,28},{5,13,21..., dimensions={0} | all-to-all | bytes 589824 | tf_op jit(solution)/shard_map/all_to_all | solution.py:48
  129.2 4.7 %collective-permute-start.6 = (bf16[528,256]{1,0:T(8,128)(2,1)S(1)}, bf16[528,256]{1,0:T(8,128)(2,1)S(1)}, u32[]{:S(2)}, u32[]{:S(2)}) collective-permute-start(bf16[528,256]{1,0:T(8,128)(2,1)S(1)} %fold.1.l0), channel_id=1, source_target_pairs={{0,6},{1,7},{2,0},{3,1},{4,2},{5,3},{6,4},{7,5},{8,14},{9,15},{10,... | collective-permute-start | bytes 811016 | tf_op jit(solution)/shard_map/ppermute | solution.py:25
  133.9 2.0 %collective-permute-start.5 = (bf16[528,256]{1,0:T(8,128)(2,1)S(1)}, bf16[528,256]{1,0:T(8,128)(2,1)S(1)}, u32[]{:S(2)}, u32[]{:S(2)}) collective-permute-start(bf16[528,256]{1,0:T(8,128)(2,1)S(1)} %fold.1.l0), channel_id=1, source_target_pairs={{0,4},{1,5},{2,6},{3,7},{4,0},{5,1},{6,2},{7,3},{8,12},{9,13},{10,... | collective-permute-start | bytes 811016 | tf_op jit(solution)/shard_map/ppermute | solution.py:25
  135.9 2.6 %collective-permute-start.4 = (bf16[528,256]{1,0:T(8,128)(2,1)S(1)}, bf16[528,256]{1,0:T(8,128)(2,1)S(1)}, u32[]{:S(2)}, u32[]{:S(2)}) collective-permute-start(bf16[528,256]{1,0:T(8,128)(2,1)S(1)} %fold.1.l0), channel_id=1, source_target_pairs={{0,2},{1,3},{2,4},{3,5},{4,6},{5,7},{6,0},{7,1},{8,10},{9,11},{10,... | collective-permute-start | bytes 811016 | tf_op jit(solution)/shard_map/ppermute | solution.py:25
  138.5 0.6 collective-permute-done.6.l3
  139.1 3.6 %collective-permute-done.5.l2 = bf16[528,256]{1,0:T(8,128)(2,1)S(1)} collective-permute-done((bf16[528,256]{1,0:T(8,128)(2,1)S(1)}, bf16[528,256]{1,0:T(8,128)(2,1)S(1)}, u32[]{:S(2)}, u32[]{:S(2)}) %collective-permute-start.5) | collective-permute-done | bytes 270368 | tf_op jit(solution)/shard_map/ppermute | solution.py:25
  142.7 3.3 %collective-permute-done.4.l1 = bf16[528,256]{1,0:T(8,128)(2,1)S(1)} collective-permute-done((bf16[528,256]{1,0:T(8,128)(2,1)S(1)}, bf16[528,256]{1,0:T(8,128)(2,1)S(1)}, u32[]{:S(2)}, u32[]{:S(2)}) %collective-permute-start.4) | collective-permute-done | bytes 270368 | tf_op jit(solution)/shard_map/ppermute | solution.py:25
  146.0 0.6 collect.1.grads.mine
  146.6 7.9 %collective-permute-start.7 = (bf16[2064,256]{1,0:T(8,128)(2,1)S(1)}, bf16[2064,256]{1,0:T(8,128)(2,1)S(1)}, u32[]{:S(2)}, u32[]{:S(2)}) collective-permute-start(bf16[2064,256]{1,0:T(8,128)(2,1)S(1)} %collect.1.grads.mine), channel_id=1, source_target_pairs={{0,1},{1,0},{2,3},{3,2},{4,5},{5,4},{6,7},{7,6},{8,9},{9,8},{10,11... | collective-permute-start | bytes 3170312 | tf_op jit(solution)/shard_map/ppermute | solution.py:34
  154.5 1.4 first.1.start
  156.0 0.8 collective-permute-done.7.grads
  156.8 1.4 second.1
  158.2 3.3 %collective-permute-start.8 = (bf16[528,256]{1,0:T(8,128)(2,1)S(1)}, bf16[528,256]{1,0:T(8,128)(2,1)S(1)}, u32[]{:S(2)}, u32[]{:S(2)}) collective-permute-start(bf16[528,256]{1,0:T(8,128)(2,1)S(1)} %get-tuple-element.36), channel_id=1, source_target_pairs={{0,64},{32,96},{64,0},{96,32},{128,192},{160,224},{192,128},{224,1... | collective-permute-start | bytes 811016 | tf_op jit(solution)/shard_map/ppermute | solution.py:30
  161.6 2.1 %collective-permute-start.9 = (bf16[528,256]{1,0:T(8,128)(2,1)S(1)}, bf16[528,256]{1,0:T(8,128)(2,1)S(1)}, u32[]{:S(2)}, u32[]{:S(2)}) collective-permute-start(bf16[528,256]{1,0:T(8,128)(2,1)S(1)} %get-tuple-element.37), channel_id=1, source_target_pairs={{0,32},{32,64},{64,96},{96,0},{128,160},{160,192},{192,224},{224,1... | collective-permute-start | bytes 811016 | tf_op jit(solution)/shard_map/ppermute | solution.py:30
  163.7 4.4 %collective-permute-start.10 = (bf16[528,256]{1,0:T(8,128)(2,1)S(1)}, bf16[528,256]{1,0:T(8,128)(2,1)S(1)}, u32[]{:S(2)}, u32[]{:S(2)}) collective-permute-start(bf16[528,256]{1,0:T(8,128)(2,1)S(1)} %get-tuple-element.38), channel_id=1, source_target_pairs={{0,96},{32,0},{64,32},{96,64},{128,224},{160,128},{192,160},{224,1... | collective-permute-start | bytes 811016 | tf_op jit(solution)/shard_map/ppermute | solution.py:30
  168.1 0.0 collective-permute-done.8.p2
  168.1 6.4 %collective-permute-done.9.p1 = bf16[528,256]{1,0:T(8,128)(2,1)S(1)} collective-permute-done((bf16[528,256]{1,0:T(8,128)(2,1)S(1)}, bf16[528,256]{1,0:T(8,128)(2,1)S(1)}, u32[]{:S(2)}, u32[]{:S(2)}) %collective-permute-start.9) | collective-permute-done | bytes 270368 | tf_op jit(solution)/shard_map/ppermute | solution.py:30
  174.5 0.0 collective-permute-done.10.p3
  174.5 0.7 merge.1
  175.2 16.3 %all_to_all.29.got = bf16[4,192,256]{2,1,0:T(8,128)(2,1)S(1)} all-to-all(bf16[4,192,256]{2,1,0:T(8,128)(2,1)S(1)} %merge.1), channel_id=1, replica_groups={{0,128,256,384},{32,160,288,416},{64,192,320,448},{96,224,352,480},{1,1..., dimensions={0} | all-to-all | bytes 786432 | tf_op jit(solution)/shard_map/all_to_all | solution.py:43
  191.5 0.8 last.1
  (2 shorter events, 0.1 us)
Async XLA Ops:
  0.6 35.4 %copy-start.3 = (s32[1,1,128]{2,1,0:T(1,128)S(1)}, s32[1,1,128]{2,1,0:T(1,128)}, u32[]{:S(2)}) copy-start(s32[1,1,128]{2,1,0:T(1,128)} %cols.7) | copy-start | bytes 1540
  0.6 35.4 %copy-start.2 = (s32[1,1,128]{2,1,0:T(1,128)S(1)}, s32[1,1,128]{2,1,0:T(1,128)}, u32[]{:S(2)}) copy-start(s32[1,1,128]{2,1,0:T(1,128)} %rows.7) | copy-start | bytes 1540
  38.4 9.4 %collective-permute-start = (bf16[16,128,256]{2,1,0:T(8,128)(2,1)S(1)}, bf16[16,128,256]{2,1,0:T(8,128)(2,1)S(1)}, u32[]{:S(2)}, u32[]{:S(2)}) collective-permute-start(bf16[16,128,256]{2,1,0:T(8,128)(2,1)S(1)} %forward.3), channel_id=1, source_target_pairs={{0,1},{1,0},{2,3},{3,2},{4,5},{5,4},{6,7},{7,6},{8,9},{9,8},{10,11... | collective-permute-start | bytes 3145736 | tf_op jit(solution)/shard_map/ppermute | solution.py:34
  48.0 11.9 %collective-permute-start.1 = (bf16[4,128,256]{2,1,0:T(8,128)(2,1)S(1)}, bf16[4,128,256]{2,1,0:T(8,128)(2,1)S(1)}, u32[]{:S(2)}, u32[]{:S(2)}) collective-permute-start(bf16[4,128,256]{2,1,0:T(8,128)(2,1)S(1)} %get-tuple-element.27), channel_id=1, source_target_pairs={{0,4},{1,5},{2,6},{3,7},{4,0},{5,1},{6,2},{7,3},{8,12},{9,13},{10,... | collective-permute-start | bytes 786440 | tf_op jit(solution)/shard_map/ppermute | solution.py:25
  51.2 13.9 %collective-permute-start.2 = (bf16[4,128,256]{2,1,0:T(8,128)(2,1)S(1)}, bf16[4,128,256]{2,1,0:T(8,128)(2,1)S(1)}, u32[]{:S(2)}, u32[]{:S(2)}) collective-permute-start(bf16[4,128,256]{2,1,0:T(8,128)(2,1)S(1)} %get-tuple-element.28), channel_id=1, source_target_pairs={{0,2},{1,3},{2,4},{3,5},{4,6},{5,7},{6,0},{7,1},{8,10},{9,11},{10,... | collective-permute-start | bytes 786440 | tf_op jit(solution)/shard_map/ppermute | solution.py:25
  53.4 41.5 %copy-start = (bf16[256,256]{1,0:T(8,128)(2,1)S(1)}, bf16[256,256]{1,0:T(8,128)(2,1)}, u32[]{:S(2)}) copy-start(bf16[256,256]{1,0:T(8,128)(2,1)} %w.3) | copy-start | bytes 393220
  53.4 41.5 %copy-start.1 = (bf16[128,256]{1,0:T(8,128)(2,1)S(1)}, bf16[128,256]{1,0:T(8,128)(2,1)}, u32[]{:S(2)}) copy-start(bf16[128,256]{1,0:T(8,128)(2,1)} %cot.1) | copy-start | bytes 196612
  53.4 11.7 %collective-permute-start.3 = (bf16[4,128,256]{2,1,0:T(8,128)(2,1)S(1)}, bf16[4,128,256]{2,1,0:T(8,128)(2,1)S(1)}, u32[]{:S(2)}, u32[]{:S(2)}) collective-permute-start(bf16[4,128,256]{2,1,0:T(8,128)(2,1)S(1)} %get-tuple-element.29), channel_id=1, source_target_pairs={{0,6},{1,7},{2,0},{3,1},{4,2},{5,3},{6,4},{7,5},{8,14},{9,15},{10,... | collective-permute-start | bytes 786440 | tf_op jit(solution)/shard_map/ppermute | solution.py:25
  129.2 9.9 %collective-permute-start.6 = (bf16[528,256]{1,0:T(8,128)(2,1)S(1)}, bf16[528,256]{1,0:T(8,128)(2,1)S(1)}, u32[]{:S(2)}, u32[]{:S(2)}) collective-permute-start(bf16[528,256]{1,0:T(8,128)(2,1)S(1)} %fold.1.l0), channel_id=1, source_target_pairs={{0,6},{1,7},{2,0},{3,1},{4,2},{5,3},{6,4},{7,5},{8,14},{9,15},{10,... | collective-permute-start | bytes 811016 | tf_op jit(solution)/shard_map/ppermute | solution.py:25
  133.9 8.8 %collective-permute-start.5 = (bf16[528,256]{1,0:T(8,128)(2,1)S(1)}, bf16[528,256]{1,0:T(8,128)(2,1)S(1)}, u32[]{:S(2)}, u32[]{:S(2)}) collective-permute-start(bf16[528,256]{1,0:T(8,128)(2,1)S(1)} %fold.1.l0), channel_id=1, source_target_pairs={{0,4},{1,5},{2,6},{3,7},{4,0},{5,1},{6,2},{7,3},{8,12},{9,13},{10,... | collective-permute-start | bytes 811016 | tf_op jit(solution)/shard_map/ppermute | solution.py:25
  135.9 10.1 %collective-permute-start.4 = (bf16[528,256]{1,0:T(8,128)(2,1)S(1)}, bf16[528,256]{1,0:T(8,128)(2,1)S(1)}, u32[]{:S(2)}, u32[]{:S(2)}) collective-permute-start(bf16[528,256]{1,0:T(8,128)(2,1)S(1)} %fold.1.l0), channel_id=1, source_target_pairs={{0,2},{1,3},{2,4},{3,5},{4,6},{5,7},{6,0},{7,1},{8,10},{9,11},{10,... | collective-permute-start | bytes 811016 | tf_op jit(solution)/shard_map/ppermute | solution.py:25
  146.6 10.2 %collective-permute-start.7 = (bf16[2064,256]{1,0:T(8,128)(2,1)S(1)}, bf16[2064,256]{1,0:T(8,128)(2,1)S(1)}, u32[]{:S(2)}, u32[]{:S(2)}) collective-permute-start(bf16[2064,256]{1,0:T(8,128)(2,1)S(1)} %collect.1.grads.mine), channel_id=1, source_target_pairs={{0,1},{1,0},{2,3},{3,2},{4,5},{5,4},{6,7},{7,6},{8,9},{9,8},{10,11... | collective-permute-start | bytes 3170312 | tf_op jit(solution)/shard_map/ppermute | solution.py:34
  158.2 9.8 %collective-permute-start.8 = (bf16[528,256]{1,0:T(8,128)(2,1)S(1)}, bf16[528,256]{1,0:T(8,128)(2,1)S(1)}, u32[]{:S(2)}, u32[]{:S(2)}) collective-permute-start(bf16[528,256]{1,0:T(8,128)(2,1)S(1)} %get-tuple-element.36), channel_id=1, source_target_pairs={{0,64},{32,96},{64,0},{96,32},{128,192},{160,224},{192,128},{224,1... | collective-permute-start | bytes 811016 | tf_op jit(solution)/shard_map/ppermute | solution.py:30
  161.6 13.0 %collective-permute-start.9 = (bf16[528,256]{1,0:T(8,128)(2,1)S(1)}, bf16[528,256]{1,0:T(8,128)(2,1)S(1)}, u32[]{:S(2)}, u32[]{:S(2)}) collective-permute-start(bf16[528,256]{1,0:T(8,128)(2,1)S(1)} %get-tuple-element.37), channel_id=1, source_target_pairs={{0,32},{32,64},{64,96},{96,0},{128,160},{160,192},{192,224},{224,1... | collective-permute-start | bytes 811016 | tf_op jit(solution)/shard_map/ppermute | solution.py:30
  163.7 10.8 %collective-permute-start.10 = (bf16[528,256]{1,0:T(8,128)(2,1)S(1)}, bf16[528,256]{1,0:T(8,128)(2,1)S(1)}, u32[]{:S(2)}, u32[]{:S(2)}) collective-permute-start(bf16[528,256]{1,0:T(8,128)(2,1)S(1)} %get-tuple-element.38), channel_id=1, source_target_pairs={{0,96},{32,0},{64,32},{96,64},{128,224},{160,128},{192,160},{224,1... | collective-permute-start | bytes 811016 | tf_op jit(solution)/shard_map/ppermute | solution.py:30

commit v9 on v8

--- a/solution.py
+++ b/solution.py
@@ -38,9 +38,8 @@
     return lax.all_to_all(v, "row", 0, 0)
 
 
-def trade_zl(v):
-    groups = [[zl * 4 + x for zl in range(4)] for x in range(4)]
-    return lax.all_to_all(v, "row", 0, 0, axis_index_groups=groups)
+def send_zl(v, k):
+    return lax.ppermute(v, "row", [(r, (r + 4 * k) % ROWS) for r in range(ROWS)])
 
 
 def trade_zh(v):
@@ -355,47 +354,52 @@
     return none, one, two, three
 
 
-def merge_kernel(where, p0, p2, p1, p3, out):
-    x = where[4]
+def merge_kernel(where, p0, p2, p1, p3, o0, o2, o1, o3):
+    x, zl = where[4], where[5]
     parts = (p0, p1, p2, p3)
     extra = p0.shape[0] - 4 * TILE
-    for i in range(4):
-        block = slice(TILE * i, TILE * (i + 1))
+    for i, out in enumerate((o0, o1, o2, o3)):
+        block = pl.ds(pl.multiple_of(((zl + i) & 3) * TILE, TILE), TILE)
         total = p0[block].astype(F32)
         for part in parts[1:]:
             total = total + part[block].astype(F32)
-        out[i, :TILE] = total.astype(BF16)
+        out[:TILE] = total.astype(BF16)
         for k, part in enumerate(parts):
             at = pl.multiple_of(TILE + ((x - k) & 3) * extra, extra)
-            out[i, pl.ds(at, extra)] = part[4 * TILE :]
+            out[pl.ds(at, extra)] = part[4 * TILE :]
 
 
 def merge(where, parts):
     rows, width = parts[0].shape
-    return pl.pallas_call(
+    block = jax.ShapeDtypeStruct((TILE + 4 * (rows - 4 * TILE), width), BF16)
+    none, two, one, three = pl.pallas_call(
         merge_kernel,
-        out_shape=jax.ShapeDtypeStruct((4, TILE + 4 * (rows - 4 * TILE), width), BF16),
+        out_shape=(block,) * 4,
         in_specs=[smem()] + [vmem()] * 4,
-        out_specs=vmem(),
+        out_specs=(vmem(),) * 4,
         compiler_params=params(),
         cost_estimate=cost(0, 2),
         name="merge",
     )(where, parts[0], parts[2], parts[1], parts[3])
-
-
-def last_kernel(scale, got, w, grad_out, weight_out):
-    total = got[0, :TILE].astype(F32)
-    for i in range(1, 4):
-        total = total + got[i, :TILE].astype(F32)
+    return none, one, two, three
+
+
+def last_kernel(scale, where, p0, p2, p1, p3, w, grad_out, weight_out):
+    zl = where[5]
+    parts = (p0, p1, p2, p3)
+    total = p0[:TILE].astype(F32)
+    for part in parts[1:]:
+        total = total + part[:TILE].astype(F32)
     grad_out[...] = lax.dot_general(
         total.astype(BF16), w[...], (((1,), (1,)), ((), ())), preferred_element_type=F32
     ).astype(BF16)
-    extra = got.shape[1] - TILE
-    for i in range(4):
-        weight_out[extra * i : extra * (i + 1)] = got[i, TILE:].astype(F32) * scale
-
-
-def last(got, w, scale):
+    extra = p0.shape[0] - TILE
+    for k, part in enumerate(parts):
+        at = pl.multiple_of(((zl - k) & 3) * extra, extra)
+        weight_out[pl.ds(at, extra)] = part[TILE:].astype(F32) * scale
+
+
+def last(where, parts, w, scale):
     width = w.shape[0]
     return pl.pallas_call(
         functools.partial(last_kernel, scale),
@@ -403,17 +407,19 @@
             jax.ShapeDtypeStruct((TILE, width), BF16),
             jax.ShapeDtypeStruct((width, width), F32),
         ),
+        in_specs=[smem()] + [vmem()] * 5,
+        out_specs=(vmem(), vmem()),
         compiler_params=params(),
         cost_estimate=cost(2 * TILE * width * width, 1),
         name="last",
-    )(got, w)
+    )(where, parts[0], parts[2], parts[1], parts[3], w)
 
 
 def shards(features, weight, tile_values, tile_rows, tile_cols, tile_count, cotangent):
     node_dev = features.shape[0]
     grad_scale = 1.0 / math.sqrt(node_dev * lax.axis_size("row") * lax.axis_size("col"))
     r, c = lax.axis_index("row"), lax.axis_index("col")
-    where = jnp.stack([c >> 3, (c >> 1) & 3, c & 1, tile_count[0, 0], r & 3]).astype(jnp.int32)
+    where = jnp.stack([c >> 3, (c >> 1) & 3, c & 1, tile_count[0, 0], r & 3, r >> 2]).astype(jnp.int32)
 
     features, where = lax.optimization_barrier((features, where))
     xs = trade_row(jnp.broadcast_to(features[None], (ROWS,) + features.shape))
@@ -433,7 +439,9 @@
     mine = collect(where, [line] + [send_y(line, k) for k in (1, 2, 3)])
     spread = backward(*block, turned, mine, send_core(mine))
     spread = [spread[0]] + [send_x(spread[k], k) for k in (1, 2, 3)]
-    grad_features, grad_weight = last(trade_zl(merge(where, spread)), weight, grad_scale)
+    pieces = merge(where, spread)
+    pieces = [pieces[0]] + [send_zl(pieces[k], k) for k in (1, 2, 3)]
+    grad_features, grad_weight = last(where, pieces, weight, grad_scale)
     return (activated, grad_features, grad_weight)
 
 

time: 194 us -> 195 us (level)
  blocking collectives: 113 us -> 99.3 us
  starting transfers between devices: 43.8 us -> 53.7 us
  waiting for transfers between devices: 20 us -> 24.6 us
    all_to_all x1 -> x0, blocking collectives: 16.3 us -> none  [trade_zl(): return lax.all_to_all(v, 'row', 0, 0, axis_index_groups=groups)]
    ppermute x0 -> x3, starting transfers between devices: none -> 12.9 us  [send_zl(): lax.ppermute(v, 'row', [(r, (r + 4 * k) % ROWS) for r in range(ROWS)])]
    all_to_all x2, blocking collectives: 47.5 us -> 52.6 us  [trade_row(): return lax.all_to_all(v, 'row', 0, 0)]
    ppermute x0 -> x3, waiting for transfers between devices: none -> 3.32 us  [send_zl(): lax.ppermute(v, 'row', [(r, (r + 4 * k) % ROWS) for r in range(ROWS)])]
    ppermute x3, waiting for transfers between devices: 6.45 us -> 9.06 us  [send_x(): return lax.ppermute(v, 'row', pairs)]
    all_to_all x2, blocking collectives: 49.2 us -> 46.6 us  [trade_zh(): return lax.all_to_all(v, 'col', 0, 0, axis_index_groups=groups)]
    ppermute x2, starting transfers between devices: 14.9 us -> 12.4 us  [send_core(): return lax.ppermute(v, 'col', [(c, c ^ 1) for c in range(COLS)])]
  transfers between devices with their start and end apart: 11 -> 14, of which waited for: 6 -> 9; matrix products, arithmetic and copies ran while one was open for 0% -> 0% of each run, Pallas kernels for 3% -> 3%
where the time goes in v9:
time: 195 us
  blocking collectives  99.3 us (51%)
  starting transfers between devices  53.7 us (28%)
  waiting for transfers between devices  24.6 us (13%)
  Pallas kernels  14.4 us (7%)
    all_to_all x2, blocking collectives, trade_row(): return lax.all_to_all(v, 'row', 0, 0)  52.6 us
    all_to_all x2, blocking collectives, trade_zh(): return lax.all_to_all(v, 'col', 0, 0, axis_index_groups=groups)  46.6 us
    ppermute x6, starting transfers between devices, send_y(): return lax.ppermute(v, 'col', pairs)  19.9 us
    ppermute x3, starting transfers between devices, send_zl(): lax.ppermute(v, 'row', [(r, (r + 4 * k) % ROWS) for r in range(ROWS)])  12.9 us
    ppermute x2, starting transfers between devices, send_core(): return lax.ppermute(v, 'col', [(c, c ^ 1) for c in range(COLS)])  12.4 us
    ppermute x6, waiting for transfers between devices, send_y(): return lax.ppermute(v, 'col', pairs)  11.4 us
    ppermute x3, waiting for transfers between devices, send_x(): return lax.ppermute(v, 'row', pairs)  9.06 us
    ppermute x3, starting transfers between devices, send_x(): return lax.ppermute(v, 'row', pairs)  8.51 us
  transfers between devices with their start and end apart: 14, of which 9 were waited for; matrix products, arithmetic and copies ran while one was open for 0% of the time, Pallas kernels for 3%

profile of v9, /device:TPU:1, one launch (start us, length us, event | category | flops | bytes accessed | tf_op | source)
XLA Modules:
  0.0 194.7 jit_solution(9108185159626339778)
XLA Ops:
  1.3 0.1 stack.23.where
  1.4 0.9 broadcast_in_dim.2
  2.3 33.7 %all_to_all.20.xs = bf16[16,128,256]{2,1,0:T(8,128)(2,1)S(1)} all-to-all(bf16[16,128,256]{2,1,0:T(8,128)(2,1)S(1)} %broadcast_in_dim.2), channel_id=1, replica_groups=mesh['row'=16,'col'=32] {'row'}, dimensions={0} | all-to-all | bytes 2097152 | tf_op jit(solution)/shard_map/all_to_all | solution.py:38
  36.0 0.0 copy-done.2
  36.0 2.8 %forward.3 = bf16[16,128,256]{2,1,0:T(8,128)(2,1)S(1)} custom-call(s32[6]{0:T(128)S(1)} %stack.23.where, s32[1,1,128]{2,1,0:T(1,128)S(1)} %copy-done.2, s32[1,1,128]{2,1,0:T(1,128)S(1)} %copy-done.3, bf16[1,1,128,128,128]{4,3,2,1,0:T(8,128)(2,1)} %v.5, bf16[16,128,256]{2,1,0:T(8,128)(2,1)S(1)} %all_to_all.20.xs), custom_call_target="tpu_custom_call" | custom-call | flops 536870912 | bytes 7340032 | tf_op jit(solution)/shard_map/forward/pallas_call | solution.py:159
  38.8 4.8 %collective-permute-start = (bf16[16,128,256]{2,1,0:T(8,128)(2,1)S(1)}, bf16[16,128,256]{2,1,0:T(8,128)(2,1)S(1)}, u32[]{:S(2)}, u32[]{:S(2)}) collective-permute-start(bf16[16,128,256]{2,1,0:T(8,128)(2,1)S(1)} %forward.3), channel_id=1, source_target_pairs={{0,1},{1,0},{2,3},{3,2},{4,5},{5,4},{6,7},{7,6},{8,9},{9,8},{10,11... | collective-permute-start | bytes 3145736 | tf_op jit(solution)/shard_map/ppermute | solution.py:34
  43.7 2.4 %forward.2.a = bf16[16,128,256]{2,1,0:T(8,128)(2,1)S(1)} custom-call(s32[6]{0:T(128)S(1)} %stack.23.where, s32[1,1,128]{2,1,0:T(1,128)S(1)} %copy-done.2, s32[1,1,128]{2,1,0:T(1,128)S(1)} %copy-done.3, bf16[1,1,128,128,128]{4,3,2,1,0:T(8,128)(2,1)} %v.5, bf16[16,128,256]{2,1,0:T(8,128)(2,1)S(1)} %all_to_all.20.xs), custom_call_target="tpu_custom_call" | custom-call | flops 536870912 | bytes 7340032 | tf_op jit(solution)/shard_map/forward/pallas_call | solution.py:159
  46.1 0.0 collective-permute-done.b
  46.1 0.2 pair.1
  46.3 5.1 %collective-permute-start.1 = (bf16[4,128,256]{2,1,0:T(8,128)(2,1)S(1)}, bf16[4,128,256]{2,1,0:T(8,128)(2,1)S(1)}, u32[]{:S(2)}, u32[]{:S(2)}) collective-permute-start(bf16[4,128,256]{2,1,0:T(8,128)(2,1)S(1)} %get-tuple-element.31), channel_id=1, source_target_pairs={{0,4},{1,5},{2,6},{3,7},{4,0},{5,1},{6,2},{7,3},{8,12},{9,13},{10,... | collective-permute-start | bytes 786440 | tf_op jit(solution)/shard_map/ppermute | solution.py:25
  51.4 2.7 %collective-permute-start.2 = (bf16[4,128,256]{2,1,0:T(8,128)(2,1)S(1)}, bf16[4,128,256]{2,1,0:T(8,128)(2,1)S(1)}, u32[]{:S(2)}, u32[]{:S(2)}) collective-permute-start(bf16[4,128,256]{2,1,0:T(8,128)(2,1)S(1)} %get-tuple-element.32), channel_id=1, source_target_pairs={{0,2},{1,3},{2,4},{3,5},{4,6},{5,7},{6,0},{7,1},{8,10},{9,11},{10,... | collective-permute-start | bytes 786440 | tf_op jit(solution)/shard_map/ppermute | solution.py:25
  54.1 0.0 copy-start
  54.1 0.0 copy-start.1
  54.1 3.9 %collective-permute-start.3 = (bf16[4,128,256]{2,1,0:T(8,128)(2,1)S(1)}, bf16[4,128,256]{2,1,0:T(8,128)(2,1)S(1)}, u32[]{:S(2)}, u32[]{:S(2)}) collective-permute-start(bf16[4,128,256]{2,1,0:T(8,128)(2,1)S(1)} %get-tuple-element.33), channel_id=1, source_target_pairs={{0,6},{1,7},{2,0},{3,1},{4,2},{5,3},{6,4},{7,5},{8,14},{9,15},{10,... | collective-permute-start | bytes 786440 | tf_op jit(solution)/shard_map/ppermute | solution.py:25
  58.1 2.0 %turn.1.v = bf16[128,128,128]{2,1,0:T(8,128)(2,1)S(1)} custom-call(s32[6]{0:T(128)S(1)} %stack.23.where, bf16[1,1,128,128,128]{4,3,2,1,0:T(8,128)(2,1)} %v.5), custom_call_target="tpu_custom_call" | custom-call | bytes 10485760 | tf_op jit(solution)/shard_map/turn/pallas_call | solution.py:189
  60.1 0.0 collective-permute-done.1
  60.1 3.3 %collective-permute-done.2 = bf16[4,128,256]{2,1,0:T(8,128)(2,1)S(1)} collective-permute-done((bf16[4,128,256]{2,1,0:T(8,128)(2,1)S(1)}, bf16[4,128,256]{2,1,0:T(8,128)(2,1)S(1)}, u32[]{:S(2)}, u32[]{:S(2)}) %collective-permute-start.2) | collective-permute-done | bytes 262176 | tf_op jit(solution)/shard_map/ppermute | solution.py:25
  63.5 0.0 collective-permute-done.3
  63.5 0.1 add_convert_fusion
  63.6 26.7 %all_to_all.21.got = bf16[4,128,256]{2,1,0:T(8,128)(2,1)S(1)} all-to-all(bf16[4,128,256]{2,1,0:T(8,128)(2,1)S(1)} %add_convert_fusion), channel_id=1, replica_groups={{0,8,16,24},{1,9,17,25},{2,10,18,26},{3,11,19,27},{4,12,20,28},{5,13,21..., dimensions={0} | all-to-all | bytes 524288 | tf_op jit(solution)/shard_map/all_to_all | solution.py:47
  90.3 0.8 middle.1
  91.2 19.0 %all_to_all.22.parts = bf16[16,16,256]{2,1,0:T(8,128)(2,1)S(1)} all-to-all(bf16[16,16,256]{2,1,0:T(8,128)(2,1)S(1)} %get-tuple-element.38), channel_id=1, replica_groups=mesh['row'=16,'col'=32] {'row'}, dimensions={0} | all-to-all | bytes 262144 | tf_op jit(solution)/shard_map/all_to_all | solution.py:38
  110.2 19.9 %all_to_all.23.got = bf16[4,144,256]{2,1,0:T(8,128)(2,1)S(1)} all-to-all(bf16[4,144,256]{2,1,0:T(8,128)(2,1)S(1)} %pack.1), channel_id=1, replica_groups={{0,8,16,24},{1,9,17,25},{2,10,18,26},{3,11,19,27},{4,12,20,28},{5,13,21..., dimensions={0} | all-to-all | bytes 589824 | tf_op jit(solution)/shard_map/all_to_all | solution.py:47
  130.1 3.8 %collective-permute-start.6 = (bf16[528,256]{1,0:T(8,128)(2,1)S(1)}, bf16[528,256]{1,0:T(8,128)(2,1)S(1)}, u32[]{:S(2)}, u32[]{:S(2)}) collective-permute-start(bf16[528,256]{1,0:T(8,128)(2,1)S(1)} %fold.1.l0), channel_id=1, source_target_pairs={{0,6},{1,7},{2,0},{3,1},{4,2},{5,3},{6,4},{7,5},{8,14},{9,15},{10,... | collective-permute-start | bytes 811016 | tf_op jit(solution)/shard_map/ppermute | solution.py:25
  134.0 1.9 collective-permute-start.5
  135.9 2.5 %collective-permute-start.4 = (bf16[528,256]{1,0:T(8,128)(2,1)S(1)}, bf16[528,256]{1,0:T(8,128)(2,1)S(1)}, u32[]{:S(2)}, u32[]{:S(2)}) collective-permute-start(bf16[528,256]{1,0:T(8,128)(2,1)S(1)} %fold.1.l0), channel_id=1, source_target_pairs={{0,2},{1,3},{2,4},{3,5},{4,6},{5,7},{6,0},{7,1},{8,10},{9,11},{10,... | collective-permute-start | bytes 811016 | tf_op jit(solution)/shard_map/ppermute | solution.py:25
  138.4 1.3 collective-permute-done.6.l3
  139.7 3.1 %collective-permute-done.5.l2 = bf16[528,256]{1,0:T(8,128)(2,1)S(1)} collective-permute-done((bf16[528,256]{1,0:T(8,128)(2,1)S(1)}, bf16[528,256]{1,0:T(8,128)(2,1)S(1)}, u32[]{:S(2)}, u32[]{:S(2)}) %collective-permute-start.5) | collective-permute-done | bytes 270368 | tf_op jit(solution)/shard_map/ppermute | solution.py:25
  142.8 3.6 %collective-permute-done.4.l1 = bf16[528,256]{1,0:T(8,128)(2,1)S(1)} collective-permute-done((bf16[528,256]{1,0:T(8,128)(2,1)S(1)}, bf16[528,256]{1,0:T(8,128)(2,1)S(1)}, u32[]{:S(2)}, u32[]{:S(2)}) %collective-permute-start.4) | collective-permute-done | bytes 270368 | tf_op jit(solution)/shard_map/ppermute | solution.py:25
  146.4 0.6 collect.1.grads.mine
  147.0 7.6 %collective-permute-start.7 = (bf16[2064,256]{1,0:T(8,128)(2,1)S(1)}, bf16[2064,256]{1,0:T(8,128)(2,1)S(1)}, u32[]{:S(2)}, u32[]{:S(2)}) collective-permute-start(bf16[2064,256]{1,0:T(8,128)(2,1)S(1)} %collect.1.grads.mine), channel_id=1, source_target_pairs={{0,1},{1,0},{2,3},{3,2},{4,5},{5,4},{6,7},{7,6},{8,9},{9,8},{10,11... | collective-permute-start | bytes 3170312 | tf_op jit(solution)/shard_map/ppermute | solution.py:34
  154.6 1.4 first.1.start
  156.0 0.8 collective-permute-done.7.grads
  156.9 1.9 second.1
  158.8 2.0 %collective-permute-start.8 = (bf16[528,256]{1,0:T(8,128)(2,1)S(1)}, bf16[528,256]{1,0:T(8,128)(2,1)S(1)}, u32[]{:S(2)}, u32[]{:S(2)}) collective-permute-start(bf16[528,256]{1,0:T(8,128)(2,1)S(1)} %get-tuple-element.40), channel_id=1, source_target_pairs={{0,64},{32,96},{64,0},{96,32},{128,192},{160,224},{192,128},{224,1... | collective-permute-start | bytes 811016 | tf_op jit(solution)/shard_map/ppermute | solution.py:30
  160.8 2.9 %collective-permute-start.9 = (bf16[528,256]{1,0:T(8,128)(2,1)S(1)}, bf16[528,256]{1,0:T(8,128)(2,1)S(1)}, u32[]{:S(2)}, u32[]{:S(2)}) collective-permute-start(bf16[528,256]{1,0:T(8,128)(2,1)S(1)} %get-tuple-element.41), channel_id=1, source_target_pairs={{0,32},{32,64},{64,96},{96,0},{128,160},{160,192},{192,224},{224,1... | collective-permute-start | bytes 811016 | tf_op jit(solution)/shard_map/ppermute | solution.py:30
  163.7 3.6 %collective-permute-start.10 = (bf16[528,256]{1,0:T(8,128)(2,1)S(1)}, bf16[528,256]{1,0:T(8,128)(2,1)S(1)}, u32[]{:S(2)}, u32[]{:S(2)}) collective-permute-start(bf16[528,256]{1,0:T(8,128)(2,1)S(1)} %get-tuple-element.42), channel_id=1, source_target_pairs={{0,96},{32,0},{64,32},{96,64},{128,224},{160,128},{192,160},{224,1... | collective-permute-start | bytes 811016 | tf_op jit(solution)/shard_map/ppermute | solution.py:30
  167.3 2.4 %collective-permute-done.8.p2 = bf16[528,256]{1,0:T(8,128)(2,1)S(1)} collective-permute-done((bf16[528,256]{1,0:T(8,128)(2,1)S(1)}, bf16[528,256]{1,0:T(8,128)(2,1)S(1)}, u32[]{:S(2)}, u32[]{:S(2)}) %collective-permute-start.8) | collective-permute-done | bytes 270368 | tf_op jit(solution)/shard_map/ppermute | solution.py:30
  169.7 6.6 %collective-permute-done.9.p1 = bf16[528,256]{1,0:T(8,128)(2,1)S(1)} collective-permute-done((bf16[528,256]{1,0:T(8,128)(2,1)S(1)}, bf16[528,256]{1,0:T(8,128)(2,1)S(1)}, u32[]{:S(2)}, u32[]{:S(2)}) %collective-permute-start.9) | collective-permute-done | bytes 270368 | tf_op jit(solution)/shard_map/ppermute | solution.py:30
  176.4 0.0 collective-permute-done.10.p3
  176.4 0.7 merge.1
  177.0 5.8 %collective-permute-start.11 = (bf16[192,256]{1,0:T(8,128)(2,1)S(1)}, bf16[192,256]{1,0:T(8,128)(2,1)S(1)}, u32[]{:S(2)}, u32[]{:S(2)}) collective-permute-start(bf16[192,256]{1,0:T(8,128)(2,1)S(1)} %get-tuple-element.44), channel_id=1, source_target_pairs={{0,256},{32,288},{64,320},{96,352},{128,384},{160,416},{192,448},{... | collective-permute-start | bytes 294920 | tf_op jit(solution)/shard_map/ppermute | solution.py:42
  182.9 1.9 collective-permute-start.12
  184.8 5.2 %collective-permute-start.13 = (bf16[192,256]{1,0:T(8,128)(2,1)S(1)}, bf16[192,256]{1,0:T(8,128)(2,1)S(1)}, u32[]{:S(2)}, u32[]{:S(2)}) collective-permute-start(bf16[192,256]{1,0:T(8,128)(2,1)S(1)} %get-tuple-element.46), channel_id=1, source_target_pairs={{0,384},{32,416},{64,448},{96,480},{128,0},{160,32},{192,64},{224,... | collective-permute-start | bytes 294920 | tf_op jit(solution)/shard_map/ppermute | solution.py:42
  190.0 0.0 collective-permute-done.11.p2
  190.0 0.2 collective-permute-done.12.p1
  190.1 3.2 %collective-permute-done.13.p3 = bf16[192,256]{1,0:T(8,128)(2,1)S(1)} collective-permute-done((bf16[192,256]{1,0:T(8,128)(2,1)S(1)}, bf16[192,256]{1,0:T(8,128)(2,1)S(1)}, u32[]{:S(2)}, u32[]{:S(2)}) %collective-permute-start.13) | collective-permute-done | bytes 98336 | tf_op jit(solution)/shard_map/ppermute | solution.py:42
  193.3 1.4 last.1
  (7 shorter events, 0.1 us)
Async XLA Ops:
  0.6 35.4 %copy-start.3 = (s32[1,1,128]{2,1,0:T(1,128)S(1)}, s32[1,1,128]{2,1,0:T(1,128)}, u32[]{:S(2)}) copy-start(s32[1,1,128]{2,1,0:T(1,128)} %cols.7) | copy-start | bytes 1540
  0.6 35.4 %copy-start.2 = (s32[1,1,128]{2,1,0:T(1,128)S(1)}, s32[1,1,128]{2,1,0:T(1,128)}, u32[]{:S(2)}) copy-start(s32[1,1,128]{2,1,0:T(1,128)} %rows.7) | copy-start | bytes 1540
  38.8 7.2 %collective-permute-start = (bf16[16,128,256]{2,1,0:T(8,128)(2,1)S(1)}, bf16[16,128,256]{2,1,0:T(8,128)(2,1)S(1)}, u32[]{:S(2)}, u32[]{:S(2)}) collective-permute-start(bf16[16,128,256]{2,1,0:T(8,128)(2,1)S(1)} %forward.3), channel_id=1, source_target_pairs={{0,1},{1,0},{2,3},{3,2},{4,5},{5,4},{6,7},{7,6},{8,9},{9,8},{10,11... | collective-permute-start | bytes 3145736 | tf_op jit(solution)/shard_map/ppermute | solution.py:34
  46.3 13.8 %collective-permute-start.1 = (bf16[4,128,256]{2,1,0:T(8,128)(2,1)S(1)}, bf16[4,128,256]{2,1,0:T(8,128)(2,1)S(1)}, u32[]{:S(2)}, u32[]{:S(2)}) collective-permute-start(bf16[4,128,256]{2,1,0:T(8,128)(2,1)S(1)} %get-tuple-element.31), channel_id=1, source_target_pairs={{0,4},{1,5},{2,6},{3,7},{4,0},{5,1},{6,2},{7,3},{8,12},{9,13},{10,... | collective-permute-start | bytes 786440 | tf_op jit(solution)/shard_map/ppermute | solution.py:25
  51.4 12.1 %collective-permute-start.2 = (bf16[4,128,256]{2,1,0:T(8,128)(2,1)S(1)}, bf16[4,128,256]{2,1,0:T(8,128)(2,1)S(1)}, u32[]{:S(2)}, u32[]{:S(2)}) collective-permute-start(bf16[4,128,256]{2,1,0:T(8,128)(2,1)S(1)} %get-tuple-element.32), channel_id=1, source_target_pairs={{0,2},{1,3},{2,4},{3,5},{4,6},{5,7},{6,0},{7,1},{8,10},{9,11},{10,... | collective-permute-start | bytes 786440 | tf_op jit(solution)/shard_map/ppermute | solution.py:25
  54.1 36.2 %copy-start = (bf16[256,256]{1,0:T(8,128)(2,1)S(1)}, bf16[256,256]{1,0:T(8,128)(2,1)}, u32[]{:S(2)}) copy-start(bf16[256,256]{1,0:T(8,128)(2,1)} %w.3) | copy-start | bytes 393220
  54.1 36.2 %copy-start.1 = (bf16[128,256]{1,0:T(8,128)(2,1)S(1)}, bf16[128,256]{1,0:T(8,128)(2,1)}, u32[]{:S(2)}) copy-start(bf16[128,256]{1,0:T(8,128)(2,1)} %cot.1) | copy-start | bytes 196612
  54.1 9.4 %collective-permute-start.3 = (bf16[4,128,256]{2,1,0:T(8,128)(2,1)S(1)}, bf16[4,128,256]{2,1,0:T(8,128)(2,1)S(1)}, u32[]{:S(2)}, u32[]{:S(2)}) collective-permute-start(bf16[4,128,256]{2,1,0:T(8,128)(2,1)S(1)} %get-tuple-element.33), channel_id=1, source_target_pairs={{0,6},{1,7},{2,0},{3,1},{4,2},{5,3},{6,4},{7,5},{8,14},{9,15},{10,... | collective-permute-start | bytes 786440 | tf_op jit(solution)/shard_map/ppermute | solution.py:25
  130.1 9.5 %collective-permute-start.6 = (bf16[528,256]{1,0:T(8,128)(2,1)S(1)}, bf16[528,256]{1,0:T(8,128)(2,1)S(1)}, u32[]{:S(2)}, u32[]{:S(2)}) collective-permute-start(bf16[528,256]{1,0:T(8,128)(2,1)S(1)} %fold.1.l0), channel_id=1, source_target_pairs={{0,6},{1,7},{2,0},{3,1},{4,2},{5,3},{6,4},{7,5},{8,14},{9,15},{10,... | collective-permute-start | bytes 811016 | tf_op jit(solution)/shard_map/ppermute | solution.py:25
  134.0 8.8 %collective-permute-start.5 = (bf16[528,256]{1,0:T(8,128)(2,1)S(1)}, bf16[528,256]{1,0:T(8,128)(2,1)S(1)}, u32[]{:S(2)}, u32[]{:S(2)}) collective-permute-start(bf16[528,256]{1,0:T(8,128)(2,1)S(1)} %fold.1.l0), channel_id=1, source_target_pairs={{0,4},{1,5},{2,6},{3,7},{4,0},{5,1},{6,2},{7,3},{8,12},{9,13},{10,... | collective-permute-start | bytes 811016 | tf_op jit(solution)/shard_map/ppermute | solution.py:25
  135.9 10.5 %collective-permute-start.4 = (bf16[528,256]{1,0:T(8,128)(2,1)S(1)}, bf16[528,256]{1,0:T(8,128)(2,1)S(1)}, u32[]{:S(2)}, u32[]{:S(2)}) collective-permute-start(bf16[528,256]{1,0:T(8,128)(2,1)S(1)} %fold.1.l0), channel_id=1, source_target_pairs={{0,2},{1,3},{2,4},{3,5},{4,6},{5,7},{6,0},{7,1},{8,10},{9,11},{10,... | collective-permute-start | bytes 811016 | tf_op jit(solution)/shard_map/ppermute | solution.py:25
  147.0 9.8 %collective-permute-start.7 = (bf16[2064,256]{1,0:T(8,128)(2,1)S(1)}, bf16[2064,256]{1,0:T(8,128)(2,1)S(1)}, u32[]{:S(2)}, u32[]{:S(2)}) collective-permute-start(bf16[2064,256]{1,0:T(8,128)(2,1)S(1)} %collect.1.grads.mine), channel_id=1, source_target_pairs={{0,1},{1,0},{2,3},{3,2},{4,5},{5,4},{6,7},{7,6},{8,9},{9,8},{10,11... | collective-permute-start | bytes 3170312 | tf_op jit(solution)/shard_map/ppermute | solution.py:34
  158.8 11.0 %collective-permute-start.8 = (bf16[528,256]{1,0:T(8,128)(2,1)S(1)}, bf16[528,256]{1,0:T(8,128)(2,1)S(1)}, u32[]{:S(2)}, u32[]{:S(2)}) collective-permute-start(bf16[528,256]{1,0:T(8,128)(2,1)S(1)} %get-tuple-element.40), channel_id=1, source_target_pairs={{0,64},{32,96},{64,0},{96,32},{128,192},{160,224},{192,128},{224,1... | collective-permute-start | bytes 811016 | tf_op jit(solution)/shard_map/ppermute | solution.py:30
  160.8 15.6 %collective-permute-start.9 = (bf16[528,256]{1,0:T(8,128)(2,1)S(1)}, bf16[528,256]{1,0:T(8,128)(2,1)S(1)}, u32[]{:S(2)}, u32[]{:S(2)}) collective-permute-start(bf16[528,256]{1,0:T(8,128)(2,1)S(1)} %get-tuple-element.41), channel_id=1, source_target_pairs={{0,32},{32,64},{64,96},{96,0},{128,160},{160,192},{192,224},{224,1... | collective-permute-start | bytes 811016 | tf_op jit(solution)/shard_map/ppermute | solution.py:30
  163.7 12.7 %collective-permute-start.10 = (bf16[528,256]{1,0:T(8,128)(2,1)S(1)}, bf16[528,256]{1,0:T(8,128)(2,1)S(1)}, u32[]{:S(2)}, u32[]{:S(2)}) collective-permute-start(bf16[528,256]{1,0:T(8,128)(2,1)S(1)} %get-tuple-element.42), channel_id=1, source_target_pairs={{0,96},{32,0},{64,32},{96,64},{128,224},{160,128},{192,160},{224,1... | collective-permute-start | bytes 811016 | tf_op jit(solution)/shard_map/ppermute | solution.py:30
  177.0 12.9 %collective-permute-start.11 = (bf16[192,256]{1,0:T(8,128)(2,1)S(1)}, bf16[192,256]{1,0:T(8,128)(2,1)S(1)}, u32[]{:S(2)}, u32[]{:S(2)}) collective-permute-start(bf16[192,256]{1,0:T(8,128)(2,1)S(1)} %get-tuple-element.44), channel_id=1, source_target_pairs={{0,256},{32,288},{64,320},{96,352},{128,384},{160,416},{192,448},{... | collective-permute-start | bytes 294920 | tf_op jit(solution)/shard_map/ppermute | solution.py:42
  182.9 7.3 %collective-permute-start.12 = (bf16[192,256]{1,0:T(8,128)(2,1)S(1)}, bf16[192,256]{1,0:T(8,128)(2,1)S(1)}, u32[]{:S(2)}, u32[]{:S(2)}) collective-permute-start(bf16[192,256]{1,0:T(8,128)(2,1)S(1)} %get-tuple-element.45), channel_id=1, source_target_pairs={{0,128},{32,160},{64,192},{96,224},{128,256},{160,288},{192,320},{... | collective-permute-start | bytes 294920 | tf_op jit(solution)/shard_map/ppermute | solution.py:42
  184.8 8.5 %collective-permute-start.13 = (bf16[192,256]{1,0:T(8,128)(2,1)S(1)}, bf16[192,256]{1,0:T(8,128)(2,1)S(1)}, u32[]{:S(2)}, u32[]{:S(2)}) collective-permute-start(bf16[192,256]{1,0:T(8,128)(2,1)S(1)} %get-tuple-element.46), channel_id=1, source_target_pairs={{0,384},{32,416},{64,448},{96,480},{128,0},{160,32},{192,64},{224,... | collective-permute-start | bytes 294920 | tf_op jit(solution)/shard_map/ppermute | solution.py:42

commit v10 on v8

--- a/solution.py
+++ b/solution.py
@@ -20,14 +20,28 @@
 F32 = jnp.float32
 
 
-def send_y(v, k):
-    pairs = [(c, (c // 8) * 8 + ((c // 2 + k) % 4) * 2 + c % 2) for c in range(COLS)]
+FIRST, SECOND, TWO = 0, 1, 2
+
+
+def distance(which, core):
+    return 2 if which == TWO else 1 + 2 * (core ^ which)
+
+
+def send_y(v, which):
+    pairs = []
+    for c in range(COLS):
+        zh, y, core = c // 8, (c // 2) % 4, c % 2
+        pairs.append((c, zh * 8 + (y + distance(which, core)) % 4 * 2 + core))
     return lax.ppermute(v, "col", pairs)
 
 
-def send_x(v, k):
-    pairs = [(r, (r // 4) * 4 + (r + k) % 4) for r in range(ROWS)]
-    return lax.ppermute(v, "row", pairs)
+def send_x(v, which):
+    pairs = []
+    for r in range(ROWS):
+        for c in range(COLS):
+            to = r // 4 * 4 + (r + distance(which, c % 2)) % 4
+            pairs.append((r * COLS + c, to * COLS + c))
+    return lax.ppermute(v, ("row", "col"), pairs)
 
 
 def send_core(v):
@@ -97,22 +111,27 @@
     pl.when(done < found)(lambda: group(found, done))
 
 
-def pair_kernel(a, b, o0, o2, o1, o3):
-    for k, out in enumerate((o0, o1, o2, o3)):
-        block = slice(4 * k, 4 * (k + 1))
-        out[...] = (a[block].astype(F32) + b[block].astype(F32)).astype(BF16)
-
-
-def pair(a, b):
+def distances(core):
+    return (0, 2, 1 + 2 * core, 3 - 2 * core)
+
+
+def pair_kernel(where, a, b, *outs):
+    for k, out in zip(distances(where[2]), outs):
+        span = pl.ds(4 * k, 4)
+        out[...] = (a[span].astype(F32) + b[span].astype(F32)).astype(BF16)
+
+
+def pair(where, a, b):
     block = jax.ShapeDtypeStruct((4,) + a.shape[1:], BF16)
-    none, two, one, three = pl.pallas_call(
+    return pl.pallas_call(
         pair_kernel,
         out_shape=(block,) * 4,
+        in_specs=[smem()] + [vmem()] * 2,
+        out_specs=(vmem(),) * 4,
         compiler_params=params(),
         cost_estimate=cost(0, 4),
         name="pair",
-    )(a, b)
-    return none, one, two, three
+    )(where, a, b)
 
 
 def fetch_chunks(live, v, tiles, sems):
@@ -269,11 +288,11 @@
     )(got)
 
 
-def collect_kernel(where, l0, l1, l2, l3, out, slices):
+def collect_kernel(where, stays, first, second, two, out, slices):
     y = where[1]
     rows = 4 * TILE
-    for k, line in enumerate((l0, l1, l2, l3)):
-        out[rows * k : rows * (k + 1)] = line[:rows]
+    for k, line in zip(distances(where[2]), (stays, two, first, second)):
+        out[pl.ds(pl.multiple_of(rows * k, rows), rows)] = line[:rows]
         slices[(y - k) & 3] = line[rows:].astype(F32)
     out[4 * rows :] = ((slices[0] + slices[1]) + (slices[2] + slices[3])).astype(BF16)
 
@@ -316,13 +335,13 @@
     out[...] = acc[:HALF]
 
 
-def second_kernel(where, rows, cols, v, grads, mine, start, o0, o2, o1, o3, slots, acc):
+def second_kernel(where, rows, cols, v, grads, mine, start, o0, o1, o2, o3, slots, acc):
     acc[:HALF] = start[...]
     acc[HALF] = jnp.zeros_like(acc[HALF])
     backward_half(1, where, rows, cols, v, grads, slots, acc)
     rest = HALF * TILE
     part = (mine[rest:].astype(F32) + grads[rest:].astype(F32)).astype(BF16)
-    for k, out in enumerate((o0, o1, o2, o3)):
+    for k, out in zip(distances(where[2]), (o0, o1, o2, o3)):
         for i in range(4):
             out[TILE * i : TILE * (i + 1)] = acc[4 * k + i].astype(BF16)
         out[4 * TILE :] = part
@@ -342,7 +361,7 @@
         cost_estimate=work,
         name="first",
     )(where, rows, cols, v, mine)
-    none, two, one, three = pl.pallas_call(
+    return pl.pallas_call(
         second_kernel,
         out_shape=(jax.ShapeDtypeStruct((4 * TILE + extra, width), BF16),) * 4,
         in_specs=[smem()] * 3 + [vmem()] * 4,
@@ -352,10 +371,8 @@
         cost_estimate=work,
         name="second",
     )(where, rows, cols, v, theirs, mine, first)
-    return none, one, two, three
-
-
-def merge_kernel(where, p0, p2, p1, p3, out):
+
+def merge_kernel(where, p0, p1, p2, p3, out):
     x = where[4]
     parts = (p0, p1, p2, p3)
     extra = p0.shape[0] - 4 * TILE
@@ -365,7 +382,7 @@
         for part in parts[1:]:
             total = total + part[block].astype(F32)
         out[i, :TILE] = total.astype(BF16)
-        for k, part in enumerate(parts):
+        for k, part in zip(distances(where[2]), parts):
             at = pl.multiple_of(TILE + ((x - k) & 3) * extra, extra)
             out[i, pl.ds(at, extra)] = part[4 * TILE :]
 
@@ -380,7 +397,7 @@
         compiler_params=params(),
         cost_estimate=cost(0, 2),
         name="merge",
-    )(where, parts[0], parts[2], parts[1], parts[3])
+    )(where, *parts)
 
 
 def last_kernel(scale, got, w, grad_out, weight_out):
@@ -421,8 +438,8 @@
     block = (where, tile_rows, tile_cols)
     got = send_core(forward(1, *block, tile_values, xs))
     keep = forward(0, *block, tile_values, xs)
-    paired = pair(keep, got)
-    got = [paired[0]] + [send_y(paired[k], k) for k in (2, 1, 3)]
+    stays, two, first, second = pair(where, keep, got)
+    got = [stays, send_y(two, TWO), send_y(first, FIRST), send_y(second, SECOND)]
     got = [v.astype(F32) for v in got]
     rows = (got[0] + got[1] + got[2] + got[3]).astype(BF16)
     turned = turn_tiles(where, tile_values)
@@ -430,9 +447,9 @@
     activated, grad_pre, part = middle(trade_zh(rows), weight, cotangent)
 
     line = fold(trade_zh(pack(grad_pre, trade_row(part))))
-    mine = collect(where, [line] + [send_y(line, k) for k in (1, 2, 3)])
-    spread = backward(*block, turned, mine, send_core(mine))
-    spread = [spread[0]] + [send_x(spread[k], k) for k in (1, 2, 3)]
+    mine = collect(where, [line] + [send_y(line, which) for which in (FIRST, SECOND, TWO)])
+    stays, two, first, second = backward(*block, turned, mine, send_core(mine))
+    spread = [stays, send_x(two, TWO), send_x(first, FIRST), send_x(second, SECOND)]
     grad_features, grad_weight = last(trade_zl(merge(where, spread)), weight, grad_scale)
     return (activated, grad_features, grad_weight)
 

time: 194 us -> 194 us (level)
  Pallas kernels: 12.9 us -> 16.3 us
  waiting for transfers between devices: 20 us -> 17.7 us
    all_to_all x2, blocking collectives: 47.5 us -> 53 us  [trade_row(): return lax.all_to_all(v, 'row', 0, 0)]
    all_to_all x2, blocking collectives: 49.2 us -> 45 us  [trade_zh(): return lax.all_to_all(v, 'col', 0, 0, axis_index_groups=groups)]
    ppermute x2, starting transfers between devices: 14.9 us -> 11.6 us  [send_core(): return lax.ppermute(v, 'col', [(c, c ^ 1) for c in range(COLS)])]
  transfers between devices with their start and end apart: 11 -> 11, of which waited for: 6 -> 8; matrix products, arithmetic and copies ran while one was open for 0% -> 0% of each run, Pallas kernels for 3% -> 4%
where the time goes in v10:
time: 194 us
  blocking collectives  114 us (59%)
  starting transfers between devices  43 us (22%)
  waiting for transfers between devices  17.7 us (9%)
  Pallas kernels  16.3 us (8%)
    all_to_all x2, blocking collectives, trade_row(): return lax.all_to_all(v, 'row', 0, 0)  53 us
    all_to_all x2, blocking collectives, trade_zh(): return lax.all_to_all(v, 'col', 0, 0, axis_index_groups=groups)  45 us
    ppermute x6, starting transfers between devices, send_y(): return lax.ppermute(v, 'col', pairs)  20.6 us
    all_to_all x1, blocking collectives, trade_zl(): return lax.all_to_all(v, 'row', 0, 0, axis_index_groups=groups)  16 us
    ppermute x2, starting transfers between devices, send_core(): return lax.ppermute(v, 'col', [(c, c ^ 1) for c in range(COLS)])  11.6 us
    ppermute x6, waiting for transfers between devices, send_y(): return lax.ppermute(v, 'col', pairs)  10.8 us
    ppermute x3, starting transfers between devices, send_x(): return lax.ppermute(v, ('row', 'col'), pairs)  10.7 us
    ppermute x3, waiting for transfers between devices, send_x(): return lax.ppermute(v, ('row', 'col'), pairs)  6.64 us
  transfers between devices with their start and end apart: 11, of which 8 were waited for; matrix products, arithmetic and copies ran while one was open for 0% of the time, Pallas kernels for 4%

profile of v10, /device:TPU:1, one launch (start us, length us, event | category | flops | bytes accessed | tf_op | source)
XLA Modules:
  0.0 193.7 jit_solution(9010103637091478460)
XLA Ops:
  0.6 0.0 copy-start.3
  0.6 0.0 copy-start.2
  1.3 0.1 stack.19.where
  1.4 0.9 broadcast_in_dim.2
  2.3 33.7 %all_to_all.25.xs = bf16[16,128,256]{2,1,0:T(8,128)(2,1)S(1)} all-to-all(bf16[16,128,256]{2,1,0:T(8,128)(2,1)S(1)} %broadcast_in_dim.2), channel_id=1, replica_groups=mesh['row'=16,'col'=32] {'row'}, dimensions={0} | all-to-all | bytes 2097152 | tf_op jit(solution)/shard_map/all_to_all | solution.py:52
  36.0 0.0 copy-done.3
  36.0 0.0 copy-done.2
  36.0 3.0 %forward.3 = bf16[16,128,256]{2,1,0:T(8,128)(2,1)S(1)} custom-call(s32[5]{0:T(128)S(1)} %stack.19.where, s32[1,1,128]{2,1,0:T(1,128)S(1)} %copy-done.2, s32[1,1,128]{2,1,0:T(1,128)S(1)} %copy-done.3, bf16[1,1,128,128,128]{4,3,2,1,0:T(8,128)(2,1)} %v.5, bf16[16,128,256]{2,1,0:T(8,128)(2,1)S(1)} %all_to_all.25.xs), custom_call_target="tpu_custom_call" | custom-call | flops 536870912 | bytes 7340032 | tf_op jit(solution)/shard_map/forward/pallas_call | solution.py:179
  39.0 4.6 %collective-permute-start = (bf16[16,128,256]{2,1,0:T(8,128)(2,1)S(1)}, bf16[16,128,256]{2,1,0:T(8,128)(2,1)S(1)}, u32[]{:S(2)}, u32[]{:S(2)}) collective-permute-start(bf16[16,128,256]{2,1,0:T(8,128)(2,1)S(1)} %forward.3), channel_id=1, source_target_pairs={{0,1},{1,0},{2,3},{3,2},{4,5},{5,4},{6,7},{7,6},{8,9},{9,8},{10,11... | collective-permute-start | bytes 3145736 | tf_op jit(solution)/shard_map/ppermute | solution.py:48
  43.6 3.1 %forward.2.a = bf16[16,128,256]{2,1,0:T(8,128)(2,1)S(1)} custom-call(s32[5]{0:T(128)S(1)} %stack.19.where, s32[1,1,128]{2,1,0:T(1,128)S(1)} %copy-done.2, s32[1,1,128]{2,1,0:T(1,128)S(1)} %copy-done.3, bf16[1,1,128,128,128]{4,3,2,1,0:T(8,128)(2,1)} %v.5, bf16[16,128,256]{2,1,0:T(8,128)(2,1)S(1)} %all_to_all.25.xs), custom_call_target="tpu_custom_call" | custom-call | flops 536870912 | bytes 7340032 | tf_op jit(solution)/shard_map/forward/pallas_call | solution.py:179
  46.7 0.0 collective-permute-done.b
  46.7 0.8 pair.1
  47.5 4.1 %collective-permute-start.1 = (bf16[4,128,256]{2,1,0:T(8,128)(2,1)S(1)}, bf16[4,128,256]{2,1,0:T(8,128)(2,1)S(1)}, u32[]{:S(2)}, u32[]{:S(2)}) collective-permute-start(bf16[4,128,256]{2,1,0:T(8,128)(2,1)S(1)} %get-tuple-element.27), channel_id=1, source_target_pairs={{0,4},{1,5},{2,6},{3,7},{4,0},{5,1},{6,2},{7,3},{8,12},{9,13},{10,... | collective-permute-start | bytes 786440 | tf_op jit(solution)/shard_map/ppermute | solution.py:35
  51.6 2.3 %collective-permute-start.2 = (bf16[4,128,256]{2,1,0:T(8,128)(2,1)S(1)}, bf16[4,128,256]{2,1,0:T(8,128)(2,1)S(1)}, u32[]{:S(2)}, u32[]{:S(2)}) collective-permute-start(bf16[4,128,256]{2,1,0:T(8,128)(2,1)S(1)} %get-tuple-element.28), channel_id=1, source_target_pairs={{0,2},{1,7},{2,4},{3,1},{4,6},{5,3},{6,0},{7,5},{8,10},{9,15},{10,... | collective-permute-start | bytes 786440 | tf_op jit(solution)/shard_map/ppermute | solution.py:35
  53.9 0.0 copy-start
  53.9 0.0 copy-start.1
  53.9 3.1 %collective-permute-start.3 = (bf16[4,128,256]{2,1,0:T(8,128)(2,1)S(1)}, bf16[4,128,256]{2,1,0:T(8,128)(2,1)S(1)}, u32[]{:S(2)}, u32[]{:S(2)}) collective-permute-start(bf16[4,128,256]{2,1,0:T(8,128)(2,1)S(1)} %get-tuple-element.29), channel_id=1, source_target_pairs={{0,6},{1,3},{2,0},{3,5},{4,2},{5,7},{6,4},{7,1},{8,14},{9,11},{10,... | collective-permute-start | bytes 786440 | tf_op jit(solution)/shard_map/ppermute | solution.py:35
  57.1 2.4 %turn.1.v = bf16[128,128,128]{2,1,0:T(8,128)(2,1)S(1)} custom-call(s32[5]{0:T(128)S(1)} %stack.19.where, bf16[1,1,128,128,128]{4,3,2,1,0:T(8,128)(2,1)} %v.5), custom_call_target="tpu_custom_call" | custom-call | bytes 10485760 | tf_op jit(solution)/shard_map/turn/pallas_call | solution.py:209
  59.5 0.0 collective-permute-done.1
  59.5 4.4 %collective-permute-done.2 = bf16[4,128,256]{2,1,0:T(8,128)(2,1)S(1)} collective-permute-done((bf16[4,128,256]{2,1,0:T(8,128)(2,1)S(1)}, bf16[4,128,256]{2,1,0:T(8,128)(2,1)S(1)}, u32[]{:S(2)}, u32[]{:S(2)}) %collective-permute-start.2) | collective-permute-done | bytes 262176 | tf_op jit(solution)/shard_map/ppermute | solution.py:35
  63.9 0.6 collective-permute-done.3
  64.5 0.1 add_convert_fusion
  64.7 25.5 %all_to_all.26.got = bf16[4,128,256]{2,1,0:T(8,128)(2,1)S(1)} all-to-all(bf16[4,128,256]{2,1,0:T(8,128)(2,1)S(1)} %add_convert_fusion), channel_id=1, replica_groups={{0,8,16,24},{1,9,17,25},{2,10,18,26},{3,11,19,27},{4,12,20,28},{5,13,21..., dimensions={0} | all-to-all | bytes 524288 | tf_op jit(solution)/shard_map/all_to_all | solution.py:62
  90.2 0.0 copy-done
  90.2 0.0 copy-done.1
  90.2 0.8 middle.1
  91.0 19.3 %all_to_all.27.parts = bf16[16,16,256]{2,1,0:T(8,128)(2,1)S(1)} all-to-all(bf16[16,16,256]{2,1,0:T(8,128)(2,1)S(1)} %get-tuple-element.34), channel_id=1, replica_groups=mesh['row'=16,'col'=32] {'row'}, dimensions={0} | all-to-all | bytes 262144 | tf_op jit(solution)/shard_map/all_to_all | solution.py:52
  110.4 19.5 %all_to_all.28.got = bf16[4,144,256]{2,1,0:T(8,128)(2,1)S(1)} all-to-all(bf16[4,144,256]{2,1,0:T(8,128)(2,1)S(1)} %pack.1), channel_id=1, replica_groups={{0,8,16,24},{1,9,17,25},{2,10,18,26},{3,11,19,27},{4,12,20,28},{5,13,21..., dimensions={0} | all-to-all | bytes 589824 | tf_op jit(solution)/shard_map/all_to_all | solution.py:62
  129.9 4.6 %collective-permute-start.6 = (bf16[528,256]{1,0:T(8,128)(2,1)S(1)}, bf16[528,256]{1,0:T(8,128)(2,1)S(1)}, u32[]{:S(2)}, u32[]{:S(2)}) collective-permute-start(bf16[528,256]{1,0:T(8,128)(2,1)S(1)} %fold.1.stays), channel_id=1, source_target_pairs={{0,4},{1,5},{2,6},{3,7},{4,0},{5,1},{6,2},{7,3},{8,12},{9,13},{10,... | collective-permute-start | bytes 811016 | tf_op jit(solution)/shard_map/ppermute | solution.py:35
  134.5 1.9 collective-permute-start.5
  136.4 4.6 %collective-permute-start.4 = (bf16[528,256]{1,0:T(8,128)(2,1)S(1)}, bf16[528,256]{1,0:T(8,128)(2,1)S(1)}, u32[]{:S(2)}, u32[]{:S(2)}) collective-permute-start(bf16[528,256]{1,0:T(8,128)(2,1)S(1)} %fold.1.stays), channel_id=1, source_target_pairs={{0,2},{1,7},{2,4},{3,1},{4,6},{5,3},{6,0},{7,5},{8,10},{9,15},{10,... | collective-permute-start | bytes 811016 | tf_op jit(solution)/shard_map/ppermute | solution.py:35
  141.0 0.0 collective-permute-done.6.two
  141.0 4.8 %collective-permute-done.5.second = bf16[528,256]{1,0:T(8,128)(2,1)S(1)} collective-permute-done((bf16[528,256]{1,0:T(8,128)(2,1)S(1)}, bf16[528,256]{1,0:T(8,128)(2,1)S(1)}, u32[]{:S(2)}, u32[]{:S(2)}) %collective-permute-start.5) | collective-permute-done | bytes 270368 | tf_op jit(solution)/shard_map/ppermute | solution.py:35
  145.8 1.0 collective-permute-done.4.first
  146.8 0.6 collect.1.grads.mine
  147.4 7.0 %collective-permute-start.7 = (bf16[2064,256]{1,0:T(8,128)(2,1)S(1)}, bf16[2064,256]{1,0:T(8,128)(2,1)S(1)}, u32[]{:S(2)}, u32[]{:S(2)}) collective-permute-start(bf16[2064,256]{1,0:T(8,128)(2,1)S(1)} %collect.1.grads.mine), channel_id=1, source_target_pairs={{0,1},{1,0},{2,3},{3,2},{4,5},{5,4},{6,7},{7,6},{8,9},{9,8},{10,11... | collective-permute-start | bytes 3170312 | tf_op jit(solution)/shard_map/ppermute | solution.py:48
  154.4 2.0 %first.1.start = f32[16,128,256]{2,1,0:T(8,128)S(1)} custom-call(s32[5]{0:T(128)S(1)} %stack.19.where, s32[1,1,128]{2,1,0:T(1,128)S(1)} %copy-done.2, s32[1,1,128]{2,1,0:T(1,128)S(1)} %copy-done.3, bf16[128,128,128]{2,1,0:T(8,128)(2,1)S(1)} %turn.1.v, bf16[2064,256]{1,0:T(8,128)(2,1)S(1)} %collect.1.grads.mine), custom_call_target="tpu_custom_call" | custom-call | flops 536870912 | bytes 8388608 | tf_op jit(solution)/shard_map/first/pallas_call | solution.py:354
  156.5 0.3 collective-permute-done.7.grads
  156.7 2.0 %second.1 = (bf16[528,256]{1,0:T(8,128)(2,1)S(1)}, bf16[528,256]{1,0:T(8,128)(2,1)S(1)}, bf16[528,256]{1,0:T(8,128)(2,1)S(1)}, bf16[528,256]{1,0:T(8,128)(2,1)S(1)}) custom-call(s32[5]{0:T(128)S(1)} %stack.19.where, s32[1,1,128]{2,1,0:T(1,128)S(1)} %copy-done.2, s32[1,1,128]{2,1,0:T(1,128)S(1)} %copy-done.3, bf16[128,128,128]{2,1,0:T(8,128)(2,1)S(1)} %turn.1.v, ...), custom_call_target="tpu_custom_call" | custom-call | flops 536870912 | bytes 8388608 | tf_op jit(solution)/shard_map/second/pallas_call | solution.py:364
  158.7 3.0 %collective-permute-start.8 = (bf16[528,256]{1,0:T(8,128)(2,1)S(1)}, bf16[528,256]{1,0:T(8,128)(2,1)S(1)}, u32[]{:S(2)}, u32[]{:S(2)}) collective-permute-start(bf16[528,256]{1,0:T(8,128)(2,1)S(1)} %get-tuple-element.36), channel_id=1, source_target_pairs={{0,64},{1,65},{2,66},{3,67},{4,68},{5,69},{6,70},{7,71},{8,72},{9,... | collective-permute-start | bytes 811016 | tf_op jit(solution)/shard_map/ppermute | solution.py:44
  161.7 5.8 %collective-permute-start.9 = (bf16[528,256]{1,0:T(8,128)(2,1)S(1)}, bf16[528,256]{1,0:T(8,128)(2,1)S(1)}, u32[]{:S(2)}, u32[]{:S(2)}) collective-permute-start(bf16[528,256]{1,0:T(8,128)(2,1)S(1)} %get-tuple-element.37), channel_id=1, source_target_pairs={{0,32},{1,97},{2,34},{3,99},{4,36},{5,101},{6,38},{7,103},{8,40},{... | collective-permute-start | bytes 811016 | tf_op jit(solution)/shard_map/ppermute | solution.py:44
  167.6 1.9 collective-permute-start.10
  169.5 0.4 collective-permute-done.8.p1
  169.9 4.3 %collective-permute-done.9.p2 = bf16[528,256]{1,0:T(8,128)(2,1)S(1)} collective-permute-done((bf16[528,256]{1,0:T(8,128)(2,1)S(1)}, bf16[528,256]{1,0:T(8,128)(2,1)S(1)}, u32[]{:S(2)}, u32[]{:S(2)}) %collective-permute-start.9) | collective-permute-done | bytes 270368 | tf_op jit(solution)/shard_map/ppermute | solution.py:44
  174.2 1.9 collective-permute-done.10.p3
  176.1 0.7 merge.1
  176.8 16.0 %all_to_all.29.got = bf16[4,192,256]{2,1,0:T(8,128)(2,1)S(1)} all-to-all(bf16[4,192,256]{2,1,0:T(8,128)(2,1)S(1)} %merge.1), channel_id=1, replica_groups={{0,128,256,384},{32,160,288,416},{64,192,320,448},{96,224,352,480},{1,1..., dimensions={0} | all-to-all | bytes 786432 | tf_op jit(solution)/shard_map/all_to_all | solution.py:57
  192.8 0.8 last.1
  (2 shorter events, 0.1 us)
Async XLA Ops:
  0.6 35.4 %copy-start.3 = (s32[1,1,128]{2,1,0:T(1,128)S(1)}, s32[1,1,128]{2,1,0:T(1,128)}, u32[]{:S(2)}) copy-start(s32[1,1,128]{2,1,0:T(1,128)} %cols.7) | copy-start | bytes 1540
  0.6 35.4 %copy-start.2 = (s32[1,1,128]{2,1,0:T(1,128)S(1)}, s32[1,1,128]{2,1,0:T(1,128)}, u32[]{:S(2)}) copy-start(s32[1,1,128]{2,1,0:T(1,128)} %rows.7) | copy-start | bytes 1540
  39.0 7.7 %collective-permute-start = (bf16[16,128,256]{2,1,0:T(8,128)(2,1)S(1)}, bf16[16,128,256]{2,1,0:T(8,128)(2,1)S(1)}, u32[]{:S(2)}, u32[]{:S(2)}) collective-permute-start(bf16[16,128,256]{2,1,0:T(8,128)(2,1)S(1)} %forward.3), channel_id=1, source_target_pairs={{0,1},{1,0},{2,3},{3,2},{4,5},{5,4},{6,7},{7,6},{8,9},{9,8},{10,11... | collective-permute-start | bytes 3145736 | tf_op jit(solution)/shard_map/ppermute | solution.py:48
  47.5 12.0 %collective-permute-start.1 = (bf16[4,128,256]{2,1,0:T(8,128)(2,1)S(1)}, bf16[4,128,256]{2,1,0:T(8,128)(2,1)S(1)}, u32[]{:S(2)}, u32[]{:S(2)}) collective-permute-start(bf16[4,128,256]{2,1,0:T(8,128)(2,1)S(1)} %get-tuple-element.27), channel_id=1, source_target_pairs={{0,4},{1,5},{2,6},{3,7},{4,0},{5,1},{6,2},{7,3},{8,12},{9,13},{10,... | collective-permute-start | bytes 786440 | tf_op jit(solution)/shard_map/ppermute | solution.py:35
  51.6 12.3 %collective-permute-start.2 = (bf16[4,128,256]{2,1,0:T(8,128)(2,1)S(1)}, bf16[4,128,256]{2,1,0:T(8,128)(2,1)S(1)}, u32[]{:S(2)}, u32[]{:S(2)}) collective-permute-start(bf16[4,128,256]{2,1,0:T(8,128)(2,1)S(1)} %get-tuple-element.28), channel_id=1, source_target_pairs={{0,2},{1,7},{2,4},{3,1},{4,6},{5,3},{6,0},{7,5},{8,10},{9,15},{10,... | collective-permute-start | bytes 786440 | tf_op jit(solution)/shard_map/ppermute | solution.py:35
  53.9 36.3 %copy-start = (bf16[256,256]{1,0:T(8,128)(2,1)S(1)}, bf16[256,256]{1,0:T(8,128)(2,1)}, u32[]{:S(2)}) copy-start(bf16[256,256]{1,0:T(8,128)(2,1)} %w.3) | copy-start | bytes 393220
  53.9 36.3 %copy-start.1 = (bf16[128,256]{1,0:T(8,128)(2,1)S(1)}, bf16[128,256]{1,0:T(8,128)(2,1)}, u32[]{:S(2)}) copy-start(bf16[128,256]{1,0:T(8,128)(2,1)} %cot.1) | copy-start | bytes 196612
  53.9 10.6 %collective-permute-start.3 = (bf16[4,128,256]{2,1,0:T(8,128)(2,1)S(1)}, bf16[4,128,256]{2,1,0:T(8,128)(2,1)S(1)}, u32[]{:S(2)}, u32[]{:S(2)}) collective-permute-start(bf16[4,128,256]{2,1,0:T(8,128)(2,1)S(1)} %get-tuple-element.29), channel_id=1, source_target_pairs={{0,6},{1,3},{2,0},{3,5},{4,2},{5,7},{6,4},{7,1},{8,14},{9,11},{10,... | collective-permute-start | bytes 786440 | tf_op jit(solution)/shard_map/ppermute | solution.py:35
  129.9 11.1 %collective-permute-start.6 = (bf16[528,256]{1,0:T(8,128)(2,1)S(1)}, bf16[528,256]{1,0:T(8,128)(2,1)S(1)}, u32[]{:S(2)}, u32[]{:S(2)}) collective-permute-start(bf16[528,256]{1,0:T(8,128)(2,1)S(1)} %fold.1.stays), channel_id=1, source_target_pairs={{0,4},{1,5},{2,6},{3,7},{4,0},{5,1},{6,2},{7,3},{8,12},{9,13},{10,... | collective-permute-start | bytes 811016 | tf_op jit(solution)/shard_map/ppermute | solution.py:35
  134.5 11.3 %collective-permute-start.5 = (bf16[528,256]{1,0:T(8,128)(2,1)S(1)}, bf16[528,256]{1,0:T(8,128)(2,1)S(1)}, u32[]{:S(2)}, u32[]{:S(2)}) collective-permute-start(bf16[528,256]{1,0:T(8,128)(2,1)S(1)} %fold.1.stays), channel_id=1, source_target_pairs={{0,6},{1,3},{2,0},{3,5},{4,2},{5,7},{6,4},{7,1},{8,14},{9,11},{10,... | collective-permute-start | bytes 811016 | tf_op jit(solution)/shard_map/ppermute | solution.py:35
  136.4 10.4 %collective-permute-start.4 = (bf16[528,256]{1,0:T(8,128)(2,1)S(1)}, bf16[528,256]{1,0:T(8,128)(2,1)S(1)}, u32[]{:S(2)}, u32[]{:S(2)}) collective-permute-start(bf16[528,256]{1,0:T(8,128)(2,1)S(1)} %fold.1.stays), channel_id=1, source_target_pairs={{0,2},{1,7},{2,4},{3,1},{4,6},{5,3},{6,0},{7,5},{8,10},{9,15},{10,... | collective-permute-start | bytes 811016 | tf_op jit(solution)/shard_map/ppermute | solution.py:35
  147.4 9.3 %collective-permute-start.7 = (bf16[2064,256]{1,0:T(8,128)(2,1)S(1)}, bf16[2064,256]{1,0:T(8,128)(2,1)S(1)}, u32[]{:S(2)}, u32[]{:S(2)}) collective-permute-start(bf16[2064,256]{1,0:T(8,128)(2,1)S(1)} %collect.1.grads.mine), channel_id=1, source_target_pairs={{0,1},{1,0},{2,3},{3,2},{4,5},{5,4},{6,7},{7,6},{8,9},{9,8},{10,11... | collective-permute-start | bytes 3170312 | tf_op jit(solution)/shard_map/ppermute | solution.py:48
  158.7 11.2 %collective-permute-start.8 = (bf16[528,256]{1,0:T(8,128)(2,1)S(1)}, bf16[528,256]{1,0:T(8,128)(2,1)S(1)}, u32[]{:S(2)}, u32[]{:S(2)}) collective-permute-start(bf16[528,256]{1,0:T(8,128)(2,1)S(1)} %get-tuple-element.36), channel_id=1, source_target_pairs={{0,64},{1,65},{2,66},{3,67},{4,68},{5,69},{6,70},{7,71},{8,72},{9,... | collective-permute-start | bytes 811016 | tf_op jit(solution)/shard_map/ppermute | solution.py:44
  161.7 12.5 %collective-permute-start.9 = (bf16[528,256]{1,0:T(8,128)(2,1)S(1)}, bf16[528,256]{1,0:T(8,128)(2,1)S(1)}, u32[]{:S(2)}, u32[]{:S(2)}) collective-permute-start(bf16[528,256]{1,0:T(8,128)(2,1)S(1)} %get-tuple-element.37), channel_id=1, source_target_pairs={{0,32},{1,97},{2,34},{3,99},{4,36},{5,101},{6,38},{7,103},{8,40},{... | collective-permute-start | bytes 811016 | tf_op jit(solution)/shard_map/ppermute | solution.py:44
  167.6 8.6 %collective-permute-start.10 = (bf16[528,256]{1,0:T(8,128)(2,1)S(1)}, bf16[528,256]{1,0:T(8,128)(2,1)S(1)}, u32[]{:S(2)}, u32[]{:S(2)}) collective-permute-start(bf16[528,256]{1,0:T(8,128)(2,1)S(1)} %get-tuple-element.38), channel_id=1, source_target_pairs={{0,96},{1,33},{2,98},{3,35},{4,100},{5,37},{6,102},{7,39},{8,104},... | collective-permute-start | bytes 811016 | tf_op jit(solution)/shard_map/ppermute | solution.py:44

commit v11 on v10

--- a/solution.py
+++ b/solution.py
@@ -15,6 +15,7 @@
 GROUP = 16
 CHUNK = 16
 SLOTS = 128
+ROW, COL, PLACE = 0, 1, 2
 VMEM_LIMIT = 24 * 1024 * 1024
 BF16 = jnp.bfloat16
 F32 = jnp.float32
@@ -78,16 +79,16 @@
     return pl.CostEstimate(flops=flops, bytes_accessed=mib * 1024 * 1024, transcendentals=0)
 
 
-def choose_slots(parity, where, rows, slots, first, found):
+def choose_slots(parity, block, slots, first, found):
     for u in range(CHUNK):
         s = first + u
         slots[found] = s
-        chosen = ((rows[0, 0, s] & 1) == parity) & (s < where[3])
+        chosen = ((block[ROW, s] & 1) == parity) & (s < block[PLACE, 3])
         found = found + jnp.where(chosen, 1, 0)
     return found
 
 
-def add_products(parity, where, rows, slots, arrive, tile, source, target, acc):
+def add_products(parity, block, slots, arrive, tile, source, target, acc):
     def group(found, first):
         products, targets = [], []
         for u in range(GROUP):
@@ -101,12 +102,12 @@
     def chunk(i, state):
         found, done = state
         arrive(i)
-        found = choose_slots(parity, where, rows, slots, i * CHUNK, found)
+        found = choose_slots(parity, block, slots, i * CHUNK, found)
         full = (found - done) >= GROUP
         pl.when(full)(lambda: group(found, done))
         return found, jnp.where(full, done + GROUP, done)
 
-    chunks = (where[3] + CHUNK - 1) // CHUNK
+    chunks = (block[PLACE, 3] + CHUNK - 1) // CHUNK
     found, done = lax.fori_loop(0, chunks, chunk, (jnp.int32(0), jnp.int32(0)))
     pl.when(done < found)(lambda: group(found, done))
 
@@ -115,23 +116,23 @@
     return (0, 2, 1 + 2 * core, 3 - 2 * core)
 
 
-def pair_kernel(where, a, b, *outs):
-    for k, out in zip(distances(where[2]), outs):
+def pair_kernel(block, a, b, *outs):
+    for k, out in zip(distances(block[PLACE, 2]), outs):
         span = pl.ds(4 * k, 4)
         out[...] = (a[span].astype(F32) + b[span].astype(F32)).astype(BF16)
 
 
-def pair(where, a, b):
-    block = jax.ShapeDtypeStruct((4,) + a.shape[1:], BF16)
+def pair(table, a, b):
+    quarter = jax.ShapeDtypeStruct((4,) + a.shape[1:], BF16)
     return pl.pallas_call(
         pair_kernel,
-        out_shape=(block,) * 4,
+        out_shape=(quarter,) * 4,
         in_specs=[smem()] + [vmem()] * 2,
         out_specs=(vmem(),) * 4,
         compiler_params=params(),
         cost_estimate=cost(0, 4),
         name="pair",
-    )(where, a, b)
+    )(table, a, b)
 
 
 def fetch_chunks(live, v, tiles, sems):
@@ -144,23 +145,22 @@
     return chunk
 
 
-def forward_kernel(other, where, rows, cols, v, xs, out, slots, acc, tiles, sems):
-    y, core = where[1], where[2]
-    chunks = fetch_chunks(where[3], v, tiles, sems)
+def forward_kernel(other, block, v, xs, out, slots, acc, tiles, sems):
+    y, core = block[PLACE, 1], block[PLACE, 2]
+    chunks = fetch_chunks(block[PLACE, 3], v, tiles, sems)
     acc[...] = jnp.zeros_like(acc)
 
     def target(s):
-        r = rows[0, 0, s]
+        r = block[ROW, s]
         return ((((r >> 1) & 3) - y) & 3) * 4 + (r >> 3)
 
     add_products(
         core ^ other,
-        where,
-        rows,
+        block,
         slots,
         lambda i: chunks(i).wait(),
         lambda s: tiles[s],
-        lambda s: xs[cols[0, 0, s]],
+        lambda s: xs[block[COL, s]],
         target,
         acc,
     )
@@ -174,12 +174,12 @@
     ]
 
 
-def forward(other, where, rows, cols, values, xs):
+def forward(other, block, values, xs):
     width = xs.shape[-1]
     return pl.pallas_call(
         functools.partial(forward_kernel, other),
         out_shape=jax.ShapeDtypeStruct((HALF, TILE, width), BF16),
-        in_specs=[smem()] * 3 + [pl.BlockSpec(memory_space=pltpu.HBM), vmem()],
+        in_specs=[smem()] + [pl.BlockSpec(memory_space=pltpu.HBM), vmem()],
         out_specs=vmem(),
         scratch_shapes=[
             *list_and_sums(width),
@@ -189,11 +189,11 @@
         compiler_params=pltpu.CompilerParams(vmem_limit_bytes=50 * 1024 * 1024),
         cost_estimate=cost(2 * 64 * TILE * TILE * width, 7),
         name="forward",
-    )(where, rows, cols, values, xs)
-
-
-def turn_kernel(where, v, out, tiles, sems):
-    chunks = fetch_chunks(where[3], v, tiles, sems)
+    )(block, values, xs)
+
+
+def turn_kernel(block, v, out, tiles, sems):
+    chunks = fetch_chunks(block[PLACE, 3], v, tiles, sems)
 
     def step(i, _):
         chunks(i).wait()
@@ -201,10 +201,10 @@
             out[i * CHUNK + u] = tiles[i * CHUNK + u].T
         return 0
 
-    lax.fori_loop(0, (where[3] + CHUNK - 1) // CHUNK, step, 0)
-
-
-def turn_tiles(where, v):
+    lax.fori_loop(0, (block[PLACE, 3] + CHUNK - 1) // CHUNK, step, 0)
+
+
+def turn_tiles(block, v):
     shape = v.shape[2:]
     return pl.pallas_call(
         turn_kernel,
@@ -218,7 +218,7 @@
         compiler_params=pltpu.CompilerParams(vmem_limit_bytes=46 * 1024 * 1024),
         cost_estimate=cost(0, 10),
         name="turn",
-    )(where, v)
+    )(block, v)
 
 
 def middle_kernel(got, w, cot, act_out, grad_out, part_out):
@@ -288,16 +288,16 @@
     )(got)
 
 
-def collect_kernel(where, stays, first, second, two, out, slices):
-    y = where[1]
+def collect_kernel(block, stays, first, second, two, out, slices):
+    y = block[PLACE, 1]
     rows = 4 * TILE
-    for k, line in zip(distances(where[2]), (stays, two, first, second)):
+    for k, line in zip(distances(block[PLACE, 2]), (stays, two, first, second)):
         out[pl.ds(pl.multiple_of(rows * k, rows), rows)] = line[:rows]
         slices[(y - k) & 3] = line[rows:].astype(F32)
     out[4 * rows :] = ((slices[0] + slices[1]) + (slices[2] + slices[3])).astype(BF16)
 
 
-def collect(where, lines):
+def collect(block, lines):
     rows, width = lines[0].shape
     extra = rows - 4 * TILE
     return pl.pallas_call(
@@ -309,85 +309,85 @@
         compiler_params=params(),
         cost_estimate=cost(0, 3),
         name="collect",
-    )(where, *lines)
-
-
-def backward_half(other, where, rows, cols, v, grads, slots, acc):
-    y, core, x = where[1], where[2], where[4]
+    )(block, *lines)
+
+
+def backward_half(other, block, v, grads, slots, acc):
+    y, core, x = block[PLACE, 1], block[PLACE, 2], block[PLACE, 4]
 
     def source(s):
-        r = rows[0, 0, s]
+        r = block[ROW, s]
         at = ((y - ((r >> 1) & 3)) & 3) * 4 + (r >> 3)
         return grads[pl.ds(pl.multiple_of(at * TILE, TILE), TILE)]
 
     def target(s):
-        c = cols[0, 0, s]
+        c = block[COL, s]
         return (((c & 3) - x) & 3) * 4 + (c >> 2)
 
     add_products(
-        core ^ other, where, rows, slots, lambda i: None, lambda s: v[s], source, target, acc
+        core ^ other, block, slots, lambda i: None, lambda s: v[s], source, target, acc
     )
 
 
-def first_kernel(where, rows, cols, v, grads, out, slots, acc):
+def first_kernel(block, v, grads, out, slots, acc):
     acc[...] = jnp.zeros_like(acc)
-    backward_half(0, where, rows, cols, v, grads, slots, acc)
+    backward_half(0, block, v, grads, slots, acc)
     out[...] = acc[:HALF]
 
 
-def second_kernel(where, rows, cols, v, grads, mine, start, o0, o1, o2, o3, slots, acc):
+def second_kernel(block, v, grads, mine, start, o0, o1, o2, o3, slots, acc):
     acc[:HALF] = start[...]
     acc[HALF] = jnp.zeros_like(acc[HALF])
-    backward_half(1, where, rows, cols, v, grads, slots, acc)
+    backward_half(1, block, v, grads, slots, acc)
     rest = HALF * TILE
     part = (mine[rest:].astype(F32) + grads[rest:].astype(F32)).astype(BF16)
-    for k, out in zip(distances(where[2]), (o0, o1, o2, o3)):
+    for k, out in zip(distances(block[PLACE, 2]), (o0, o1, o2, o3)):
         for i in range(4):
             out[TILE * i : TILE * (i + 1)] = acc[4 * k + i].astype(BF16)
         out[4 * TILE :] = part
 
 
-def backward(where, rows, cols, v, mine, theirs):
+def backward(block, v, mine, theirs):
     extra, width = mine.shape[0] - HALF * TILE, mine.shape[1]
     scratch = list_and_sums(width)
     work = cost(2 * 64 * TILE * TILE * width, 8)
     first = pl.pallas_call(
         first_kernel,
         out_shape=jax.ShapeDtypeStruct((HALF, TILE, width), F32),
-        in_specs=[smem()] * 3 + [vmem()] * 2,
+        in_specs=[smem()] + [vmem()] * 2,
         out_specs=vmem(),
         scratch_shapes=scratch,
         compiler_params=params(),
         cost_estimate=work,
         name="first",
-    )(where, rows, cols, v, mine)
+    )(block, v, mine)
     return pl.pallas_call(
         second_kernel,
         out_shape=(jax.ShapeDtypeStruct((4 * TILE + extra, width), BF16),) * 4,
-        in_specs=[smem()] * 3 + [vmem()] * 4,
+        in_specs=[smem()] + [vmem()] * 4,
         out_specs=(vmem(),) * 4,
         scratch_shapes=scratch,
         compiler_params=params(),
         cost_estimate=work,
         name="second",
-    )(where, rows, cols, v, theirs, mine, first)
-
-def merge_kernel(where, p0, p1, p2, p3, out):
-    x = where[4]
+    )(block, v, theirs, mine, first)
+
+def merge_kernel(block, p0, p1, p2, p3, out):
+    x = block[PLACE, 4]
     parts = (p0, p1, p2, p3)
     extra = p0.shape[0] - 4 * TILE
     for i in range(4):
-        block = slice(TILE * i, TILE * (i + 1))
-        total = p0[block].astype(F32)
+        span = slice(TILE * i, TILE * (i + 1))
+        total = p0[span].astype(F32)
         for part in parts[1:]:
-            total = total + part[block].astype(F32)
+            total = total + part[span].astype(F32)
         out[i, :TILE] = total.astype(BF16)
-        for k, part in zip(distances(where[2]), parts):
+        for k, part in zip(distances(block[PLACE, 2]), parts):
             at = pl.multiple_of(TILE + ((x - k) & 3) * extra, extra)
             out[i, pl.ds(at, extra)] = part[4 * TILE :]
 
 
-def merge(where, parts):
+def merge(block, parts):
     rows, width = parts[0].shape
     return pl.pallas_call(
         merge_kernel,
@@ -397,7 +397,7 @@
         compiler_params=params(),
         cost_estimate=cost(0, 2),
         name="merge",
-    )(where, *parts)
+    )(block, *parts)
 
 
 def last_kernel(scale, got, w, grad_out, weight_out):
@@ -430,27 +430,28 @@
     node_dev = features.shape[0]
     grad_scale = 1.0 / math.sqrt(node_dev * lax.axis_size("row") * lax.axis_size("col"))
     r, c = lax.axis_index("row"), lax.axis_index("col")
-    where = jnp.stack([c >> 3, (c >> 1) & 3, c & 1, tile_count[0, 0], r & 3]).astype(jnp.int32)
-
-    features, where = lax.optimization_barrier((features, where))
+    place = jnp.stack([c >> 3, (c >> 1) & 3, c & 1, tile_count[0, 0], r & 3]).astype(jnp.int32)
+    place = jnp.pad(place, (0, SLOTS - place.shape[0]))
+    block = jnp.concatenate([tile_rows[0], tile_cols[0], place[None]], axis=0)
+
+    features, block = lax.optimization_barrier((features, block))
     xs = trade_row(jnp.broadcast_to(features[None], (ROWS,) + features.shape))
-    xs, where = lax.optimization_barrier((xs, where))
-    block = (where, tile_rows, tile_cols)
-    got = send_core(forward(1, *block, tile_values, xs))
-    keep = forward(0, *block, tile_values, xs)
-    stays, two, first, second = pair(where, keep, got)
+    xs, block = lax.optimization_barrier((xs, block))
+    got = send_core(forward(1, block, tile_values, xs))
+    keep = forward(0, block, tile_values, xs)
+    stays, two, first, second = pair(block, keep, got)
     got = [stays, send_y(two, TWO), send_y(first, FIRST), send_y(second, SECOND)]
     got = [v.astype(F32) for v in got]
     rows = (got[0] + got[1] + got[2] + got[3]).astype(BF16)
-    turned = turn_tiles(where, tile_values)
+    turned = turn_tiles(block, tile_values)
     rows, turned = lax.optimization_barrier((rows, turned))
     activated, grad_pre, part = middle(trade_zh(rows), weight, cotangent)
 
     line = fold(trade_zh(pack(grad_pre, trade_row(part))))
-    mine = collect(where, [line] + [send_y(line, which) for which in (FIRST, SECOND, TWO)])
-    stays, two, first, second = backward(*block, turned, mine, send_core(mine))
+    mine = collect(block, [line] + [send_y(line, which) for which in (FIRST, SECOND, TWO)])
+    stays, two, first, second = backward(block, turned, mine, send_core(mine))
     spread = [stays, send_x(two, TWO), send_x(first, FIRST), send_x(second, SECOND)]
-    grad_features, grad_weight = last(trade_zl(merge(where, spread)), weight, grad_scale)
+    grad_features, grad_weight = last(trade_zl(merge(block, spread)), weight, grad_scale)
     return (activated, grad_features, grad_weight)
 
 

time: 194 us -> 194 us (level)
  waiting for transfers between devices: 17.7 us -> 21.3 us
  starting transfers between devices: 43 us -> 40.9 us
    all_to_all x2, blocking collectives: 53 us -> 49.1 us  [trade_row(): return lax.all_to_all(v, 'row', 0, 0)]
    ppermute x3, waiting for transfers between devices: 6.64 us -> 9.57 us  [send_x(): return lax.ppermute(v, ('row', 'col'), pairs)]
    ppermute x3, starting transfers between devices: 10.7 us -> 7.99 us  [send_x(): return lax.ppermute(v, ('row', 'col'), pairs)]
    all_to_all x2, blocking collectives: 45 us -> 47.5 us  [trade_zh(): return lax.all_to_all(v, 'col', 0, 0, axis_index_groups=groups)]
  transfers between devices with their start and end apart: 11 -> 11, of which waited for: 8 -> 7; matrix products, arithmetic and copies ran while one was open for 0% -> 0% of each run, Pallas kernels for 4% -> 4%
where the time goes in v11:
time: 194 us
  blocking collectives  113 us (58%)
  starting transfers between devices  40.9 us (21%)
  waiting for transfers between devices  21.3 us (11%)
  Pallas kernels  16 us (8%)
    all_to_all x2, blocking collectives, trade_row(): return lax.all_to_all(v, 'row', 0, 0)  49.1 us
    all_to_all x2, blocking collectives, trade_zh(): return lax.all_to_all(v, 'col', 0, 0, axis_index_groups=groups)  47.5 us
    ppermute x6, starting transfers between devices, send_y(): return lax.ppermute(v, 'col', pairs)  21.2 us
    all_to_all x1, blocking collectives, trade_zl(): return lax.all_to_all(v, 'row', 0, 0, axis_index_groups=groups)  16 us
    ppermute x2, starting transfers between devices, send_core(): return lax.ppermute(v, 'col', [(c, c ^ 1) for c in range(COLS)])  11.7 us
    ppermute x6, waiting for transfers between devices, send_y(): return lax.ppermute(v, 'col', pairs)  11.5 us
    ppermute x3, waiting for transfers between devices, send_x(): return lax.ppermute(v, ('row', 'col'), pairs)  9.57 us
    ppermute x3, starting transfers between devices, send_x(): return lax.ppermute(v, ('row', 'col'), pairs)  7.99 us
  transfers between devices with their start and end apart: 11, of which 7 were waited for; matrix products, arithmetic and copies ran while one was open for 0% of the time, Pallas kernels for 4%

profile of v11, /device:TPU:1, one launch (start us, length us, event | category | flops | bytes accessed | tf_op | source)
XLA Modules:
  0.0 194.1 jit_solution(17298971360755952889)
XLA Ops:
  1.3 0.1 stack.19
  1.4 0.7 pad_add_fusion.block
  2.1 0.9 broadcast_in_dim.10
  3.0 33.7 %all_to_all.25.xs = bf16[16,128,256]{2,1,0:T(8,128)(2,1)S(1)} all-to-all(bf16[16,128,256]{2,1,0:T(8,128)(2,1)S(1)} %broadcast_in_dim.10), channel_id=1, replica_groups=mesh['row'=16,'col'=32] {'row'}, dimensions={0} | all-to-all | bytes 2097152 | tf_op jit(solution)/shard_map/all_to_all | solution.py:53
  36.6 3.0 %forward.3 = bf16[16,128,256]{2,1,0:T(8,128)(2,1)S(1)} custom-call(s32[3,128]{1,0:T(4,128)S(1)} %pad_add_fusion.block, bf16[1,1,128,128,128]{4,3,2,1,0:T(8,128)(2,1)} %v.5, bf16[16,128,256]{2,1,0:T(8,128)(2,1)S(1)} %all_to_all.25.xs), custom_call_target="tpu_custom_call" | custom-call | flops 536870912 | bytes 7340032 | tf_op jit(solution)/shard_map/forward/pallas_call | solution.py:179
  39.7 4.1 %collective-permute-start = (bf16[16,128,256]{2,1,0:T(8,128)(2,1)S(1)}, bf16[16,128,256]{2,1,0:T(8,128)(2,1)S(1)}, u32[]{:S(2)}, u32[]{:S(2)}) collective-permute-start(bf16[16,128,256]{2,1,0:T(8,128)(2,1)S(1)} %forward.3), channel_id=1, source_target_pairs={{0,1},{1,0},{2,3},{3,2},{4,5},{5,4},{6,7},{7,6},{8,9},{9,8},{10,11... | collective-permute-start | bytes 3145736 | tf_op jit(solution)/shard_map/ppermute | solution.py:49
  43.8 2.9 %forward.2.a = bf16[16,128,256]{2,1,0:T(8,128)(2,1)S(1)} custom-call(s32[3,128]{1,0:T(4,128)S(1)} %pad_add_fusion.block, bf16[1,1,128,128,128]{4,3,2,1,0:T(8,128)(2,1)} %v.5, bf16[16,128,256]{2,1,0:T(8,128)(2,1)S(1)} %all_to_all.25.xs), custom_call_target="tpu_custom_call" | custom-call | flops 536870912 | bytes 7340032 | tf_op jit(solution)/shard_map/forward/pallas_call | solution.py:179
  46.7 0.0 collective-permute-done.b
  46.7 0.8 pair.1
  47.5 5.0 %collective-permute-start.1 = (bf16[4,128,256]{2,1,0:T(8,128)(2,1)S(1)}, bf16[4,128,256]{2,1,0:T(8,128)(2,1)S(1)}, u32[]{:S(2)}, u32[]{:S(2)}) collective-permute-start(bf16[4,128,256]{2,1,0:T(8,128)(2,1)S(1)} %get-tuple-element.27), channel_id=1, source_target_pairs={{0,4},{1,5},{2,6},{3,7},{4,0},{5,1},{6,2},{7,3},{8,12},{9,13},{10,... | collective-permute-start | bytes 786440 | tf_op jit(solution)/shard_map/ppermute | solution.py:36
  52.5 3.9 %collective-permute-start.2 = (bf16[4,128,256]{2,1,0:T(8,128)(2,1)S(1)}, bf16[4,128,256]{2,1,0:T(8,128)(2,1)S(1)}, u32[]{:S(2)}, u32[]{:S(2)}) collective-permute-start(bf16[4,128,256]{2,1,0:T(8,128)(2,1)S(1)} %get-tuple-element.28), channel_id=1, source_target_pairs={{0,2},{1,7},{2,4},{3,1},{4,6},{5,3},{6,0},{7,5},{8,10},{9,15},{10,... | collective-permute-start | bytes 786440 | tf_op jit(solution)/shard_map/ppermute | solution.py:36
  56.4 0.0 copy-start
  56.4 0.0 copy-start.1
  56.4 2.2 %collective-permute-start.3 = (bf16[4,128,256]{2,1,0:T(8,128)(2,1)S(1)}, bf16[4,128,256]{2,1,0:T(8,128)(2,1)S(1)}, u32[]{:S(2)}, u32[]{:S(2)}) collective-permute-start(bf16[4,128,256]{2,1,0:T(8,128)(2,1)S(1)} %get-tuple-element.29), channel_id=1, source_target_pairs={{0,6},{1,3},{2,0},{3,5},{4,2},{5,7},{6,4},{7,1},{8,14},{9,11},{10,... | collective-permute-start | bytes 786440 | tf_op jit(solution)/shard_map/ppermute | solution.py:36
  58.6 2.3 %turn.1.v = bf16[128,128,128]{2,1,0:T(8,128)(2,1)S(1)} custom-call(s32[3,128]{1,0:T(4,128)S(1)} %pad_add_fusion.block, bf16[1,1,128,128,128]{4,3,2,1,0:T(8,128)(2,1)} %v.5), custom_call_target="tpu_custom_call" | custom-call | bytes 10485760 | tf_op jit(solution)/shard_map/turn/pallas_call | solution.py:209
  60.9 0.0 collective-permute-done.1
  60.9 5.7 %collective-permute-done.2 = bf16[4,128,256]{2,1,0:T(8,128)(2,1)S(1)} collective-permute-done((bf16[4,128,256]{2,1,0:T(8,128)(2,1)S(1)}, bf16[4,128,256]{2,1,0:T(8,128)(2,1)S(1)}, u32[]{:S(2)}, u32[]{:S(2)}) %collective-permute-start.2) | collective-permute-done | bytes 262176 | tf_op jit(solution)/shard_map/ppermute | solution.py:36
  66.6 0.0 collective-permute-done.3
  66.6 0.1 add_convert_fusion
  66.7 27.5 %all_to_all.26.got = bf16[4,128,256]{2,1,0:T(8,128)(2,1)S(1)} all-to-all(bf16[4,128,256]{2,1,0:T(8,128)(2,1)S(1)} %add_convert_fusion), channel_id=1, replica_groups={{0,8,16,24},{1,9,17,25},{2,10,18,26},{3,11,19,27},{4,12,20,28},{5,13,21..., dimensions={0} | all-to-all | bytes 524288 | tf_op jit(solution)/shard_map/all_to_all | solution.py:63
  94.2 0.0 copy-done
  94.2 0.0 copy-done.1
  94.2 0.8 middle.1
  95.0 15.4 %all_to_all.27.parts = bf16[16,16,256]{2,1,0:T(8,128)(2,1)S(1)} all-to-all(bf16[16,16,256]{2,1,0:T(8,128)(2,1)S(1)} %get-tuple-element.34), channel_id=1, replica_groups=mesh['row'=16,'col'=32] {'row'}, dimensions={0} | all-to-all | bytes 262144 | tf_op jit(solution)/shard_map/all_to_all | solution.py:53
  110.5 20.0 %all_to_all.28.got = bf16[4,144,256]{2,1,0:T(8,128)(2,1)S(1)} all-to-all(bf16[4,144,256]{2,1,0:T(8,128)(2,1)S(1)} %pack.1), channel_id=1, replica_groups={{0,8,16,24},{1,9,17,25},{2,10,18,26},{3,11,19,27},{4,12,20,28},{5,13,21..., dimensions={0} | all-to-all | bytes 589824 | tf_op jit(solution)/shard_map/all_to_all | solution.py:63
  130.6 3.7 %collective-permute-start.6 = (bf16[528,256]{1,0:T(8,128)(2,1)S(1)}, bf16[528,256]{1,0:T(8,128)(2,1)S(1)}, u32[]{:S(2)}, u32[]{:S(2)}) collective-permute-start(bf16[528,256]{1,0:T(8,128)(2,1)S(1)} %fold.1.stays), channel_id=1, source_target_pairs={{0,4},{1,5},{2,6},{3,7},{4,0},{5,1},{6,2},{7,3},{8,12},{9,13},{10,... | collective-permute-start | bytes 811016 | tf_op jit(solution)/shard_map/ppermute | solution.py:36
  134.2 1.9 collective-permute-start.5
  136.2 4.6 %collective-permute-start.4 = (bf16[528,256]{1,0:T(8,128)(2,1)S(1)}, bf16[528,256]{1,0:T(8,128)(2,1)S(1)}, u32[]{:S(2)}, u32[]{:S(2)}) collective-permute-start(bf16[528,256]{1,0:T(8,128)(2,1)S(1)} %fold.1.stays), channel_id=1, source_target_pairs={{0,2},{1,7},{2,4},{3,1},{4,6},{5,3},{6,0},{7,5},{8,10},{9,15},{10,... | collective-permute-start | bytes 811016 | tf_op jit(solution)/shard_map/ppermute | solution.py:36
  140.8 0.0 collective-permute-done.6.two
  140.8 5.0 %collective-permute-done.5.second = bf16[528,256]{1,0:T(8,128)(2,1)S(1)} collective-permute-done((bf16[528,256]{1,0:T(8,128)(2,1)S(1)}, bf16[528,256]{1,0:T(8,128)(2,1)S(1)}, u32[]{:S(2)}, u32[]{:S(2)}) %collective-permute-start.5) | collective-permute-done | bytes 270368 | tf_op jit(solution)/shard_map/ppermute | solution.py:36
  145.7 0.8 collective-permute-done.4.first
  146.5 0.6 collect.1.grads.mine
  147.2 7.6 %collective-permute-start.7 = (bf16[2064,256]{1,0:T(8,128)(2,1)S(1)}, bf16[2064,256]{1,0:T(8,128)(2,1)S(1)}, u32[]{:S(2)}, u32[]{:S(2)}) collective-permute-start(bf16[2064,256]{1,0:T(8,128)(2,1)S(1)} %collect.1.grads.mine), channel_id=1, source_target_pairs={{0,1},{1,0},{2,3},{3,2},{4,5},{5,4},{6,7},{7,6},{8,9},{9,8},{10,11... | collective-permute-start | bytes 3170312 | tf_op jit(solution)/shard_map/ppermute | solution.py:49
  154.8 1.9 %first.1.start = f32[16,128,256]{2,1,0:T(8,128)S(1)} custom-call(s32[3,128]{1,0:T(4,128)S(1)} %pad_add_fusion.block, bf16[128,128,128]{2,1,0:T(8,128)(2,1)S(1)} %turn.1.v, bf16[2064,256]{1,0:T(8,128)(2,1)S(1)} %collect.1.grads.mine), custom_call_target="tpu_custom_call" | custom-call | flops 536870912 | bytes 8388608 | tf_op jit(solution)/shard_map/first/pallas_call | solution.py:354
  156.8 0.3 collective-permute-done.7.grads
  157.1 1.9 second.1
  159.0 2.7 %collective-permute-start.8 = (bf16[528,256]{1,0:T(8,128)(2,1)S(1)}, bf16[528,256]{1,0:T(8,128)(2,1)S(1)}, u32[]{:S(2)}, u32[]{:S(2)}) collective-permute-start(bf16[528,256]{1,0:T(8,128)(2,1)S(1)} %get-tuple-element.36), channel_id=1, source_target_pairs={{0,64},{1,65},{2,66},{3,67},{4,68},{5,69},{6,70},{7,71},{8,72},{9,... | collective-permute-start | bytes 811016 | tf_op jit(solution)/shard_map/ppermute | solution.py:45
  161.7 3.2 %collective-permute-start.9 = (bf16[528,256]{1,0:T(8,128)(2,1)S(1)}, bf16[528,256]{1,0:T(8,128)(2,1)S(1)}, u32[]{:S(2)}, u32[]{:S(2)}) collective-permute-start(bf16[528,256]{1,0:T(8,128)(2,1)S(1)} %get-tuple-element.37), channel_id=1, source_target_pairs={{0,32},{1,97},{2,34},{3,99},{4,36},{5,101},{6,38},{7,103},{8,40},{... | collective-permute-start | bytes 811016 | tf_op jit(solution)/shard_map/ppermute | solution.py:45
  165.0 2.1 %collective-permute-start.10 = (bf16[528,256]{1,0:T(8,128)(2,1)S(1)}, bf16[528,256]{1,0:T(8,128)(2,1)S(1)}, u32[]{:S(2)}, u32[]{:S(2)}) collective-permute-start(bf16[528,256]{1,0:T(8,128)(2,1)S(1)} %get-tuple-element.38), channel_id=1, source_target_pairs={{0,96},{1,33},{2,98},{3,35},{4,100},{5,37},{6,102},{7,39},{8,104},... | collective-permute-start | bytes 811016 | tf_op jit(solution)/shard_map/ppermute | solution.py:45
  167.0 3.6 %collective-permute-done.8.p1 = bf16[528,256]{1,0:T(8,128)(2,1)S(1)} collective-permute-done((bf16[528,256]{1,0:T(8,128)(2,1)S(1)}, bf16[528,256]{1,0:T(8,128)(2,1)S(1)}, u32[]{:S(2)}, u32[]{:S(2)}) %collective-permute-start.8) | collective-permute-done | bytes 270368 | tf_op jit(solution)/shard_map/ppermute | solution.py:45
  170.6 3.1 %collective-permute-done.9.p2 = bf16[528,256]{1,0:T(8,128)(2,1)S(1)} collective-permute-done((bf16[528,256]{1,0:T(8,128)(2,1)S(1)}, bf16[528,256]{1,0:T(8,128)(2,1)S(1)}, u32[]{:S(2)}, u32[]{:S(2)}) %collective-permute-start.9) | collective-permute-done | bytes 270368 | tf_op jit(solution)/shard_map/ppermute | solution.py:45
  173.7 2.9 %collective-permute-done.10.p3 = bf16[528,256]{1,0:T(8,128)(2,1)S(1)} collective-permute-done((bf16[528,256]{1,0:T(8,128)(2,1)S(1)}, bf16[528,256]{1,0:T(8,128)(2,1)S(1)}, u32[]{:S(2)}, u32[]{:S(2)}) %collective-permute-start.10) | collective-permute-done | bytes 270368 | tf_op jit(solution)/shard_map/ppermute | solution.py:45
  176.6 0.7 merge.1
  177.3 16.0 %all_to_all.29.got = bf16[4,192,256]{2,1,0:T(8,128)(2,1)S(1)} all-to-all(bf16[4,192,256]{2,1,0:T(8,128)(2,1)S(1)} %merge.1), channel_id=1, replica_groups={{0,128,256,384},{32,160,288,416},{64,192,320,448},{96,224,352,480},{1,1..., dimensions={0} | all-to-all | bytes 786432 | tf_op jit(solution)/shard_map/all_to_all | solution.py:58
  193.3 0.8 last.1
  (3 shorter events, 0.1 us)
Async XLA Ops:
  39.7 7.0 %collective-permute-start = (bf16[16,128,256]{2,1,0:T(8,128)(2,1)S(1)}, bf16[16,128,256]{2,1,0:T(8,128)(2,1)S(1)}, u32[]{:S(2)}, u32[]{:S(2)}) collective-permute-start(bf16[16,128,256]{2,1,0:T(8,128)(2,1)S(1)} %forward.3), channel_id=1, source_target_pairs={{0,1},{1,0},{2,3},{3,2},{4,5},{5,4},{6,7},{7,6},{8,9},{9,8},{10,11... | collective-permute-start | bytes 3145736 | tf_op jit(solution)/shard_map/ppermute | solution.py:49
  47.5 13.4 %collective-permute-start.1 = (bf16[4,128,256]{2,1,0:T(8,128)(2,1)S(1)}, bf16[4,128,256]{2,1,0:T(8,128)(2,1)S(1)}, u32[]{:S(2)}, u32[]{:S(2)}) collective-permute-start(bf16[4,128,256]{2,1,0:T(8,128)(2,1)S(1)} %get-tuple-element.27), channel_id=1, source_target_pairs={{0,4},{1,5},{2,6},{3,7},{4,0},{5,1},{6,2},{7,3},{8,12},{9,13},{10,... | collective-permute-start | bytes 786440 | tf_op jit(solution)/shard_map/ppermute | solution.py:36
  52.5 14.1 %collective-permute-start.2 = (bf16[4,128,256]{2,1,0:T(8,128)(2,1)S(1)}, bf16[4,128,256]{2,1,0:T(8,128)(2,1)S(1)}, u32[]{:S(2)}, u32[]{:S(2)}) collective-permute-start(bf16[4,128,256]{2,1,0:T(8,128)(2,1)S(1)} %get-tuple-element.28), channel_id=1, source_target_pairs={{0,2},{1,7},{2,4},{3,1},{4,6},{5,3},{6,0},{7,5},{8,10},{9,15},{10,... | collective-permute-start | bytes 786440 | tf_op jit(solution)/shard_map/ppermute | solution.py:36
  56.4 37.8 %copy-start = (bf16[256,256]{1,0:T(8,128)(2,1)S(1)}, bf16[256,256]{1,0:T(8,128)(2,1)}, u32[]{:S(2)}) copy-start(bf16[256,256]{1,0:T(8,128)(2,1)} %w.3) | copy-start | bytes 393220
  56.4 37.8 %copy-start.1 = (bf16[128,256]{1,0:T(8,128)(2,1)S(1)}, bf16[128,256]{1,0:T(8,128)(2,1)}, u32[]{:S(2)}) copy-start(bf16[128,256]{1,0:T(8,128)(2,1)} %cot.1) | copy-start | bytes 196612
  56.4 10.2 %collective-permute-start.3 = (bf16[4,128,256]{2,1,0:T(8,128)(2,1)S(1)}, bf16[4,128,256]{2,1,0:T(8,128)(2,1)S(1)}, u32[]{:S(2)}, u32[]{:S(2)}) collective-permute-start(bf16[4,128,256]{2,1,0:T(8,128)(2,1)S(1)} %get-tuple-element.29), channel_id=1, source_target_pairs={{0,6},{1,3},{2,0},{3,5},{4,2},{5,7},{6,4},{7,1},{8,14},{9,11},{10,... | collective-permute-start | bytes 786440 | tf_op jit(solution)/shard_map/ppermute | solution.py:36
  130.6 10.2 %collective-permute-start.6 = (bf16[528,256]{1,0:T(8,128)(2,1)S(1)}, bf16[528,256]{1,0:T(8,128)(2,1)S(1)}, u32[]{:S(2)}, u32[]{:S(2)}) collective-permute-start(bf16[528,256]{1,0:T(8,128)(2,1)S(1)} %fold.1.stays), channel_id=1, source_target_pairs={{0,4},{1,5},{2,6},{3,7},{4,0},{5,1},{6,2},{7,3},{8,12},{9,13},{10,... | collective-permute-start | bytes 811016 | tf_op jit(solution)/shard_map/ppermute | solution.py:36
  134.2 11.5 %collective-permute-start.5 = (bf16[528,256]{1,0:T(8,128)(2,1)S(1)}, bf16[528,256]{1,0:T(8,128)(2,1)S(1)}, u32[]{:S(2)}, u32[]{:S(2)}) collective-permute-start(bf16[528,256]{1,0:T(8,128)(2,1)S(1)} %fold.1.stays), channel_id=1, source_target_pairs={{0,6},{1,3},{2,0},{3,5},{4,2},{5,7},{6,4},{7,1},{8,14},{9,11},{10,... | collective-permute-start | bytes 811016 | tf_op jit(solution)/shard_map/ppermute | solution.py:36
  136.2 10.4 %collective-permute-start.4 = (bf16[528,256]{1,0:T(8,128)(2,1)S(1)}, bf16[528,256]{1,0:T(8,128)(2,1)S(1)}, u32[]{:S(2)}, u32[]{:S(2)}) collective-permute-start(bf16[528,256]{1,0:T(8,128)(2,1)S(1)} %fold.1.stays), channel_id=1, source_target_pairs={{0,2},{1,7},{2,4},{3,1},{4,6},{5,3},{6,0},{7,5},{8,10},{9,15},{10,... | collective-permute-start | bytes 811016 | tf_op jit(solution)/shard_map/ppermute | solution.py:36
  147.2 9.9 %collective-permute-start.7 = (bf16[2064,256]{1,0:T(8,128)(2,1)S(1)}, bf16[2064,256]{1,0:T(8,128)(2,1)S(1)}, u32[]{:S(2)}, u32[]{:S(2)}) collective-permute-start(bf16[2064,256]{1,0:T(8,128)(2,1)S(1)} %collect.1.grads.mine), channel_id=1, source_target_pairs={{0,1},{1,0},{2,3},{3,2},{4,5},{5,4},{6,7},{7,6},{8,9},{9,8},{10,11... | collective-permute-start | bytes 3170312 | tf_op jit(solution)/shard_map/ppermute | solution.py:49
  159.0 11.6 %collective-permute-start.8 = (bf16[528,256]{1,0:T(8,128)(2,1)S(1)}, bf16[528,256]{1,0:T(8,128)(2,1)S(1)}, u32[]{:S(2)}, u32[]{:S(2)}) collective-permute-start(bf16[528,256]{1,0:T(8,128)(2,1)S(1)} %get-tuple-element.36), channel_id=1, source_target_pairs={{0,64},{1,65},{2,66},{3,67},{4,68},{5,69},{6,70},{7,71},{8,72},{9,... | collective-permute-start | bytes 811016 | tf_op jit(solution)/shard_map/ppermute | solution.py:45
  161.7 12.0 %collective-permute-start.9 = (bf16[528,256]{1,0:T(8,128)(2,1)S(1)}, bf16[528,256]{1,0:T(8,128)(2,1)S(1)}, u32[]{:S(2)}, u32[]{:S(2)}) collective-permute-start(bf16[528,256]{1,0:T(8,128)(2,1)S(1)} %get-tuple-element.37), channel_id=1, source_target_pairs={{0,32},{1,97},{2,34},{3,99},{4,36},{5,101},{6,38},{7,103},{8,40},{... | collective-permute-start | bytes 811016 | tf_op jit(solution)/shard_map/ppermute | solution.py:45
  165.0 11.6 %collective-permute-start.10 = (bf16[528,256]{1,0:T(8,128)(2,1)S(1)}, bf16[528,256]{1,0:T(8,128)(2,1)S(1)}, u32[]{:S(2)}, u32[]{:S(2)}) collective-permute-start(bf16[528,256]{1,0:T(8,128)(2,1)S(1)} %get-tuple-element.38), channel_id=1, source_target_pairs={{0,96},{1,33},{2,98},{3,35},{4,100},{5,37},{6,102},{7,39},{8,104},... | collective-permute-start | bytes 811016 | tf_op jit(solution)/shard_map/ppermute | solution.py:45
